TPU v7x, 32 devices: a whole 2x2x4 slice. The times are simulated.
32 devices in a mesh: fsdp: 4 (over x, core), branch: 8 (over z, y).
Axes of the slice: x: 2, y: 2, z: 4, core: 2. Of those that a mesh axis runs over, the one named last changes fastest.
Arguments:
- hidden: bfloat16 [24, 128, 8192], P('branch', None, 'fsdp')
- parents: int32 [24], replicated, may hold values from -1 to 22, as said below
- lengths: int32 [24], replicated, may hold values from 32 to 128, as said below
- gain: float32 [8192], replicated, may hold values from 0.1 to 1.9
- w_query: bfloat16 [8192, 4096], P('branch', 'fsdp')
- w_key: bfloat16 [8192, 512], P('branch', 'fsdp')
- w_value: bfloat16 [8192, 512], P('branch', 'fsdp'), may hold values from -0.0625 to 0.0625
- query_bias: float32 [4096], P('fsdp'), may hold values from -4 to 4
- key_bias: float32 [512], P('fsdp'), may hold values from -4 to 4
- value_bias: float32 [512], P('fsdp'), may hold values from -4 to 4
Outputs:
- attended: bfloat16 [24, 128, 4096], P('branch', None, 'fsdp')
Inputs may be any that keep to these rules, and one draw needn't show every extreme that they name: parents[j] < j, and only block 0 has -1. Blocks k * 3 to k * 3 + 2 form span k. Block 0 of a span k > 0 hangs under one of the first 2 blocks of an earlier span, block 1 of every span under block 0 of that span, the last block of every span under the block before it, so each span is a chain of its three blocks. No block has more than 6 ancestors outside its span, and some block has exactly 6. `lengths`: blocks 0 and 1 of every span are full.
All inputs are finite; a program needn't handle non-finite values.
Results may differ from a plain program's by a relative error of at most 0.0042.
Values may be sent and summed in bfloat16 or wider, within the bound.
No kernel may reach another device: no remote copies, remote signals or barrier semaphores. Data moves between devices by JAX's collectives and lax.ppermute only.
A program may use at most 128 MiB of HBM per device.

v0:
```python
import math

import jax
import jax.numpy as jnp
from jax import lax
from jax.sharding import PartitionSpec as P

HD = 128
STEMS = 2


def rotate(vectors, position):
    half_size = vectors.shape[-1] // 2
    freq_index = jnp.arange(half_size).astype(vectors.dtype)
    freqs = jnp.exp(freq_index * (-2.0 * math.log(1000000.0) / vectors.shape[-1]))
    angles = position.astype(vectors.dtype)[:, None, None] * freqs[None, None, :]
    cosines = jnp.cos(angles)
    sines = jnp.sin(angles)
    front_half = vectors[..., :half_size]
    back_half = vectors[..., half_size:]
    return jnp.concatenate(
        [front_half * cosines - back_half * sines, back_half * cosines + front_half * sines], -1
    )


def shards(
    hidden, parents, lengths, gain, w_query, w_key, w_value, query_bias, key_bias, value_bias
):
    local_blocks = hidden.shape[0]
    block_len = hidden.shape[1]
    feature_part = hidden.shape[2]
    head_size = HD
    kv_local = w_key.shape[1] // head_size
    head_count = w_query.shape[1] // head_size
    token_count = local_blocks * block_len
    features = gain.shape[0]
    device = lax.axis_index("branch")
    branch_count = lax.axis_size("branch")
    far_slots = STEMS * (branch_count.bit_length() - 1)
    first_block = device * local_blocks
    shard_tokens = hidden.reshape(token_count, feature_part).astype(jnp.float32)
    square_total = lax.psum(jnp.sum(shard_tokens * shard_tokens, -1), "fsdp")
    gain_part = lax.dynamic_slice_in_dim(gain, lax.axis_index("fsdp") * feature_part, feature_part)
    inverse = lax.rsqrt(square_total / features + 1e-06)
    normed_part = (shard_tokens * inverse[:, None] * gain_part).astype(jnp.bfloat16)
    normed_whole = lax.all_gather(
        normed_part.reshape(local_blocks, block_len, feature_part), "fsdp", axis=2, tiled=True
    )
    normed = normed_whole.reshape(token_count, features)
    pieces = (
        lax.all_gather(w_query, "branch", axis=0, tiled=True),
        lax.all_gather(w_key, "branch", axis=0, tiled=True),
        lax.all_gather(w_value, "branch", axis=0, tiled=True),
    )
    query_sum, key_sum, value_sum = tuple(
        (jnp.dot(normed, piece, preferred_element_type=jnp.float32) for piece in pieces)
    )
    query = query_sum + query_bias
    key = key_sum + key_bias
    value = value_sum + value_bias
    cursor = parents[first_block]
    chain_ids = []
    for level in range(far_slots):
        chain_ids.append(cursor)
        cursor = jnp.where(cursor >= 0, parents[jnp.maximum(cursor, 0)], -1)
    far_ids = jnp.stack(chain_ids)
    far_live = far_ids >= 0
    far_total = jnp.sum(far_live.astype(jnp.int32))
    own_parents = lax.dynamic_slice_in_dim(parents, first_block, local_blocks) - first_block
    own_parents = jnp.where(own_parents >= 0, own_parents, -1)
    block_ids = jnp.arange(local_blocks, dtype=jnp.int32)

    def climb(level, carry):
        walker, lineage = carry
        walker = jnp.where(walker >= 0, own_parents[jnp.maximum(walker, 0)], -1)
        return (walker, lineage | (block_ids[None, :] == walker[:, None]))

    unused, lineage = lax.fori_loop(
        0, local_blocks, climb, (block_ids, block_ids[None, :] == block_ids[:, None])
    )
    depths = far_total + jnp.sum(lineage.astype(jnp.int32), 1) - 1
    token_ids = jnp.arange(block_len, dtype=jnp.int32)
    position = (depths[:, None] * block_len + token_ids[None, :]).reshape(-1)
    rotated_query = rotate(query.reshape(token_count, head_count, head_size), position).astype(
        jnp.bfloat16
    )
    rotated_key = rotate(key.reshape(token_count, kv_local, head_size), position).astype(
        jnp.bfloat16
    )
    value_bf16 = value.reshape(token_count, kv_local, head_size).astype(jnp.bfloat16)
    stem_keys = rotated_key.reshape(local_blocks, block_len, kv_local, head_size)[:STEMS]
    stem_values = value_bf16.reshape(local_blocks, block_len, kv_local, head_size)[:STEMS]
    all_keys, all_values = (
        lax.all_gather(stem_keys, "branch", axis=0, tiled=True),
        lax.all_gather(stem_values, "branch", axis=0, tiled=True),
    )
    safe_ids = jnp.maximum(far_ids, 0)
    stem_slot = safe_ids // local_blocks * STEMS + safe_ids % local_blocks
    far_keys = all_keys[stem_slot].reshape(far_slots * block_len, kv_local, head_size)
    far_values = all_values[stem_slot].reshape(far_slots * block_len, kv_local, head_size)
    far_ok = (far_live[:, None] & (token_ids[None, :] < lengths[safe_ids][:, None])).reshape(-1)
    own_lengths = lax.dynamic_slice_in_dim(lengths, first_block, local_blocks)
    keys_joined = jnp.concatenate([far_keys, rotated_key], 0)
    values_joined = jnp.concatenate([far_values, value_bf16], 0)
    queries = rotated_query.reshape(
        local_blocks, block_len, kv_local, head_count // kv_local, head_size
    )
    scale = head_size ** (-0.5)

    def attend(block):
        query_block = queries[block]
        near_ok = lineage[block][:, None] & (token_ids[None, :] < own_lengths[:, None])
        causal = (block_ids[None, :, None] != block) | (
            token_ids[None, None, :] <= token_ids[:, None, None]
        )
        visible = jnp.concatenate(
            [
                jnp.broadcast_to(far_ok[None, :], (block_len, far_ok.shape[0])),
                (near_ok[None] & causal).reshape(block_len, -1),
            ],
            1,
        )
        scores = (
            jnp.einsum(
                "tkgh,skh->kgts", query_block, keys_joined, preferred_element_type=jnp.float32
            )
            * scale
        )
        scores = jnp.where(visible[None, None], scores, -1e30)
        row_max = jnp.max(scores, -1, keepdims=True)
        exps = jnp.exp(scores - row_max)
        weights = (exps / jnp.sum(exps, -1, keepdims=True)).astype(jnp.bfloat16)
        output = jnp.einsum(
            "kgts,skh->tkgh", weights, values_joined, preferred_element_type=jnp.float32
        )
        output = jnp.where((token_ids < own_lengths[block])[:, None, None, None], output, 0.0)
        return output.reshape(block_len, head_count * head_size).astype(jnp.bfloat16)

    return lax.map(attend, block_ids)


def solution(mesh):
    return jax.shard_map(
        shards,
        mesh=mesh,
        in_specs=(
            P("branch", None, "fsdp"),
            P(),
            P(),
            P(),
            P("branch", "fsdp"),
            P("branch", "fsdp"),
            P("branch", "fsdp"),
            P("fsdp"),
            P("fsdp"),
            P("fsdp"),
        ),
        out_specs=P("branch", None, "fsdp"),
        check_vma=False,
    )
```

profile of v0, /device:TPU:0, one launch (start us, length us, event | category | flops | bytes accessed | tf_op | source)
XLA Modules:
  0.0 446.3 jit_solution(14245924669016800723)
XLA Ops:
  6.5 0.7 all-gather.9.cloned.1.call-update
  7.3 0.7 dynamic_slice.50
  8.0 1.8 fusion.30
  9.8 8.3 %psum.7 = f32[384]{0:T(512)S(1)} all-reduce(f32[384]{0:T(512)S(1)} %bitcast.171), channel_id=1, replica_groups=mesh['fsdp'=4,'branch'=8] {'fsdp'}, use_global_device_ids=true, to_apply=%region_1.0 | all-reduce | flops 384 | bytes 3072 | tf_op jit(solution)/shard_map/psum | solution.py:42
  18.2 3.1 fusion.32
  33.4 2.2 while.25
  36.5 1.1 multiply_cosine_fusion.1
  37.5 24.0 %all-gather.9.cloned.1.call-done = bf16[8192,128]{1,0:T(8,128)(2,1)} async-done(((bf16[1024,128]{1,0:T(8,128)(2,1)}), bf16[8192,128]{1,0:T(8,128)(2,1)}) %all-gather.9.cloned.1.call-update) | async-done | bytes 2097168 | tf_op jit(solution)/shard_map/all_gather | solution.py:52
  61.5 46.5 %all-gather.5.cloned.1.call-done = bf16[3,128,8192]{2,1,0:T(8,128)(2,1)} async-done(((bf16[3,128,2048]{2,1,0:T(8,128)(2,1)}), bf16[3,128,8192]{2,1,0:T(8,128)(2,1)}) %all-gather.5.cloned.1.call-update) | async-done | bytes 6291472 | tf_op jit(solution)/shard_map/all_gather | solution.py:46
  108.0 5.3 %fusion.33 = f32[384,1,128]{0,2,1:T(8,128)S(1)} fusion(bf16[384,8192]{1,0:T(8,128)(2,1)} %bitcast.159, bf16[8192,128]{1,0:T(8,128)(2,1)} %all-gather.9.cloned.1.call-done, f32[128]{0:T(128)S(1)} %copy-done.3), kind=kOutput, calls=%fused_computation.52 | convolution fusion | flops 805355520 | bytes 8585728 | tf_op jit(solution)/shard_map/dot_general | solution.py:56
  114.0 45.4 %all-gather.11.cloned.1.call-done = bf16[8192,128]{1,0:T(8,128)(2,1)} async-done(((bf16[1024,128]{1,0:T(8,128)(2,1)}), bf16[8192,128]{1,0:T(8,128)(2,1)}) %all-gather.11.cloned.1.call-update) | async-done | bytes 2097168 | tf_op jit(solution)/shard_map/all_gather | solution.py:53
  159.4 5.2 %fusion.34 = bf16[384,128]{1,0:T(8,128)(2,1)S(1)} fusion(bf16[384,8192]{1,0:T(8,128)(2,1)} %bitcast.160, bf16[8192,128]{1,0:T(8,128)(2,1)} %all-gather.11.cloned.1.call-done, f32[128]{0:T(128)S(1)} %copy-done.2), kind=kOutput, calls=%fused_computation.53 | convolution fusion | flops 805404672 | bytes 8487424 | tf_op jit(solution)/shard_map/dot_general | solution.py:56
  164.7 33.5 %all_gather.21 = bf16[16,128,1,128]{3,1,2,0:T(8,128)(2,1)S(1)} all-gather(bf16[2,128,1,128]{3,1,2,0:T(8,128)(2,1)S(1)} %bitcast.169), channel_id=1, replica_groups=mesh['fsdp'=4,'branch'=8] {'branch'}, dimensions={0}, use_global_device_ids=true | all-gather | bytes 589824 | tf_op jit(solution)/shard_map/all_gather | solution.py:94
  198.8 33.5 %all_gather.23 = bf16[16,128,1,128]{3,1,2,0:T(8,128)(2,1)S(1)} all-gather(bf16[2,128,1,128]{3,1,2,0:T(8,128)(2,1)S(1)} %bitcast.170), channel_id=1, replica_groups=mesh['fsdp'=4,'branch'=8] {'branch'}, dimensions={0}, use_global_device_ids=true | all-gather | bytes 589824 | tf_op jit(solution)/shard_map/all_gather | solution.py:95
  233.0 0.9 copy.31
  233.9 161.8 %all-gather.7.cloned.1.call-done = bf16[8192,1024]{1,0:T(8,128)(2,1)} async-done(((bf16[1024,1024]{1,0:T(8,128)(2,1)}), bf16[8192,1024]{1,0:T(8,128)(2,1)}) %all-gather.7.cloned.1.call-update) | async-done | bytes 16777232 | tf_op jit(solution)/shard_map/all_gather | solution.py:51
  395.7 12.0 %convolution_add_fusion = f32[384,1024]{1,0:T(8,128)S(1)} fusion(bf16[384,8192]{1,0:T(8,128)(2,1)} %bitcast.161, bf16[8192,1024]{1,0:T(8,128)(2,1)} %all-gather.7.cloned.1.call-done, f32[1024]{0:T(1024)S(1)} %copy-done.5), kind=kOutput, calls=%fused_computation.49 | convolution fusion | flops 6442844160 | bytes 24645632 | tf_op jit(solution)/shard_map/dot_general | solution.py:56
  408.2 1.2 subtract_convert_fusion
  410.3 0.7 copy.30
  411.0 28.7 %while.26 = (s32[]{:T(128)}, bf16[3,128,1024]{2,1,0:T(8,128)(2,1)}, s32[3]{0:T(128)S(1)}, s32[3]{0:T(128)S(1)}, pred[3,3]{1,0:T(4,128)(4,1)S(1)}, /*index=5*/bf1...) while((s32[]{:T(128)}, bf16[3,128,1024]{2,1,0:T(8,128)(2,1)}, ...), condition=%wide.region_9.10_spmd.clone.clone, body=%wide.region_6.9_spmd.clone.clone.sunk | while | flops 616300928 | bytes 17167636 | solution.py:139
  414.9 1.1 fusion.67
  416.0 1.1 fusion.68
  418.4 1.4 fusion.69
  419.9 0.7 constant_dynamic-update-slice_fusion.2
  424.4 1.1 fusion.67
  425.6 1.1 fusion.68
  427.9 1.4 fusion.69
  429.5 0.7 constant_dynamic-update-slice_fusion.2
  434.0 1.1 fusion.67
  435.1 1.1 fusion.68
  437.5 1.4 fusion.69
  439.0 0.7 constant_dynamic-update-slice_fusion.2
  (118 shorter events, 24.0 us)
Async XLA Ops:
  6.5 16.0 %copy-start.4 = (s32[24]{0:T(128)S(1)}, s32[24]{0:T(128)}, u32[]{:S(2)}) copy-start(s32[24]{0:T(128)} %param.15) | copy-start | bytes 292
  6.5 24.7 %copy-start = (s32[24]{0:T(128)S(1)}, s32[24]{0:T(128)}, u32[]{:S(2)}) copy-start(s32[24]{0:T(128)} %param.16) | copy-start | bytes 292
  6.5 55.0 %all-gather.9.cloned.1.call-start = ((), (), s32[]{:S(2)}) async-start(), calls=%async_computation.2 | async-start | bytes 2359296 | tf_op jit(solution)/shard_map/all_gather | solution.py:52
  7.3 100.7 %all-gather.5.cloned.1.call-start = ((), (), s32[]{:S(2)}) async-start(), calls=%async_computation | async-start | bytes 7864320 | tf_op jit(solution)/shard_map/all_gather | solution.py:46
  18.2 89.8 %copy-start.3 = (f32[128]{0:T(128)S(1)}, f32[128]{0:T(128)}, u32[]{:S(2)}) copy-start(f32[128]{0:T(128)} %param.22) | copy-start | bytes 1540
  21.2 138.2 %all-gather.11.cloned.1.call-start = ((), (), s32[]{:S(2)}) async-start(), calls=%async_computation.3 | async-start | bytes 2359296 | tf_op jit(solution)/shard_map/all_gather | solution.py:53
  22.0 373.7 %all-gather.7.cloned.1.call-start = ((), (), s32[]{:S(2)}) async-start(), calls=%async_computation.1 | async-start | bytes 18874368 | tf_op jit(solution)/shard_map/all_gather | solution.py:51
  108.0 51.5 %copy-start.2 = (f32[128]{0:T(128)S(1)}, f32[128]{0:T(128)}, u32[]{:S(2)}) copy-start(f32[128]{0:T(128)} %param.23) | copy-start | bytes 1540
  114.0 281.7 %copy-start.5 = (f32[1024]{0:T(1024)S(1)}, f32[1024]{0:T(1024)}, u32[]{:S(2)}) copy-start(f32[1024]{0:T(1024)} %param.21) | copy-start | bytes 12292
  408.2 2.8 copy-start.1
Sparse Core Ops, SparseCore 0:
  9.5 51.9 all-gather.8
  63.1 44.8 all-gather.4
  110.1 49.2 all-gather.10
  161.4 234.2 all-gather.6
where the time goes:
time: 447 us; the launch traced here: 446 us
  waiting for transfers between devices  280 us (63%)
  blocking collectives  75.4 us (17%)
  matrix products  30.1 us (7%)
  local copies, waits for them, and re-layouts  19.3 us (4%)
  other arithmetic  18.3 us (4%)
  between operations  17.7 us (4%)
  loops' own time  5.79 us (1%)
    all_gather x1, waiting for transfers between devices, shards(): lax.all_gather(w_query, 'branch', axis=0, tiled=True)  162 us
    all_gather x1, waiting for transfers between devices, shards(): lax.all_gather(normed_part.reshape(local_blocks, block_len, feature_part)...  46.5 us
    all_gather x1, waiting for transfers between devices, shards(): lax.all_gather(w_value, 'branch', axis=0, tiled=True)  45.4 us
    all_gather x1, blocking collectives, shards(): lax.all_gather(stem_values, 'branch', axis=0, tiled=True)  33.5 us
    all_gather x1, blocking collectives, shards(): lax.all_gather(stem_keys, 'branch', axis=0, tiled=True)  33.5 us
    all_gather x1, waiting for transfers between devices, shards(): lax.all_gather(w_key, 'branch', axis=0, tiled=True)  24 us
    dot_general x3, matrix products, shards(): jnp.dot(normed, piece, preferred_element_type=jnp.float32)  22.6 us
  transfers between devices with their start and end apart: 4, of which 4 were waited for; matrix products, arithmetic and copies ran while one was open for 7% of the time, Pallas kernels for 0%

commit v1 on v0

v1 whole, which is shorter than its diff:
```python
import functools
import math

import jax
import jax.numpy as jnp
from jax import lax
from jax.experimental import pallas as pl
from jax.experimental.pallas import tpu as pltpu
from jax.sharding import PartitionSpec as P

HD = 128
STEMS = 2
THETA = 1000000.0
NEG = -1e30


def bits_of(count):
    return count.bit_length() - 1


def far_chain(parents_ref, first_block, far_slots):
    cursor = parents_ref[first_block]
    ids = []
    total = jnp.int32(0)
    for level in range(far_slots):
        ids.append(cursor)
        total = total + jnp.where(cursor >= 0, 1, 0)
        above = parents_ref[jnp.maximum(cursor, 0)]
        cursor = jnp.where(cursor >= 0, above, -1)
    return ids, total


def merge(right_ref, left_ref, own, inverse_ref, bias):
    total = own + right_ref[...].astype(jnp.float32) + left_ref[...].astype(jnp.float32)
    inverse = inverse_ref[...]
    scaled = jnp.where(inverse > 0, total * inverse, 0.0)
    return scaled + bias


def turn(vectors, cos, sin):
    half = vectors.shape[-1] // 2
    return vectors * cos + pltpu.roll(vectors, half, 1) * sin


def kv_kernel(
    far_slots, block_len, meta_ref, parents_ref, right_ref, left_ref, own_ref, inverse_ref,
    bias_ref, kv_ref, cos_ref, sin_ref,
):
    tokens = kv_ref.shape[0]
    blocks = meta_ref[2]
    first_block = meta_ref[1] * blocks
    unused, far_total = far_chain(parents_ref, first_block, far_slots)
    rows = lax.broadcasted_iota(jnp.int32, (tokens, HD), 0)
    lanes = lax.broadcasted_iota(jnp.int32, (tokens, HD), 1)
    front = lanes < HD // 2
    pair = jnp.where(front, lanes, lanes - HD // 2).astype(jnp.float32)
    freqs = jnp.exp(pair * (-2.0 * math.log(THETA) / HD))
    angles = (rows + far_total * block_len).astype(jnp.float32) * freqs
    cos = jnp.cos(angles)
    sin = jnp.sin(angles)
    sin = jnp.where(front, -sin, sin)
    cos_ref[...] = cos
    sin_ref[...] = sin
    inverse = inverse_ref[...]
    total = own_ref[0] + right_ref[...].astype(jnp.float32) + left_ref[...].astype(jnp.float32)
    key = jnp.where(inverse > 0, total[:, :HD] * inverse, 0.0) + bias_ref[:, :HD]
    value = jnp.where(inverse > 0, total[:, HD:] * inverse, 0.0) + bias_ref[:, HD:]
    kv_ref[:, :HD] = turn(key, cos, sin).astype(jnp.bfloat16)
    kv_ref[:, HD:] = value.astype(jnp.bfloat16)


def attend_kernel(
    far_slots, blocks, meta_ref, parents_ref, lengths_ref, right_ref, left_ref, own_ref,
    inverse_ref, bias_ref, cos_ref, sin_ref, kv_ref, stems_ref, out_ref, far_key, far_value,
    far_mask,
):
    tokens = kv_ref.shape[0]
    block_len = tokens // blocks
    device = meta_ref[1]
    first_block = device * blocks

    @pl.when(pl.program_id(0) == 0)
    def _():
        ids, unused = far_chain(parents_ref, first_block, far_slots)
        for level in range(far_slots):
            live = ids[level] >= 0
            safe = jnp.maximum(ids[level], 0)
            owner = lax.div(safe, jnp.int32(blocks))
            inner = lax.rem(safe, jnp.int32(blocks))
            where = lax.bitwise_xor(owner, device)
            start = pl.multiple_of(inner * block_len, block_len)
            here = pl.ds(level * block_len, block_len)
            far_key[here, :] = stems_ref[where, pl.ds(start, block_len), :HD]
            far_value[here, :] = stems_ref[where, pl.ds(start, block_len), HD:]
            far_mask[:, here] = jnp.broadcast_to(jnp.where(live, 0.0, NEG), (8, block_len))

    query = merge(right_ref, left_ref, own_ref[0], inverse_ref, bias_ref[...])
    query = turn(query, cos_ref[...], sin_ref[...]).astype(jnp.bfloat16)
    factor = HD ** (-0.5) * math.log2(math.e)
    contract = (((1,), (1,)), ((), ()))
    row = lax.broadcasted_iota(jnp.int32, (block_len, block_len), 0)
    column = lax.broadcasted_iota(jnp.int32, (block_len, block_len), 1)
    for block in range(blocks):
        here = slice(block * block_len, (block + 1) * block_len)
        query_block = query[here]
        far = lax.dot_general(
            query_block, far_key[...], contract, preferred_element_type=jnp.float32
        )
        far = far + far_mask[0:1, :]
        parts = [far]
        for other in range(block + 1):
            near = lax.dot_general(
                query_block,
                kv_ref[other * block_len : (other + 1) * block_len, :HD],
                contract,
                preferred_element_type=jnp.float32,
            )
            if other == block or other >= STEMS:
                seen = column < lengths_ref[first_block + other]
                if other == block:
                    seen = seen & (column <= row)
                near = jnp.where(seen, near, NEG)
            parts.append(near)
        peak = functools.reduce(jnp.maximum, [jnp.max(part, -1, keepdims=True) for part in parts])
        peak = peak * factor
        exps = [jnp.exp2(part * factor - peak) for part in parts]
        total = functools.reduce(jnp.add, [jnp.sum(part, -1, keepdims=True) for part in exps])
        output = jnp.dot(
            exps[0].astype(jnp.bfloat16), far_value[...], preferred_element_type=jnp.float32
        )
        for other in range(block + 1):
            output += jnp.dot(
                exps[1 + other].astype(jnp.bfloat16),
                kv_ref[other * block_len : (other + 1) * block_len, HD:],
                preferred_element_type=jnp.float32,
            )
        output = output / total
        if block >= STEMS:
            output = jnp.where(row[:, :1] < lengths_ref[first_block + block], output, 0.0)
        out_ref[here, :] = output.astype(jnp.bfloat16)


def shards(
    hidden, parents, lengths, gain, w_query, w_key, w_value, query_bias, key_bias, value_bias
):
    blocks, block_len, feature_part = hidden.shape
    tokens = blocks * block_len
    features = gain.shape[0]
    rows = w_query.shape[0]
    columns = w_query.shape[1]
    head_count = columns // HD
    lines = lax.axis_size("fsdp")
    branches = lax.axis_size("branch")
    groups = branches // lines
    far_slots = STEMS * bits_of(branches)
    part = lax.axis_index("fsdp")
    device = lax.axis_index("branch")
    member = device % groups
    level = device // groups
    bf16 = jnp.bfloat16
    f32 = jnp.float32

    def swap(array, axis, bit):
        size = lax.axis_size(axis)
        return lax.ppermute(array, axis, [(i, i ^ bit) for i in range(size)])

    w_kv = jnp.concatenate([w_key, w_value], 1)
    query_chunks = 2
    width = columns // query_chunks
    w_chunks = [w_kv] + [
        lax.slice_in_dim(w_query, c * width, (c + 1) * width, axis=1) for c in range(query_chunks)
    ]
    w_rows = [
        [chunk] + [swap(chunk, "branch", j) for j in range(1, groups)] for chunk in w_chunks
    ]

    raw = hidden.reshape(tokens, feature_part)
    pieces = []
    for j in range(groups):
        start = (member ^ j) * rows
        gain_here = lax.dynamic_slice_in_dim(gain, part * feature_part + start, rows)
        piece = lax.dynamic_slice_in_dim(raw, start, rows, axis=1).astype(f32) * gain_here
        pieces.append(piece.astype(bf16))
    scaled = jnp.concatenate(pieces, 1)

    half_lines = lines // 2
    shift = bits_of(half_lines)

    def landing(z, feature):
        return ((z ^ feature) & 1) * half_lines + (z >> 1)

    exchange = []
    for z in range(lines):
        for g in range(groups):
            for feature in range(lines):
                source = feature * branches + z * groups + g
                target = landing(z, feature) * branches + feature * groups + g
                exchange.append((source, target))
    halves = 2
    span = tokens // halves
    gathered = []
    for h in range(halves):
        sent = lax.slice_in_dim(scaled, h * span, (h + 1) * span, axis=0)
        held = {0: lax.ppermute(sent, ("fsdp", "branch"), exchange)}
        bit = half_lines
        while bit:
            for j in list(held):
                held[j | bit] = swap(held[j], "fsdp", bit)
            bit //= 2

        order = [None] * lines
        for j in range(lines):
            order[((j & (half_lines - 1)) << 1) | (j >> shift)] = held[j]
        gathered.append(jnp.stack(order))
    base = ((part & (half_lines - 1)) << 1) | ((part >> shift) ^ (level & 1))
    everything = jnp.concatenate(gathered, 1).reshape(lines * tokens, feature_part)

    squares = jnp.sum(jnp.square(raw.astype(f32)), -1).reshape(blocks, block_len)
    bit = 1
    while bit < lines:
        squares = squares + swap(squares, "fsdp", bit)
        bit *= 2
    inverse = lax.rsqrt(squares / features + 1e-06).reshape(tokens)
    inverse = jnp.broadcast_to(inverse[:, None], (tokens, HD))

    def product(chunk):
        total = None
        for j in range(groups):
            term = jnp.dot(
                everything[:, j * rows : (j + 1) * rows], chunk[j], preferred_element_type=f32
            )
            total = term if total is None else total + term
        return total.reshape(lines, tokens, -1)

    up = [[((z * groups + g), (z + 1) * groups + g) for z in range(s + 1) for g in range(groups)]
          for s in range(lines - 1)]
    down = [[((lines - 1 - z) * groups + g, (lines - 2 - z) * groups + g)
             for z in range(s + 1) for g in range(groups)] for s in range(lines - 1)]

    def reduce_line(partial):
        def of(target):
            target = jnp.clip(target, 0, lines - 1)
            return lax.dynamic_index_in_dim(partial, target ^ base, 0, keepdims=False)

        right = left = None
        for s in range(lines - 1):
            ahead = of(level + (lines - 1 - s))
            behind = of(level - (lines - 1 - s))
            if s:
                ahead = ahead + right.astype(f32)
                behind = behind + left.astype(f32)
            right = lax.ppermute(ahead.astype(bf16), "branch", up[s])
            left = lax.ppermute(behind.astype(bf16), "branch", down[s])
        return right, left

    meta = jnp.stack([level ^ base, device, jnp.int32(blocks)]).astype(jnp.int32)

    partial = product(w_rows[0])
    right, left = reduce_line(partial)
    kv_width = 2 * HD
    bias = jnp.concatenate([key_bias, value_bias])[None]
    full = lambda *shape: pl.BlockSpec(shape, lambda *unused: (0,) * len(shape))
    kv, cos, sin = pl.pallas_call(
        functools.partial(kv_kernel, far_slots, block_len),
        grid_spec=pltpu.PrefetchScalarGridSpec(
            num_scalar_prefetch=2,
            grid=(1,),
            in_specs=[
                full(tokens, kv_width),
                full(tokens, kv_width),
                pl.BlockSpec((1, tokens, kv_width), lambda i, meta, parents: (meta[0], 0, 0)),
                full(tokens, HD),
                full(1, kv_width),
            ],
            out_specs=[full(tokens, kv_width), full(tokens, HD), full(tokens, HD)],
        ),
        out_shape=[
            jax.ShapeDtypeStruct((tokens, kv_width), bf16),
            jax.ShapeDtypeStruct((tokens, HD), f32),
            jax.ShapeDtypeStruct((tokens, HD), f32),
        ],
        name="finish_kv",
    )(meta, parents, right, left, partial, inverse, bias)

    stems = kv[None, : STEMS * block_len]
    bit = 1
    while bit < branches:
        stems = jnp.concatenate([stems, swap(stems, "branch", bit)], 0)
        bit *= 2

    output = None
    chunk_heads = head_count // query_chunks
    for c in range(query_chunks):
        partial = product(w_rows[1 + c])
        right, left = reduce_line(partial)
        first_head = c * chunk_heads
        in_specs = [
            pl.BlockSpec((tokens, HD), lambda i, *s: (0, i)),
            pl.BlockSpec((tokens, HD), lambda i, *s: (0, i)),
            pl.BlockSpec((1, tokens, HD), lambda i, meta, *s: (meta[0], 0, i)),
            full(tokens, HD),
            pl.BlockSpec((1, HD), lambda i, *s, first_head=first_head: (0, first_head + i)),
            full(tokens, HD),
            full(tokens, HD),
            full(tokens, kv_width),
            full(branches, STEMS * block_len, kv_width),
        ]
        operands = [
            meta, parents, lengths, right, left, partial, inverse, query_bias[None], cos, sin,
            kv, stems,
        ]
        kernel = functools.partial(attend_kernel, far_slots, blocks)
        aliases = {}
        if output is not None:
            in_specs.append(pl.BlockSpec(memory_space=pl.ANY))
            operands.append(output)
            aliases = {len(operands) - 1: 0}
            kernel = functools.partial(with_output, kernel)
        output = pl.pallas_call(
            kernel,
            grid_spec=pltpu.PrefetchScalarGridSpec(
                num_scalar_prefetch=3,
                grid=(chunk_heads,),
                in_specs=in_specs,
                out_specs=pl.BlockSpec(
                    (tokens, HD), lambda i, *s, first_head=first_head: (0, first_head + i)
                ),
                scratch_shapes=[
                    pltpu.VMEM((far_slots * block_len, HD), bf16),
                    pltpu.VMEM((far_slots * block_len, HD), bf16),
                    pltpu.VMEM((8, far_slots * block_len), f32),
                ],
            ),
            out_shape=jax.ShapeDtypeStruct((tokens, columns), bf16),
            input_output_aliases=aliases,
            compiler_params=pltpu.CompilerParams(vmem_limit_bytes=40 * 2**20),
            name="attend",
        )(*operands)
    return output.reshape(blocks, block_len, columns)


def with_output(kernel, *refs):
    kernel(*refs[:12], *refs[13:])


def solution(mesh):
    return jax.shard_map(
        shards,
        mesh=mesh,
        in_specs=(
            P("branch", None, "fsdp"),
            P(),
            P(),
            P(),
            P("branch", "fsdp"),
            P("branch", "fsdp"),
            P("branch", "fsdp"),
            P("fsdp"),
            P("fsdp"),
            P("fsdp"),
        ),
        out_specs=P("branch", None, "fsdp"),
        check_vma=False,
    )
```

time: 447 us -> 278 us (0.62)
  waiting for transfers between devices: 280 us -> 57.6 us
  starting transfers between devices: 0.12 us -> 169 us
  blocking collectives: 75.4 us -> 0 us
  matrix products: 30.1 us -> 10.6 us
  Pallas kernels: 0 us -> 18.2 us
  between operations: 17.7 us -> 0.57 us
  local copies, waits for them, and re-layouts: 19.3 us -> 6.13 us
  loops' own time: 5.79 us -> 0 us
  other arithmetic: 18.3 us -> 13.1 us
    all_gather x4 -> x0, waiting for transfers between devices: 278 us -> none  [the longest x1 162 us: shards(): lax.all_gather(w_query, 'branch', axis=0, tiled=True)]
    ppermute x0 -> x34, starting transfers between devices: none -> 169 us  [the longest x14 89.3 us: swap(): return lax.ppermute(array, axis, [(i, i ^ bit) for i in range(size)])]
    all_gather x2 -> x0, blocking collectives: 67.1 us -> none  [the longest x1 33.5 us: shards(): lax.all_gather(stem_values, 'branch', axis=0, tiled=True)]
    ppermute x0 -> x34, waiting for transfers between devices: none -> 57.6 us  [the longest x14 47.3 us: swap(): return lax.ppermute(array, axis, [(i, i ^ bit) for i in range(size)])]
    dot_general x9 -> x6, matrix products: 30.1 us -> 10.6 us  [product(): jnp.dot(everything[:, j * rows:(j + 1) * rows], chunk[j], preferred_eleme...]
    pallas_call x0 -> x3, Pallas kernels: none -> 18.2 us  [the longest x2 14.6 us: shards(): pl.pallas_call(kernel, grid_spec=pltpu.PrefetchScalarGridSpec(num_scalar_...]
    psum x1 -> x0, blocking collectives: 8.34 us -> none  [shards(): square_total = lax.psum(jnp.sum(shard_tokens * shard_tokens, -1), 'fsdp')]
    dynamic_slice x17 -> x1, local copies, waits for them, and re-layouts: 8.09 us -> 0.7 us  [shards(): lax.dynamic_slice_in_dim(gain, part * feature_part + start, rows)]
  transfers between devices with their start and end apart: 4 -> 34, of which waited for: 4 -> 7; matrix products, arithmetic and copies ran while one was open for 7% -> 10% of each run, Pallas kernels for 0% -> 4%
where the time goes in v1:
time: 278 us; the launch traced here: 275 us
  starting transfers between devices  169 us (61%)
  waiting for transfers between devices  57.6 us (21%)
  Pallas kernels  18.2 us (7%)
  other arithmetic  13.1 us (5%)
  matrix products  10.6 us (4%)
  local copies, waits for them, and re-layouts  6.13 us (2%)
    ppermute x14, starting transfers between devices, swap(): return lax.ppermute(array, axis, [(i, i ^ bit) for i in range(size)])  89.3 us
    ppermute x9, starting transfers between devices, reduce_line(): right = lax.ppermute(ahead.astype(bf16), 'branch', up[s])  66.6 us
    ppermute x14, waiting for transfers between devices, swap(): return lax.ppermute(array, axis, [(i, i ^ bit) for i in range(size)])  47.3 us
    pallas_call x2, Pallas kernels, shards(): pl.pallas_call(kernel, grid_spec=pltpu.PrefetchScalarGridSpec(num_scalar_...  14.6 us
    dot_general x6, matrix products, product(): jnp.dot(everything[:, j * rows:(j + 1) * rows], chunk[j], preferred_eleme...  10.6 us
    ppermute x9, waiting for transfers between devices, reduce_line(): right = lax.ppermute(ahead.astype(bf16), 'branch', up[s])  10.2 us
    ppermute x9, starting transfers between devices, reduce_line(): left = lax.ppermute(behind.astype(bf16), 'branch', down[s])  9.54 us
  transfers between devices with their start and end apart: 34, of which 7 were waited for; matrix products, arithmetic and copies ran while one was open for 10% of the time, Pallas kernels for 4%

profile of v1, /device:TPU:0, one launch (start us, length us, event | category | flops | bytes accessed | tf_op | source)
XLA Modules:
  0.0 274.9 jit_solution(8896862182801665271)
XLA Ops:
  0.7 1.9 multiply_convert_fusion.1
  2.8 1.7 collective-permute-start.4
  6.1 21.8 %collective-permute-start.5 = (bf16[192,2048]{1,0:T(8,128)(2,1)}, bf16[192,2048]{1,0:T(8,128)(2,1)}, u32[]{:S(2)}, u32[]{:S(2)}) collective-permute-start(bf16[192,2048]{1,0:T(8,128)(2,1)} %collective-permute-done.4), channel_id=1, source_target_pairs={{0,16},{8,24},{16,0},{24,8},{1,17},{9,25},{17,1},{25,9},{2,18},{10... | collective-permute-start | bytes 2359304 | tf_op jit(solution)/shard_map/ppermute | solution.py:165
  27.9 18.3 %collective-permute-start.1 = (bf16[192,2048]{1,0:T(8,128)(2,1)}, bf16[192,2048]{1,0:T(8,128)(2,1)}, u32[]{:S(2)}, u32[]{:S(2)}) collective-permute-start(bf16[192,2048]{1,0:T(8,128)(2,1)} %collective-permute-done), channel_id=1, source_target_pairs={{0,16},{8,24},{16,0},{24,8},{1,17},{9,25},{17,1},{25,9},{2,18},{10... | collective-permute-start | bytes 2359304 | tf_op jit(solution)/shard_map/ppermute | solution.py:165
  46.6 31.4 %collective-permute-start.15 = (f32[3,128]{1,0:T(4,128)S(1)}, f32[3,128]{1,0:T(4,128)S(1)}, u32[]{:S(2)}, u32[]{:S(2)}) collective-permute-start(f32[3,128]{1,0:T(4,128)S(1)} %multiply_reduce_fusion), channel_id=1, source_target_pairs={{0,8},{8,0},{16,24},{24,16},{1,9},{9,1},{17,25},{25,17},{2,10},{10... | collective-permute-start | bytes 4616 | tf_op jit(solution)/shard_map/ppermute | solution.py:165
  79.2 9.4 %collective-permute-start.3 = (bf16[192,2048]{1,0:T(8,128)(2,1)}, bf16[192,2048]{1,0:T(8,128)(2,1)}, u32[]{:S(2)}, u32[]{:S(2)}) collective-permute-start(bf16[192,2048]{1,0:T(8,128)(2,1)} %collective-permute-done.1), channel_id=1, source_target_pairs={{0,8},{8,0},{16,24},{24,16},{1,9},{9,1},{17,25},{25,17},{2,10},{10... | collective-permute-start | bytes 2359304 | tf_op jit(solution)/shard_map/ppermute | solution.py:165
  92.1 3.3 %collective-permute-done.16 = f32[3,128]{1,0:T(4,128)S(1)} collective-permute-done((f32[3,128]{1,0:T(4,128)S(1)}, f32[3,128]{1,0:T(4,128)S(1)}, u32[]{:S(2)}, u32[]{:S(2)}) %collective-permute-start.16) | collective-permute-done | bytes 1568 | tf_op jit(solution)/shard_map/ppermute | solution.py:165
  99.0 3.8 %maximum_maximum_fusion = bf16[4,384,2048]{2,1,0:T(8,128)(2,1)S(1)} fusion(bf16[1,192,2048]{2,1,0:T(8,128)(2,1)} %bitcast.10, bf16[1,192,2048]{2,1,0:T(8,128)(2,1)} %bitcast.9, bf16[1,192,2048]{2,1,0:T(8,128)(2,1)} %bitcast.8, bf16[1,192,2048]{2,1,0:T(8,128)(2,1)} %bitcast.7, bf16[1,192,2048]{2,1,0:T(8,128)(2,1)} %bitcast.6, bf16[1,192,2048]{2,1,0:T(8,128)(2,1)} %bitcast.5, ...), kind=kLoop, calls=%fused_computation | loop fusion | flops 50331648 | bytes 12582912 | tf_op jit(solution)/shard_map/concatenate | solution.py:216
  102.9 18.8 %collective-permute-done.27 = bf16[1024,512]{1,0:T(8,128)(2,1)S(1)} collective-permute-done((bf16[1024,512]{1,0:T(8,128)(2,1)}, bf16[1024,512]{1,0:T(8,128)(2,1)S(1)}, u32[]{:S(2)}, u32[]{:S(2)}) %collective-permute-start.27) | collective-permute-done | bytes 1048608 | tf_op jit(solution)/shard_map/ppermute | solution.py:165
  121.7 1.8 fusion
  123.5 1.9 fusion.15
  126.2 18.8 %collective-permute-start.28 = (bf16[384,512]{1,0:T(8,128)(2,1)S(1)}, bf16[384,512]{1,0:T(8,128)(2,1)}, u32[]{:S(2)}, u32[]{:S(2)}) collective-permute-start(bf16[384,512]{1,0:T(8,128)(2,1)S(1)} %get-tuple-element.14), channel_id=1, source_target_pairs={{0,2},{1,3},{8,10},{9,11},{16,18},{17,19},{24,26},{25,27}} | collective-permute-start | bytes 1179656 | tf_op jit(solution)/shard_map/ppermute | solution.py:252
  146.1 2.0 fusion.18
  148.9 6.1 %collective-permute-start.18 = (bf16[384,256]{1,0:T(8,128)(2,1)S(1)}, bf16[384,256]{1,0:T(8,128)(2,1)S(1)}, u32[]{:S(2)}, u32[]{:S(2)}) collective-permute-start(bf16[384,256]{1,0:T(8,128)(2,1)S(1)} %get-tuple-element.24), channel_id=1, source_target_pairs={{0,2},{1,3},{8,10},{9,11},{16,18},{17,19},{24,26},{25,27}} | collective-permute-start | bytes 589832 | tf_op jit(solution)/shard_map/ppermute | solution.py:252
  155.0 1.8 fusion.4
  157.6 2.0 fusion.12
  161.1 18.4 %collective-permute-start.9 = (bf16[384,512]{1,0:T(8,128)(2,1)}, bf16[384,512]{1,0:T(8,128)(2,1)}, u32[]{:S(2)}, u32[]{:S(2)}) collective-permute-start(bf16[384,512]{1,0:T(8,128)(2,1)} %get-tuple-element.18), channel_id=1, source_target_pairs={{0,2},{1,3},{8,10},{9,11},{16,18},{17,19},{24,26},{25,27}} | collective-permute-start | bytes 1179656 | tf_op jit(solution)/shard_map/ppermute | solution.py:252
  179.6 2.0 collective-permute-start.19
  184.0 6.4 %collective-permute-done.19 = bf16[384,256]{1,0:T(8,128)(2,1)S(1)} collective-permute-done((bf16[384,256]{1,0:T(8,128)(2,1)S(1)}, bf16[384,256]{1,0:T(8,128)(2,1)S(1)}, u32[]{:S(2)}, u32[]{:S(2)}) %collective-permute-start.19) | collective-permute-done | bytes 196640 | tf_op jit(solution)/shard_map/ppermute | solution.py:252
  191.7 5.7 %collective-permute-start.20 = (bf16[384,256]{1,0:T(8,128)(2,1)S(1)}, bf16[384,256]{1,0:T(8,128)(2,1)}, u32[]{:S(2)}, u32[]{:S(2)}) collective-permute-start(bf16[384,256]{1,0:T(8,128)(2,1)S(1)} %fusion.37), channel_id=1, source_target_pairs={{0,2},{1,3},{2,4},{3,5},{4,6},{5,7},{8,10},{9,11},{10,12},{11,13},... | collective-permute-start | bytes 589832 | tf_op jit(solution)/shard_map/ppermute | solution.py:252
  200.7 3.6 %finish_kv.1 = (bf16[384,256]{1,0:T(8,128)(2,1)}, f32[384,128]{1,0:T(8,128)}, f32[384,128]{1,0:T(8,128)}) custom-call(s32[3]{0:T(128)} %pad_add_fusion.meta_ref.refs_0_, s32[24]{0:T(128)} %refs_1_.1, bf16[384,256]{1,0:T(8,128)(2,1)} %collective-permute-done.20.right_ref, bf16[384,256]{1,0:T(8,128)(2,1)} %collective-permute-done.23.left_ref, ...), custom_call_target="tpu_custom_call" | custom-call | tf_op jit(solution)/shard_map/finish_kv/pallas_call | solution.py:263
  206.9 1.8 fusion.23
  208.7 4.8 %collective-permute-start.29 = (bf16[384,512]{1,0:T(8,128)(2,1)S(1)}, bf16[384,512]{1,0:T(8,128)(2,1)S(1)}, u32[]{:S(2)}, u32[]{:S(2)}) collective-permute-start(bf16[384,512]{1,0:T(8,128)(2,1)S(1)} %get-tuple-element.12), channel_id=1, source_target_pairs={{0,2},{1,3},{2,4},{3,5},{8,10},{9,11},{10,12},{11,13},{16,18},{17,... | collective-permute-start | bytes 1179656 | tf_op jit(solution)/shard_map/ppermute | solution.py:252
  213.6 2.3 collective-permute-start.25
  217.2 2.0 collective-permute-start.10
  222.0 6.6 %collective-permute-done.25 = bf16[2,256,256]{2,1,0:T(8,128)(2,1)S(1)} collective-permute-done((bf16[2,256,256]{2,1,0:T(8,128)(2,1)S(1)}, bf16[2,256,256]{2,1,0:T(8,128)(2,1)S(1)}, u32[]{:S(2)}, u32[]{:S(2)}) %collective-permute-start.25) | collective-permute-done | bytes 262176 | tf_op jit(solution)/shard_map/ppermute | solution.py:165
  229.0 4.4 %collective-permute-start.30 = (bf16[384,512]{1,0:T(8,128)(2,1)S(1)}, bf16[384,512]{1,0:T(8,128)(2,1)S(1)}, u32[]{:S(2)}, u32[]{:S(2)}) collective-permute-start(bf16[384,512]{1,0:T(8,128)(2,1)S(1)} %fusion.25), channel_id=1, source_target_pairs={{0,2},{1,3},{2,4},{3,5},{4,6},{5,7},{8,10},{9,11},{10,12},{11,13},... | collective-permute-start | bytes 1179656 | tf_op jit(solution)/shard_map/ppermute | solution.py:252
  233.4 3.7 %collective-permute-done.10 = bf16[384,512]{1,0:T(8,128)(2,1)S(1)} collective-permute-done((bf16[384,512]{1,0:T(8,128)(2,1)S(1)}, bf16[384,512]{1,0:T(8,128)(2,1)S(1)}, u32[]{:S(2)}, u32[]{:S(2)}) %collective-permute-start.10) | collective-permute-done | bytes 393248 | tf_op jit(solution)/shard_map/ppermute | solution.py:252
  237.2 4.4 %collective-permute-start.11 = (bf16[384,512]{1,0:T(8,128)(2,1)S(1)}, bf16[384,512]{1,0:T(8,128)(2,1)S(1)}, u32[]{:S(2)}, u32[]{:S(2)}) collective-permute-start(bf16[384,512]{1,0:T(8,128)(2,1)S(1)} %fusion.29), channel_id=1, source_target_pairs={{0,2},{1,3},{2,4},{3,5},{4,6},{5,7},{8,10},{9,11},{10,12},{11,13},... | collective-permute-start | bytes 1179656 | tf_op jit(solution)/shard_map/ppermute | solution.py:252
  241.6 18.5 %collective-permute-done.26 = bf16[4,256,256]{2,1,0:T(8,128)(2,1)S(1)} collective-permute-done((bf16[4,256,256]{2,1,0:T(8,128)(2,1)S(1)}, bf16[4,256,256]{2,1,0:T(8,128)(2,1)S(1)}, u32[]{:S(2)}, u32[]{:S(2)}) %collective-permute-start.26) | collective-permute-done | bytes 524320 | tf_op jit(solution)/shard_map/ppermute | solution.py:165
  260.3 7.3 %attend.2.refs_12_ = bf16[384,1024]{1,0:T(8,128)(2,1)} custom-call(s32[3]{0:T(128)S(1)} %copy-done.7, s32[24]{0:T(128)S(1)} %copy-done.8, s32[24]{0:T(128)S(1)} %copy-done.9, bf16[384,512]{1,0:T(8,128)(2,1)S(1)} %collective-permute-done.30.right_ref, bf16[384,512]{1,0:T(8,128)(2,1)S(1)} %collective-permute-done.33.left_ref, f32[4,384,512]{2,1,0:T(8,128)S(1)} %bitcast.95, ...), custom_call_target="tpu_custom_call" | custom-call | tf_op jit(solution)/shard_map/attend/pallas_call | solution.py:319
  267.6 7.3 %attend.3 = bf16[384,1024]{1,0:T(8,128)(2,1)} custom-call(s32[3]{0:T(128)S(1)} %copy-done.7, s32[24]{0:T(128)S(1)} %copy-done.8, s32[24]{0:T(128)S(1)} %copy-done.9, bf16[384,512]{1,0:T(8,128)(2,1)S(1)} %collective-permute-done.11.refs_3_, bf16[384,512]{1,0:T(8,128)(2,1)S(1)} %collective-permute-done.14.refs_4_, ...), custom_call_target="tpu_custom_call", output_to_operand_aliasing={{}: (12, {})} | custom-call | tf_op jit(solution)/shard_map/attend/pallas_call | solution.py:319
  (110 shorter events, 30.1 us)
Async XLA Ops:
  4.5 23.4 %collective-permute-start = (bf16[192,2048]{1,0:T(8,128)(2,1)S(1)}, bf16[192,2048]{1,0:T(8,128)(2,1)}, u32[]{:S(2)}, u32[]{:S(2)}) collective-permute-start(bf16[192,2048]{1,0:T(8,128)(2,1)S(1)} %get-tuple-element.25), channel_id=1, source_target_pairs={{0,0},{8,18},{16,4},{24,22},{1,1},{9,19},{17,5},{25,23},{2,16},{10... | collective-permute-start | bytes 2359304 | tf_op jit(solution)/shard_map/ppermute | solution.py:204
  6.1 73.2 %collective-permute-start.5 = (bf16[192,2048]{1,0:T(8,128)(2,1)}, bf16[192,2048]{1,0:T(8,128)(2,1)}, u32[]{:S(2)}, u32[]{:S(2)}) collective-permute-start(bf16[192,2048]{1,0:T(8,128)(2,1)} %collective-permute-done.4), channel_id=1, source_target_pairs={{0,16},{8,24},{16,0},{24,8},{1,17},{9,25},{17,1},{25,9},{2,18},{10... | collective-permute-start | bytes 2359304 | tf_op jit(solution)/shard_map/ppermute | solution.py:165
  27.9 51.3 %collective-permute-start.1 = (bf16[192,2048]{1,0:T(8,128)(2,1)}, bf16[192,2048]{1,0:T(8,128)(2,1)}, u32[]{:S(2)}, u32[]{:S(2)}) collective-permute-start(bf16[192,2048]{1,0:T(8,128)(2,1)} %collective-permute-done), channel_id=1, source_target_pairs={{0,16},{8,24},{16,0},{24,8},{1,17},{9,25},{17,1},{25,9},{2,18},{10... | collective-permute-start | bytes 2359304 | tf_op jit(solution)/shard_map/ppermute | solution.py:165
  46.6 45.2 %collective-permute-start.15 = (f32[3,128]{1,0:T(4,128)S(1)}, f32[3,128]{1,0:T(4,128)S(1)}, u32[]{:S(2)}, u32[]{:S(2)}) collective-permute-start(f32[3,128]{1,0:T(4,128)S(1)} %multiply_reduce_fusion), channel_id=1, source_target_pairs={{0,8},{8,0},{16,24},{24,16},{1,9},{9,1},{17,25},{25,17},{2,10},{10... | collective-permute-start | bytes 4616 | tf_op jit(solution)/shard_map/ppermute | solution.py:165
  78.7 18.2 %collective-permute-start.2 = (bf16[192,2048]{1,0:T(8,128)(2,1)}, bf16[192,2048]{1,0:T(8,128)(2,1)}, u32[]{:S(2)}, u32[]{:S(2)}) collective-permute-start(bf16[192,2048]{1,0:T(8,128)(2,1)} %collective-permute-done), channel_id=1, source_target_pairs={{0,8},{8,0},{16,24},{24,16},{1,9},{9,1},{17,25},{25,17},{2,10},{10... | collective-permute-start | bytes 2359304 | tf_op jit(solution)/shard_map/ppermute | solution.py:165
  78.7 18.8 %collective-permute-start.6 = (bf16[192,2048]{1,0:T(8,128)(2,1)}, bf16[192,2048]{1,0:T(8,128)(2,1)}, u32[]{:S(2)}, u32[]{:S(2)}) collective-permute-start(bf16[192,2048]{1,0:T(8,128)(2,1)} %collective-permute-done.4), channel_id=1, source_target_pairs={{0,8},{8,0},{16,24},{24,16},{1,9},{9,1},{17,25},{25,17},{2,10},{10... | collective-permute-start | bytes 2359304 | tf_op jit(solution)/shard_map/ppermute | solution.py:165
  79.2 19.8 %collective-permute-start.7 = (bf16[192,2048]{1,0:T(8,128)(2,1)}, bf16[192,2048]{1,0:T(8,128)(2,1)}, u32[]{:S(2)}, u32[]{:S(2)}) collective-permute-start(bf16[192,2048]{1,0:T(8,128)(2,1)} %collective-permute-done.5), channel_id=1, source_target_pairs={{0,8},{8,0},{16,24},{24,16},{1,9},{9,1},{17,25},{25,17},{2,10},{10... | collective-permute-start | bytes 2359304 | tf_op jit(solution)/shard_map/ppermute | solution.py:165
  79.2 19.8 %collective-permute-start.3 = (bf16[192,2048]{1,0:T(8,128)(2,1)}, bf16[192,2048]{1,0:T(8,128)(2,1)}, u32[]{:S(2)}, u32[]{:S(2)}) collective-permute-start(bf16[192,2048]{1,0:T(8,128)(2,1)} %collective-permute-done.1), channel_id=1, source_target_pairs={{0,8},{8,0},{16,24},{24,16},{1,9},{9,1},{17,25},{25,17},{2,10},{10... | collective-permute-start | bytes 2359304 | tf_op jit(solution)/shard_map/ppermute | solution.py:165
  95.4 26.3 %collective-permute-start.27 = (bf16[1024,512]{1,0:T(8,128)(2,1)}, bf16[1024,512]{1,0:T(8,128)(2,1)S(1)}, u32[]{:S(2)}, u32[]{:S(2)}) collective-permute-start(bf16[1024,512]{1,0:T(8,128)(2,1)} %get-tuple-element.19), channel_id=1, source_target_pairs={{0,1},{1,0},{2,3},{3,2},{4,5},{5,4},{6,7},{7,6},{8,9},{9,8},{10,11... | collective-permute-start | bytes 3145736 | tf_op jit(solution)/shard_map/ppermute | solution.py:165
  96.9 48.2 %collective-permute-start.17 = (bf16[1024,256]{1,0:T(8,128)(2,1)}, bf16[1024,256]{1,0:T(8,128)(2,1)S(1)}, u32[]{:S(2)}, u32[]{:S(2)}) collective-permute-start(bf16[1024,256]{1,0:T(8,128)(2,1)} %constant_dynamic-update-slice_fusion), channel_id=1, source_target_pairs={{0,1},{1,0},{2,3},{3,2},{4,5},{5,4},{6,7},{7,6},{8,9},{9,8},{10,11... | collective-permute-start | bytes 1572872 | tf_op jit(solution)/shard_map/ppermute | solution.py:165
  97.5 57.5 %collective-permute-start.8 = (bf16[1024,512]{1,0:T(8,128)(2,1)S(1)}, bf16[1024,512]{1,0:T(8,128)(2,1)S(1)}, u32[]{:S(2)}, u32[]{:S(2)}) collective-permute-start(bf16[1024,512]{1,0:T(8,128)(2,1)S(1)} %get-tuple-element.20), channel_id=1, source_target_pairs={{0,1},{1,0},{2,3},{3,2},{4,5},{5,4},{6,7},{7,6},{8,9},{9,8},{10,11... | collective-permute-start | bytes 3145736 | tf_op jit(solution)/shard_map/ppermute | solution.py:165
  125.6 56.1 %collective-permute-start.31 = (bf16[384,512]{1,0:T(8,128)(2,1)S(1)}, bf16[384,512]{1,0:T(8,128)(2,1)S(1)}, u32[]{:S(2)}, u32[]{:S(2)}) collective-permute-start(bf16[384,512]{1,0:T(8,128)(2,1)S(1)} %get-tuple-element.13), channel_id=1, source_target_pairs={{6,4},{7,5},{14,12},{15,13},{22,20},{23,21},{30,28},{31,29}} | collective-permute-start | bytes 1179656 | tf_op jit(solution)/shard_map/ppermute | solution.py:253
  126.2 80.6 %collective-permute-start.28 = (bf16[384,512]{1,0:T(8,128)(2,1)S(1)}, bf16[384,512]{1,0:T(8,128)(2,1)}, u32[]{:S(2)}, u32[]{:S(2)}) collective-permute-start(bf16[384,512]{1,0:T(8,128)(2,1)S(1)} %get-tuple-element.14), channel_id=1, source_target_pairs={{0,2},{1,3},{8,10},{9,11},{16,18},{17,19},{24,26},{25,27}} | collective-permute-start | bytes 1179656 | tf_op jit(solution)/shard_map/ppermute | solution.py:252
  148.2 8.6 %collective-permute-start.21 = (bf16[384,256]{1,0:T(8,128)(2,1)S(1)}, bf16[384,256]{1,0:T(8,128)(2,1)S(1)}, u32[]{:S(2)}, u32[]{:S(2)}) collective-permute-start(bf16[384,256]{1,0:T(8,128)(2,1)S(1)} %get-tuple-element.23), channel_id=1, source_target_pairs={{6,4},{7,5},{14,12},{15,13},{22,20},{23,21},{30,28},{31,29}} | collective-permute-start | bytes 589832 | tf_op jit(solution)/shard_map/ppermute | solution.py:253
  148.9 12.2 %collective-permute-start.18 = (bf16[384,256]{1,0:T(8,128)(2,1)S(1)}, bf16[384,256]{1,0:T(8,128)(2,1)S(1)}, u32[]{:S(2)}, u32[]{:S(2)}) collective-permute-start(bf16[384,256]{1,0:T(8,128)(2,1)S(1)} %get-tuple-element.24), channel_id=1, source_target_pairs={{0,2},{1,3},{8,10},{9,11},{16,18},{17,19},{24,26},{25,27}} | collective-permute-start | bytes 589832 | tf_op jit(solution)/shard_map/ppermute | solution.py:252
  156.9 22.6 %collective-permute-start.22 = (bf16[384,256]{1,0:T(8,128)(2,1)S(1)}, bf16[384,256]{1,0:T(8,128)(2,1)S(1)}, u32[]{:S(2)}, u32[]{:S(2)}) collective-permute-start(bf16[384,256]{1,0:T(8,128)(2,1)S(1)} %fusion.34), channel_id=1, source_target_pairs={{6,4},{7,5},{4,2},{5,3},{14,12},{15,13},{12,10},{13,11},{22,20},{2... | collective-permute-start | bytes 589832 | tf_op jit(solution)/shard_map/ppermute | solution.py:253
  160.4 31.3 %collective-permute-start.12 = (bf16[384,512]{1,0:T(8,128)(2,1)S(1)}, bf16[384,512]{1,0:T(8,128)(2,1)S(1)}, u32[]{:S(2)}, u32[]{:S(2)}) collective-permute-start(bf16[384,512]{1,0:T(8,128)(2,1)S(1)} %get-tuple-element.17), channel_id=1, source_target_pairs={{6,4},{7,5},{14,12},{15,13},{22,20},{23,21},{30,28},{31,29}} | collective-permute-start | bytes 1179656 | tf_op jit(solution)/shard_map/ppermute | solution.py:253
  161.1 54.7 %collective-permute-start.9 = (bf16[384,512]{1,0:T(8,128)(2,1)}, bf16[384,512]{1,0:T(8,128)(2,1)}, u32[]{:S(2)}, u32[]{:S(2)}) collective-permute-start(bf16[384,512]{1,0:T(8,128)(2,1)} %get-tuple-element.18), channel_id=1, source_target_pairs={{0,2},{1,3},{8,10},{9,11},{16,18},{17,19},{24,26},{25,27}} | collective-permute-start | bytes 1179656 | tf_op jit(solution)/shard_map/ppermute | solution.py:252
  179.6 10.7 %collective-permute-start.19 = (bf16[384,256]{1,0:T(8,128)(2,1)S(1)}, bf16[384,256]{1,0:T(8,128)(2,1)S(1)}, u32[]{:S(2)}, u32[]{:S(2)}) collective-permute-start(bf16[384,256]{1,0:T(8,128)(2,1)S(1)} %get-tuple-element.22), channel_id=1, source_target_pairs={{0,2},{1,3},{2,4},{3,5},{8,10},{9,11},{10,12},{11,13},{16,18},{17,... | collective-permute-start | bytes 589832 | tf_op jit(solution)/shard_map/ppermute | solution.py:252
  182.5 24.3 %collective-permute-start.32 = (bf16[384,512]{1,0:T(8,128)(2,1)}, bf16[384,512]{1,0:T(8,128)(2,1)}, u32[]{:S(2)}, u32[]{:S(2)}) collective-permute-start(bf16[384,512]{1,0:T(8,128)(2,1)} %fusion.22), channel_id=1, source_target_pairs={{6,4},{7,5},{4,2},{5,3},{14,12},{15,13},{12,10},{13,11},{22,20},{2... | collective-permute-start | bytes 1179656 | tf_op jit(solution)/shard_map/ppermute | solution.py:253
  190.4 8.1 %collective-permute-start.23 = (bf16[384,256]{1,0:T(8,128)(2,1)S(1)}, bf16[384,256]{1,0:T(8,128)(2,1)}, u32[]{:S(2)}, u32[]{:S(2)}) collective-permute-start(bf16[384,256]{1,0:T(8,128)(2,1)S(1)} %get-tuple-element.21), channel_id=1, source_target_pairs={{6,4},{7,5},{4,2},{5,3},{2,0},{3,1},{14,12},{15,13},{12,10},{13,11... | collective-permute-start | bytes 589832 | tf_op jit(solution)/shard_map/ppermute | solution.py:253
  191.7 8.2 %collective-permute-start.20 = (bf16[384,256]{1,0:T(8,128)(2,1)S(1)}, bf16[384,256]{1,0:T(8,128)(2,1)}, u32[]{:S(2)}, u32[]{:S(2)}) collective-permute-start(bf16[384,256]{1,0:T(8,128)(2,1)S(1)} %fusion.37), channel_id=1, source_target_pairs={{0,2},{1,3},{2,4},{3,5},{4,6},{5,7},{8,10},{9,11},{10,12},{11,13},... | collective-permute-start | bytes 589832 | tf_op jit(solution)/shard_map/ppermute | solution.py:252
  198.5 17.4 %collective-permute-start.13 = (bf16[384,512]{1,0:T(8,128)(2,1)}, bf16[384,512]{1,0:T(8,128)(2,1)}, u32[]{:S(2)}, u32[]{:S(2)}) collective-permute-start(bf16[384,512]{1,0:T(8,128)(2,1)} %fusion.26), channel_id=1, source_target_pairs={{6,4},{7,5},{4,2},{5,3},{14,12},{15,13},{12,10},{13,11},{22,20},{2... | collective-permute-start | bytes 1179656 | tf_op jit(solution)/shard_map/ppermute | solution.py:253
  205.3 8.2 %collective-permute-start.24 = (bf16[1,256,256]{2,1,0:T(8,128)(2,1)S(1)}, bf16[1,256,256]{2,1,0:T(8,128)(2,1)S(1)}, u32[]{:S(2)}, u32[]{:S(2)}) collective-permute-start(bf16[1,256,256]{2,1,0:T(8,128)(2,1)S(1)} %slice_bitcast_fusion), channel_id=1, source_target_pairs={{0,1},{1,0},{2,3},{3,2},{4,5},{5,4},{6,7},{7,6},{8,9},{9,8},{10,11... | collective-permute-start | bytes 393224 | tf_op jit(solution)/shard_map/ppermute | solution.py:165
  208.7 20.1 %collective-permute-start.29 = (bf16[384,512]{1,0:T(8,128)(2,1)S(1)}, bf16[384,512]{1,0:T(8,128)(2,1)S(1)}, u32[]{:S(2)}, u32[]{:S(2)}) collective-permute-start(bf16[384,512]{1,0:T(8,128)(2,1)S(1)} %get-tuple-element.12), channel_id=1, source_target_pairs={{0,2},{1,3},{2,4},{3,5},{8,10},{9,11},{10,12},{11,13},{16,18},{17,... | collective-permute-start | bytes 1179656 | tf_op jit(solution)/shard_map/ppermute | solution.py:252
  213.6 15.1 %collective-permute-start.25 = (bf16[2,256,256]{2,1,0:T(8,128)(2,1)S(1)}, bf16[2,256,256]{2,1,0:T(8,128)(2,1)S(1)}, u32[]{:S(2)}, u32[]{:S(2)}) collective-permute-start(bf16[2,256,256]{2,1,0:T(8,128)(2,1)S(1)} %pad_maximum_fusion.3), channel_id=1, source_target_pairs={{0,2},{1,3},{2,0},{3,1},{4,6},{5,7},{6,4},{7,5},{8,10},{9,11},{10,... | collective-permute-start | bytes 786440 | tf_op jit(solution)/shard_map/ppermute | solution.py:165
  217.2 19.9 %collective-permute-start.10 = (bf16[384,512]{1,0:T(8,128)(2,1)S(1)}, bf16[384,512]{1,0:T(8,128)(2,1)S(1)}, u32[]{:S(2)}, u32[]{:S(2)}) collective-permute-start(bf16[384,512]{1,0:T(8,128)(2,1)S(1)} %get-tuple-element.16), channel_id=1, source_target_pairs={{0,2},{1,3},{2,4},{3,5},{8,10},{9,11},{10,12},{11,13},{16,18},{17,... | collective-permute-start | bytes 1179656 | tf_op jit(solution)/shard_map/ppermute | solution.py:252
  219.2 41.0 %collective-permute-start.33 = (bf16[384,512]{1,0:T(8,128)(2,1)S(1)}, bf16[384,512]{1,0:T(8,128)(2,1)S(1)}, u32[]{:S(2)}, u32[]{:S(2)}) collective-permute-start(bf16[384,512]{1,0:T(8,128)(2,1)S(1)} %get-tuple-element.11), channel_id=1, source_target_pairs={{6,4},{7,5},{4,2},{5,3},{2,0},{3,1},{14,12},{15,13},{12,10},{13,11... | collective-permute-start | bytes 1179656 | tf_op jit(solution)/shard_map/ppermute | solution.py:253
  220.6 47.0 %collective-permute-start.14 = (bf16[384,512]{1,0:T(8,128)(2,1)S(1)}, bf16[384,512]{1,0:T(8,128)(2,1)S(1)}, u32[]{:S(2)}, u32[]{:S(2)}) collective-permute-start(bf16[384,512]{1,0:T(8,128)(2,1)S(1)} %get-tuple-element.15), channel_id=1, source_target_pairs={{6,4},{7,5},{4,2},{5,3},{2,0},{3,1},{14,12},{15,13},{12,10},{13,11... | collective-permute-start | bytes 1179656 | tf_op jit(solution)/shard_map/ppermute | solution.py:253
  228.7 31.4 %collective-permute-start.26 = (bf16[4,256,256]{2,1,0:T(8,128)(2,1)S(1)}, bf16[4,256,256]{2,1,0:T(8,128)(2,1)S(1)}, u32[]{:S(2)}, u32[]{:S(2)}) collective-permute-start(bf16[4,256,256]{2,1,0:T(8,128)(2,1)S(1)} %pad_maximum_fusion.2), channel_id=1, source_target_pairs={{0,4},{1,5},{2,6},{3,7},{4,0},{5,1},{6,2},{7,3},{8,12},{9,13},{10,... | collective-permute-start | bytes 1572872 | tf_op jit(solution)/shard_map/ppermute | solution.py:165
  229.0 31.3 %collective-permute-start.30 = (bf16[384,512]{1,0:T(8,128)(2,1)S(1)}, bf16[384,512]{1,0:T(8,128)(2,1)S(1)}, u32[]{:S(2)}, u32[]{:S(2)}) collective-permute-start(bf16[384,512]{1,0:T(8,128)(2,1)S(1)} %fusion.25), channel_id=1, source_target_pairs={{0,2},{1,3},{2,4},{3,5},{4,6},{5,7},{8,10},{9,11},{10,12},{11,13},... | collective-permute-start | bytes 1179656 | tf_op jit(solution)/shard_map/ppermute | solution.py:252
  237.2 30.4 %collective-permute-start.11 = (bf16[384,512]{1,0:T(8,128)(2,1)S(1)}, bf16[384,512]{1,0:T(8,128)(2,1)S(1)}, u32[]{:S(2)}, u32[]{:S(2)}) collective-permute-start(bf16[384,512]{1,0:T(8,128)(2,1)S(1)} %fusion.29), channel_id=1, source_target_pairs={{0,2},{1,3},{2,4},{3,5},{4,6},{5,7},{8,10},{9,11},{10,12},{11,13},... | collective-permute-start | bytes 1179656 | tf_op jit(solution)/shard_map/ppermute | solution.py:252
  (20 other events, 920.2 us)

commit v2 on v1

--- a/solution.py
+++ b/solution.py
@@ -16,6 +16,10 @@
 
 def bits_of(count):
     return count.bit_length() - 1
+
+
+def tie(array, *others):
+    return lax.optimization_barrier((array,) + others)[0]
 
 
 def far_chain(parents_ref, first_block, far_slots):
@@ -183,38 +187,6 @@
         pieces.append(piece.astype(bf16))
     scaled = jnp.concatenate(pieces, 1)
 
-    half_lines = lines // 2
-    shift = bits_of(half_lines)
-
-    def landing(z, feature):
-        return ((z ^ feature) & 1) * half_lines + (z >> 1)
-
-    exchange = []
-    for z in range(lines):
-        for g in range(groups):
-            for feature in range(lines):
-                source = feature * branches + z * groups + g
-                target = landing(z, feature) * branches + feature * groups + g
-                exchange.append((source, target))
-    halves = 2
-    span = tokens // halves
-    gathered = []
-    for h in range(halves):
-        sent = lax.slice_in_dim(scaled, h * span, (h + 1) * span, axis=0)
-        held = {0: lax.ppermute(sent, ("fsdp", "branch"), exchange)}
-        bit = half_lines
-        while bit:
-            for j in list(held):
-                held[j | bit] = swap(held[j], "fsdp", bit)
-            bit //= 2
-
-        order = [None] * lines
-        for j in range(lines):
-            order[((j & (half_lines - 1)) << 1) | (j >> shift)] = held[j]
-        gathered.append(jnp.stack(order))
-    base = ((part & (half_lines - 1)) << 1) | ((part >> shift) ^ (level & 1))
-    everything = jnp.concatenate(gathered, 1).reshape(lines * tokens, feature_part)
-
     squares = jnp.sum(jnp.square(raw.astype(f32)), -1).reshape(blocks, block_len)
     bit = 1
     while bit < lines:
@@ -222,6 +194,52 @@
         bit *= 2
     inverse = lax.rsqrt(squares / features + 1e-06).reshape(tokens)
     inverse = jnp.broadcast_to(inverse[:, None], (tokens, HD))
+
+    half_lines = lines // 2
+    top = bits_of(half_lines)
+
+    def column(z, feature):
+        return (z ^ feature) & (half_lines - 1)
+
+    def middle(z, feature):
+        return (column(z, feature) << 1) | ((feature >> top) ^ (z & 1))
+
+    def landing(z, feature):
+        return (column(z, feature) << 1) | (z >> top)
+
+    first_hop = []
+    second_hop = []
+    for z in range(lines):
+        for g in range(groups):
+            for feature in range(lines):
+                here = z * groups + g
+                there = feature * groups + g
+                stop = middle(z, feature) * branches + here
+                first_hop.append((feature * branches + here, stop))
+                second_hop.append((stop, landing(z, feature) * branches + there))
+    axes = ("fsdp", "branch")
+    sent = [scaled[h * block_len : (h + 1) * block_len] for h in range(blocks)]
+    sent = [lax.ppermute(piece, axes, first_hop) for piece in sent]
+    sent[1] = tie(sent[1], w_rows[0][-1])
+    sent[2] = tie(sent[2], squares)
+    sent = [lax.ppermute(piece, axes, second_hop) for piece in sent]
+    held = [{0: piece} for piece in sent]
+    held[1][0] = tie(held[1][0], w_rows[1][-1])
+    bit = half_lines
+    while bit:
+        for piece in held:
+            for j in list(piece):
+                piece[j | bit] = swap(piece[j], "fsdp", bit)
+        bit //= 2
+        held[-1][0] = tie(held[-1][0], w_rows[-1][-1])
+    gathered = []
+    for piece in held:
+        order = [None] * lines
+        for j in range(lines):
+            order[((j & 1) << top) | (j >> 1)] = piece[j]
+        gathered.append(jnp.stack(order))
+    base = ((part & 1) << top) | ((part >> 1) ^ (level & (half_lines - 1)))
+    everything = jnp.concatenate(gathered, 1).reshape(lines * tokens, feature_part)
 
     def product(chunk):
         total = None
@@ -291,7 +309,9 @@
     output = None
     chunk_heads = head_count // query_chunks
     for c in range(query_chunks):
-        partial = product(w_rows[1 + c])
+        chunk = w_rows[1 + c]
+        chunk[0] = tie(chunk[0], partial)
+        partial = product(chunk)
         right, left = reduce_line(partial)
         first_head = c * chunk_heads
         in_specs = [

time: 278 us -> 226 us (0.81)
  starting transfers between devices: 169 us -> 85.6 us
  waiting for transfers between devices: 57.6 us -> 90.6 us
    ppermute x14 -> x17, starting transfers between devices: 89.3 us -> 37.6 us  [swap(): return lax.ppermute(array, axis, [(i, i ^ bit) for i in range(size)])]
    ppermute x9, starting transfers between devices: 66.6 us -> 34.2 us  [reduce_line(): right = lax.ppermute(ahead.astype(bf16), 'branch', up[s])]
    ppermute x14 -> x17, waiting for transfers between devices: 47.3 us -> 73.6 us  [swap(): return lax.ppermute(array, axis, [(i, i ^ bit) for i in range(size)])]
    ppermute x9, waiting for transfers between devices: 10.2 us -> 16 us  [reduce_line(): right = lax.ppermute(ahead.astype(bf16), 'branch', up[s])]
  transfers between devices with their start and end apart: 34 -> 41, of which waited for: 7 -> 12; matrix products, arithmetic and copies ran while one was open for 10% -> 6% of each run, Pallas kernels for 4% -> 5%
where the time goes in v2:
time: 226 us; the launch traced here: 223 us
  waiting for transfers between devices  90.6 us (40%)
  starting transfers between devices  85.6 us (38%)
  Pallas kernels  18.2 us (8%)
  other arithmetic  14.1 us (6%)
  matrix products  9.32 us (4%)
  local copies, waits for them, and re-layouts  4.05 us (2%)
    ppermute x17, waiting for transfers between devices, swap(): return lax.ppermute(array, axis, [(i, i ^ bit) for i in range(size)])  73.6 us
    ppermute x17, starting transfers between devices, swap(): return lax.ppermute(array, axis, [(i, i ^ bit) for i in range(size)])  37.6 us
    ppermute x9, starting transfers between devices, reduce_line(): right = lax.ppermute(ahead.astype(bf16), 'branch', up[s])  34.2 us
    ppermute x9, waiting for transfers between devices, reduce_line(): right = lax.ppermute(ahead.astype(bf16), 'branch', up[s])  16 us
    pallas_call x2, Pallas kernels, shards(): pl.pallas_call(kernel, grid_spec=pltpu.PrefetchScalarGridSpec(num_scalar_...  14.6 us
    ppermute x9, starting transfers between devices, reduce_line(): left = lax.ppermute(behind.astype(bf16), 'branch', down[s])  9.64 us
    dot_general x6, matrix products, product(): jnp.dot(everything[:, j * rows:(j + 1) * rows], chunk[j], preferred_eleme...  9.32 us
    convert_element_type x6, other arithmetic, reduce_line(): left = lax.ppermute(behind.astype(bf16), 'branch', down[s])  5.13 us
  transfers between devices with their start and end apart: 41, of which 12 were waited for; matrix products, arithmetic and copies ran while one was open for 6% of the time, Pallas kernels for 5%

profile of v2, /device:TPU:0, one launch (start us, length us, event | category | flops | bytes accessed | tf_op | source)
XLA Modules:
  0.0 222.7 jit_solution(5401215308325315966)
XLA Ops:
  0.7 1.9 multiply_convert_fusion.1
  3.9 3.0 %collective-permute-start.16 = (bf16[1024,512]{1,0:T(8,128)(2,1)S(1)}, bf16[1024,512]{1,0:T(8,128)(2,1)S(1)}, u32[]{:S(2)}, u32[]{:S(2)}) collective-permute-start(bf16[1024,512]{1,0:T(8,128)(2,1)S(1)} %get-tuple-element.21), channel_id=1, source_target_pairs={{0,1},{1,0},{2,3},{3,2},{4,5},{5,4},{6,7},{7,6},{8,9},{9,8},{10,11... | collective-permute-start | bytes 3145736 | tf_op jit(solution)/shard_map/ppermute | solution.py:169
  7.3 2.6 %collective-permute-start.13 = (f32[3,128]{1,0:T(4,128)S(1)}, f32[3,128]{1,0:T(4,128)S(1)}, u32[]{:S(2)}, u32[]{:S(2)}) collective-permute-start(f32[3,128]{1,0:T(4,128)S(1)} %multiply_reduce_fusion), channel_id=1, source_target_pairs={{0,8},{8,0},{16,24},{24,16},{1,9},{9,1},{17,25},{25,17},{2,10},{10... | collective-permute-start | bytes 4616 | tf_op jit(solution)/shard_map/ppermute | solution.py:169
  10.7 2.9 %collective-permute-start.14 = (f32[3,128]{1,0:T(4,128)S(1)}, f32[3,128]{1,0:T(4,128)S(1)}, u32[]{:S(2)}, u32[]{:S(2)}) collective-permute-start(f32[3,128]{1,0:T(4,128)S(1)} %add.137), channel_id=1, source_target_pairs={{0,16},{8,24},{16,0},{24,8},{1,17},{9,25},{17,1},{25,9},{2,18},{10... | collective-permute-start | bytes 4616 | tf_op jit(solution)/shard_map/ppermute | solution.py:169
  14.5 6.1 %collective-permute-done.14 = f32[3,128]{1,0:T(4,128)S(1)} collective-permute-done((f32[3,128]{1,0:T(4,128)S(1)}, f32[3,128]{1,0:T(4,128)S(1)}, u32[]{:S(2)}, u32[]{:S(2)}) %collective-permute-start.14) | collective-permute-done | bytes 1568 | tf_op jit(solution)/shard_map/ppermute | solution.py:169
  23.6 16.2 %collective-permute-done.6 = bf16[1024,256]{1,0:T(8,128)(2,1)S(1)} collective-permute-done((bf16[1024,256]{1,0:T(8,128)(2,1)S(1)}, bf16[1024,256]{1,0:T(8,128)(2,1)S(1)}, u32[]{:S(2)}, u32[]{:S(2)}) %collective-permute-start.6) | collective-permute-done | bytes 524320 | tf_op jit(solution)/shard_map/ppermute | solution.py:169
  41.2 10.0 %collective-permute-start.18 = (bf16[128,2048]{1,0:T(8,128)(2,1)S(1)}, bf16[128,2048]{1,0:T(8,128)(2,1)S(1)}, u32[]{:S(2)}, u32[]{:S(2)}) collective-permute-start(bf16[128,2048]{1,0:T(8,128)(2,1)S(1)} %collective-permute-done.15), channel_id=1, source_target_pairs={{0,8},{8,0},{16,24},{24,16},{1,9},{9,1},{17,25},{25,17},{2,10},{10... | collective-permute-start | bytes 1572872 | tf_op jit(solution)/shard_map/ppermute | solution.py:169
  52.6 9.6 %collective-permute-done.8 = bf16[1024,512]{1,0:T(8,128)(2,1)S(1)} collective-permute-done((bf16[1024,512]{1,0:T(8,128)(2,1)S(1)}, bf16[1024,512]{1,0:T(8,128)(2,1)S(1)}, u32[]{:S(2)}, u32[]{:S(2)}) %collective-permute-start.8) | collective-permute-done | bytes 1048608 | tf_op jit(solution)/shard_map/ppermute | solution.py:169
  62.2 3.2 %collective-permute-start.9 = (bf16[128,2048]{1,0:T(8,128)(2,1)S(1)}, bf16[128,2048]{1,0:T(8,128)(2,1)}, u32[]{:S(2)}, u32[]{:S(2)}) collective-permute-start(bf16[128,2048]{1,0:T(8,128)(2,1)S(1)} %collective-permute-done.7), channel_id=1, source_target_pairs={{0,16},{8,24},{16,0},{24,8},{1,17},{9,25},{17,1},{25,9},{2,18},{10... | collective-permute-start | bytes 1572872 | tf_op jit(solution)/shard_map/ppermute | solution.py:169
  65.5 6.1 %collective-permute-start.2 = (bf16[128,2048]{1,0:T(8,128)(2,1)S(1)}, bf16[128,2048]{1,0:T(8,128)(2,1)}, u32[]{:S(2)}, u32[]{:S(2)}) collective-permute-start(bf16[128,2048]{1,0:T(8,128)(2,1)S(1)} %collective-permute-done.1), channel_id=1, source_target_pairs={{0,16},{8,24},{16,0},{24,8},{1,17},{9,25},{17,1},{25,9},{2,18},{10... | collective-permute-start | bytes 1572872 | tf_op jit(solution)/shard_map/ppermute | solution.py:169
  72.9 5.1 %collective-permute-done.9 = bf16[128,2048]{1,0:T(8,128)(2,1)} collective-permute-done((bf16[128,2048]{1,0:T(8,128)(2,1)S(1)}, bf16[128,2048]{1,0:T(8,128)(2,1)}, u32[]{:S(2)}, u32[]{:S(2)}) %collective-permute-start.9) | collective-permute-done | bytes 524320 | tf_op jit(solution)/shard_map/ppermute | solution.py:169
  78.8 10.5 %collective-permute-done.2 = bf16[128,2048]{1,0:T(8,128)(2,1)} collective-permute-done((bf16[128,2048]{1,0:T(8,128)(2,1)S(1)}, bf16[128,2048]{1,0:T(8,128)(2,1)}, u32[]{:S(2)}, u32[]{:S(2)}) %collective-permute-start.2) | collective-permute-done | bytes 524320 | tf_op jit(solution)/shard_map/ppermute | solution.py:169
  91.6 4.9 %maximum_maximum_fusion = bf16[4,384,2048]{2,1,0:T(8,128)(2,1)S(1)} fusion(bf16[1,128,2048]{2,1,0:T(8,128)(2,1)} %bitcast.14, bf16[1,128,2048]{2,1,0:T(8,128)(2,1)S(1)} %bitcast.119, bf16[1,128,2048]{2,1,0:T(8,128)(2,1)} %bitcast.12, bf16[1,128,2048]{2,1,0:T(8,128)(2,1)S(1)} %bitcast.116, bf16[1,128,2048]{2,1,0:T(8,128)(2,1)} %bitcast.10, ...), kind=kLoop, calls=%fused_computation | loop fusion | flops 75497472 | bytes 12582912 | tf_op jit(solution)/shard_map/concatenate | solution.py:242
  103.3 4.3 %collective-permute-start.26 = (bf16[384,256]{1,0:T(8,128)(2,1)S(1)}, bf16[384,256]{1,0:T(8,128)(2,1)S(1)}, u32[]{:S(2)}, u32[]{:S(2)}) collective-permute-start(bf16[384,256]{1,0:T(8,128)(2,1)S(1)} %get-tuple-element.40), channel_id=1, source_target_pairs={{0,2},{1,3},{8,10},{9,11},{16,18},{17,19},{24,26},{25,27}} | collective-permute-start | bytes 589832 | tf_op jit(solution)/shard_map/ppermute | solution.py:270
  111.1 1.9 fusion.15
  114.5 2.7 %collective-permute-start.20 = (bf16[384,512]{1,0:T(8,128)(2,1)}, bf16[384,512]{1,0:T(8,128)(2,1)}, u32[]{:S(2)}, u32[]{:S(2)}) collective-permute-start(bf16[384,512]{1,0:T(8,128)(2,1)} %get-tuple-element.34), channel_id=1, source_target_pairs={{0,2},{1,3},{8,10},{9,11},{16,18},{17,19},{24,26},{25,27}} | collective-permute-start | bytes 1179656 | tf_op jit(solution)/shard_map/ppermute | solution.py:270
  117.1 2.0 collective-permute-start.35
  119.3 4.0 %collective-permute-start.27 = (bf16[384,256]{1,0:T(8,128)(2,1)S(1)}, bf16[384,256]{1,0:T(8,128)(2,1)S(1)}, u32[]{:S(2)}, u32[]{:S(2)}) collective-permute-start(bf16[384,256]{1,0:T(8,128)(2,1)S(1)} %get-tuple-element.38), channel_id=1, source_target_pairs={{0,2},{1,3},{2,4},{3,5},{8,10},{9,11},{10,12},{11,13},{16,18},{17,... | collective-permute-start | bytes 589832 | tf_op jit(solution)/shard_map/ppermute | solution.py:270
  125.6 12.3 %collective-permute-done.27 = bf16[384,256]{1,0:T(8,128)(2,1)S(1)} collective-permute-done((bf16[384,256]{1,0:T(8,128)(2,1)S(1)}, bf16[384,256]{1,0:T(8,128)(2,1)S(1)}, u32[]{:S(2)}, u32[]{:S(2)}) %collective-permute-start.27) | collective-permute-done | bytes 196640 | tf_op jit(solution)/shard_map/ppermute | solution.py:270
  139.3 5.7 %collective-permute-start.28 = (bf16[384,256]{1,0:T(8,128)(2,1)S(1)}, bf16[384,256]{1,0:T(8,128)(2,1)}, u32[]{:S(2)}, u32[]{:S(2)}) collective-permute-start(bf16[384,256]{1,0:T(8,128)(2,1)S(1)} %fusion.38), channel_id=1, source_target_pairs={{0,2},{1,3},{2,4},{3,5},{4,6},{5,7},{8,10},{9,11},{10,12},{11,13},... | collective-permute-start | bytes 589832 | tf_op jit(solution)/shard_map/ppermute | solution.py:270
  149.1 3.6 %finish_kv.1 = (bf16[384,256]{1,0:T(8,128)(2,1)}, f32[384,128]{1,0:T(8,128)}, f32[384,128]{1,0:T(8,128)}) custom-call(s32[3]{0:T(128)} %pad_add_fusion.meta_ref.refs_0_, s32[24]{0:T(128)} %refs_1_.1, bf16[384,256]{1,0:T(8,128)(2,1)} %collective-permute-done.28.right_ref, bf16[384,256]{1,0:T(8,128)(2,1)} %collective-permute-done.31.left_ref, ...), custom_call_target="tpu_custom_call" | custom-call | tf_op jit(solution)/shard_map/finish_kv/pallas_call | solution.py:281
  155.2 1.8 fusion.22
  157.0 4.5 %collective-permute-start.36 = (bf16[384,512]{1,0:T(8,128)(2,1)S(1)}, bf16[384,512]{1,0:T(8,128)(2,1)S(1)}, u32[]{:S(2)}, u32[]{:S(2)}) collective-permute-start(bf16[384,512]{1,0:T(8,128)(2,1)S(1)} %get-tuple-element.28), channel_id=1, source_target_pairs={{0,2},{1,3},{2,4},{3,5},{8,10},{9,11},{10,12},{11,13},{16,18},{17,... | collective-permute-start | bytes 1179656 | tf_op jit(solution)/shard_map/ppermute | solution.py:270
  161.6 2.0 collective-permute-start.33
  165.0 2.0 collective-permute-start.21
  169.8 6.9 %collective-permute-done.33 = bf16[2,256,256]{2,1,0:T(8,128)(2,1)S(1)} collective-permute-done((bf16[2,256,256]{2,1,0:T(8,128)(2,1)S(1)}, bf16[2,256,256]{2,1,0:T(8,128)(2,1)S(1)}, u32[]{:S(2)}, u32[]{:S(2)}) %collective-permute-start.33) | collective-permute-done | bytes 262176 | tf_op jit(solution)/shard_map/ppermute | solution.py:169
  177.0 4.4 %collective-permute-start.37 = (bf16[384,512]{1,0:T(8,128)(2,1)S(1)}, bf16[384,512]{1,0:T(8,128)(2,1)S(1)}, u32[]{:S(2)}, u32[]{:S(2)}) collective-permute-start(bf16[384,512]{1,0:T(8,128)(2,1)S(1)} %fusion.24), channel_id=1, source_target_pairs={{0,2},{1,3},{2,4},{3,5},{4,6},{5,7},{8,10},{9,11},{10,12},{11,13},... | collective-permute-start | bytes 1179656 | tf_op jit(solution)/shard_map/ppermute | solution.py:270
  181.4 3.7 %collective-permute-done.21 = bf16[384,512]{1,0:T(8,128)(2,1)S(1)} collective-permute-done((bf16[384,512]{1,0:T(8,128)(2,1)S(1)}, bf16[384,512]{1,0:T(8,128)(2,1)S(1)}, u32[]{:S(2)}, u32[]{:S(2)}) %collective-permute-start.21) | collective-permute-done | bytes 393248 | tf_op jit(solution)/shard_map/ppermute | solution.py:270
  185.3 4.4 %collective-permute-start.22 = (bf16[384,512]{1,0:T(8,128)(2,1)S(1)}, bf16[384,512]{1,0:T(8,128)(2,1)S(1)}, u32[]{:S(2)}, u32[]{:S(2)}) collective-permute-start(bf16[384,512]{1,0:T(8,128)(2,1)S(1)} %fusion.28), channel_id=1, source_target_pairs={{0,2},{1,3},{2,4},{3,5},{4,6},{5,7},{8,10},{9,11},{10,12},{11,13},... | collective-permute-start | bytes 1179656 | tf_op jit(solution)/shard_map/ppermute | solution.py:270
  189.7 18.2 %collective-permute-done.34 = bf16[4,256,256]{2,1,0:T(8,128)(2,1)S(1)} collective-permute-done((bf16[4,256,256]{2,1,0:T(8,128)(2,1)S(1)}, bf16[4,256,256]{2,1,0:T(8,128)(2,1)S(1)}, u32[]{:S(2)}, u32[]{:S(2)}) %collective-permute-start.34) | collective-permute-done | bytes 524320 | tf_op jit(solution)/shard_map/ppermute | solution.py:169
  208.1 7.3 %attend.2.refs_12_ = bf16[384,1024]{1,0:T(8,128)(2,1)} custom-call(s32[3]{0:T(128)S(1)} %copy-done.7, s32[24]{0:T(128)S(1)} %copy-done.8, s32[24]{0:T(128)S(1)} %copy-done.9, bf16[384,512]{1,0:T(8,128)(2,1)S(1)} %collective-permute-done.37.right_ref, bf16[384,512]{1,0:T(8,128)(2,1)S(1)} %collective-permute-done.40.left_ref, f32[4,384,512]{2,1,0:T(8,128)S(1)} %bitcast.101, ...), custom_call_target="tpu_custom_call" | custom-call | tf_op jit(solution)/shard_map/attend/pallas_call | solution.py:339
  215.4 7.3 %attend.3 = bf16[384,1024]{1,0:T(8,128)(2,1)} custom-call(s32[3]{0:T(128)S(1)} %copy-done.7, s32[24]{0:T(128)S(1)} %copy-done.8, s32[24]{0:T(128)S(1)} %copy-done.9, bf16[384,512]{1,0:T(8,128)(2,1)S(1)} %collective-permute-done.22.refs_3_, bf16[384,512]{1,0:T(8,128)(2,1)S(1)} %collective-permute-done.25.refs_4_, ...), custom_call_target="tpu_custom_call", output_to_operand_aliasing={{}: (12, {})} | custom-call | tf_op jit(solution)/shard_map/attend/pallas_call | solution.py:339
  (142 shorter events, 40.6 us)
Async XLA Ops:
  2.8 19.3 %collective-permute-start.12 = (bf16[128,2048]{1,0:T(8,128)(2,1)S(1)}, bf16[128,2048]{1,0:T(8,128)(2,1)S(1)}, u32[]{:S(2)}, u32[]{:S(2)}) collective-permute-start(bf16[128,2048]{1,0:T(8,128)(2,1)S(1)} %get-tuple-element.42), channel_id=1, source_target_pairs={{0,0},{8,16},{16,8},{24,24},{1,1},{9,17},{17,9},{25,25},{2,26},{10... | collective-permute-start | bytes 1572872 | tf_op jit(solution)/shard_map/ppermute | solution.py:222
  3.9 37.3 %collective-permute-start.16 = (bf16[1024,512]{1,0:T(8,128)(2,1)S(1)}, bf16[1024,512]{1,0:T(8,128)(2,1)S(1)}, u32[]{:S(2)}, u32[]{:S(2)}) collective-permute-start(bf16[1024,512]{1,0:T(8,128)(2,1)S(1)} %get-tuple-element.21), channel_id=1, source_target_pairs={{0,1},{1,0},{2,3},{3,2},{4,5},{5,4},{6,7},{7,6},{8,9},{9,8},{10,11... | collective-permute-start | bytes 3145736 | tf_op jit(solution)/shard_map/ppermute | solution.py:169
  9.9 13.0 %collective-permute-start.5 = (bf16[128,2048]{1,0:T(8,128)(2,1)S(1)}, bf16[128,2048]{1,0:T(8,128)(2,1)S(1)}, u32[]{:S(2)}, u32[]{:S(2)}) collective-permute-start(bf16[128,2048]{1,0:T(8,128)(2,1)S(1)} %get-tuple-element.43), channel_id=1, source_target_pairs={{0,0},{8,16},{16,8},{24,24},{1,1},{9,17},{17,9},{25,25},{2,26},{10... | collective-permute-start | bytes 1572872 | tf_op jit(solution)/shard_map/ppermute | solution.py:222
  13.7 26.1 %collective-permute-start.6 = (bf16[1024,256]{1,0:T(8,128)(2,1)S(1)}, bf16[1024,256]{1,0:T(8,128)(2,1)S(1)}, u32[]{:S(2)}, u32[]{:S(2)}) collective-permute-start(bf16[1024,256]{1,0:T(8,128)(2,1)S(1)} %constant_dynamic-update-slice_fusion), channel_id=1, source_target_pairs={{0,1},{1,0},{2,3},{3,2},{4,5},{5,4},{6,7},{7,6},{8,9},{9,8},{10,11... | collective-permute-start | bytes 1572872 | tf_op jit(solution)/shard_map/ppermute | solution.py:169
  20.6 41.6 %collective-permute-start.8 = (bf16[1024,512]{1,0:T(8,128)(2,1)S(1)}, bf16[1024,512]{1,0:T(8,128)(2,1)S(1)}, u32[]{:S(2)}, u32[]{:S(2)}) collective-permute-start(bf16[1024,512]{1,0:T(8,128)(2,1)S(1)} %get-tuple-element.20), channel_id=1, source_target_pairs={{0,1},{1,0},{2,3},{3,2},{4,5},{5,4},{6,7},{7,6},{8,9},{9,8},{10,11... | collective-permute-start | bytes 3145736 | tf_op jit(solution)/shard_map/ppermute | solution.py:169
  22.1 18.3 %collective-permute-start = (bf16[128,2048]{1,0:T(8,128)(2,1)S(1)}, bf16[128,2048]{1,0:T(8,128)(2,1)S(1)}, u32[]{:S(2)}, u32[]{:S(2)}) collective-permute-start(bf16[128,2048]{1,0:T(8,128)(2,1)S(1)} %get-tuple-element.41), channel_id=1, source_target_pairs={{0,0},{8,16},{16,8},{24,24},{1,1},{9,17},{17,9},{25,25},{2,26},{10... | collective-permute-start | bytes 1572872 | tf_op jit(solution)/shard_map/ppermute | solution.py:222
  22.9 18.3 %collective-permute-start.15 = (bf16[128,2048]{1,0:T(8,128)(2,1)S(1)}, bf16[128,2048]{1,0:T(8,128)(2,1)S(1)}, u32[]{:S(2)}, u32[]{:S(2)}) collective-permute-start(bf16[128,2048]{1,0:T(8,128)(2,1)S(1)} %collective-permute-done.12), channel_id=1, source_target_pairs={{0,0},{16,18},{8,4},{24,22},{1,1},{17,19},{9,5},{25,23},{26,16},{1... | collective-permute-start | bytes 1572872 | tf_op jit(solution)/shard_map/ppermute | solution.py:225
  39.8 12.8 %collective-permute-start.7 = (bf16[128,2048]{1,0:T(8,128)(2,1)S(1)}, bf16[128,2048]{1,0:T(8,128)(2,1)S(1)}, u32[]{:S(2)}, u32[]{:S(2)}) collective-permute-start(bf16[128,2048]{1,0:T(8,128)(2,1)S(1)} %collective-permute-done.5), channel_id=1, source_target_pairs={{0,0},{16,18},{8,4},{24,22},{1,1},{17,19},{9,5},{25,23},{26,16},{1... | collective-permute-start | bytes 1572872 | tf_op jit(solution)/shard_map/ppermute | solution.py:225
  40.5 25.0 %collective-permute-start.1 = (bf16[128,2048]{1,0:T(8,128)(2,1)S(1)}, bf16[128,2048]{1,0:T(8,128)(2,1)S(1)}, u32[]{:S(2)}, u32[]{:S(2)}) collective-permute-start(bf16[128,2048]{1,0:T(8,128)(2,1)S(1)} %collective-permute-done), channel_id=1, source_target_pairs={{0,0},{16,18},{8,4},{24,22},{1,1},{17,19},{9,5},{25,23},{26,16},{1... | collective-permute-start | bytes 1572872 | tf_op jit(solution)/shard_map/ppermute | solution.py:225
  41.2 31.2 %collective-permute-start.18 = (bf16[128,2048]{1,0:T(8,128)(2,1)S(1)}, bf16[128,2048]{1,0:T(8,128)(2,1)S(1)}, u32[]{:S(2)}, u32[]{:S(2)}) collective-permute-start(bf16[128,2048]{1,0:T(8,128)(2,1)S(1)} %collective-permute-done.15), channel_id=1, source_target_pairs={{0,8},{8,0},{16,24},{24,16},{1,9},{9,1},{17,25},{25,17},{2,10},{10... | collective-permute-start | bytes 1572872 | tf_op jit(solution)/shard_map/ppermute | solution.py:169
  51.2 21.2 %collective-permute-start.17 = (bf16[128,2048]{1,0:T(8,128)(2,1)S(1)}, bf16[128,2048]{1,0:T(8,128)(2,1)}, u32[]{:S(2)}, u32[]{:S(2)}) collective-permute-start(bf16[128,2048]{1,0:T(8,128)(2,1)S(1)} %collective-permute-done.15), channel_id=1, source_target_pairs={{0,16},{8,24},{16,0},{24,8},{1,17},{9,25},{17,1},{25,9},{2,18},{10... | collective-permute-start | bytes 1572872 | tf_op jit(solution)/shard_map/ppermute | solution.py:169
  62.2 15.8 %collective-permute-start.9 = (bf16[128,2048]{1,0:T(8,128)(2,1)S(1)}, bf16[128,2048]{1,0:T(8,128)(2,1)}, u32[]{:S(2)}, u32[]{:S(2)}) collective-permute-start(bf16[128,2048]{1,0:T(8,128)(2,1)S(1)} %collective-permute-done.7), channel_id=1, source_target_pairs={{0,16},{8,24},{16,0},{24,8},{1,17},{9,25},{17,1},{25,9},{2,18},{10... | collective-permute-start | bytes 1572872 | tf_op jit(solution)/shard_map/ppermute | solution.py:169
  65.5 23.8 %collective-permute-start.2 = (bf16[128,2048]{1,0:T(8,128)(2,1)S(1)}, bf16[128,2048]{1,0:T(8,128)(2,1)}, u32[]{:S(2)}, u32[]{:S(2)}) collective-permute-start(bf16[128,2048]{1,0:T(8,128)(2,1)S(1)} %collective-permute-done.1), channel_id=1, source_target_pairs={{0,16},{8,24},{16,0},{24,8},{1,17},{9,25},{17,1},{25,9},{2,18},{10... | collective-permute-start | bytes 1572872 | tf_op jit(solution)/shard_map/ppermute | solution.py:169
  71.6 19.1 %collective-permute-start.10 = (bf16[128,2048]{1,0:T(8,128)(2,1)S(1)}, bf16[128,2048]{1,0:T(8,128)(2,1)}, u32[]{:S(2)}, u32[]{:S(2)}) collective-permute-start(bf16[128,2048]{1,0:T(8,128)(2,1)S(1)} %collective-permute-done.7), channel_id=1, source_target_pairs={{0,8},{8,0},{16,24},{24,16},{1,9},{9,1},{17,25},{25,17},{2,10},{10... | collective-permute-start | bytes 1572872 | tf_op jit(solution)/shard_map/ppermute | solution.py:169
  72.4 18.2 %collective-permute-start.3 = (bf16[128,2048]{1,0:T(8,128)(2,1)S(1)}, bf16[128,2048]{1,0:T(8,128)(2,1)}, u32[]{:S(2)}, u32[]{:S(2)}) collective-permute-start(bf16[128,2048]{1,0:T(8,128)(2,1)S(1)} %collective-permute-done.1), channel_id=1, source_target_pairs={{0,8},{8,0},{16,24},{24,16},{1,9},{9,1},{17,25},{25,17},{2,10},{10... | collective-permute-start | bytes 1572872 | tf_op jit(solution)/shard_map/ppermute | solution.py:169
  72.4 18.2 %collective-permute-start.19 = (bf16[128,2048]{1,0:T(8,128)(2,1)}, bf16[128,2048]{1,0:T(8,128)(2,1)}, u32[]{:S(2)}, u32[]{:S(2)}) collective-permute-start(bf16[128,2048]{1,0:T(8,128)(2,1)} %collective-permute-done.17), channel_id=1, source_target_pairs={{0,8},{8,0},{16,24},{24,16},{1,9},{9,1},{17,25},{25,17},{2,10},{10... | collective-permute-start | bytes 1572872 | tf_op jit(solution)/shard_map/ppermute | solution.py:169
  103.3 13.8 %collective-permute-start.26 = (bf16[384,256]{1,0:T(8,128)(2,1)S(1)}, bf16[384,256]{1,0:T(8,128)(2,1)S(1)}, u32[]{:S(2)}, u32[]{:S(2)}) collective-permute-start(bf16[384,256]{1,0:T(8,128)(2,1)S(1)} %get-tuple-element.40), channel_id=1, source_target_pairs={{0,2},{1,3},{8,10},{9,11},{16,18},{17,19},{24,26},{25,27}} | collective-permute-start | bytes 589832 | tf_op jit(solution)/shard_map/ppermute | solution.py:270
  107.6 15.7 %collective-permute-start.38 = (bf16[384,512]{1,0:T(8,128)(2,1)S(1)}, bf16[384,512]{1,0:T(8,128)(2,1)S(1)}, u32[]{:S(2)}, u32[]{:S(2)}) collective-permute-start(bf16[384,512]{1,0:T(8,128)(2,1)S(1)} %get-tuple-element.29), channel_id=1, source_target_pairs={{6,4},{7,5},{14,12},{15,13},{22,20},{23,21},{30,28},{31,29}} | collective-permute-start | bytes 1179656 | tf_op jit(solution)/shard_map/ppermute | solution.py:271
  113.8 25.5 %collective-permute-start.23 = (bf16[384,512]{1,0:T(8,128)(2,1)S(1)}, bf16[384,512]{1,0:T(8,128)(2,1)S(1)}, u32[]{:S(2)}, u32[]{:S(2)}) collective-permute-start(bf16[384,512]{1,0:T(8,128)(2,1)S(1)} %get-tuple-element.33), channel_id=1, source_target_pairs={{6,4},{7,5},{14,12},{15,13},{22,20},{23,21},{30,28},{31,29}} | collective-permute-start | bytes 1179656 | tf_op jit(solution)/shard_map/ppermute | solution.py:271
  114.5 49.1 %collective-permute-start.20 = (bf16[384,512]{1,0:T(8,128)(2,1)}, bf16[384,512]{1,0:T(8,128)(2,1)}, u32[]{:S(2)}, u32[]{:S(2)}) collective-permute-start(bf16[384,512]{1,0:T(8,128)(2,1)} %get-tuple-element.34), channel_id=1, source_target_pairs={{0,2},{1,3},{8,10},{9,11},{16,18},{17,19},{24,26},{25,27}} | collective-permute-start | bytes 1179656 | tf_op jit(solution)/shard_map/ppermute | solution.py:270
  117.1 38.0 %collective-permute-start.35 = (bf16[384,512]{1,0:T(8,128)(2,1)S(1)}, bf16[384,512]{1,0:T(8,128)(2,1)}, u32[]{:S(2)}, u32[]{:S(2)}) collective-permute-start(bf16[384,512]{1,0:T(8,128)(2,1)S(1)} %get-tuple-element.30), channel_id=1, source_target_pairs={{0,2},{1,3},{8,10},{9,11},{16,18},{17,19},{24,26},{25,27}} | collective-permute-start | bytes 1179656 | tf_op jit(solution)/shard_map/ppermute | solution.py:270
  119.3 18.6 %collective-permute-start.27 = (bf16[384,256]{1,0:T(8,128)(2,1)S(1)}, bf16[384,256]{1,0:T(8,128)(2,1)S(1)}, u32[]{:S(2)}, u32[]{:S(2)}) collective-permute-start(bf16[384,256]{1,0:T(8,128)(2,1)S(1)} %get-tuple-element.38), channel_id=1, source_target_pairs={{0,2},{1,3},{2,4},{3,5},{8,10},{9,11},{10,12},{11,13},{16,18},{17,... | collective-permute-start | bytes 589832 | tf_op jit(solution)/shard_map/ppermute | solution.py:270
  124.2 31.0 %collective-permute-start.39 = (bf16[384,512]{1,0:T(8,128)(2,1)}, bf16[384,512]{1,0:T(8,128)(2,1)}, u32[]{:S(2)}, u32[]{:S(2)}) collective-permute-start(bf16[384,512]{1,0:T(8,128)(2,1)} %fusion.21), channel_id=1, source_target_pairs={{6,4},{7,5},{4,2},{5,3},{14,12},{15,13},{12,10},{13,11},{22,20},{2... | collective-permute-start | bytes 1179656 | tf_op jit(solution)/shard_map/ppermute | solution.py:271
  146.8 16.8 %collective-permute-start.24 = (bf16[384,512]{1,0:T(8,128)(2,1)}, bf16[384,512]{1,0:T(8,128)(2,1)}, u32[]{:S(2)}, u32[]{:S(2)}) collective-permute-start(bf16[384,512]{1,0:T(8,128)(2,1)} %fusion.25), channel_id=1, source_target_pairs={{6,4},{7,5},{4,2},{5,3},{14,12},{15,13},{12,10},{13,11},{22,20},{2... | collective-permute-start | bytes 1179656 | tf_op jit(solution)/shard_map/ppermute | solution.py:271
  157.0 19.8 %collective-permute-start.36 = (bf16[384,512]{1,0:T(8,128)(2,1)S(1)}, bf16[384,512]{1,0:T(8,128)(2,1)S(1)}, u32[]{:S(2)}, u32[]{:S(2)}) collective-permute-start(bf16[384,512]{1,0:T(8,128)(2,1)S(1)} %get-tuple-element.28), channel_id=1, source_target_pairs={{0,2},{1,3},{2,4},{3,5},{8,10},{9,11},{10,12},{11,13},{16,18},{17,... | collective-permute-start | bytes 1179656 | tf_op jit(solution)/shard_map/ppermute | solution.py:270
  161.6 15.1 %collective-permute-start.33 = (bf16[2,256,256]{2,1,0:T(8,128)(2,1)S(1)}, bf16[2,256,256]{2,1,0:T(8,128)(2,1)S(1)}, u32[]{:S(2)}, u32[]{:S(2)}) collective-permute-start(bf16[2,256,256]{2,1,0:T(8,128)(2,1)S(1)} %pad_maximum_fusion.3), channel_id=1, source_target_pairs={{0,2},{1,3},{2,0},{3,1},{4,6},{5,7},{6,4},{7,5},{8,10},{9,11},{10,... | collective-permute-start | bytes 786440 | tf_op jit(solution)/shard_map/ppermute | solution.py:169
  165.0 20.2 %collective-permute-start.21 = (bf16[384,512]{1,0:T(8,128)(2,1)S(1)}, bf16[384,512]{1,0:T(8,128)(2,1)S(1)}, u32[]{:S(2)}, u32[]{:S(2)}) collective-permute-start(bf16[384,512]{1,0:T(8,128)(2,1)S(1)} %get-tuple-element.32), channel_id=1, source_target_pairs={{0,2},{1,3},{2,4},{3,5},{8,10},{9,11},{10,12},{11,13},{16,18},{17,... | collective-permute-start | bytes 1179656 | tf_op jit(solution)/shard_map/ppermute | solution.py:270
  167.0 48.4 %collective-permute-start.25 = (bf16[384,512]{1,0:T(8,128)(2,1)S(1)}, bf16[384,512]{1,0:T(8,128)(2,1)S(1)}, u32[]{:S(2)}, u32[]{:S(2)}) collective-permute-start(bf16[384,512]{1,0:T(8,128)(2,1)S(1)} %get-tuple-element.31), channel_id=1, source_target_pairs={{6,4},{7,5},{4,2},{5,3},{2,0},{3,1},{14,12},{15,13},{12,10},{13,11... | collective-permute-start | bytes 1179656 | tf_op jit(solution)/shard_map/ppermute | solution.py:271
  168.4 39.6 %collective-permute-start.40 = (bf16[384,512]{1,0:T(8,128)(2,1)S(1)}, bf16[384,512]{1,0:T(8,128)(2,1)S(1)}, u32[]{:S(2)}, u32[]{:S(2)}) collective-permute-start(bf16[384,512]{1,0:T(8,128)(2,1)S(1)} %get-tuple-element.27), channel_id=1, source_target_pairs={{6,4},{7,5},{4,2},{5,3},{2,0},{3,1},{14,12},{15,13},{12,10},{13,11... | collective-permute-start | bytes 1179656 | tf_op jit(solution)/shard_map/ppermute | solution.py:271
  176.8 31.1 %collective-permute-start.34 = (bf16[4,256,256]{2,1,0:T(8,128)(2,1)S(1)}, bf16[4,256,256]{2,1,0:T(8,128)(2,1)S(1)}, u32[]{:S(2)}, u32[]{:S(2)}) collective-permute-start(bf16[4,256,256]{2,1,0:T(8,128)(2,1)S(1)} %pad_maximum_fusion.2), channel_id=1, source_target_pairs={{0,4},{1,5},{2,6},{3,7},{4,0},{5,1},{6,2},{7,3},{8,12},{9,13},{10,... | collective-permute-start | bytes 1572872 | tf_op jit(solution)/shard_map/ppermute | solution.py:169
  177.0 31.0 %collective-permute-start.37 = (bf16[384,512]{1,0:T(8,128)(2,1)S(1)}, bf16[384,512]{1,0:T(8,128)(2,1)S(1)}, u32[]{:S(2)}, u32[]{:S(2)}) collective-permute-start(bf16[384,512]{1,0:T(8,128)(2,1)S(1)} %fusion.24), channel_id=1, source_target_pairs={{0,2},{1,3},{2,4},{3,5},{4,6},{5,7},{8,10},{9,11},{10,12},{11,13},... | collective-permute-start | bytes 1179656 | tf_op jit(solution)/shard_map/ppermute | solution.py:270
  185.3 30.1 %collective-permute-start.22 = (bf16[384,512]{1,0:T(8,128)(2,1)S(1)}, bf16[384,512]{1,0:T(8,128)(2,1)S(1)}, u32[]{:S(2)}, u32[]{:S(2)}) collective-permute-start(bf16[384,512]{1,0:T(8,128)(2,1)S(1)} %fusion.28), channel_id=1, source_target_pairs={{0,2},{1,3},{2,4},{3,5},{4,6},{5,7},{8,10},{9,11},{10,12},{11,13},... | collective-permute-start | bytes 1179656 | tf_op jit(solution)/shard_map/ppermute | solution.py:270
  (36 other events, 892.3 us)

commit v3 on v2

v3 whole, which is shorter than its diff:
```python
import functools
import math

import jax
import jax.numpy as jnp
from jax import lax
from jax.experimental import pallas as pl
from jax.experimental.pallas import tpu as pltpu
from jax.sharding import PartitionSpec as P

HD = 128
STEMS = 2
THETA = 1000000.0
NEG = -1e30


def bits_of(count):
    return count.bit_length() - 1


def tie(array, *others):
    return lax.optimization_barrier((array,) + others)[0]


def far_chain(parents_ref, first_block, far_slots):
    cursor = parents_ref[first_block]
    ids = []
    total = jnp.int32(0)
    for level in range(far_slots):
        ids.append(cursor)
        total = total + jnp.where(cursor >= 0, 1, 0)
        above = parents_ref[jnp.maximum(cursor, 0)]
        cursor = jnp.where(cursor >= 0, above, -1)
    return ids, total


def add_up(refs, inverse, bias, columns):
    total = refs[0][0, :, columns]
    for ref in refs[1:]:
        total = total + ref[0, :, columns].astype(jnp.float32)
    repeats = total.shape[1] // HD
    inverse = jnp.concatenate([inverse] * repeats, 1)
    return jnp.where(inverse > 0, total * inverse, 0.0) + bias


def turn(vectors, cos, sin):
    half = vectors.shape[-1] // 2
    return vectors * cos + pltpu.roll(vectors, half, 1) * sin


def table_kernel(far_slots, blocks, block_len, device_ref, parents_ref, cos_ref, sin_ref):
    tokens = cos_ref.shape[0]
    unused, far_total = far_chain(parents_ref, device_ref[0] * blocks, far_slots)
    rows = lax.broadcasted_iota(jnp.int32, (tokens, HD), 0)
    lanes = lax.broadcasted_iota(jnp.int32, (tokens, HD), 1)
    front = lanes < HD // 2
    pair = jnp.where(front, lanes, lanes - HD // 2).astype(jnp.float32)
    freqs = jnp.exp(pair * (-2.0 * math.log(THETA) / HD))
    angles = (rows + far_total * block_len).astype(jnp.float32) * freqs
    sin = jnp.sin(angles)
    cos_ref[...] = jnp.cos(angles)
    sin_ref[...] = jnp.where(front, -sin, sin)


def project_kernel(lines, blocks, groups, chunks, place_ref, *refs):
    pieces = refs[: lines * blocks]
    refs = refs[lines * blocks :]
    weights = refs[: groups * chunks]
    send_ref, keep_ref, held, sems = refs[groups * chunks :]
    half = lines // 2
    block_len = held.shape[1] // blocks
    copies = []
    for i in range(lines):
        target = lax.bitwise_xor(jnp.int32(i), place_ref[0])
        slot = jnp.where(target % 2 == 0, half, 0) + target // 2
        for block in range(blocks):
            copy = pltpu.make_async_copy(
                pieces[i * blocks + block],
                held.at[slot, pl.ds(block * block_len, block_len)],
                sems.at[i * blocks + block],
            )
            copy.start()
            copies.append(copy)
    for copy in copies:
        copy.wait()
    rows = weights[0].shape[0]

    def step(slot, carry):
        start = 0
        for chunk in range(chunks):
            total = None
            for g in range(groups):
                term = jnp.dot(
                    held[slot, :, g * rows : (g + 1) * rows],
                    weights[chunk * groups + g][...],
                    preferred_element_type=jnp.float32,
                )
                total = term if total is None else total + term
            stop = start + total.shape[1]

            @pl.when(slot < half)
            def _():
                send_ref[slot, :, start:stop] = total.astype(jnp.bfloat16)

            @pl.when(slot >= half)
            def _():
                keep_ref[slot - half, :, start:stop] = total

            start = stop
        return carry

    lax.fori_loop(0, lines, step, 0)


def kv_kernel(addends, inverse_ref, bias_ref, cos_ref, sin_ref, *refs):
    kv_ref = refs[-1]
    both = add_up(refs[:addends], inverse_ref[...], bias_ref[...], slice(0, 2 * HD))
    kv_ref[:, :HD] = turn(both[:, :HD], cos_ref[...], sin_ref[...]).astype(jnp.bfloat16)
    kv_ref[:, HD:] = both[:, HD:].astype(jnp.bfloat16)


def attend_kernel(
    far_slots, block_len, blocks, heads, first_head, parts, addends, aliased, device_ref,
    parents_ref, lengths_ref, inverse_ref, bias_ref, cos_ref, sin_ref, stems_ref, *refs,
):
    keys = refs[:2]
    refs = refs[2:]
    sums = [refs[p * addends : (p + 1) * addends] for p in range(len(parts))]
    refs = refs[len(parts) * addends + aliased :]
    out_ref, far_key, far_value, far_mask, held, sems = refs
    device = device_ref[0]
    first_block = device * blocks
    ids, unused = far_chain(parents_ref, first_block, far_slots)
    for level in range(far_slots):
        live = ids[level] >= 0
        safe = jnp.maximum(ids[level], 0)
        owner = lax.div(safe, jnp.int32(blocks))
        inner = lax.rem(safe, jnp.int32(blocks))
        where = lax.bitwise_xor(owner, device)
        start = pl.multiple_of(inner * block_len, block_len)
        here = pl.ds(level * block_len, block_len)
        far_key[here, :] = stems_ref[where, pl.ds(start, block_len), :HD]
        far_value[here, :] = stems_ref[where, pl.ds(start, block_len), HD:]
        far_mask[:, here] = jnp.broadcast_to(jnp.where(live, 0.0, NEG), (8, block_len))

    factor = HD ** (-0.5) * math.log2(math.e)
    contract = (((1,), (1,)), ((), ()))
    rows = heads * block_len
    column = lax.broadcasted_iota(jnp.int32, (rows, block_len), 1)
    row = lax.broadcasted_iota(jnp.int32, (rows, block_len), 0) % block_len
    near = [(keys[0], block * block_len) for block in range(STEMS)]
    near += [(keys[1], (block - STEMS) * block_len) for block in range(STEMS, blocks)]
    copies = []
    for p, (first, count, offset) in enumerate(parts):
        for inside in range(count):
            block = first + inside
            here = slice(block * block_len, (block + 1) * block_len)
            mine = slice(inside * block_len, (inside + 1) * block_len)
            total = sums[p][0][0, mine, offset : offset + heads * HD]
            for ref in sums[p][1:]:
                total = total + ref[0, mine, offset : offset + heads * HD].astype(jnp.float32)
            inverse = inverse_ref[here]
            query = []
            for head in range(heads):
                lanes = slice(head * HD, (head + 1) * HD)
                one = jnp.where(inverse > 0, total[:, lanes] * inverse, 0.0)
                one = one + bias_ref[:, lanes]
                query.append(turn(one, cos_ref[here], sin_ref[here]).astype(jnp.bfloat16))
            query = jnp.concatenate(query, 0)
            far = lax.dot_general(
                query, far_key[...], contract, preferred_element_type=jnp.float32
            )
            scores = [far + far_mask[0:1, :]]
            for other in range(block + 1):
                ref, begin = near[other]
                score = lax.dot_general(
                    query,
                    ref[begin : begin + block_len, :HD],
                    contract,
                    preferred_element_type=jnp.float32,
                )
                if other == block or other >= STEMS:
                    seen = column < lengths_ref[first_block + other]
                    if other == block:
                        seen = seen & (column <= row)
                    score = jnp.where(seen, score, NEG)
                scores.append(score)
            peak = functools.reduce(
                jnp.maximum, [jnp.max(score, -1, keepdims=True) for score in scores]
            )
            peak = peak * factor
            exps = [jnp.exp2(score * factor - peak) for score in scores]
            total = functools.reduce(jnp.add, [jnp.sum(e, -1, keepdims=True) for e in exps])
            output = jnp.dot(
                exps[0].astype(jnp.bfloat16), far_value[...], preferred_element_type=jnp.float32
            )
            for other in range(block + 1):
                ref, begin = near[other]
                output += jnp.dot(
                    exps[1 + other].astype(jnp.bfloat16),
                    ref[begin : begin + block_len, HD:],
                    preferred_element_type=jnp.float32,
                )
            output = output / total
            if block >= STEMS:
                output = jnp.where(row < lengths_ref[first_block + block], output, 0.0)
            output = output.astype(jnp.bfloat16)
            for head in range(heads):
                lanes = slice(head * HD, (head + 1) * HD)
                held[here, lanes] = output[head * block_len : (head + 1) * block_len]
            copy = pltpu.make_async_copy(
                held.at[pl.ds(block * block_len, block_len)],
                out_ref.at[pl.ds(block * block_len, block_len), pl.ds(first_head * HD, heads * HD)],
                sems.at[block],
            )
            copy.start()
            copies.append(copy)
    for copy in copies:
        copy.wait()


def shards(
    hidden, parents, lengths, gain, w_query, w_key, w_value, query_bias, key_bias, value_bias
):
    blocks, block_len, feature_part = hidden.shape
    tokens = blocks * block_len
    features = gain.shape[0]
    rows = w_query.shape[0]
    columns = w_query.shape[1]
    head_count = columns // HD
    lines = lax.axis_size("fsdp")
    branches = lax.axis_size("branch")
    groups = branches // lines
    far_slots = STEMS * bits_of(branches)
    part = lax.axis_index("fsdp")
    device = lax.axis_index("branch")
    member = device % groups
    level = device // groups
    bf16 = jnp.bfloat16
    f32 = jnp.float32
    half_lines = lines // 2
    top = bits_of(half_lines)
    kv_width = 2 * HD

    def swap(array, axis, bit):
        size = lax.axis_size(axis)
        return lax.ppermute(array, axis, [(i, i ^ bit) for i in range(size)])

    def spread(index):
        return ((index & 1) << top) | (index >> 1)

    smem = pl.BlockSpec(memory_space=pltpu.SMEM)
    vmem = pl.BlockSpec(memory_space=pltpu.VMEM)
    anywhere = pl.BlockSpec(memory_space=pl.ANY)
    device_id = device.astype(jnp.int32)[None]
    place = spread(part).astype(jnp.int32)[None]

    raw = hidden.reshape(tokens, feature_part)
    pieces = []
    for j in range(groups):
        start = (member ^ j) * rows
        gain_here = lax.dynamic_slice_in_dim(gain, part * feature_part + start, rows)
        piece = lax.dynamic_slice_in_dim(raw, start, rows, axis=1).astype(f32) * gain_here
        pieces.append(piece.astype(bf16))
    scaled = jnp.concatenate(pieces, 1)

    def column(z, feature):
        return (z ^ feature) & (half_lines - 1)

    def middle(z, feature):
        return (column(z, feature) << 1) | ((feature >> top) ^ (z & 1))

    def landing(z, feature):
        return (column(z, feature) << 1) | ((z ^ feature) >> top)

    first_hop = []
    second_hop = []
    for z in range(lines):
        for g in range(groups):
            for feature in range(lines):
                here = z * groups + g
                there = feature * groups + g
                stop = middle(z, feature) * branches + here
                first_hop.append((feature * branches + here, stop))
                second_hop.append((stop, landing(z, feature) * branches + there))
    axes = ("fsdp", "branch")
    sent = [scaled[h * block_len : (h + 1) * block_len] for h in range(blocks)]
    sent = [lax.ppermute(piece, axes, first_hop) for piece in sent]

    head_cuts = [0, (5 * head_count + 7) // 8, head_count]
    w_rows = []
    w_chunks = [jnp.concatenate([w_key, w_value], 1)] + [
        lax.slice_in_dim(w_query, low * HD, high * HD, axis=1)
        for low, high in zip(head_cuts, head_cuts[1:])
    ]
    waits = [None, sent[0], None]
    for chunk, wait in zip(w_chunks, waits):
        outgoing = chunk if wait is None else tie(chunk, wait)
        if len(w_rows) == 2:
            outgoing = tie(chunk, w_rows[0][-1])
        w_rows.append([chunk] + [swap(outgoing, "branch", j) for j in range(1, groups)])

    sent = [lax.ppermute(piece, axes, second_hop) for piece in sent]
    held = [{0: piece} for piece in sent]
    bit = half_lines
    while bit:
        for piece in held:
            for j in list(piece):
                piece[j | bit] = swap(piece[j], "fsdp", bit)
        bit //= 2
    held = [[piece[j] for j in sorted(piece, key=spread)] for piece in held]

    squares = jnp.sum(jnp.square(raw.astype(f32)), -1).reshape(blocks, block_len)
    bit = 1
    while bit < lines:
        squares = squares + swap(squares, "fsdp", bit)
        bit *= 2
    inverse = lax.rsqrt(squares / features + 1e-06).reshape(tokens)
    inverse = jnp.broadcast_to(inverse[:, None], (tokens, HD))

    cos, sin = pl.pallas_call(
        functools.partial(table_kernel, far_slots, blocks, block_len),
        in_specs=[smem, smem],
        out_specs=[vmem, vmem],
        out_shape=[jax.ShapeDtypeStruct((tokens, HD), f32)] * 2,
        name="tables",
    )(device_id, parents)

    order = [None]

    def project(which, chunks):
        count = len(which)
        length = count * block_len
        weights = [w for chunk in chunks for w in w_rows[chunk]]
        width = sum(w_rows[chunk][0].shape[1] for chunk in chunks)
        operands = [held[block][i] for i in range(lines) for block in which]
        if order[0] is not None:
            weights[0] = tie(weights[0], order[0])
        flops = 2 * lines * length * feature_part * width
        send, keep = pl.pallas_call(
            functools.partial(project_kernel, lines, count, groups, len(chunks)),
            in_specs=[smem] + [anywhere] * len(operands) + [vmem] * len(weights),
            out_specs=[vmem, vmem],
            out_shape=[
                jax.ShapeDtypeStruct((half_lines, length, width), bf16),
                jax.ShapeDtypeStruct((half_lines, length, width), f32),
            ],
            scratch_shapes=[
                pltpu.VMEM((lines, length, feature_part), bf16),
                pltpu.SemaphoreType.DMA((len(operands),)),
            ],
            compiler_params=pltpu.CompilerParams(vmem_limit_bytes=32 * 2**20),
            cost_estimate=pl.CostEstimate(
                flops=flops, bytes_accessed=2 * lines * length * feature_part, transcendentals=0
            ),
            name="project",
        )(place, *operands, *weights)
        order[0] = send
        return send, keep

    def halve(send, keep):
        addends = [keep]
        total = keep
        bit = 1
        while bit < lines:
            came = swap(send, "branch", bit * groups)
            addends.append(came)
            bit *= 2
            if bit < lines:
                total = total + came.astype(f32)
                send = total[1::2].astype(bf16)
                total = total[0::2]
        return addends

    addend_count = 1 + bits_of(lines)

    def lead(array):
        return pl.BlockSpec((1,) + array.shape[1:], lambda i: (0, 0, 0))

    def whole(array):
        return pl.BlockSpec(array.shape, lambda i: (0,) * array.ndim)

    kv_bias = jnp.concatenate([key_bias, value_bias])[None]

    def finish_kv(addends, first, count):
        low, high = first * block_len, (first + count) * block_len
        operands = [inverse[low:high], kv_bias, cos[low:high], sin[low:high]]
        return pl.pallas_call(
            functools.partial(kv_kernel, addend_count),
            grid=(1,),
            in_specs=[whole(x) for x in operands] + [lead(x) for x in addends],
            out_specs=pl.BlockSpec((high - low, kv_width), lambda i: (0, 0)),
            out_shape=jax.ShapeDtypeStruct((high - low, kv_width), bf16),
            compiler_params=pltpu.CompilerParams(vmem_limit_bytes=16 * 2**20),
            name="finish_kv",
        )(*operands, *addends)

    early = list(range(STEMS))
    late = list(range(STEMS, blocks))
    first_sums = project(early, [0])
    second_sums = project(early, [1])
    first_sums = halve(*first_sums)
    stem_kv = finish_kv(first_sums, 0, STEMS)
    second_sums = halve(*second_sums)
    third_sums = halve(*project(late, [0, 1]))
    late_kv = finish_kv(third_sums, STEMS, blocks - STEMS)
    fourth_sums = halve(*project(early + late, [2]))

    stems = stem_kv[None]
    bit = 1
    while bit < branches:
        stems = jnp.concatenate([stems, swap(stems, "branch", bit)], 0)
        bit *= 2

    def attend(heads, first_head, parts, sums, output):
        operands = [
            inverse, query_bias[None, first_head * HD : (first_head + heads) * HD], cos, sin,
            stems, stem_kv, late_kv,
        ]
        in_specs = [smem] * 3 + [whole(x) for x in operands]
        for addends in sums:
            operands += addends
            in_specs += [lead(x) for x in addends]
        aliases = {}
        if output is not None:
            aliases = {3 + len(operands): 0}
            operands.append(output)
            in_specs.append(anywhere)
        kernel = functools.partial(
            attend_kernel, far_slots, block_len, blocks, heads, first_head, parts, addend_count,
            len(aliases),
        )
        keys = (far_slots * len(parts) + blocks) * block_len
        return pl.pallas_call(
            kernel,
            grid=(1,),
            in_specs=in_specs,
            out_specs=anywhere,
            scratch_shapes=[
                pltpu.VMEM((far_slots * block_len, HD), bf16),
                pltpu.VMEM((far_slots * block_len, HD), bf16),
                pltpu.VMEM((8, far_slots * block_len), f32),
                pltpu.VMEM((tokens, heads * HD), bf16),
                pltpu.SemaphoreType.DMA((blocks,)),
            ],
            out_shape=jax.ShapeDtypeStruct((tokens, columns), bf16),
            input_output_aliases=aliases,
            compiler_params=pltpu.CompilerParams(vmem_limit_bytes=40 * 2**20),
            cost_estimate=pl.CostEstimate(
                flops=4 * tokens * heads * keys * HD,
                bytes_accessed=2 * tokens * heads * HD,
                transcendentals=tokens * heads * keys,
            ),
            name="attend",
        )(device_id, parents, lengths, *operands)

    output = attend(
        head_cuts[1], 0, [(0, STEMS, 0), (STEMS, blocks - STEMS, kv_width)],
        [second_sums, third_sums], None,
    )
    output = attend(
        head_count - head_cuts[1], head_cuts[1], [(0, blocks, 0)], [fourth_sums], output
    )
    return output.reshape(blocks, block_len, columns)


def solution(mesh):
    return jax.shard_map(
        shards,
        mesh=mesh,
        in_specs=(
            P("branch", None, "fsdp"),
            P(),
            P(),
            P(),
            P("branch", "fsdp"),
            P("branch", "fsdp"),
            P("branch", "fsdp"),
            P("fsdp"),
            P("fsdp"),
            P("fsdp"),
        ),
        out_specs=P("branch", None, "fsdp"),
        check_vma=False,
    )
```

time: 226 us -> 198 us (0.88); the launches traced: 223 us -> 197 us
  Pallas kernels: 18.2 us -> 36.1 us
  waiting for transfers between devices: 90.6 us -> 75.3 us
  starting transfers between devices: 85.6 us -> 73 us
  other arithmetic: 14.1 us -> 3.36 us
  matrix products: 9.32 us -> 0 us
  local copies, waits for them, and re-layouts: 4.05 us -> 8.9 us
    ppermute x18 -> x0, starting transfers between devices: 43.8 us -> none  [the longest x9 34.2 us: reduce_line(): right = lax.ppermute(ahead.astype(bf16), 'branch', up[s])]
    ppermute x17 -> x25, starting transfers between devices: 37.6 us -> 67.1 us  [swap(): return lax.ppermute(array, axis, [(i, i ^ bit) for i in range(size)])]
    pallas_call x3 -> x9, Pallas kernels: 18.2 us -> 36.1 us  [the longest x4 24.9 us: project(): pl.pallas_call(functools.partial(project_kernel, lines, count, groups, le...]
    ppermute x18 -> x0, waiting for transfers between devices: 17 us -> none  [the longest x9 16 us: reduce_line(): right = lax.ppermute(ahead.astype(bf16), 'branch', up[s])]
    dot_general x6 -> x0, matrix products: 9.32 us -> none  [product(): jnp.dot(everything[:, j * rows:(j + 1) * rows], chunk[j], preferred_eleme...]
    convert_element_type x9 -> x0, other arithmetic: 5.45 us -> none  [the longest x6 5.13 us: reduce_line(): left = lax.ppermute(behind.astype(bf16), 'branch', down[s])]
    concatenate x2 -> x1, other arithmetic: 5.46 us -> 0.68 us  [shards(): kv_bias = jnp.concatenate([key_bias, value_bias])[None]]
    slice x1 -> x9, local copies, waits for them, and re-layouts: 0.16 us -> 4.88 us  [the longest x6 3.52 us: finish_kv(): operands = [inverse[low:high], kv_bias, cos[low:high], sin[low:high]]]
  transfers between devices with their start and end apart: 41 -> 31, of which waited for: 12 -> 9; matrix products, arithmetic and copies ran while one was open for 6% -> 3% of each run, Pallas kernels for 5% -> 16%
where the time goes in v3:
time: 198 us; the launch traced here: 197 us
  waiting for transfers between devices  75.3 us (38%)
  starting transfers between devices  73 us (37%)
  Pallas kernels  36.1 us (18%)
  local copies, waits for them, and re-layouts  8.9 us (4%)
  other arithmetic  3.36 us (2%)
    ppermute x25, waiting for transfers between devices, swap(): return lax.ppermute(array, axis, [(i, i ^ bit) for i in range(size)])  75.3 us
    ppermute x25, starting transfers between devices, swap(): return lax.ppermute(array, axis, [(i, i ^ bit) for i in range(size)])  67.1 us
    pallas_call x4, Pallas kernels, project(): pl.pallas_call(functools.partial(project_kernel, lines, count, groups, le...  24.9 us
    pallas_call x2, Pallas kernels, attend(): pl.pallas_call(kernel, grid=(1,), in_specs=in_specs, out_specs=anywhere,...  8.77 us
  transfers between devices with their start and end apart: 31, of which 9 were waited for; matrix products, arithmetic and copies ran while one was open for 3% of the time, Pallas kernels for 16%

profile of v3, /device:TPU:0, one launch (start us, length us, event | category | flops | bytes accessed | tf_op | source)
XLA Modules:
  0.0 197.3 jit_solution(8050430432551101011)
XLA Ops:
  0.7 1.8 multiply_convert_fusion
  5.1 1.4 collective-permute-start.5
  7.3 3.0 %collective-permute-start.12 = (bf16[1024,256]{1,0:T(8,128)(2,1)S(1)}, bf16[1024,256]{1,0:T(8,128)(2,1)S(1)}, u32[]{:S(2)}, u32[]{:S(2)}) collective-permute-start(bf16[1024,256]{1,0:T(8,128)(2,1)S(1)} %constant_dynamic-update-slice_fusion.refs_8_.refs_4_), channel_id=1, source_target_pairs={{0,1},{1,0},{2,3},{3,2},{4,5},{5,4},{6,7},{7,6},{8,9},{9,8},{10,11... | collective-permute-start | bytes 1572872 | tf_op jit(solution)/shard_map/ppermute | solution.py:247
  10.4 21.4 %collective-permute-start.6 = (bf16[128,2048]{1,0:T(8,128)(2,1)S(1)}, bf16[128,2048]{1,0:T(8,128)(2,1)}, u32[]{:S(2)}, u32[]{:S(2)}) collective-permute-start(bf16[128,2048]{1,0:T(8,128)(2,1)S(1)} %collective-permute-done.3.refs_0_), channel_id=1, source_target_pairs={{0,16},{8,24},{16,0},{24,8},{1,17},{9,25},{17,1},{25,9},{2,18},{10... | collective-permute-start | bytes 1572872 | tf_op jit(solution)/shard_map/ppermute | solution.py:247
  31.8 11.3 %collective-permute-start.7 = (bf16[128,2048]{1,0:T(8,128)(2,1)}, bf16[128,2048]{1,0:T(8,128)(2,1)}, u32[]{:S(2)}, u32[]{:S(2)}) collective-permute-start(bf16[128,2048]{1,0:T(8,128)(2,1)} %collective-permute-done.5.refs_1_), channel_id=1, source_target_pairs={{0,16},{8,24},{16,0},{24,8},{1,17},{9,25},{17,1},{25,9},{2,18},{10... | collective-permute-start | bytes 1572872 | tf_op jit(solution)/shard_map/ppermute | solution.py:247
  43.1 1.4 collective-permute-start.19
  45.0 1.4 collective-permute-start
  48.1 9.7 %collective-permute-done.7.refs_3_.refs_4_ = bf16[128,2048]{1,0:T(8,128)(2,1)} collective-permute-done((bf16[128,2048]{1,0:T(8,128)(2,1)}, bf16[128,2048]{1,0:T(8,128)(2,1)}, u32[]{:S(2)}, u32[]{:S(2)}) %collective-permute-start.7) | collective-permute-done | bytes 524320 | tf_op jit(solution)/shard_map/ppermute | solution.py:247
  58.0 1.6 collective-permute-start.23
  60.7 2.2 %tables.1 = (f32[384,128]{1,0:T(8,128)}, f32[384,128]{1,0:T(8,128)}) custom-call(s32[1]{0:T(128)} %bitcast.device_ref, s32[24]{0:T(128)} %parents_ref.5), custom_call_target="tpu_custom_call" | custom-call | tf_op jit(solution)/shard_map/tables/pallas_call | solution.py:321
  66.4 1.2 slice.82.refs_12_
  68.4 1.8 collective-permute-start.1
  72.3 3.8 %project.4 = (bf16[2,256,256]{2,1,0:T(8,128)(2,1)S(1)}, f32[2,256,256]{2,1,0:T(8,128)S(1)}) custom-call(s32[1]{0:T(128)} %bitcast.4.place_ref, bf16[128,2048]{1,0:T(8,128)(2,1)S(1)} %collective-permute-done.3.refs_0_, bf16[128,2048]{1,0:T(8,128)(2,1)} %collective-permute-done.5.refs_1_, bf16[128,2048]{1,0:T(8,128)(2,1)} %collective-permute-done.6.refs_2_.refs_3_, ...), custom_call_target="tpu_custom_call" | custom-call | flops 1073741824 | bytes 4194304 | tf_op jit(solution)/shard_map/project/pallas_call | solution.py:340
  77.2 1.3 collective-permute-start.21
  79.1 4.9 %collective-permute-done.13.refs_1_ = bf16[2,256,256]{2,1,0:T(8,128)(2,1)S(1)} collective-permute-done((bf16[2,256,256]{2,1,0:T(8,128)(2,1)S(1)}, bf16[2,256,256]{2,1,0:T(8,128)(2,1)S(1)}, u32[]{:S(2)}, u32[]{:S(2)}) %collective-permute-start.13) | collective-permute-done | bytes 262176 | tf_op jit(solution)/shard_map/ppermute | solution.py:247
  84.1 2.1 %collective-permute-start.14 = (bf16[1,256,256]{2,1,0:T(8,128)(2,1)S(1)}, bf16[1,256,256]{2,1,0:T(8,128)(2,1)S(1)}, u32[]{:S(2)}, u32[]{:S(2)}) collective-permute-start(bf16[1,256,256]{2,1,0:T(8,128)(2,1)S(1)} %fusion.5), channel_id=1, source_target_pairs={{0,4},{1,5},{2,6},{3,7},{4,0},{5,1},{6,2},{7,3},{8,12},{9,13},{10,... | collective-permute-start | bytes 393224 | tf_op jit(solution)/shard_map/ppermute | solution.py:247
  86.1 1.5 collective-permute-done.23.refs_9_.refs_7_
  87.6 7.4 %project.5 = (bf16[2,256,640]{2,1,0:T(8,128)(2,1)S(1)}, f32[2,256,640]{2,1,0:T(8,128)S(1)}) custom-call(s32[1]{0:T(128)} %bitcast.4.place_ref, bf16[128,2048]{1,0:T(8,128)(2,1)S(1)} %collective-permute-done.3.refs_0_, bf16[128,2048]{1,0:T(8,128)(2,1)} %collective-permute-done.5.refs_1_, bf16[128,2048]{1,0:T(8,128)(2,1)} %collective-permute-done.6.refs_2_.refs_3_, ...), custom_call_target="tpu_custom_call" | custom-call | flops 2684354560 | bytes 4194304 | tf_op jit(solution)/shard_map/project/pallas_call | solution.py:340
  95.0 3.2 %collective-permute-start.29 = (bf16[2,256,640]{2,1,0:T(8,128)(2,1)S(1)}, bf16[2,256,640]{2,1,0:T(8,128)(2,1)S(1)}, u32[]{:S(2)}, u32[]{:S(2)}) collective-permute-start(bf16[2,256,640]{2,1,0:T(8,128)(2,1)S(1)} %get-tuple-element.26), channel_id=1, source_target_pairs={{0,2},{1,3},{2,0},{3,1},{4,6},{5,7},{6,4},{7,5},{8,10},{9,11},{10,... | collective-permute-start | bytes 1966088 | tf_op jit(solution)/shard_map/ppermute | solution.py:247
  98.5 1.6 collective-permute-start.15
  100.1 7.3 %project.6 = (bf16[2,128,896]{2,1,0:T(8,128)(2,1)S(1)}, f32[2,128,896]{2,1,0:T(8,128)S(1)}) custom-call(s32[1]{0:T(128)} %bitcast.4.place_ref, bf16[128,2048]{1,0:T(8,128)(2,1)} %collective-permute-done.19.refs_0_.refs_2_, bf16[128,2048]{1,0:T(8,128)(2,1)} %collective-permute-done.20.refs_1_.refs_5_, ...), custom_call_target="tpu_custom_call" | custom-call | flops 1879048192 | bytes 2097152 | tf_op jit(solution)/shard_map/project/pallas_call | solution.py:340
  107.5 2.1 %collective-permute-start.16 = (bf16[2,256,256]{2,1,0:T(8,128)(2,1)S(1)}, bf16[2,256,256]{2,1,0:T(8,128)(2,1)S(1)}, u32[]{:S(2)}, u32[]{:S(2)}) collective-permute-start(bf16[2,256,256]{2,1,0:T(8,128)(2,1)S(1)} %pad_maximum_fusion.3), channel_id=1, source_target_pairs={{0,2},{1,3},{2,0},{3,1},{4,6},{5,7},{6,4},{7,5},{8,10},{9,11},{10,... | collective-permute-start | bytes 786440 | tf_op jit(solution)/shard_map/ppermute | solution.py:247
  109.5 6.4 %project.7 = (bf16[2,384,384]{2,1,0:T(8,128)(2,1)S(1)}, f32[2,384,384]{2,1,0:T(8,128)S(1)}) custom-call(s32[1]{0:T(128)} %bitcast.4.place_ref, bf16[128,2048]{1,0:T(8,128)(2,1)S(1)} %collective-permute-done.3.refs_0_, bf16[128,2048]{1,0:T(8,128)(2,1)} %collective-permute-done.5.refs_1_, bf16[128,2048]{1,0:T(8,128)(2,1)} %collective-permute-done.19.refs_0_.refs_2_, ...), custom_call_target="tpu_custom_call" | custom-call | flops 2415919104 | bytes 6291456 | tf_op jit(solution)/shard_map/project/pallas_call | solution.py:340
  116.1 12.2 %collective-permute-done.16 = bf16[2,256,256]{2,1,0:T(8,128)(2,1)S(1)} collective-permute-done((bf16[2,256,256]{2,1,0:T(8,128)(2,1)S(1)}, bf16[2,256,256]{2,1,0:T(8,128)(2,1)S(1)}, u32[]{:S(2)}, u32[]{:S(2)}) %collective-permute-start.16) | collective-permute-done | bytes 262176 | tf_op jit(solution)/shard_map/ppermute | solution.py:247
  128.3 4.9 %collective-permute-start.17 = (bf16[4,256,256]{2,1,0:T(8,128)(2,1)S(1)}, bf16[4,256,256]{2,1,0:T(8,128)(2,1)S(1)}, u32[]{:S(2)}, u32[]{:S(2)}) collective-permute-start(bf16[4,256,256]{2,1,0:T(8,128)(2,1)S(1)} %pad_maximum_fusion.2), channel_id=1, source_target_pairs={{0,4},{1,5},{2,6},{3,7},{4,0},{5,1},{6,2},{7,3},{8,12},{9,13},{10,... | collective-permute-start | bytes 1572872 | tf_op jit(solution)/shard_map/ppermute | solution.py:247
  133.5 3.0 %collective-permute-start.30 = (bf16[1,256,640]{2,1,0:T(8,128)(2,1)S(1)}, bf16[1,256,640]{2,1,0:T(8,128)(2,1)S(1)}, u32[]{:S(2)}, u32[]{:S(2)}) collective-permute-start(bf16[1,256,640]{2,1,0:T(8,128)(2,1)S(1)} %fusion), channel_id=1, source_target_pairs={{0,4},{1,5},{2,6},{3,7},{4,0},{5,1},{6,2},{7,3},{8,12},{9,13},{10,... | collective-permute-start | bytes 983048 | tf_op jit(solution)/shard_map/ppermute | solution.py:247
  136.4 11.4 %collective-permute-done.27.refs_3_ = bf16[2,384,384]{2,1,0:T(8,128)(2,1)S(1)} collective-permute-done((bf16[2,384,384]{2,1,0:T(8,128)(2,1)S(1)}, bf16[2,384,384]{2,1,0:T(8,128)(2,1)S(1)}, u32[]{:S(2)}, u32[]{:S(2)}) %collective-permute-start.27) | collective-permute-done | bytes 589856 | tf_op jit(solution)/shard_map/ppermute | solution.py:247
  147.9 5.3 %collective-permute-start.28 = (bf16[1,384,384]{2,1,0:T(8,128)(2,1)S(1)}, bf16[1,384,384]{2,1,0:T(8,128)(2,1)S(1)}, u32[]{:S(2)}, u32[]{:S(2)}) collective-permute-start(bf16[1,384,384]{2,1,0:T(8,128)(2,1)S(1)} %fusion.1), channel_id=1, source_target_pairs={{0,4},{1,5},{2,6},{3,7},{4,0},{5,1},{6,2},{7,3},{8,12},{9,13},{10,... | collective-permute-start | bytes 884744 | tf_op jit(solution)/shard_map/ppermute | solution.py:247
  153.2 26.9 %collective-permute-done.25.refs_2_.refs_7_ = bf16[1,128,896]{2,1,0:T(8,128)(2,1)S(1)} collective-permute-done((bf16[1,128,896]{2,1,0:T(8,128)(2,1)S(1)}, bf16[1,128,896]{2,1,0:T(8,128)(2,1)S(1)}, u32[]{:S(2)}, u32[]{:S(2)}) %collective-permute-start.25) | collective-permute-done | bytes 229408 | tf_op jit(solution)/shard_map/ppermute | solution.py:247
  180.4 6.7 %collective-permute-done.30.refs_4_ = bf16[1,256,640]{2,1,0:T(8,128)(2,1)S(1)} collective-permute-done((bf16[1,256,640]{2,1,0:T(8,128)(2,1)S(1)}, bf16[1,256,640]{2,1,0:T(8,128)(2,1)S(1)}, u32[]{:S(2)}, u32[]{:S(2)}) %collective-permute-start.30) | collective-permute-done | bytes 327712 | tf_op jit(solution)/shard_map/ppermute | solution.py:247
  187.2 5.0 %attend.2.refs_5_ = bf16[384,1024]{1,0:T(8,128)(2,1)} custom-call(s32[1]{0:T(128)} %bitcast.device_ref, s32[24]{0:T(128)S(1)} %copy-done.7, s32[24]{0:T(128)S(1)} %copy-done.8, f32[384,128]{1,0:T(8,128)S(1)} %broadcast_in_dim.33.inverse_ref, f32[1,640]{1,0:T(1,128)S(1)} %broadcast_in_dim.40.bias_ref, f32[384,128]{1,0:T(8,128)S(1)} %copy-done, ...), custom_call_target="tpu_custom_call" | custom-call | flops 1887436800 | bytes 491520 | tf_op jit(solution)/shard_map/attend/pallas_call | solution.py:434
  193.4 3.8 %attend.3 = bf16[384,1024]{1,0:T(8,128)(2,1)} custom-call(s32[1]{0:T(128)} %bitcast.device_ref, s32[24]{0:T(128)S(1)} %copy-done.7, s32[24]{0:T(128)S(1)} %copy-done.8, f32[384,128]{1,0:T(8,128)S(1)} %broadcast_in_dim.33.inverse_ref, f32[1,384]{1,0:T(1,128)S(1)} %broadcast_in_dim.34.bias_ref, ...), custom_call_target="tpu_custom_call", output_to_operand_aliasing={{}: (13, {})} | custom-call | flops 679477248 | bytes 294912 | tf_op jit(solution)/shard_map/attend/pallas_call | solution.py:434
  (97 shorter events, 17.7 us)
Async XLA Ops:
  2.6 55.2 %copy-start.10 = (bf16[1024,1024]{1,0:T(8,128)(2,1)S(1)}, bf16[1024,1024]{1,0:T(8,128)(2,1)}, u32[]{:S(2)}) copy-start(bf16[1024,1024]{1,0:T(8,128)(2,1)} %param.14) | copy-start | bytes 6291460
  2.7 1.7 collective-permute-start.2
  3.5 1.5 collective-permute-start.4
  4.3 6.0 %collective-permute-start.3 = (bf16[128,2048]{1,0:T(8,128)(2,1)S(1)}, bf16[128,2048]{1,0:T(8,128)(2,1)S(1)}, u32[]{:S(2)}, u32[]{:S(2)}) collective-permute-start(bf16[128,2048]{1,0:T(8,128)(2,1)S(1)} %collective-permute-done.2), channel_id=1, source_target_pairs={{0,0},{16,18},{8,12},{24,30},{1,1},{17,19},{9,13},{25,31},{26,16},... | collective-permute-start | bytes 1572872 | tf_op jit(solution)/shard_map/ppermute | solution.py:303
  5.1 26.7 %collective-permute-start.5 = (bf16[128,2048]{1,0:T(8,128)(2,1)S(1)}, bf16[128,2048]{1,0:T(8,128)(2,1)}, u32[]{:S(2)}, u32[]{:S(2)}) collective-permute-start(bf16[128,2048]{1,0:T(8,128)(2,1)S(1)} %collective-permute-done.4), channel_id=1, source_target_pairs={{0,0},{16,18},{8,12},{24,30},{1,1},{17,19},{9,13},{25,31},{26,16},... | collective-permute-start | bytes 1572872 | tf_op jit(solution)/shard_map/ppermute | solution.py:303
  6.5 36.6 %collective-permute-start.18 = (bf16[128,2048]{1,0:T(8,128)(2,1)S(1)}, bf16[128,2048]{1,0:T(8,128)(2,1)S(1)}, u32[]{:S(2)}, u32[]{:S(2)}) collective-permute-start(bf16[128,2048]{1,0:T(8,128)(2,1)S(1)} %get-tuple-element.35), channel_id=1, source_target_pairs={{0,0},{8,16},{16,8},{24,24},{1,1},{9,17},{17,9},{25,25},{2,26},{10... | collective-permute-start | bytes 1572872 | tf_op jit(solution)/shard_map/ppermute | solution.py:288
  7.3 40.2 %collective-permute-start.12 = (bf16[1024,256]{1,0:T(8,128)(2,1)S(1)}, bf16[1024,256]{1,0:T(8,128)(2,1)S(1)}, u32[]{:S(2)}, u32[]{:S(2)}) collective-permute-start(bf16[1024,256]{1,0:T(8,128)(2,1)S(1)} %constant_dynamic-update-slice_fusion.refs_8_.refs_4_), channel_id=1, source_target_pairs={{0,1},{1,0},{2,3},{3,2},{4,5},{5,4},{6,7},{7,6},{8,9},{9,8},{10,11... | collective-permute-start | bytes 1572872 | tf_op jit(solution)/shard_map/ppermute | solution.py:247
  10.4 37.4 %collective-permute-start.6 = (bf16[128,2048]{1,0:T(8,128)(2,1)S(1)}, bf16[128,2048]{1,0:T(8,128)(2,1)}, u32[]{:S(2)}, u32[]{:S(2)}) collective-permute-start(bf16[128,2048]{1,0:T(8,128)(2,1)S(1)} %collective-permute-done.3.refs_0_), channel_id=1, source_target_pairs={{0,16},{8,24},{16,0},{24,8},{1,17},{9,25},{17,1},{25,9},{2,18},{10... | collective-permute-start | bytes 1572872 | tf_op jit(solution)/shard_map/ppermute | solution.py:247
  31.8 26.0 %collective-permute-start.7 = (bf16[128,2048]{1,0:T(8,128)(2,1)}, bf16[128,2048]{1,0:T(8,128)(2,1)}, u32[]{:S(2)}, u32[]{:S(2)}) collective-permute-start(bf16[128,2048]{1,0:T(8,128)(2,1)} %collective-permute-done.5.refs_1_), channel_id=1, source_target_pairs={{0,16},{8,24},{16,0},{24,8},{1,17},{9,25},{17,1},{25,9},{2,18},{10... | collective-permute-start | bytes 1572872 | tf_op jit(solution)/shard_map/ppermute | solution.py:247
  43.1 14.9 %collective-permute-start.19 = (bf16[128,2048]{1,0:T(8,128)(2,1)S(1)}, bf16[128,2048]{1,0:T(8,128)(2,1)}, u32[]{:S(2)}, u32[]{:S(2)}) collective-permute-start(bf16[128,2048]{1,0:T(8,128)(2,1)S(1)} %collective-permute-done.18), channel_id=1, source_target_pairs={{0,0},{16,18},{8,12},{24,30},{1,1},{17,19},{9,13},{25,31},{26,16},... | collective-permute-start | bytes 1572872 | tf_op jit(solution)/shard_map/ppermute | solution.py:303
  45.0 2.3 %collective-permute-start = (f32[3,128]{1,0:T(4,128)S(1)}, f32[3,128]{1,0:T(4,128)S(1)}, u32[]{:S(2)}, u32[]{:S(2)}) collective-permute-start(f32[3,128]{1,0:T(4,128)S(1)} %multiply_reduce_fusion), channel_id=1, source_target_pairs={{0,8},{8,0},{16,24},{24,16},{1,9},{9,1},{17,25},{25,17},{2,10},{10... | collective-permute-start | bytes 4616 | tf_op jit(solution)/shard_map/ppermute | solution.py:247
  47.2 12.4 %collective-permute-start.8 = (bf16[128,2048]{1,0:T(8,128)(2,1)S(1)}, bf16[128,2048]{1,0:T(8,128)(2,1)S(1)}, u32[]{:S(2)}, u32[]{:S(2)}) collective-permute-start(bf16[128,2048]{1,0:T(8,128)(2,1)S(1)} %collective-permute-done.3.refs_0_), channel_id=1, source_target_pairs={{0,8},{8,0},{16,24},{24,16},{1,9},{9,1},{17,25},{25,17},{2,10},{10... | collective-permute-start | bytes 1572872 | tf_op jit(solution)/shard_map/ppermute | solution.py:247
  47.6 20.8 %collective-permute-start.9 = (bf16[128,2048]{1,0:T(8,128)(2,1)}, bf16[128,2048]{1,0:T(8,128)(2,1)}, u32[]{:S(2)}, u32[]{:S(2)}) collective-permute-start(bf16[128,2048]{1,0:T(8,128)(2,1)} %collective-permute-done.5.refs_1_), channel_id=1, source_target_pairs={{0,8},{8,0},{16,24},{24,16},{1,9},{9,1},{17,25},{25,17},{2,10},{10... | collective-permute-start | bytes 1572872 | tf_op jit(solution)/shard_map/ppermute | solution.py:247
  47.7 22.4 %collective-permute-start.10 = (bf16[128,2048]{1,0:T(8,128)(2,1)}, bf16[128,2048]{1,0:T(8,128)(2,1)}, u32[]{:S(2)}, u32[]{:S(2)}) collective-permute-start(bf16[128,2048]{1,0:T(8,128)(2,1)} %collective-permute-done.6.refs_2_.refs_3_), channel_id=1, source_target_pairs={{0,8},{8,0},{16,24},{24,16},{1,9},{9,1},{17,25},{25,17},{2,10},{10... | collective-permute-start | bytes 1572872 | tf_op jit(solution)/shard_map/ppermute | solution.py:247
  57.8 12.3 %collective-permute-start.11 = (bf16[128,2048]{1,0:T(8,128)(2,1)}, bf16[128,2048]{1,0:T(8,128)(2,1)}, u32[]{:S(2)}, u32[]{:S(2)}) collective-permute-start(bf16[128,2048]{1,0:T(8,128)(2,1)} %collective-permute-done.7.refs_3_.refs_4_), channel_id=1, source_target_pairs={{0,8},{8,0},{16,24},{24,16},{1,9},{9,1},{17,25},{25,17},{2,10},{10... | collective-permute-start | bytes 1572872 | tf_op jit(solution)/shard_map/ppermute | solution.py:247
  58.0 29.6 %collective-permute-start.23 = (bf16[1024,640]{1,0:T(8,128)(2,1)S(1)}, bf16[1024,640]{1,0:T(8,128)(2,1)}, u32[]{:S(2)}, u32[]{:S(2)}) collective-permute-start(bf16[1024,640]{1,0:T(8,128)(2,1)S(1)} %slice.80.refs_8_.refs_6_), channel_id=1, source_target_pairs={{0,1},{1,0},{2,3},{3,2},{4,5},{5,4},{6,7},{7,6},{8,9},{9,8},{10,11... | collective-permute-start | bytes 3932168 | tf_op jit(solution)/shard_map/ppermute | solution.py:247
  60.4 18.1 %collective-permute-start.20 = (bf16[128,2048]{1,0:T(8,128)(2,1)}, bf16[128,2048]{1,0:T(8,128)(2,1)}, u32[]{:S(2)}, u32[]{:S(2)}) collective-permute-start(bf16[128,2048]{1,0:T(8,128)(2,1)} %collective-permute-done.19.refs_0_.refs_2_), channel_id=1, source_target_pairs={{0,16},{8,24},{16,0},{24,8},{1,17},{9,25},{17,1},{25,9},{2,18},{10... | collective-permute-start | bytes 1572872 | tf_op jit(solution)/shard_map/ppermute | solution.py:247
  68.4 8.8 %collective-permute-start.1 = (f32[3,128]{1,0:T(4,128)S(1)}, f32[3,128]{1,0:T(4,128)S(1)}, u32[]{:S(2)}, u32[]{:S(2)}) collective-permute-start(f32[3,128]{1,0:T(4,128)S(1)} %add.46), channel_id=1, source_target_pairs={{0,16},{8,24},{16,0},{24,8},{1,17},{9,25},{17,1},{25,9},{2,18},{10... | collective-permute-start | bytes 4616 | tf_op jit(solution)/shard_map/ppermute | solution.py:247
  76.1 7.9 %collective-permute-start.13 = (bf16[2,256,256]{2,1,0:T(8,128)(2,1)S(1)}, bf16[2,256,256]{2,1,0:T(8,128)(2,1)S(1)}, u32[]{:S(2)}, u32[]{:S(2)}) collective-permute-start(bf16[2,256,256]{2,1,0:T(8,128)(2,1)S(1)} %get-tuple-element.23), channel_id=1, source_target_pairs={{0,2},{1,3},{2,0},{3,1},{4,6},{5,7},{6,4},{7,5},{8,10},{9,11},{10,... | collective-permute-start | bytes 786440 | tf_op jit(solution)/shard_map/ppermute | solution.py:247
  77.2 22.9 %collective-permute-start.21 = (bf16[128,2048]{1,0:T(8,128)(2,1)}, bf16[128,2048]{1,0:T(8,128)(2,1)S(1)}, u32[]{:S(2)}, u32[]{:S(2)}) collective-permute-start(bf16[128,2048]{1,0:T(8,128)(2,1)} %collective-permute-done.19.refs_0_.refs_2_), channel_id=1, source_target_pairs={{0,8},{8,0},{16,24},{24,16},{1,9},{9,1},{17,25},{25,17},{2,10},{10... | collective-permute-start | bytes 1572872 | tf_op jit(solution)/shard_map/ppermute | solution.py:247
  78.5 21.6 %collective-permute-start.22 = (bf16[128,2048]{1,0:T(8,128)(2,1)}, bf16[128,2048]{1,0:T(8,128)(2,1)S(1)}, u32[]{:S(2)}, u32[]{:S(2)}) collective-permute-start(bf16[128,2048]{1,0:T(8,128)(2,1)} %collective-permute-done.20.refs_1_.refs_5_), channel_id=1, source_target_pairs={{0,8},{8,0},{16,24},{24,16},{1,9},{9,1},{17,25},{25,17},{2,10},{10... | collective-permute-start | bytes 1572872 | tf_op jit(solution)/shard_map/ppermute | solution.py:247
  78.6 30.9 %collective-permute-start.26 = (bf16[1024,384]{1,0:T(8,128)(2,1)S(1)}, bf16[1024,384]{1,0:T(8,128)(2,1)S(1)}, u32[]{:S(2)}, u32[]{:S(2)}) collective-permute-start(bf16[1024,384]{1,0:T(8,128)(2,1)S(1)} %slice.82.refs_12_), channel_id=1, source_target_pairs={{0,1},{1,0},{2,3},{3,2},{4,5},{5,4},{6,7},{7,6},{8,9},{9,8},{10,11... | collective-permute-start | bytes 2359304 | tf_op jit(solution)/shard_map/ppermute | solution.py:247
  84.1 14.2 %collective-permute-start.14 = (bf16[1,256,256]{2,1,0:T(8,128)(2,1)S(1)}, bf16[1,256,256]{2,1,0:T(8,128)(2,1)S(1)}, u32[]{:S(2)}, u32[]{:S(2)}) collective-permute-start(bf16[1,256,256]{2,1,0:T(8,128)(2,1)S(1)} %fusion.5), channel_id=1, source_target_pairs={{0,4},{1,5},{2,6},{3,7},{4,0},{5,1},{6,2},{7,3},{8,12},{9,13},{10,... | collective-permute-start | bytes 393224 | tf_op jit(solution)/shard_map/ppermute | solution.py:247
  95.0 38.4 %collective-permute-start.29 = (bf16[2,256,640]{2,1,0:T(8,128)(2,1)S(1)}, bf16[2,256,640]{2,1,0:T(8,128)(2,1)S(1)}, u32[]{:S(2)}, u32[]{:S(2)}) collective-permute-start(bf16[2,256,640]{2,1,0:T(8,128)(2,1)S(1)} %get-tuple-element.26), channel_id=1, source_target_pairs={{0,2},{1,3},{2,0},{3,1},{4,6},{5,7},{6,4},{7,5},{8,10},{9,11},{10,... | collective-permute-start | bytes 1966088 | tf_op jit(solution)/shard_map/ppermute | solution.py:247
  98.5 8.9 %collective-permute-start.15 = (bf16[1,256,256]{2,1,0:T(8,128)(2,1)S(1)}, bf16[1,256,256]{2,1,0:T(8,128)(2,1)S(1)}, u32[]{:S(2)}, u32[]{:S(2)}) collective-permute-start(bf16[1,256,256]{2,1,0:T(8,128)(2,1)S(1)} %bitcast.12), channel_id=1, source_target_pairs={{0,1},{1,0},{2,3},{3,2},{4,5},{5,4},{6,7},{7,6},{8,9},{9,8},{10,11... | collective-permute-start | bytes 393224 | tf_op jit(solution)/shard_map/ppermute | solution.py:247
  107.3 25.9 %collective-permute-start.24 = (bf16[2,128,896]{2,1,0:T(8,128)(2,1)S(1)}, bf16[2,128,896]{2,1,0:T(8,128)(2,1)S(1)}, u32[]{:S(2)}, u32[]{:S(2)}) collective-permute-start(bf16[2,128,896]{2,1,0:T(8,128)(2,1)S(1)} %get-tuple-element.29), channel_id=1, source_target_pairs={{0,2},{1,3},{2,0},{3,1},{4,6},{5,7},{6,4},{7,5},{8,10},{9,11},{10,... | collective-permute-start | bytes 1376264 | tf_op jit(solution)/shard_map/ppermute | solution.py:247
  107.5 20.8 %collective-permute-start.16 = (bf16[2,256,256]{2,1,0:T(8,128)(2,1)S(1)}, bf16[2,256,256]{2,1,0:T(8,128)(2,1)S(1)}, u32[]{:S(2)}, u32[]{:S(2)}) collective-permute-start(bf16[2,256,256]{2,1,0:T(8,128)(2,1)S(1)} %pad_maximum_fusion.3), channel_id=1, source_target_pairs={{0,2},{1,3},{2,0},{3,1},{4,6},{5,7},{6,4},{7,5},{8,10},{9,11},{10,... | collective-permute-start | bytes 786440 | tf_op jit(solution)/shard_map/ppermute | solution.py:247
  116.0 31.8 %collective-permute-start.27 = (bf16[2,384,384]{2,1,0:T(8,128)(2,1)S(1)}, bf16[2,384,384]{2,1,0:T(8,128)(2,1)S(1)}, u32[]{:S(2)}, u32[]{:S(2)}) collective-permute-start(bf16[2,384,384]{2,1,0:T(8,128)(2,1)S(1)} %get-tuple-element.33), channel_id=1, source_target_pairs={{0,2},{1,3},{2,0},{3,1},{4,6},{5,7},{6,4},{7,5},{8,10},{9,11},{10,... | collective-permute-start | bytes 1769480 | tf_op jit(solution)/shard_map/ppermute | solution.py:247
  128.3 52.0 %collective-permute-start.17 = (bf16[4,256,256]{2,1,0:T(8,128)(2,1)S(1)}, bf16[4,256,256]{2,1,0:T(8,128)(2,1)S(1)}, u32[]{:S(2)}, u32[]{:S(2)}) collective-permute-start(bf16[4,256,256]{2,1,0:T(8,128)(2,1)S(1)} %pad_maximum_fusion.2), channel_id=1, source_target_pairs={{0,4},{1,5},{2,6},{3,7},{4,0},{5,1},{6,2},{7,3},{8,12},{9,13},{10,... | collective-permute-start | bytes 1572872 | tf_op jit(solution)/shard_map/ppermute | solution.py:247
  133.3 46.7 %collective-permute-start.25 = (bf16[1,128,896]{2,1,0:T(8,128)(2,1)S(1)}, bf16[1,128,896]{2,1,0:T(8,128)(2,1)S(1)}, u32[]{:S(2)}, u32[]{:S(2)}) collective-permute-start(bf16[1,128,896]{2,1,0:T(8,128)(2,1)S(1)} %fusion.4), channel_id=1, source_target_pairs={{0,4},{1,5},{2,6},{3,7},{4,0},{5,1},{6,2},{7,3},{8,12},{9,13},{10,... | collective-permute-start | bytes 688136 | tf_op jit(solution)/shard_map/ppermute | solution.py:247
  133.5 53.6 %collective-permute-start.30 = (bf16[1,256,640]{2,1,0:T(8,128)(2,1)S(1)}, bf16[1,256,640]{2,1,0:T(8,128)(2,1)S(1)}, u32[]{:S(2)}, u32[]{:S(2)}) collective-permute-start(bf16[1,256,640]{2,1,0:T(8,128)(2,1)S(1)} %fusion), channel_id=1, source_target_pairs={{0,4},{1,5},{2,6},{3,7},{4,0},{5,1},{6,2},{7,3},{8,12},{9,13},{10,... | collective-permute-start | bytes 983048 | tf_op jit(solution)/shard_map/ppermute | solution.py:247
  147.9 45.5 %collective-permute-start.28 = (bf16[1,384,384]{2,1,0:T(8,128)(2,1)S(1)}, bf16[1,384,384]{2,1,0:T(8,128)(2,1)S(1)}, u32[]{:S(2)}, u32[]{:S(2)}) collective-permute-start(bf16[1,384,384]{2,1,0:T(8,128)(2,1)S(1)} %fusion.1), channel_id=1, source_target_pairs={{0,4},{1,5},{2,6},{3,7},{4,0},{5,1},{6,2},{7,3},{8,12},{9,13},{10,... | collective-permute-start | bytes 884744 | tf_op jit(solution)/shard_map/ppermute | solution.py:247
  (13 other events, 120.8 us)

commit v4 on v3

--- a/solution.py
+++ b/solution.py
@@ -62,54 +62,38 @@
     sin_ref[...] = jnp.where(front, -sin, sin)
 
 
-def project_kernel(lines, blocks, groups, chunks, place_ref, *refs):
+def project_kernel(lines, blocks, chunks, place_ref, *refs):
     pieces = refs[: lines * blocks]
-    refs = refs[lines * blocks :]
-    weights = refs[: groups * chunks]
-    send_ref, keep_ref, held, sems = refs[groups * chunks :]
+    weights = refs[lines * blocks : lines * blocks + chunks]
+    send_ref, keep_ref, held, sems = refs[lines * blocks + chunks :]
     half = lines // 2
-    block_len = held.shape[1] // blocks
+    block_len = pieces[0].shape[0]
     copies = []
     for i in range(lines):
         target = lax.bitwise_xor(jnp.int32(i), place_ref[0])
         slot = jnp.where(target % 2 == 0, half, 0) + target // 2
         for block in range(blocks):
+            start = pl.multiple_of((slot * blocks + block) * block_len, block_len)
             copy = pltpu.make_async_copy(
                 pieces[i * blocks + block],
-                held.at[slot, pl.ds(block * block_len, block_len)],
+                held.at[pl.ds(start, block_len)],
                 sems.at[i * blocks + block],
             )
             copy.start()
             copies.append(copy)
     for copy in copies:
         copy.wait()
-    rows = weights[0].shape[0]
-
-    def step(slot, carry):
-        start = 0
-        for chunk in range(chunks):
-            total = None
-            for g in range(groups):
-                term = jnp.dot(
-                    held[slot, :, g * rows : (g + 1) * rows],
-                    weights[chunk * groups + g][...],
-                    preferred_element_type=jnp.float32,
-                )
-                total = term if total is None else total + term
-            stop = start + total.shape[1]
-
-            @pl.when(slot < half)
-            def _():
-                send_ref[slot, :, start:stop] = total.astype(jnp.bfloat16)
-
-            @pl.when(slot >= half)
-            def _():
-                keep_ref[slot - half, :, start:stop] = total
-
-            start = stop
-        return carry
-
-    lax.fori_loop(0, lines, step, 0)
+    middle = held.shape[0] // 2
+    start = 0
+    for weight in weights:
+        stop = start + weight.shape[1]
+        send_ref[:, start:stop] = jnp.dot(
+            held[:middle], weight[...], preferred_element_type=jnp.float32
+        ).astype(jnp.bfloat16)
+        keep_ref[:, start:stop] = jnp.dot(
+            held[middle:], weight[...], preferred_element_type=jnp.float32
+        )
+        start = stop
 
 
 def kv_kernel(addends, inverse_ref, bias_ref, cos_ref, sin_ref, *refs):
@@ -234,8 +218,6 @@
     far_slots = STEMS * bits_of(branches)
     part = lax.axis_index("fsdp")
     device = lax.axis_index("branch")
-    member = device % groups
-    level = device // groups
     bf16 = jnp.bfloat16
     f32 = jnp.float32
     half_lines = lines // 2
@@ -256,13 +238,7 @@
     place = spread(part).astype(jnp.int32)[None]
 
     raw = hidden.reshape(tokens, feature_part)
-    pieces = []
-    for j in range(groups):
-        start = (member ^ j) * rows
-        gain_here = lax.dynamic_slice_in_dim(gain, part * feature_part + start, rows)
-        piece = lax.dynamic_slice_in_dim(raw, start, rows, axis=1).astype(f32) * gain_here
-        pieces.append(piece.astype(bf16))
-    scaled = jnp.concatenate(pieces, 1)
+    gain_part = lax.dynamic_slice_in_dim(gain, part * feature_part, feature_part)
 
     def column(z, feature):
         return (z ^ feature) & (half_lines - 1)
@@ -284,22 +260,43 @@
                 first_hop.append((feature * branches + here, stop))
                 second_hop.append((stop, landing(z, feature) * branches + there))
     axes = ("fsdp", "branch")
-    sent = [scaled[h * block_len : (h + 1) * block_len] for h in range(blocks)]
-    sent = [lax.ppermute(piece, axes, first_hop) for piece in sent]
+    first_sent = (raw[:block_len].astype(f32) * gain_part).astype(bf16)
+    rest_sent = tie(raw, first_sent)[block_len:]
+    rest_sent = (rest_sent.astype(f32) * gain_part).astype(bf16)
+    first_sent = lax.ppermute(first_sent, axes, first_hop)
+    rest_sent = lax.ppermute(rest_sent, axes, first_hop)
+    sent = [first_sent] + [
+        rest_sent[i * block_len : (i + 1) * block_len] for i in range(blocks - 1)
+    ]
 
     head_cuts = [0, (5 * head_count + 7) // 8, head_count]
-    w_rows = []
     w_chunks = [jnp.concatenate([w_key, w_value], 1)] + [
         lax.slice_in_dim(w_query, low * HD, high * HD, axis=1)
         for low, high in zip(head_cuts, head_cuts[1:])
     ]
-    waits = [None, sent[0], None]
-    for chunk, wait in zip(w_chunks, waits):
-        outgoing = chunk if wait is None else tie(chunk, wait)
-        if len(w_rows) == 2:
-            outgoing = tie(chunk, w_rows[0][-1])
-        w_rows.append([chunk] + [swap(outgoing, "branch", j) for j in range(1, groups)])
-
+    teams = [[z * groups + g for g in range(groups)] for z in range(lines)]
+    w_rows = [
+        lax.all_gather(chunk, "branch", axis_index_groups=teams, axis=0, tiled=True)
+        for chunk in w_chunks
+    ]
+
+    squares = jnp.sum(jnp.square(raw.astype(f32)), -1).reshape(blocks, block_len)
+    bit = 1
+    while bit < lines:
+        squares = squares + swap(squares, "fsdp", bit)
+        bit *= 2
+    inverse = lax.rsqrt(squares / features + 1e-06).reshape(tokens)
+    inverse = jnp.broadcast_to(inverse[:, None], (tokens, HD))
+
+    cos, sin = pl.pallas_call(
+        functools.partial(table_kernel, far_slots, blocks, block_len),
+        in_specs=[smem, smem],
+        out_specs=[vmem, vmem],
+        out_shape=[jax.ShapeDtypeStruct((tokens, HD), f32)] * 2,
+        name="tables",
+    )(device_id, parents)
+
+    sent[0] = tie(sent[0], cos, sin, *w_chunks)
     sent = [lax.ppermute(piece, axes, second_hop) for piece in sent]
     held = [{0: piece} for piece in sent]
     bit = half_lines
@@ -310,43 +307,27 @@
         bit //= 2
     held = [[piece[j] for j in sorted(piece, key=spread)] for piece in held]
 
-    squares = jnp.sum(jnp.square(raw.astype(f32)), -1).reshape(blocks, block_len)
-    bit = 1
-    while bit < lines:
-        squares = squares + swap(squares, "fsdp", bit)
-        bit *= 2
-    inverse = lax.rsqrt(squares / features + 1e-06).reshape(tokens)
-    inverse = jnp.broadcast_to(inverse[:, None], (tokens, HD))
-
-    cos, sin = pl.pallas_call(
-        functools.partial(table_kernel, far_slots, blocks, block_len),
-        in_specs=[smem, smem],
-        out_specs=[vmem, vmem],
-        out_shape=[jax.ShapeDtypeStruct((tokens, HD), f32)] * 2,
-        name="tables",
-    )(device_id, parents)
-
     order = [None]
 
     def project(which, chunks):
         count = len(which)
         length = count * block_len
-        weights = [w for chunk in chunks for w in w_rows[chunk]]
-        width = sum(w_rows[chunk][0].shape[1] for chunk in chunks)
+        weights = [w_rows[chunk] for chunk in chunks]
+        width = sum(w.shape[1] for w in weights)
         operands = [held[block][i] for i in range(lines) for block in which]
         if order[0] is not None:
             weights[0] = tie(weights[0], order[0])
         flops = 2 * lines * length * feature_part * width
         send, keep = pl.pallas_call(
-            functools.partial(project_kernel, lines, count, groups, len(chunks)),
+            functools.partial(project_kernel, lines, count, len(chunks)),
             in_specs=[smem] + [anywhere] * len(operands) + [vmem] * len(weights),
             out_specs=[vmem, vmem],
             out_shape=[
-                jax.ShapeDtypeStruct((half_lines, length, width), bf16),
-                jax.ShapeDtypeStruct((half_lines, length, width), f32),
+                jax.ShapeDtypeStruct((half_lines * length, width), bf16),
+                jax.ShapeDtypeStruct((half_lines * length, width), f32),
             ],
             scratch_shapes=[
-                pltpu.VMEM((lines, length, feature_part), bf16),
+                pltpu.VMEM((lines * length, feature_part), bf16),
                 pltpu.SemaphoreType.DMA((len(operands),)),
             ],
             compiler_params=pltpu.CompilerParams(vmem_limit_bytes=32 * 2**20),
@@ -356,7 +337,7 @@
             name="project",
         )(place, *operands, *weights)
         order[0] = send
-        return send, keep
+        return send.reshape(half_lines, length, width), keep.reshape(half_lines, length, width)
 
     def halve(send, keep):
         addends = [keep]

time: 198 us -> 213 us (1.076)
  between operations: 0.6 us -> 13.6 us
  local copies, waits for them, and re-layouts: 8.9 us -> 18.3 us
  starting transfers between devices: 73 us -> 67.2 us
  Pallas kernels: 36.1 us -> 30.6 us
  other arithmetic: 3.36 us -> 6.1 us
    unnamed x29 -> x51, local copies, waits for them, and re-layouts: 2.98 us -> 11.6 us
    ppermute x25 -> x22, starting transfers between devices: 67.1 us -> 60.7 us  [swap(): return lax.ppermute(array, axis, [(i, i ^ bit) for i in range(size)])]
    pallas_call x4, Pallas kernels: 24.9 us -> 18.8 us  [project(): pl.pallas_call(functools.partial(project_kernel, lines, count, len(chunks...]
    concatenate x3, other arithmetic: 0.19 us -> 2.79 us  [shards(): stems = jnp.concatenate([stems, swap(stems, 'branch', bit)], 0)]
    slice x6, local copies, waits for them, and re-layouts: 3.52 us -> 1.23 us  [finish_kv(): operands = [inverse[low:high], kv_bias, cos[low:high], sin[low:high]]]
    ppermute x25 -> x22, waiting for transfers between devices: 75.3 us -> 76.5 us  [swap(): return lax.ppermute(array, axis, [(i, i ^ bit) for i in range(size)])]
  transfers between devices with their start and end apart: 31 -> 30, of which waited for: 9 -> 8; matrix products, arithmetic and copies ran while one was open for 3% -> 6% of each run, Pallas kernels for 16% -> 13%
where the time goes in v4:
time: 213 us; the launch traced here: 212 us
  waiting for transfers between devices  76.6 us (36%)
  starting transfers between devices  67.2 us (32%)
  Pallas kernels  30.6 us (14%)
  local copies, waits for them, and re-layouts  18.3 us (9%)
  between operations  13.6 us (6%)
  other arithmetic  6.1 us (3%)
    ppermute x22, waiting for transfers between devices, swap(): return lax.ppermute(array, axis, [(i, i ^ bit) for i in range(size)])  76.5 us
    ppermute x22, starting transfers between devices, swap(): return lax.ppermute(array, axis, [(i, i ^ bit) for i in range(size)])  60.7 us
    pallas_call x4, Pallas kernels, project(): pl.pallas_call(functools.partial(project_kernel, lines, count, len(chunks...  18.8 us
    unnamed x51, local copies, waits for them, and re-layouts  11.6 us
    pallas_call x2, Pallas kernels, attend(): pl.pallas_call(kernel, grid=(1,), in_specs=in_specs, out_specs=anywhere,...  9.29 us
  transfers between devices with their start and end apart: 30, of which 8 were waited for; matrix products, arithmetic and copies ran while one was open for 6% of the time, Pallas kernels for 13%

profile of v4, /device:TPU:0, one launch (start us, length us, event | category | flops | bytes accessed | tf_op | source)
XLA Modules:
  0.0 212.3 jit_solution(11828956373758782503)
XLA Ops:
  11.9 1.2 slice.77
  13.2 1.5 collective-permute-start.2
  14.6 2.1 slice.78
  16.7 2.2 %tables.1 = (f32[384,128]{1,0:T(8,128)}, f32[384,128]{1,0:T(8,128)}) custom-call(s32[1]{0:T(128)} %bitcast.device_ref, s32[24]{0:T(128)} %parents_ref.5), custom_call_target="tpu_custom_call" | custom-call | tf_op jit(solution)/shard_map/tables/pallas_call | solution.py:291
  19.0 1.7 collective-permute-start.3
  21.7 30.1 %collective-permute-start.6 = (bf16[128,2048]{1,0:T(8,128)(2,1)S(1)}, bf16[128,2048]{1,0:T(8,128)(2,1)S(1)}, u32[]{:S(2)}, u32[]{:S(2)}) collective-permute-start(bf16[128,2048]{1,0:T(8,128)(2,1)S(1)} %collective-permute-done.3.refs_0_), channel_id=1, source_target_pairs={{0,16},{8,24},{16,0},{24,8},{1,17},{9,25},{17,1},{25,9},{2,18},{10... | collective-permute-start | bytes 1572872 | tf_op jit(solution)/shard_map/ppermute | solution.py:229
  51.8 11.2 %collective-permute-start.7 = (bf16[128,2048]{1,0:T(8,128)(2,1)S(1)}, bf16[128,2048]{1,0:T(8,128)(2,1)S(1)}, u32[]{:S(2)}, u32[]{:S(2)}) collective-permute-start(bf16[128,2048]{1,0:T(8,128)(2,1)S(1)} %collective-permute-done.5.refs_1_), channel_id=1, source_target_pairs={{0,16},{8,24},{16,0},{24,8},{1,17},{9,25},{17,1},{25,9},{2,18},{10... | collective-permute-start | bytes 1572872 | tf_op jit(solution)/shard_map/ppermute | solution.py:229
  63.0 1.6 collective-permute-start.17
  64.6 1.8 multiply_reduce_fusion
  68.1 7.6 %collective-permute-done.7.refs_3_.refs_4_ = bf16[128,2048]{1,0:T(8,128)(2,1)S(1)} collective-permute-done((bf16[128,2048]{1,0:T(8,128)(2,1)S(1)}, bf16[128,2048]{1,0:T(8,128)(2,1)S(1)}, u32[]{:S(2)}, u32[]{:S(2)}) %collective-permute-start.7) | collective-permute-done | bytes 524320 | tf_op jit(solution)/shard_map/ppermute | solution.py:229
  75.8 2.7 %collective-permute-start.18 = (bf16[128,2048]{1,0:T(8,128)(2,1)}, bf16[128,2048]{1,0:T(8,128)(2,1)}, u32[]{:S(2)}, u32[]{:S(2)}) collective-permute-start(bf16[128,2048]{1,0:T(8,128)(2,1)} %collective-permute-done.17.refs_0_.refs_2_), channel_id=1, source_target_pairs={{0,16},{8,24},{16,0},{24,8},{1,17},{9,25},{17,1},{25,9},{2,18},{10... | collective-permute-start | bytes 1572872 | tf_op jit(solution)/shard_map/ppermute | solution.py:229
  79.5 1.2 copy-done
  81.8 3.0 %project.4 = (bf16[512,256]{1,0:T(8,128)(2,1)S(1)}, f32[512,256]{1,0:T(8,128)S(1)}) custom-call(s32[1]{0:T(128)} %bitcast.4.place_ref, bf16[128,2048]{1,0:T(8,128)(2,1)S(1)} %collective-permute-done.3.refs_0_, bf16[128,2048]{1,0:T(8,128)(2,1)S(1)} %collective-permute-done.5.refs_1_, bf16[128,2048]{1,0:T(8,128)(2,1)S(1)} %collective-permute-done.6.refs_2_.refs_3_, ...), custom_call_target="tpu_custom_call" | custom-call | flops 1073741824 | bytes 4194304 | tf_op jit(solution)/shard_map/project/pallas_call | solution.py:321
  84.8 1.7 collective-permute-start.12
  86.5 4.1 %collective-permute-done.1 = f32[3,128]{1,0:T(4,128)S(1)} collective-permute-done((f32[3,128]{1,0:T(4,128)S(1)}, f32[3,128]{1,0:T(4,128)S(1)}, u32[]{:S(2)}, u32[]{:S(2)}) %collective-permute-start.1) | collective-permute-done | bytes 1568 | tf_op jit(solution)/shard_map/ppermute | solution.py:229
  90.6 1.2 collective-permute-start.19
  92.6 2.8 %collective-permute-start.13 = (bf16[1,256,256]{2,1,0:T(8,128)(2,1)S(1)}, bf16[1,256,256]{2,1,0:T(8,128)(2,1)S(1)}, u32[]{:S(2)}, u32[]{:S(2)}) collective-permute-start(bf16[1,256,256]{2,1,0:T(8,128)(2,1)S(1)} %fusion.4), channel_id=1, source_target_pairs={{0,4},{1,5},{2,6},{3,7},{4,0},{5,1},{6,2},{7,3},{8,12},{9,13},{10,... | collective-permute-start | bytes 393224 | tf_op jit(solution)/shard_map/ppermute | solution.py:229
  96.4 1.7 copy-done.13
  98.2 5.4 %project.5 = (bf16[512,640]{1,0:T(8,128)(2,1)}, f32[512,640]{1,0:T(8,128)S(1)}) custom-call(s32[1]{0:T(128)} %bitcast.4.place_ref, bf16[128,2048]{1,0:T(8,128)(2,1)S(1)} %collective-permute-done.3.refs_0_, bf16[128,2048]{1,0:T(8,128)(2,1)S(1)} %collective-permute-done.5.refs_1_, bf16[128,2048]{1,0:T(8,128)(2,1)S(1)} %collective-permute-done.6.refs_2_.refs_3_, ...), custom_call_target="tpu_custom_call" | custom-call | flops 2684354560 | bytes 4194304 | tf_op jit(solution)/shard_map/project/pallas_call | solution.py:321
  104.7 1.7 collective-permute-start.25
  106.6 1.6 collective-permute-start.14
  108.2 4.5 %project.6 = (bf16[256,896]{1,0:T(8,128)(2,1)}, f32[256,896]{1,0:T(8,128)S(1)}) custom-call(s32[1]{0:T(128)} %bitcast.4.place_ref, bf16[128,2048]{1,0:T(8,128)(2,1)} %collective-permute-done.17.refs_0_.refs_2_, bf16[128,2048]{1,0:T(8,128)(2,1)} %collective-permute-done.18.refs_1_.refs_5_, bf16[128,2048]{1,0:T(8,128)(2,1)} %collective-permute-done.19.refs_2_.refs_8_, ...), custom_call_target="tpu_custom_call" | custom-call | flops 1879048192 | bytes 2097152 | tf_op jit(solution)/shard_map/project/pallas_call | solution.py:321
  114.5 1.7 collective-permute-start.15
  117.8 1.4 copy-done.15
  119.2 5.9 %project.7 = (bf16[768,384]{1,0:T(8,128)(2,1)S(1)}, f32[768,384]{1,0:T(8,128)S(1)}) custom-call(s32[1]{0:T(128)} %bitcast.4.place_ref, bf16[128,2048]{1,0:T(8,128)(2,1)S(1)} %collective-permute-done.3.refs_0_, bf16[128,2048]{1,0:T(8,128)(2,1)S(1)} %collective-permute-done.5.refs_1_, bf16[128,2048]{1,0:T(8,128)(2,1)} %collective-permute-done.17.refs_0_.refs_2_, ...), custom_call_target="tpu_custom_call" | custom-call | flops 2415919104 | bytes 6291456 | tf_op jit(solution)/shard_map/project/pallas_call | solution.py:321
  125.6 12.5 %collective-permute-done.15 = bf16[2,256,256]{2,1,0:T(8,128)(2,1)} collective-permute-done((bf16[2,256,256]{2,1,0:T(8,128)(2,1)}, bf16[2,256,256]{2,1,0:T(8,128)(2,1)}, u32[]{:S(2)}, u32[]{:S(2)}) %collective-permute-start.15) | collective-permute-done | bytes 262176 | tf_op jit(solution)/shard_map/ppermute | solution.py:229
  139.9 2.3 %collective-permute-start.22 = (bf16[1,128,896]{2,1,0:T(8,128)(2,1)S(1)}, bf16[1,128,896]{2,1,0:T(8,128)(2,1)S(1)}, u32[]{:S(2)}, u32[]{:S(2)}) collective-permute-start(bf16[1,128,896]{2,1,0:T(8,128)(2,1)S(1)} %fusion.3), channel_id=1, source_target_pairs={{0,4},{1,5},{2,6},{3,7},{4,0},{5,1},{6,2},{7,3},{8,12},{9,13},{10,... | collective-permute-start | bytes 688136 | tf_op jit(solution)/shard_map/ppermute | solution.py:229
  144.0 15.6 %collective-permute-done.23.refs_3_ = bf16[2,384,384]{2,1,0:T(8,128)(2,1)S(1)} collective-permute-done((bf16[2,384,384]{2,1,0:T(8,128)(2,1)S(1)}, bf16[2,384,384]{2,1,0:T(8,128)(2,1)S(1)}, u32[]{:S(2)}, u32[]{:S(2)}) %collective-permute-start.23) | collective-permute-done | bytes 589856 | tf_op jit(solution)/shard_map/ppermute | solution.py:229
  159.7 29.6 %collective-permute-done.22.refs_2_.refs_7_ = bf16[1,128,896]{2,1,0:T(8,128)(2,1)S(1)} collective-permute-done((bf16[1,128,896]{2,1,0:T(8,128)(2,1)S(1)}, bf16[1,128,896]{2,1,0:T(8,128)(2,1)S(1)}, u32[]{:S(2)}, u32[]{:S(2)}) %collective-permute-start.22) | collective-permute-done | bytes 229408 | tf_op jit(solution)/shard_map/ppermute | solution.py:229
  190.6 5.7 %collective-permute-done.26.refs_4_ = bf16[1,256,640]{2,1,0:T(8,128)(2,1)S(1)} collective-permute-done((bf16[1,256,640]{2,1,0:T(8,128)(2,1)S(1)}, bf16[1,256,640]{2,1,0:T(8,128)(2,1)S(1)}, u32[]{:S(2)}, u32[]{:S(2)}) %collective-permute-start.26) | collective-permute-done | bytes 327712 | tf_op jit(solution)/shard_map/ppermute | solution.py:229
  196.4 5.5 %attend.2.refs_5_ = bf16[384,1024]{1,0:T(8,128)(2,1)} custom-call(s32[1]{0:T(128)} %bitcast.device_ref, s32[24]{0:T(128)S(1)} %copy-done.11, s32[24]{0:T(128)S(1)} %copy-done.12, f32[384,128]{1,0:T(8,128)S(1)} %broadcast_in_dim.33.inverse_ref, f32[1,640]{1,0:T(1,128)S(1)} %broadcast_in_dim.40.bias_ref, f32[384,128]{1,0:T(8,128)S(1)} %copy-done.2, ...), custom_call_target="tpu_custom_call" | custom-call | flops 1887436800 | bytes 491520 | tf_op jit(solution)/shard_map/attend/pallas_call | solution.py:415
  201.9 3.8 %attend.3 = bf16[384,1024]{1,0:T(8,128)(2,1)} custom-call(s32[1]{0:T(128)} %bitcast.device_ref, s32[24]{0:T(128)S(1)} %copy-done.11, s32[24]{0:T(128)S(1)} %copy-done.12, f32[384,128]{1,0:T(8,128)S(1)} %broadcast_in_dim.33.inverse_ref, f32[1,384]{1,0:T(1,128)S(1)} %broadcast_in_dim.34.bias_ref, ...), custom_call_target="tpu_custom_call", output_to_operand_aliasing={{}: (13, {})} | custom-call | flops 679477248 | bytes 294912 | tf_op jit(solution)/shard_map/attend/pallas_call | solution.py:415
  (121 shorter events, 22.0 us)
Async XLA Ops:
  6.5 73.0 %all-gather.4.cloned.1.call-start = ((), (), s32[]{:S(2)}) async-start(), calls=%async_computation | async-start | bytes 1572864 | tf_op jit(solution)/shard_map/all_gather | solution.py:279
  9.5 82.4 %all-gather.6.cloned.1.call-start = ((), (), s32[]{:S(2)}) async-start(), calls=%async_computation.1 | async-start | bytes 3932160 | tf_op jit(solution)/shard_map/all_gather | solution.py:279
  10.6 10.1 %collective-permute-start.4 = (bf16[256,2048]{1,0:T(8,128)(2,1)S(1)}, bf16[256,2048]{1,0:T(8,128)(2,1)S(1)}, u32[]{:S(2)}, u32[]{:S(2)}) collective-permute-start(bf16[256,2048]{1,0:T(8,128)(2,1)S(1)} %multiply_convert_fusion), channel_id=1, source_target_pairs={{0,0},{8,16},{16,8},{24,24},{1,1},{9,17},{17,9},{25,25},{2,26},{10... | collective-permute-start | bytes 3145736 | tf_op jit(solution)/shard_map/ppermute | solution.py:267
  13.1 103.7 %all-gather.8.cloned.1.call-start = ((), (), s32[]{:S(2)}) async-start(), calls=%async_computation.2 | async-start | bytes 2359296 | tf_op jit(solution)/shard_map/all_gather | solution.py:279
  13.2 5.8 %collective-permute-start.2 = (bf16[128,2048]{1,0:T(8,128)(2,1)S(1)}, bf16[128,2048]{1,0:T(8,128)(2,1)}, u32[]{:S(2)}, u32[]{:S(2)}) collective-permute-start(bf16[128,2048]{1,0:T(8,128)(2,1)S(1)} %fusion), channel_id=1, source_target_pairs={{0,0},{8,16},{16,8},{24,24},{1,1},{9,17},{17,9},{25,25},{2,26},{10... | collective-permute-start | bytes 1572872 | tf_op jit(solution)/shard_map/ppermute | solution.py:266
  19.0 2.7 %collective-permute-start.3 = (bf16[128,2048]{1,0:T(8,128)(2,1)}, bf16[128,2048]{1,0:T(8,128)(2,1)S(1)}, u32[]{:S(2)}, u32[]{:S(2)}) collective-permute-start(bf16[128,2048]{1,0:T(8,128)(2,1)} %collective-permute-done.2), channel_id=1, source_target_pairs={{0,0},{16,18},{8,12},{24,30},{1,1},{17,19},{9,13},{25,31},{26,16},... | collective-permute-start | bytes 1572872 | tf_op jit(solution)/shard_map/ppermute | solution.py:300
  20.8 57.8 %copy-start.2 = (f32[384,128]{1,0:T(8,128)S(1)}, f32[384,128]{1,0:T(8,128)}, u32[]{:S(2)}) copy-start(f32[384,128]{1,0:T(8,128)} %get-tuple-element.20.cos_ref) | copy-start | bytes 589828
  20.8 57.8 %copy-start.3 = (f32[384,128]{1,0:T(8,128)S(1)}, f32[384,128]{1,0:T(8,128)}, u32[]{:S(2)}) copy-start(f32[384,128]{1,0:T(8,128)} %get-tuple-element.21.sin_ref) | copy-start | bytes 589828
  20.8 30.9 %collective-permute-start.5 = (bf16[128,2048]{1,0:T(8,128)(2,1)S(1)}, bf16[128,2048]{1,0:T(8,128)(2,1)S(1)}, u32[]{:S(2)}, u32[]{:S(2)}) collective-permute-start(bf16[128,2048]{1,0:T(8,128)(2,1)S(1)} %get-tuple-element.36), channel_id=1, source_target_pairs={{0,0},{16,18},{8,12},{24,30},{1,1},{17,19},{9,13},{25,31},{26,16},... | collective-permute-start | bytes 1572872 | tf_op jit(solution)/shard_map/ppermute | solution.py:300
  21.7 46.1 %collective-permute-start.6 = (bf16[128,2048]{1,0:T(8,128)(2,1)S(1)}, bf16[128,2048]{1,0:T(8,128)(2,1)S(1)}, u32[]{:S(2)}, u32[]{:S(2)}) collective-permute-start(bf16[128,2048]{1,0:T(8,128)(2,1)S(1)} %collective-permute-done.3.refs_0_), channel_id=1, source_target_pairs={{0,16},{8,24},{16,0},{24,8},{1,17},{9,25},{17,1},{25,9},{2,18},{10... | collective-permute-start | bytes 1572872 | tf_op jit(solution)/shard_map/ppermute | solution.py:229
  51.8 24.0 %collective-permute-start.7 = (bf16[128,2048]{1,0:T(8,128)(2,1)S(1)}, bf16[128,2048]{1,0:T(8,128)(2,1)S(1)}, u32[]{:S(2)}, u32[]{:S(2)}) collective-permute-start(bf16[128,2048]{1,0:T(8,128)(2,1)S(1)} %collective-permute-done.5.refs_1_), channel_id=1, source_target_pairs={{0,16},{8,24},{16,0},{24,8},{1,17},{9,25},{17,1},{25,9},{2,18},{10... | collective-permute-start | bytes 1572872 | tf_op jit(solution)/shard_map/ppermute | solution.py:229
  63.0 12.8 %collective-permute-start.17 = (bf16[128,2048]{1,0:T(8,128)(2,1)S(1)}, bf16[128,2048]{1,0:T(8,128)(2,1)}, u32[]{:S(2)}, u32[]{:S(2)}) collective-permute-start(bf16[128,2048]{1,0:T(8,128)(2,1)S(1)} %get-tuple-element.35), channel_id=1, source_target_pairs={{0,0},{16,18},{8,12},{24,30},{1,1},{17,19},{9,13},{25,31},{26,16},... | collective-permute-start | bytes 1572872 | tf_op jit(solution)/shard_map/ppermute | solution.py:300
  66.4 1.2 collective-permute-start
  66.6 12.8 %collective-permute-start.8 = (bf16[128,2048]{1,0:T(8,128)(2,1)S(1)}, bf16[128,2048]{1,0:T(8,128)(2,1)}, u32[]{:S(2)}, u32[]{:S(2)}) collective-permute-start(bf16[128,2048]{1,0:T(8,128)(2,1)S(1)} %collective-permute-done.3.refs_0_), channel_id=1, source_target_pairs={{0,8},{8,0},{16,24},{24,16},{1,9},{9,1},{17,25},{25,17},{2,10},{10... | collective-permute-start | bytes 1572872 | tf_op jit(solution)/shard_map/ppermute | solution.py:229
  67.6 11.9 %collective-permute-start.9 = (bf16[128,2048]{1,0:T(8,128)(2,1)S(1)}, bf16[128,2048]{1,0:T(8,128)(2,1)}, u32[]{:S(2)}, u32[]{:S(2)}) collective-permute-start(bf16[128,2048]{1,0:T(8,128)(2,1)S(1)} %collective-permute-done.5.refs_1_), channel_id=1, source_target_pairs={{0,8},{8,0},{16,24},{24,16},{1,9},{9,1},{17,25},{25,17},{2,10},{10... | collective-permute-start | bytes 1572872 | tf_op jit(solution)/shard_map/ppermute | solution.py:229
  67.8 11.7 %collective-permute-start.10 = (bf16[128,2048]{1,0:T(8,128)(2,1)S(1)}, bf16[128,2048]{1,0:T(8,128)(2,1)}, u32[]{:S(2)}, u32[]{:S(2)}) collective-permute-start(bf16[128,2048]{1,0:T(8,128)(2,1)S(1)} %collective-permute-done.6.refs_2_.refs_3_), channel_id=1, source_target_pairs={{0,8},{8,0},{16,24},{24,16},{1,9},{9,1},{17,25},{25,17},{2,10},{10... | collective-permute-start | bytes 1572872 | tf_op jit(solution)/shard_map/ppermute | solution.py:229
  75.8 3.7 %collective-permute-start.11 = (bf16[128,2048]{1,0:T(8,128)(2,1)S(1)}, bf16[128,2048]{1,0:T(8,128)(2,1)}, u32[]{:S(2)}, u32[]{:S(2)}) collective-permute-start(bf16[128,2048]{1,0:T(8,128)(2,1)S(1)} %collective-permute-done.7.refs_3_.refs_4_), channel_id=1, source_target_pairs={{0,8},{8,0},{16,24},{24,16},{1,9},{9,1},{17,25},{25,17},{2,10},{10... | collective-permute-start | bytes 1572872 | tf_op jit(solution)/shard_map/ppermute | solution.py:229
  75.8 16.0 %collective-permute-start.18 = (bf16[128,2048]{1,0:T(8,128)(2,1)}, bf16[128,2048]{1,0:T(8,128)(2,1)}, u32[]{:S(2)}, u32[]{:S(2)}) collective-permute-start(bf16[128,2048]{1,0:T(8,128)(2,1)} %collective-permute-done.17.refs_0_.refs_2_), channel_id=1, source_target_pairs={{0,16},{8,24},{16,0},{24,8},{1,17},{9,25},{17,1},{25,9},{2,18},{10... | collective-permute-start | bytes 1572872 | tf_op jit(solution)/shard_map/ppermute | solution.py:229
  79.4 11.2 %collective-permute-start.1 = (f32[3,128]{1,0:T(4,128)S(1)}, f32[3,128]{1,0:T(4,128)S(1)}, u32[]{:S(2)}, u32[]{:S(2)}) collective-permute-start(f32[3,128]{1,0:T(4,128)S(1)} %add.27), channel_id=1, source_target_pairs={{0,16},{8,24},{16,0},{24,8},{1,17},{9,25},{17,1},{25,9},{2,18},{10... | collective-permute-start | bytes 4616 | tf_op jit(solution)/shard_map/ppermute | solution.py:229
  84.8 7.8 %collective-permute-start.12 = (bf16[2,256,256]{2,1,0:T(8,128)(2,1)S(1)}, bf16[2,256,256]{2,1,0:T(8,128)(2,1)S(1)}, u32[]{:S(2)}, u32[]{:S(2)}) collective-permute-start(bf16[2,256,256]{2,1,0:T(8,128)(2,1)S(1)} %bitcast.39), channel_id=1, source_target_pairs={{0,2},{1,3},{2,0},{3,1},{4,6},{5,7},{6,4},{7,5},{8,10},{9,11},{10,... | collective-permute-start | bytes 786440 | tf_op jit(solution)/shard_map/ppermute | solution.py:229
  90.6 17.6 %collective-permute-start.19 = (bf16[128,2048]{1,0:T(8,128)(2,1)}, bf16[128,2048]{1,0:T(8,128)(2,1)}, u32[]{:S(2)}, u32[]{:S(2)}) collective-permute-start(bf16[128,2048]{1,0:T(8,128)(2,1)} %collective-permute-done.17.refs_0_.refs_2_), channel_id=1, source_target_pairs={{0,8},{8,0},{16,24},{24,16},{1,9},{9,1},{17,25},{25,17},{2,10},{10... | collective-permute-start | bytes 1572872 | tf_op jit(solution)/shard_map/ppermute | solution.py:229
  91.8 16.4 %collective-permute-start.20 = (bf16[128,2048]{1,0:T(8,128)(2,1)}, bf16[128,2048]{1,0:T(8,128)(2,1)}, u32[]{:S(2)}, u32[]{:S(2)}) collective-permute-start(bf16[128,2048]{1,0:T(8,128)(2,1)} %collective-permute-done.18.refs_1_.refs_5_), channel_id=1, source_target_pairs={{0,8},{8,0},{16,24},{24,16},{1,9},{9,1},{17,25},{25,17},{2,10},{10... | collective-permute-start | bytes 1572872 | tf_op jit(solution)/shard_map/ppermute | solution.py:229
  92.6 13.7 %collective-permute-start.13 = (bf16[1,256,256]{2,1,0:T(8,128)(2,1)S(1)}, bf16[1,256,256]{2,1,0:T(8,128)(2,1)S(1)}, u32[]{:S(2)}, u32[]{:S(2)}) collective-permute-start(bf16[1,256,256]{2,1,0:T(8,128)(2,1)S(1)} %fusion.4), channel_id=1, source_target_pairs={{0,4},{1,5},{2,6},{3,7},{4,0},{5,1},{6,2},{7,3},{8,12},{9,13},{10,... | collective-permute-start | bytes 393224 | tf_op jit(solution)/shard_map/ppermute | solution.py:229
  104.7 37.5 %collective-permute-start.25 = (bf16[2,256,640]{2,1,0:T(8,128)(2,1)}, bf16[2,256,640]{2,1,0:T(8,128)(2,1)}, u32[]{:S(2)}, u32[]{:S(2)}) collective-permute-start(bf16[2,256,640]{2,1,0:T(8,128)(2,1)} %bitcast.16), channel_id=1, source_target_pairs={{0,2},{1,3},{2,0},{3,1},{4,6},{5,7},{6,4},{7,5},{8,10},{9,11},{10,... | collective-permute-start | bytes 1966088 | tf_op jit(solution)/shard_map/ppermute | solution.py:229
  106.6 6.5 %collective-permute-start.14 = (bf16[1,256,256]{2,1,0:T(8,128)(2,1)S(1)}, bf16[1,256,256]{2,1,0:T(8,128)(2,1)S(1)}, u32[]{:S(2)}, u32[]{:S(2)}) collective-permute-start(bf16[1,256,256]{2,1,0:T(8,128)(2,1)S(1)} %bitcast.23), channel_id=1, source_target_pairs={{0,1},{1,0},{2,3},{3,2},{4,5},{5,4},{6,7},{7,6},{8,9},{9,8},{10,11... | collective-permute-start | bytes 393224 | tf_op jit(solution)/shard_map/ppermute | solution.py:229
  112.7 27.1 %collective-permute-start.21 = (bf16[2,128,896]{2,1,0:T(8,128)(2,1)}, bf16[2,128,896]{2,1,0:T(8,128)(2,1)S(1)}, u32[]{:S(2)}, u32[]{:S(2)}) collective-permute-start(bf16[2,128,896]{2,1,0:T(8,128)(2,1)} %bitcast.12), channel_id=1, source_target_pairs={{0,2},{1,3},{2,0},{3,1},{4,6},{5,7},{6,4},{7,5},{8,10},{9,11},{10,... | collective-permute-start | bytes 1376264 | tf_op jit(solution)/shard_map/ppermute | solution.py:229
  114.5 23.5 %collective-permute-start.15 = (bf16[2,256,256]{2,1,0:T(8,128)(2,1)}, bf16[2,256,256]{2,1,0:T(8,128)(2,1)}, u32[]{:S(2)}, u32[]{:S(2)}) collective-permute-start(bf16[2,256,256]{2,1,0:T(8,128)(2,1)} %pad_maximum_fusion.2), channel_id=1, source_target_pairs={{0,2},{1,3},{2,0},{3,1},{4,6},{5,7},{6,4},{7,5},{8,10},{9,11},{10,... | collective-permute-start | bytes 786440 | tf_op jit(solution)/shard_map/ppermute | solution.py:229
  125.1 34.4 %collective-permute-start.23 = (bf16[2,384,384]{2,1,0:T(8,128)(2,1)S(1)}, bf16[2,384,384]{2,1,0:T(8,128)(2,1)S(1)}, u32[]{:S(2)}, u32[]{:S(2)}) collective-permute-start(bf16[2,384,384]{2,1,0:T(8,128)(2,1)S(1)} %bitcast.38), channel_id=1, source_target_pairs={{0,2},{1,3},{2,0},{3,1},{4,6},{5,7},{6,4},{7,5},{8,10},{9,11},{10,... | collective-permute-start | bytes 1769480 | tf_op jit(solution)/shard_map/ppermute | solution.py:229
  139.1 50.5 %collective-permute-start.16 = (bf16[4,256,256]{2,1,0:T(8,128)(2,1)S(1)}, bf16[4,256,256]{2,1,0:T(8,128)(2,1)S(1)}, u32[]{:S(2)}, u32[]{:S(2)}) collective-permute-start(bf16[4,256,256]{2,1,0:T(8,128)(2,1)S(1)} %pad_maximum_fusion.1), channel_id=1, source_target_pairs={{0,4},{1,5},{2,6},{3,7},{4,0},{5,1},{6,2},{7,3},{8,12},{9,13},{10,... | collective-permute-start | bytes 1572872 | tf_op jit(solution)/shard_map/ppermute | solution.py:229
  139.9 49.4 %collective-permute-start.22 = (bf16[1,128,896]{2,1,0:T(8,128)(2,1)S(1)}, bf16[1,128,896]{2,1,0:T(8,128)(2,1)S(1)}, u32[]{:S(2)}, u32[]{:S(2)}) collective-permute-start(bf16[1,128,896]{2,1,0:T(8,128)(2,1)S(1)} %fusion.3), channel_id=1, source_target_pairs={{0,4},{1,5},{2,6},{3,7},{4,0},{5,1},{6,2},{7,3},{8,12},{9,13},{10,... | collective-permute-start | bytes 688136 | tf_op jit(solution)/shard_map/ppermute | solution.py:229
  143.2 53.1 %collective-permute-start.26 = (bf16[1,256,640]{2,1,0:T(8,128)(2,1)S(1)}, bf16[1,256,640]{2,1,0:T(8,128)(2,1)S(1)}, u32[]{:S(2)}, u32[]{:S(2)}) collective-permute-start(bf16[1,256,640]{2,1,0:T(8,128)(2,1)S(1)} %fusion.1), channel_id=1, source_target_pairs={{0,4},{1,5},{2,6},{3,7},{4,0},{5,1},{6,2},{7,3},{8,12},{9,13},{10,... | collective-permute-start | bytes 983048 | tf_op jit(solution)/shard_map/ppermute | solution.py:229
  159.6 42.3 %collective-permute-start.24 = (bf16[1,384,384]{2,1,0:T(8,128)(2,1)S(1)}, bf16[1,384,384]{2,1,0:T(8,128)(2,1)S(1)}, u32[]{:S(2)}, u32[]{:S(2)}) collective-permute-start(bf16[1,384,384]{2,1,0:T(8,128)(2,1)S(1)} %fusion.2), channel_id=1, source_target_pairs={{0,4},{1,5},{2,6},{3,7},{4,0},{5,1},{6,2},{7,3},{8,12},{9,13},{10,... | collective-permute-start | bytes 884744 | tf_op jit(solution)/shard_map/ppermute | solution.py:229
  (23 other events, 313.4 us)
Sparse Core Ops, SparseCore 0:
  9.6 23.9 all-gather.3
  35.2 39.0 all-gather.5
  78.7 26.7 all-gather.7

commit v5 on v4

--- a/solution.py
+++ b/solution.py
@@ -62,38 +62,39 @@
     sin_ref[...] = jnp.where(front, -sin, sin)
 
 
-def project_kernel(lines, blocks, chunks, place_ref, *refs):
+def project_kernel(lines, blocks, groups, place_ref, *refs):
     pieces = refs[: lines * blocks]
-    weights = refs[lines * blocks : lines * blocks + chunks]
-    send_ref, keep_ref, held, sems = refs[lines * blocks + chunks :]
+    send_ref, keep_ref, held, weight, sems = refs[-5:]
+    weights = refs[lines * blocks : -5]
     half = lines // 2
     block_len = pieces[0].shape[0]
+    rows = weights[0].shape[0]
     copies = []
+    start = 0
+    for w, ref in enumerate(weights):
+        member = lax.bitwise_xor(place_ref[1], jnp.int32(w % groups))
+        width = ref.shape[1]
+        there = weight.at[pl.ds(pl.multiple_of(member * rows, rows), rows), pl.ds(start, width)]
+        copies.append(pltpu.make_async_copy(ref, there, sems.at[w]))
+        if w % groups == groups - 1:
+            start += width
     for i in range(lines):
         target = lax.bitwise_xor(jnp.int32(i), place_ref[0])
         slot = jnp.where(target % 2 == 0, half, 0) + target // 2
         for block in range(blocks):
-            start = pl.multiple_of((slot * blocks + block) * block_len, block_len)
-            copy = pltpu.make_async_copy(
-                pieces[i * blocks + block],
-                held.at[pl.ds(start, block_len)],
-                sems.at[i * blocks + block],
-            )
-            copy.start()
-            copies.append(copy)
+            begin = pl.multiple_of((slot * blocks + block) * block_len, block_len)
+            n = i * blocks + block
+            there = held.at[pl.ds(begin, block_len)]
+            copies.append(pltpu.make_async_copy(pieces[n], there, sems.at[len(weights) + n]))
+    for copy in copies:
+        copy.start()
     for copy in copies:
         copy.wait()
     middle = held.shape[0] // 2
-    start = 0
-    for weight in weights:
-        stop = start + weight.shape[1]
-        send_ref[:, start:stop] = jnp.dot(
-            held[:middle], weight[...], preferred_element_type=jnp.float32
-        ).astype(jnp.bfloat16)
-        keep_ref[:, start:stop] = jnp.dot(
-            held[middle:], weight[...], preferred_element_type=jnp.float32
-        )
-        start = stop
+    send_ref[...] = jnp.dot(
+        held[:middle], weight[...], preferred_element_type=jnp.float32
+    ).astype(jnp.bfloat16)
+    keep_ref[...] = jnp.dot(held[middle:], weight[...], preferred_element_type=jnp.float32)
 
 
 def kv_kernel(addends, inverse_ref, bias_ref, cos_ref, sin_ref, *refs):
@@ -104,7 +105,7 @@
 
 
 def attend_kernel(
-    far_slots, block_len, blocks, heads, first_head, parts, addends, aliased, device_ref,
+    far_slots, block_len, blocks, heads, first_head, parts, addends, aliased, tour, device_ref,
     parents_ref, lengths_ref, inverse_ref, bias_ref, cos_ref, sin_ref, stems_ref, *refs,
 ):
     keys = refs[:2]
@@ -120,7 +121,10 @@
         safe = jnp.maximum(ids[level], 0)
         owner = lax.div(safe, jnp.int32(blocks))
         inner = lax.rem(safe, jnp.int32(blocks))
-        where = lax.bitwise_xor(owner, device)
+        apart = lax.bitwise_xor(owner, device)
+        where = jnp.int32(0)
+        for step, bit in enumerate(tour):
+            where = where + jnp.where(lax.bitwise_and(apart, bit) != 0, 1 << step, 0)
         start = pl.multiple_of(inner * block_len, block_len)
         here = pl.ds(level * block_len, block_len)
         far_key[here, :] = stems_ref[where, pl.ds(start, block_len), :HD]
@@ -235,7 +239,7 @@
     vmem = pl.BlockSpec(memory_space=pltpu.VMEM)
     anywhere = pl.BlockSpec(memory_space=pl.ANY)
     device_id = device.astype(jnp.int32)[None]
-    place = spread(part).astype(jnp.int32)[None]
+    place = jnp.stack([spread(part), device % groups]).astype(jnp.int32)
 
     raw = hidden.reshape(tokens, feature_part)
     gain_part = lax.dynamic_slice_in_dim(gain, part * feature_part, feature_part)
@@ -260,33 +264,33 @@
                 first_hop.append((feature * branches + here, stop))
                 second_hop.append((stop, landing(z, feature) * branches + there))
     axes = ("fsdp", "branch")
-    first_sent = (raw[:block_len].astype(f32) * gain_part).astype(bf16)
-    rest_sent = tie(raw, first_sent)[block_len:]
-    rest_sent = (rest_sent.astype(f32) * gain_part).astype(bf16)
-    first_sent = lax.ppermute(first_sent, axes, first_hop)
-    rest_sent = lax.ppermute(rest_sent, axes, first_hop)
-    sent = [first_sent] + [
-        rest_sent[i * block_len : (i + 1) * block_len] for i in range(blocks - 1)
-    ]
-
     head_cuts = [0, (5 * head_count + 7) // 8, head_count]
     w_chunks = [jnp.concatenate([w_key, w_value], 1)] + [
         lax.slice_in_dim(w_query, low * HD, high * HD, axis=1)
         for low, high in zip(head_cuts, head_cuts[1:])
     ]
-    teams = [[z * groups + g for g in range(groups)] for z in range(lines)]
-    w_rows = [
-        lax.all_gather(chunk, "branch", axis_index_groups=teams, axis=0, tiled=True)
-        for chunk in w_chunks
-    ]
-
     squares = jnp.sum(jnp.square(raw.astype(f32)), -1).reshape(blocks, block_len)
+    scaled = (raw.astype(f32) * gain_part).astype(bf16)
+    cut = STEMS * block_len
+    sent = [lax.ppermute(piece, axes, first_hop) for piece in (scaled[:cut], scaled[cut:])]
+    squares = tie(squares, sent[0])
     bit = 1
     while bit < lines:
         squares = squares + swap(squares, "fsdp", bit)
         bit *= 2
     inverse = lax.rsqrt(squares / features + 1e-06).reshape(tokens)
     inverse = jnp.broadcast_to(inverse[:, None], (tokens, HD))
+    sent = [piece[i : i + block_len] for piece in sent for i in range(0, len(piece), block_len)]
+
+    head_cuts = [0, (5 * head_count + 7) // 8, head_count]
+    w_chunks = [jnp.concatenate([w_key, w_value], 1)] + [
+        lax.slice_in_dim(w_query, low * HD, high * HD, axis=1)
+        for low, high in zip(head_cuts, head_cuts[1:])
+    ]
+    w_rows = []
+    for chunk in w_chunks:
+        outgoing = tie(chunk, w_rows[-1][-1]) if w_rows else chunk
+        w_rows.append([chunk] + [swap(outgoing, "branch", j) for j in range(1, groups)])
 
     cos, sin = pl.pallas_call(
         functools.partial(table_kernel, far_slots, blocks, block_len),
@@ -295,10 +299,13 @@
         out_shape=[jax.ShapeDtypeStruct((tokens, HD), f32)] * 2,
         name="tables",
     )(device_id, parents)
-
     sent[0] = tie(sent[0], cos, sin, *w_chunks)
+    sent[1] = tie(sent[1], w_rows[0][-1])
+    sent[2] = tie(sent[2], squares)
+
     sent = [lax.ppermute(piece, axes, second_hop) for piece in sent]
     held = [{0: piece} for piece in sent]
+    held[-1][0] = tie(held[-1][0], w_rows[1][-1])
     bit = half_lines
     while bit:
         for piece in held:
@@ -307,20 +314,17 @@
         bit //= 2
     held = [[piece[j] for j in sorted(piece, key=spread)] for piece in held]
 
-    order = [None]
-
-    def project(which, chunks):
+    def project(which, chunks, *after):
         count = len(which)
         length = count * block_len
-        weights = [w_rows[chunk] for chunk in chunks]
-        width = sum(w.shape[1] for w in weights)
+        weights = [w for chunk in chunks for w in w_rows[chunk]]
+        width = sum(w_chunks[chunk].shape[1] for chunk in chunks)
         operands = [held[block][i] for i in range(lines) for block in which]
-        if order[0] is not None:
-            weights[0] = tie(weights[0], order[0])
+        operands[0] = tie(operands[0], *after) if after else operands[0]
         flops = 2 * lines * length * feature_part * width
         send, keep = pl.pallas_call(
-            functools.partial(project_kernel, lines, count, len(chunks)),
-            in_specs=[smem] + [anywhere] * len(operands) + [vmem] * len(weights),
+            functools.partial(project_kernel, lines, count, groups),
+            in_specs=[smem] + [anywhere] * (len(operands) + len(weights)),
             out_specs=[vmem, vmem],
             out_shape=[
                 jax.ShapeDtypeStruct((half_lines * length, width), bf16),
@@ -328,7 +332,8 @@
             ],
             scratch_shapes=[
                 pltpu.VMEM((lines * length, feature_part), bf16),
-                pltpu.SemaphoreType.DMA((len(operands),)),
+                pltpu.VMEM((feature_part, width), bf16),
+                pltpu.SemaphoreType.DMA((len(operands) + len(weights),)),
             ],
             compiler_params=pltpu.CompilerParams(vmem_limit_bytes=32 * 2**20),
             cost_estimate=pl.CostEstimate(
@@ -336,22 +341,29 @@
             ),
             name="project",
         )(place, *operands, *weights)
-        order[0] = send
         return send.reshape(half_lines, length, width), keep.reshape(half_lines, length, width)
 
-    def halve(send, keep):
-        addends = [keep]
-        total = keep
-        bit = 1
-        while bit < lines:
-            came = swap(send, "branch", bit * groups)
-            addends.append(came)
-            bit *= 2
-            if bit < lines:
-                total = total + came.astype(f32)
-                send = total[1::2].astype(bf16)
-                total = total[0::2]
-        return addends
+    class Halving:
+        def __init__(self, partial):
+            self.send, self.total = partial
+            self.addends = [self.total]
+            self.bit = 1
+
+        def step(self, *after):
+            send = tie(self.send, *after) if after else self.send
+            self.came = swap(send, "branch", self.bit * groups)
+            self.addends.append(self.came)
+            self.bit *= 2
+
+        def add(self):
+            total = self.total + self.came.astype(f32)
+            self.send = total[1::2].astype(bf16)
+            self.total = total[0::2]
+
+        def rest(self, *after):
+            while self.bit < lines:
+                self.add()
+                self.step(*after)
 
     addend_count = 1 + bits_of(lines)
 
@@ -378,20 +390,37 @@
 
     early = list(range(STEMS))
     late = list(range(STEMS, blocks))
-    first_sums = project(early, [0])
-    second_sums = project(early, [1])
-    first_sums = halve(*first_sums)
-    stem_kv = finish_kv(first_sums, 0, STEMS)
-    second_sums = halve(*second_sums)
-    third_sums = halve(*project(late, [0, 1]))
-    late_kv = finish_kv(third_sums, STEMS, blocks - STEMS)
-    fourth_sums = halve(*project(early + late, [2]))
-
+    first = Halving(project(early, [0]))
+    first.step()
+    second = Halving(project(early, [1], first.send))
+    second.step()
+    first.rest(second.send)
+    third = Halving(project(late, [0, 1], second.send, first.send))
+    stem_kv = finish_kv(first.addends, 0, STEMS)
+
+    tour = [1 << i for i in range(bits_of(groups))]
+    tour += [groups << i for i in reversed(range(bits_of(lines)))]
     stems = stem_kv[None]
-    bit = 1
-    while bit < branches:
-        stems = jnp.concatenate([stems, swap(stems, "branch", bit)], 0)
-        bit *= 2
+
+    def tour_step(stems, bit, *after):
+        came = swap(tie(stems, *after) if after else stems, "branch", bit)
+        return jnp.concatenate([stems, came], 0)
+
+    for bit in tour[: bits_of(groups)]:
+        stems = tour_step(stems, bit)
+    third.step(stem_kv)
+    far_tour = tour[bits_of(groups) :]
+    stems = tour_step(stems, far_tour[0])
+    fourth = Halving(project(early + late, [2], third.send))
+    second.rest(stems if len(far_tour) == 0 else third.send)
+    fourth.step(second.came)
+    third.rest()
+    for bit in far_tour[1:]:
+        stems = tour_step(stems, bit)
+    fourth.rest(third.send)
+    third.addends[-1] = tie(third.addends[-1], fourth.send)
+    late_kv = finish_kv(third.addends, STEMS, blocks - STEMS)
+    second_sums, third_sums, fourth_sums = second.addends, third.addends, fourth.addends
 
     def attend(heads, first_head, parts, sums, output):
         operands = [
@@ -409,7 +438,7 @@
             in_specs.append(anywhere)
         kernel = functools.partial(
             attend_kernel, far_slots, block_len, blocks, heads, first_head, parts, addend_count,
-            len(aliases),
+            len(aliases), tour,
         )
         keys = (far_slots * len(parts) + blocks) * block_len
         return pl.pallas_call(

time: 213 us -> 196 us (0.920)
  between operations: 13.6 us -> 0.56 us
  local copies, waits for them, and re-layouts: 18.3 us -> 6.06 us
  waiting for transfers between devices: 76.6 us -> 82.6 us
  other arithmetic: 6.1 us -> 2.71 us
  Pallas kernels: 30.6 us -> 33.1 us
    ppermute x22 -> x25, starting transfers between devices: 60.7 us -> 46.1 us  [swap(): return lax.ppermute(array, axis, [(i, i ^ bit) for i in range(size)])]
    ppermute x2, starting transfers between devices: 2.33 us -> 14.8 us  [shards(): lax.ppermute(piece, axes, first_hop)]
    unnamed x51 -> x27, local copies, waits for them, and re-layouts: 11.6 us -> 1.54 us
    ppermute x22 -> x25, waiting for transfers between devices: 76.5 us -> 82.6 us  [swap(): return lax.ppermute(array, axis, [(i, i ^ bit) for i in range(size)])]
    ppermute x3, starting transfers between devices: 4.16 us -> 8.27 us  [shards(): sent = [lax.ppermute(piece, axes, second_hop) for piece in sent]]
    slice x1 -> x3, local copies, waits for them, and re-layouts: 0.08 us -> 3.2 us  [the longest x1 1.3 us: shards(): piece[i:i + block_len]]
    slice x2, local copies, waits for them, and re-layouts: 3.34 us -> 0.24 us  [shards(): lax.slice_in_dim(w_query, low * HD, high * HD, axis=1)]
    pallas_call x4, Pallas kernels: 18.8 us -> 21.7 us  [project(): pl.pallas_call(functools.partial(project_kernel, lines, count, groups), i...]
  transfers between devices with their start and end apart: 30 -> 30, of which waited for: 8 -> 12; matrix products, arithmetic and copies ran while one was open for 6% -> 2% of each run, Pallas kernels for 13% -> 15%
where the time goes in v5:
time: 196 us; the launch traced here: 194 us
  waiting for transfers between devices  82.6 us (42%)
  starting transfers between devices  69.2 us (35%)
  Pallas kernels  33.1 us (17%)
  local copies, waits for them, and re-layouts  6.06 us (3%)
  other arithmetic  2.71 us (1%)
    ppermute x25, waiting for transfers between devices, swap(): return lax.ppermute(array, axis, [(i, i ^ bit) for i in range(size)])  82.6 us
    ppermute x25, starting transfers between devices, swap(): return lax.ppermute(array, axis, [(i, i ^ bit) for i in range(size)])  46.1 us
    pallas_call x4, Pallas kernels, project(): pl.pallas_call(functools.partial(project_kernel, lines, count, groups), i...  21.7 us
    ppermute x2, starting transfers between devices, shards(): lax.ppermute(piece, axes, first_hop)  14.8 us
    pallas_call x2, Pallas kernels, attend(): pl.pallas_call(kernel, grid=(1,), in_specs=in_specs, out_specs=anywhere,...  8.96 us
    ppermute x3, starting transfers between devices, shards(): sent = [lax.ppermute(piece, axes, second_hop) for piece in sent]  8.27 us
  transfers between devices with their start and end apart: 30, of which 12 were waited for; matrix products, arithmetic and copies ran while one was open for 2% of the time, Pallas kernels for 15%

profile of v5, /device:TPU:0, one launch (start us, length us, event | category | flops | bytes accessed | tf_op | source)
XLA Modules:
  0.0 194.2 jit_solution(11053190154011911360)
XLA Ops:
  0.7 1.8 fusion
  3.6 9.5 %collective-permute-start = (bf16[256,2048]{1,0:T(8,128)(2,1)}, bf16[256,2048]{1,0:T(8,128)(2,1)}, u32[]{:S(2)}, u32[]{:S(2)}) collective-permute-start(bf16[256,2048]{1,0:T(8,128)(2,1)} %slice.90), channel_id=1, source_target_pairs={{0,0},{8,16},{16,8},{24,24},{1,1},{9,17},{17,9},{25,25},{2,26},{10... | collective-permute-start | bytes 3145736 | tf_op jit(solution)/shard_map/ppermute | solution.py:275
  13.2 3.0 %collective-permute-start.4 = (bf16[1024,256]{1,0:T(8,128)(2,1)S(1)}, bf16[1024,256]{1,0:T(8,128)(2,1)S(1)}, u32[]{:S(2)}, u32[]{:S(2)}) collective-permute-start(bf16[1024,256]{1,0:T(8,128)(2,1)S(1)} %constant_dynamic-update-slice_fusion.refs_8_.refs_4_), channel_id=1, source_target_pairs={{0,1},{1,0},{2,3},{3,2},{4,5},{5,4},{6,7},{7,6},{8,9},{9,8},{10,11... | collective-permute-start | bytes 1572872 | tf_op jit(solution)/shard_map/ppermute | solution.py:233
  17.1 5.4 %collective-permute-start.18 = (bf16[128,2048]{1,0:T(8,128)(2,1)}, bf16[128,2048]{1,0:T(8,128)(2,1)}, u32[]{:S(2)}, u32[]{:S(2)}) collective-permute-start(bf16[128,2048]{1,0:T(8,128)(2,1)} %slice.95), channel_id=1, source_target_pairs={{0,0},{8,16},{16,8},{24,24},{1,1},{9,17},{17,9},{25,25},{2,26},{10... | collective-permute-start | bytes 1572872 | tf_op jit(solution)/shard_map/ppermute | solution.py:275
  22.7 2.2 %tables.1 = (f32[384,128]{1,0:T(8,128)}, f32[384,128]{1,0:T(8,128)}) custom-call(s32[1]{0:T(128)} %bitcast.device_ref, s32[24]{0:T(128)} %parents_ref.5), custom_call_target="tpu_custom_call" | custom-call | tf_op jit(solution)/shard_map/tables/pallas_call | solution.py:295
  24.9 2.5 %collective-permute-done.4.refs_9_.refs_5_ = bf16[1024,256]{1,0:T(8,128)(2,1)S(1)} collective-permute-done((bf16[1024,256]{1,0:T(8,128)(2,1)S(1)}, bf16[1024,256]{1,0:T(8,128)(2,1)S(1)}, u32[]{:S(2)}, u32[]{:S(2)}) %collective-permute-start.4) | collective-permute-done | bytes 524320 | tf_op jit(solution)/shard_map/ppermute | solution.py:233
  27.4 2.5 %collective-permute-start.13 = (bf16[1024,640]{1,0:T(8,128)(2,1)S(1)}, bf16[1024,640]{1,0:T(8,128)(2,1)S(1)}, u32[]{:S(2)}, u32[]{:S(2)}) collective-permute-start(bf16[1024,640]{1,0:T(8,128)(2,1)S(1)} %slice.77.refs_8_.refs_6_), channel_id=1, source_target_pairs={{0,1},{1,0},{2,3},{3,2},{4,5},{5,4},{6,7},{7,6},{8,9},{9,8},{10,11... | collective-permute-start | bytes 3932168 | tf_op jit(solution)/shard_map/ppermute | solution.py:233
  31.2 1.5 collective-permute-start.3
  32.7 1.5 collective-permute-start.5
  34.5 3.8 %collective-permute-start.1 = (f32[3,128]{1,0:T(4,128)S(1)}, f32[3,128]{1,0:T(4,128)S(1)}, u32[]{:S(2)}, u32[]{:S(2)}) collective-permute-start(f32[3,128]{1,0:T(4,128)S(1)} %multiply_reduce_fusion), channel_id=1, source_target_pairs={{0,8},{8,0},{16,24},{24,16},{1,9},{9,1},{17,25},{25,17},{2,10},{10... | collective-permute-start | bytes 4616 | tf_op jit(solution)/shard_map/ppermute | solution.py:233
  39.2 1.6 collective-permute-start.2
  40.7 2.0 %collective-permute-done.2 = f32[3,128]{1,0:T(4,128)S(1)} collective-permute-done((f32[3,128]{1,0:T(4,128)S(1)}, f32[3,128]{1,0:T(4,128)S(1)}, u32[]{:S(2)}, u32[]{:S(2)}) %collective-permute-start.2) | collective-permute-done | bytes 1568 | tf_op jit(solution)/shard_map/ppermute | solution.py:233
  42.7 5.4 %collective-permute-start.19 = (bf16[128,2048]{1,0:T(8,128)(2,1)}, bf16[128,2048]{1,0:T(8,128)(2,1)}, u32[]{:S(2)}, u32[]{:S(2)}) collective-permute-start(bf16[128,2048]{1,0:T(8,128)(2,1)} %collective-permute-done.18), channel_id=1, source_target_pairs={{0,0},{16,18},{8,12},{24,30},{1,1},{17,19},{9,13},{25,31},{26,16},... | collective-permute-start | bytes 1572872 | tf_op jit(solution)/shard_map/ppermute | solution.py:306
  49.5 10.7 %collective-permute-start.7 = (bf16[128,2048]{1,0:T(8,128)(2,1)}, bf16[128,2048]{1,0:T(8,128)(2,1)}, u32[]{:S(2)}, u32[]{:S(2)}) collective-permute-start(bf16[128,2048]{1,0:T(8,128)(2,1)} %collective-permute-done.5.refs_1_), channel_id=1, source_target_pairs={{0,16},{8,24},{16,0},{24,8},{1,17},{9,25},{17,1},{25,9},{2,18},{10... | collective-permute-start | bytes 1572872 | tf_op jit(solution)/shard_map/ppermute | solution.py:233
  60.2 1.8 collective-permute-start.8
  62.0 5.6 %collective-permute-start.9 = (bf16[128,2048]{1,0:T(8,128)(2,1)}, bf16[128,2048]{1,0:T(8,128)(2,1)}, u32[]{:S(2)}, u32[]{:S(2)}) collective-permute-start(bf16[128,2048]{1,0:T(8,128)(2,1)} %collective-permute-done.5.refs_1_), channel_id=1, source_target_pairs={{0,8},{8,0},{16,24},{24,16},{1,9},{9,1},{17,25},{25,17},{2,10},{10... | collective-permute-start | bytes 1572872 | tf_op jit(solution)/shard_map/ppermute | solution.py:233
  67.9 5.5 %collective-permute-done.7.refs_3_.refs_4_ = bf16[128,2048]{1,0:T(8,128)(2,1)} collective-permute-done((bf16[128,2048]{1,0:T(8,128)(2,1)}, bf16[128,2048]{1,0:T(8,128)(2,1)}, u32[]{:S(2)}, u32[]{:S(2)}) %collective-permute-start.7) | collective-permute-done | bytes 524320 | tf_op jit(solution)/shard_map/ppermute | solution.py:233
  73.4 2.6 %collective-permute-start.11 = (bf16[128,2048]{1,0:T(8,128)(2,1)}, bf16[128,2048]{1,0:T(8,128)(2,1)}, u32[]{:S(2)}, u32[]{:S(2)}) collective-permute-start(bf16[128,2048]{1,0:T(8,128)(2,1)} %collective-permute-done.7.refs_3_.refs_4_), channel_id=1, source_target_pairs={{0,8},{8,0},{16,24},{24,16},{1,9},{9,1},{17,25},{25,17},{2,10},{10... | collective-permute-start | bytes 1572872 | tf_op jit(solution)/shard_map/ppermute | solution.py:233
  77.9 4.1 %project.4 = (bf16[512,256]{1,0:T(8,128)(2,1)S(1)}, f32[512,256]{1,0:T(8,128)S(1)}) custom-call(s32[2]{0:T(128)S(1)} %pad_add_fusion.place_ref, bf16[128,2048]{1,0:T(8,128)(2,1)} %collective-permute-done.3.refs_0_, bf16[128,2048]{1,0:T(8,128)(2,1)} %collective-permute-done.5.refs_1_, bf16[128,2048]{1,0:T(8,128)(2,1)} %collective-permute-done.6.refs_2_.refs_3_, ...), custom_call_target="tpu_custom_call" | custom-call | flops 1073741824 | bytes 4194304 | tf_op jit(solution)/shard_map/project/pallas_call | solution.py:325
  83.2 8.1 %collective-permute-done.20.refs_1_.refs_5_ = bf16[128,2048]{1,0:T(8,128)(2,1)} collective-permute-done((bf16[128,2048]{1,0:T(8,128)(2,1)}, bf16[128,2048]{1,0:T(8,128)(2,1)}, u32[]{:S(2)}, u32[]{:S(2)}) %collective-permute-start.20) | collective-permute-done | bytes 524320 | tf_op jit(solution)/shard_map/ppermute | solution.py:233
  91.3 6.4 %project.5 = (bf16[512,640]{1,0:T(8,128)(2,1)S(1)}, f32[512,640]{1,0:T(8,128)S(1)}) custom-call(s32[2]{0:T(128)S(1)} %pad_add_fusion.place_ref, bf16[128,2048]{1,0:T(8,128)(2,1)} %collective-permute-done.3.refs_0_, bf16[128,2048]{1,0:T(8,128)(2,1)} %collective-permute-done.5.refs_1_, bf16[128,2048]{1,0:T(8,128)(2,1)} %collective-permute-done.6.refs_2_.refs_3_, ...), custom_call_target="tpu_custom_call" | custom-call | flops 2684354560 | bytes 4194304 | tf_op jit(solution)/shard_map/project/pallas_call | solution.py:325
  99.2 16.3 %collective-permute-done.14.refs_2_ = bf16[1,256,256]{2,1,0:T(8,128)(2,1)S(1)} collective-permute-done((bf16[1,256,256]{2,1,0:T(8,128)(2,1)S(1)}, bf16[1,256,256]{2,1,0:T(8,128)(2,1)S(1)}, u32[]{:S(2)}, u32[]{:S(2)}) %collective-permute-start.14) | collective-permute-done | bytes 131104 | tf_op jit(solution)/shard_map/ppermute | solution.py:233
  116.3 4.5 %project.6 = (bf16[256,896]{1,0:T(8,128)(2,1)S(1)}, f32[256,896]{1,0:T(8,128)S(1)}) custom-call(s32[2]{0:T(128)S(1)} %pad_add_fusion.place_ref, bf16[128,2048]{1,0:T(8,128)(2,1)} %collective-permute-done.19.refs_0_.refs_2_, bf16[128,2048]{1,0:T(8,128)(2,1)} %collective-permute-done.20.refs_1_.refs_5_, ...), custom_call_target="tpu_custom_call" | custom-call | flops 1879048192 | bytes 2097152 | tf_op jit(solution)/shard_map/project/pallas_call | solution.py:325
  121.2 3.4 %collective-permute-start.16 = (bf16[2,256,256]{2,1,0:T(8,128)(2,1)S(1)}, bf16[2,256,256]{2,1,0:T(8,128)(2,1)S(1)}, u32[]{:S(2)}, u32[]{:S(2)}) collective-permute-start(bf16[2,256,256]{2,1,0:T(8,128)(2,1)S(1)} %pad_maximum_fusion.2), channel_id=1, source_target_pairs={{0,4},{1,5},{2,6},{3,7},{4,0},{5,1},{6,2},{7,3},{8,12},{9,13},{10,... | collective-permute-start | bytes 786440 | tf_op jit(solution)/shard_map/ppermute | solution.py:233
  124.8 2.8 %collective-permute-start.23 = (bf16[2,128,896]{2,1,0:T(8,128)(2,1)S(1)}, bf16[2,128,896]{2,1,0:T(8,128)(2,1)S(1)}, u32[]{:S(2)}, u32[]{:S(2)}) collective-permute-start(bf16[2,128,896]{2,1,0:T(8,128)(2,1)S(1)} %bitcast.42), channel_id=1, source_target_pairs={{0,2},{1,3},{2,0},{3,1},{4,6},{5,7},{6,4},{7,5},{8,10},{9,11},{10,... | collective-permute-start | bytes 1376264 | tf_op jit(solution)/shard_map/ppermute | solution.py:233
  127.6 6.7 %project.7 = (bf16[768,384]{1,0:T(8,128)(2,1)S(1)}, f32[768,384]{1,0:T(8,128)S(1)}) custom-call(s32[2]{0:T(128)S(1)} %pad_add_fusion.place_ref, bf16[128,2048]{1,0:T(8,128)(2,1)} %collective-permute-done.3.refs_0_, bf16[128,2048]{1,0:T(8,128)(2,1)} %collective-permute-done.5.refs_1_, bf16[128,2048]{1,0:T(8,128)(2,1)} %collective-permute-done.19.refs_0_.refs_2_, ...), custom_call_target="tpu_custom_call" | custom-call | flops 2415919104 | bytes 6291456 | tf_op jit(solution)/shard_map/project/pallas_call | solution.py:325
  134.3 15.8 %collective-permute-done.27.refs_4_ = bf16[1,256,640]{2,1,0:T(8,128)(2,1)S(1)} collective-permute-done((bf16[1,256,640]{2,1,0:T(8,128)(2,1)S(1)}, bf16[1,256,640]{2,1,0:T(8,128)(2,1)S(1)}, u32[]{:S(2)}, u32[]{:S(2)}) %collective-permute-start.27) | collective-permute-done | bytes 327712 | tf_op jit(solution)/shard_map/ppermute | solution.py:233
  150.2 2.1 %collective-permute-start.17 = (bf16[4,256,256]{2,1,0:T(8,128)(2,1)S(1)}, bf16[4,256,256]{2,1,0:T(8,128)(2,1)S(1)}, u32[]{:S(2)}, u32[]{:S(2)}) collective-permute-start(bf16[4,256,256]{2,1,0:T(8,128)(2,1)S(1)} %pad_maximum_fusion.1), channel_id=1, source_target_pairs={{0,2},{1,3},{2,0},{3,1},{4,6},{5,7},{6,4},{7,5},{8,10},{9,11},{10,... | collective-permute-start | bytes 1572872 | tf_op jit(solution)/shard_map/ppermute | solution.py:233
  153.2 21.2 %collective-permute-done.28.refs_3_ = bf16[2,384,384]{2,1,0:T(8,128)(2,1)S(1)} collective-permute-done((bf16[2,384,384]{2,1,0:T(8,128)(2,1)S(1)}, bf16[2,384,384]{2,1,0:T(8,128)(2,1)S(1)}, u32[]{:S(2)}, u32[]{:S(2)}) %collective-permute-start.28) | collective-permute-done | bytes 589856 | tf_op jit(solution)/shard_map/ppermute | solution.py:233
  174.7 8.8 %collective-permute-done.17 = bf16[4,256,256]{2,1,0:T(8,128)(2,1)S(1)} collective-permute-done((bf16[4,256,256]{2,1,0:T(8,128)(2,1)S(1)}, bf16[4,256,256]{2,1,0:T(8,128)(2,1)S(1)}, u32[]{:S(2)}, u32[]{:S(2)}) %collective-permute-start.17) | collective-permute-done | bytes 524320 | tf_op jit(solution)/shard_map/ppermute | solution.py:233
  184.2 5.1 %attend.2.refs_5_ = bf16[384,1024]{1,0:T(8,128)(2,1)} custom-call(s32[1]{0:T(128)} %bitcast.device_ref, s32[24]{0:T(128)S(1)} %copy-done.2, s32[24]{0:T(128)S(1)} %copy-done.3, f32[384,128]{1,0:T(8,128)S(1)} %broadcast_in_dim.29.inverse_ref, f32[1,640]{1,0:T(1,128)S(1)} %broadcast_in_dim.35.bias_ref, f32[384,128]{1,0:T(8,128)S(1)} %copy-done, ...), custom_call_target="tpu_custom_call" | custom-call | flops 1887436800 | bytes 491520 | tf_op jit(solution)/shard_map/attend/pallas_call | solution.py:444
  190.2 3.8 %attend.3 = bf16[384,1024]{1,0:T(8,128)(2,1)} custom-call(s32[1]{0:T(128)} %bitcast.device_ref, s32[24]{0:T(128)S(1)} %copy-done.2, s32[24]{0:T(128)S(1)} %copy-done.3, f32[384,128]{1,0:T(8,128)S(1)} %broadcast_in_dim.29.inverse_ref, f32[1,384]{1,0:T(1,128)S(1)} %broadcast_in_dim.30.bias_ref, ...), custom_call_target="tpu_custom_call", output_to_operand_aliasing={{}: (13, {})} | custom-call | flops 679477248 | bytes 294912 | tf_op jit(solution)/shard_map/attend/pallas_call | solution.py:444
  (97 shorter events, 15.7 us)
Async XLA Ops:
  2.6 19.9 %copy-start.7 = (bf16[1024,1024]{1,0:T(8,128)(2,1)S(1)}, bf16[1024,1024]{1,0:T(8,128)(2,1)}, u32[]{:S(2)}) copy-start(bf16[1024,1024]{1,0:T(8,128)(2,1)} %param.14) | copy-start | bytes 6291460
  3.6 26.3 %collective-permute-start = (bf16[256,2048]{1,0:T(8,128)(2,1)}, bf16[256,2048]{1,0:T(8,128)(2,1)}, u32[]{:S(2)}, u32[]{:S(2)}) collective-permute-start(bf16[256,2048]{1,0:T(8,128)(2,1)} %slice.90), channel_id=1, source_target_pairs={{0,0},{8,16},{16,8},{24,24},{1,1},{9,17},{17,9},{25,25},{2,26},{10... | collective-permute-start | bytes 3145736 | tf_op jit(solution)/shard_map/ppermute | solution.py:275
  13.2 14.2 %collective-permute-start.4 = (bf16[1024,256]{1,0:T(8,128)(2,1)S(1)}, bf16[1024,256]{1,0:T(8,128)(2,1)S(1)}, u32[]{:S(2)}, u32[]{:S(2)}) collective-permute-start(bf16[1024,256]{1,0:T(8,128)(2,1)S(1)} %constant_dynamic-update-slice_fusion.refs_8_.refs_4_), channel_id=1, source_target_pairs={{0,1},{1,0},{2,3},{3,2},{4,5},{5,4},{6,7},{7,6},{8,9},{9,8},{10,11... | collective-permute-start | bytes 1572872 | tf_op jit(solution)/shard_map/ppermute | solution.py:233
  17.1 25.7 %collective-permute-start.18 = (bf16[128,2048]{1,0:T(8,128)(2,1)}, bf16[128,2048]{1,0:T(8,128)(2,1)}, u32[]{:S(2)}, u32[]{:S(2)}) collective-permute-start(bf16[128,2048]{1,0:T(8,128)(2,1)} %slice.95), channel_id=1, source_target_pairs={{0,0},{8,16},{16,8},{24,24},{1,1},{9,17},{17,9},{25,25},{2,26},{10... | collective-permute-start | bytes 1572872 | tf_op jit(solution)/shard_map/ppermute | solution.py:275
  27.4 48.6 %collective-permute-start.13 = (bf16[1024,640]{1,0:T(8,128)(2,1)S(1)}, bf16[1024,640]{1,0:T(8,128)(2,1)S(1)}, u32[]{:S(2)}, u32[]{:S(2)}) collective-permute-start(bf16[1024,640]{1,0:T(8,128)(2,1)S(1)} %slice.77.refs_8_.refs_6_), channel_id=1, source_target_pairs={{0,1},{1,0},{2,3},{3,2},{4,5},{5,4},{6,7},{7,6},{8,9},{9,8},{10,11... | collective-permute-start | bytes 3932168 | tf_op jit(solution)/shard_map/ppermute | solution.py:233
  31.2 16.9 %collective-permute-start.3 = (bf16[128,2048]{1,0:T(8,128)(2,1)S(1)}, bf16[128,2048]{1,0:T(8,128)(2,1)}, u32[]{:S(2)}, u32[]{:S(2)}) collective-permute-start(bf16[128,2048]{1,0:T(8,128)(2,1)S(1)} %get-tuple-element.34), channel_id=1, source_target_pairs={{0,0},{16,18},{8,12},{24,30},{1,1},{17,19},{9,13},{25,31},{26,16},... | collective-permute-start | bytes 1572872 | tf_op jit(solution)/shard_map/ppermute | solution.py:306
  32.7 16.9 %collective-permute-start.5 = (bf16[128,2048]{1,0:T(8,128)(2,1)S(1)}, bf16[128,2048]{1,0:T(8,128)(2,1)}, u32[]{:S(2)}, u32[]{:S(2)}) collective-permute-start(bf16[128,2048]{1,0:T(8,128)(2,1)S(1)} %get-tuple-element.35), channel_id=1, source_target_pairs={{0,0},{16,18},{8,12},{24,30},{1,1},{17,19},{9,13},{25,31},{26,16},... | collective-permute-start | bytes 1572872 | tf_op jit(solution)/shard_map/ppermute | solution.py:306
  34.5 4.6 %collective-permute-start.1 = (f32[3,128]{1,0:T(4,128)S(1)}, f32[3,128]{1,0:T(4,128)S(1)}, u32[]{:S(2)}, u32[]{:S(2)}) collective-permute-start(f32[3,128]{1,0:T(4,128)S(1)} %multiply_reduce_fusion), channel_id=1, source_target_pairs={{0,8},{8,0},{16,24},{24,16},{1,9},{9,1},{17,25},{25,17},{2,10},{10... | collective-permute-start | bytes 4616 | tf_op jit(solution)/shard_map/ppermute | solution.py:233
  39.2 3.6 %collective-permute-start.2 = (f32[3,128]{1,0:T(4,128)S(1)}, f32[3,128]{1,0:T(4,128)S(1)}, u32[]{:S(2)}, u32[]{:S(2)}) collective-permute-start(f32[3,128]{1,0:T(4,128)S(1)} %add.32), channel_id=1, source_target_pairs={{0,16},{8,24},{16,0},{24,8},{1,17},{9,25},{17,1},{25,9},{2,18},{10... | collective-permute-start | bytes 4616 | tf_op jit(solution)/shard_map/ppermute | solution.py:233
  42.7 19.3 %collective-permute-start.19 = (bf16[128,2048]{1,0:T(8,128)(2,1)}, bf16[128,2048]{1,0:T(8,128)(2,1)}, u32[]{:S(2)}, u32[]{:S(2)}) collective-permute-start(bf16[128,2048]{1,0:T(8,128)(2,1)} %collective-permute-done.18), channel_id=1, source_target_pairs={{0,0},{16,18},{8,12},{24,30},{1,1},{17,19},{9,13},{25,31},{26,16},... | collective-permute-start | bytes 1572872 | tf_op jit(solution)/shard_map/ppermute | solution.py:306
  48.1 19.5 %collective-permute-start.6 = (bf16[128,2048]{1,0:T(8,128)(2,1)}, bf16[128,2048]{1,0:T(8,128)(2,1)}, u32[]{:S(2)}, u32[]{:S(2)}) collective-permute-start(bf16[128,2048]{1,0:T(8,128)(2,1)} %collective-permute-done.3.refs_0_), channel_id=1, source_target_pairs={{0,16},{8,24},{16,0},{24,8},{1,17},{9,25},{17,1},{25,9},{2,18},{10... | collective-permute-start | bytes 1572872 | tf_op jit(solution)/shard_map/ppermute | solution.py:233
  49.5 23.8 %collective-permute-start.7 = (bf16[128,2048]{1,0:T(8,128)(2,1)}, bf16[128,2048]{1,0:T(8,128)(2,1)}, u32[]{:S(2)}, u32[]{:S(2)}) collective-permute-start(bf16[128,2048]{1,0:T(8,128)(2,1)} %collective-permute-done.5.refs_1_), channel_id=1, source_target_pairs={{0,16},{8,24},{16,0},{24,8},{1,17},{9,25},{17,1},{25,9},{2,18},{10... | collective-permute-start | bytes 1572872 | tf_op jit(solution)/shard_map/ppermute | solution.py:233
  60.2 17.3 %collective-permute-start.8 = (bf16[128,2048]{1,0:T(8,128)(2,1)}, bf16[128,2048]{1,0:T(8,128)(2,1)}, u32[]{:S(2)}, u32[]{:S(2)}) collective-permute-start(bf16[128,2048]{1,0:T(8,128)(2,1)} %collective-permute-done.3.refs_0_), channel_id=1, source_target_pairs={{0,8},{8,0},{16,24},{24,16},{1,9},{9,1},{17,25},{25,17},{2,10},{10... | collective-permute-start | bytes 1572872 | tf_op jit(solution)/shard_map/ppermute | solution.py:233
  62.0 15.5 %collective-permute-start.9 = (bf16[128,2048]{1,0:T(8,128)(2,1)}, bf16[128,2048]{1,0:T(8,128)(2,1)}, u32[]{:S(2)}, u32[]{:S(2)}) collective-permute-start(bf16[128,2048]{1,0:T(8,128)(2,1)} %collective-permute-done.5.refs_1_), channel_id=1, source_target_pairs={{0,8},{8,0},{16,24},{24,16},{1,9},{9,1},{17,25},{25,17},{2,10},{10... | collective-permute-start | bytes 1572872 | tf_op jit(solution)/shard_map/ppermute | solution.py:233
  67.6 9.9 %collective-permute-start.10 = (bf16[128,2048]{1,0:T(8,128)(2,1)}, bf16[128,2048]{1,0:T(8,128)(2,1)}, u32[]{:S(2)}, u32[]{:S(2)}) collective-permute-start(bf16[128,2048]{1,0:T(8,128)(2,1)} %collective-permute-done.6.refs_2_.refs_3_), channel_id=1, source_target_pairs={{0,8},{8,0},{16,24},{24,16},{1,9},{9,1},{17,25},{25,17},{2,10},{10... | collective-permute-start | bytes 1572872 | tf_op jit(solution)/shard_map/ppermute | solution.py:233
  73.4 4.5 %collective-permute-start.11 = (bf16[128,2048]{1,0:T(8,128)(2,1)}, bf16[128,2048]{1,0:T(8,128)(2,1)}, u32[]{:S(2)}, u32[]{:S(2)}) collective-permute-start(bf16[128,2048]{1,0:T(8,128)(2,1)} %collective-permute-done.7.refs_3_.refs_4_), channel_id=1, source_target_pairs={{0,8},{8,0},{16,24},{24,16},{1,9},{9,1},{17,25},{25,17},{2,10},{10... | collective-permute-start | bytes 1572872 | tf_op jit(solution)/shard_map/ppermute | solution.py:233
  77.1 14.1 %collective-permute-start.20 = (bf16[128,2048]{1,0:T(8,128)(2,1)}, bf16[128,2048]{1,0:T(8,128)(2,1)}, u32[]{:S(2)}, u32[]{:S(2)}) collective-permute-start(bf16[128,2048]{1,0:T(8,128)(2,1)} %collective-permute-done.19.refs_0_.refs_2_), channel_id=1, source_target_pairs={{0,16},{8,24},{16,0},{24,8},{1,17},{9,25},{17,1},{25,9},{2,18},{10... | collective-permute-start | bytes 1572872 | tf_op jit(solution)/shard_map/ppermute | solution.py:233
  77.5 13.8 %copy-start.5 = (bf16[1024,640]{1,0:T(8,128)(2,1)S(1)}, bf16[1024,640]{1,0:T(8,128)(2,1)}, u32[]{:S(2)}) copy-start(bf16[1024,640]{1,0:T(8,128)(2,1)} %copy-done.4) | copy-start | bytes 3932164
  82.0 15.7 %collective-permute-start.12 = (bf16[2,256,256]{2,1,0:T(8,128)(2,1)S(1)}, bf16[2,256,256]{2,1,0:T(8,128)(2,1)S(1)}, u32[]{:S(2)}, u32[]{:S(2)}) collective-permute-start(bf16[2,256,256]{2,1,0:T(8,128)(2,1)S(1)} %bitcast.43), channel_id=1, source_target_pairs={{0,2},{1,3},{2,0},{3,1},{4,6},{5,7},{6,4},{7,5},{8,10},{9,11},{10,... | collective-permute-start | bytes 786440 | tf_op jit(solution)/shard_map/ppermute | solution.py:233
  82.2 34.1 %collective-permute-start.21 = (bf16[128,2048]{1,0:T(8,128)(2,1)}, bf16[128,2048]{1,0:T(8,128)(2,1)S(1)}, u32[]{:S(2)}, u32[]{:S(2)}) collective-permute-start(bf16[128,2048]{1,0:T(8,128)(2,1)} %collective-permute-done.19.refs_0_.refs_2_), channel_id=1, source_target_pairs={{0,8},{8,0},{16,24},{24,16},{1,9},{9,1},{17,25},{25,17},{2,10},{10... | collective-permute-start | bytes 1572872 | tf_op jit(solution)/shard_map/ppermute | solution.py:233
  82.7 44.9 %collective-permute-start.25 = (bf16[1024,384]{1,0:T(8,128)(2,1)S(1)}, bf16[1024,384]{1,0:T(8,128)(2,1)S(1)}, u32[]{:S(2)}, u32[]{:S(2)}) collective-permute-start(bf16[1024,384]{1,0:T(8,128)(2,1)S(1)} %slice.78.refs_12_), channel_id=1, source_target_pairs={{0,1},{1,0},{2,3},{3,2},{4,5},{5,4},{6,7},{7,6},{8,9},{9,8},{10,11... | collective-permute-start | bytes 2359304 | tf_op jit(solution)/shard_map/ppermute | solution.py:233
  91.3 25.1 %collective-permute-start.22 = (bf16[128,2048]{1,0:T(8,128)(2,1)}, bf16[128,2048]{1,0:T(8,128)(2,1)S(1)}, u32[]{:S(2)}, u32[]{:S(2)}) collective-permute-start(bf16[128,2048]{1,0:T(8,128)(2,1)} %collective-permute-done.20.refs_1_.refs_5_), channel_id=1, source_target_pairs={{0,8},{8,0},{16,24},{24,16},{1,9},{9,1},{17,25},{25,17},{2,10},{10... | collective-permute-start | bytes 1572872 | tf_op jit(solution)/shard_map/ppermute | solution.py:233
  97.7 26.9 %collective-permute-start.26 = (bf16[2,256,640]{2,1,0:T(8,128)(2,1)S(1)}, bf16[2,256,640]{2,1,0:T(8,128)(2,1)S(1)}, u32[]{:S(2)}, u32[]{:S(2)}) collective-permute-start(bf16[2,256,640]{2,1,0:T(8,128)(2,1)S(1)} %bitcast.40), channel_id=1, source_target_pairs={{0,2},{1,3},{2,0},{3,1},{4,6},{5,7},{6,4},{7,5},{8,10},{9,11},{10,... | collective-permute-start | bytes 1966088 | tf_op jit(solution)/shard_map/ppermute | solution.py:233
  97.8 17.7 %collective-permute-start.14 = (bf16[1,256,256]{2,1,0:T(8,128)(2,1)S(1)}, bf16[1,256,256]{2,1,0:T(8,128)(2,1)S(1)}, u32[]{:S(2)}, u32[]{:S(2)}) collective-permute-start(bf16[1,256,256]{2,1,0:T(8,128)(2,1)S(1)} %fusion.4), channel_id=1, source_target_pairs={{0,4},{1,5},{2,6},{3,7},{4,0},{5,1},{6,2},{7,3},{8,12},{9,13},{10,... | collective-permute-start | bytes 393224 | tf_op jit(solution)/shard_map/ppermute | solution.py:233
  115.7 5.4 %collective-permute-start.15 = (bf16[1,256,256]{2,1,0:T(8,128)(2,1)S(1)}, bf16[1,256,256]{2,1,0:T(8,128)(2,1)S(1)}, u32[]{:S(2)}, u32[]{:S(2)}) collective-permute-start(bf16[1,256,256]{2,1,0:T(8,128)(2,1)S(1)} %bitcast.25), channel_id=1, source_target_pairs={{0,1},{1,0},{2,3},{3,2},{4,5},{5,4},{6,7},{7,6},{8,9},{9,8},{10,11... | collective-permute-start | bytes 393224 | tf_op jit(solution)/shard_map/ppermute | solution.py:233
  121.2 28.9 %collective-permute-start.16 = (bf16[2,256,256]{2,1,0:T(8,128)(2,1)S(1)}, bf16[2,256,256]{2,1,0:T(8,128)(2,1)S(1)}, u32[]{:S(2)}, u32[]{:S(2)}) collective-permute-start(bf16[2,256,256]{2,1,0:T(8,128)(2,1)S(1)} %pad_maximum_fusion.2), channel_id=1, source_target_pairs={{0,4},{1,5},{2,6},{3,7},{4,0},{5,1},{6,2},{7,3},{8,12},{9,13},{10,... | collective-permute-start | bytes 786440 | tf_op jit(solution)/shard_map/ppermute | solution.py:233
  124.7 25.4 %collective-permute-start.27 = (bf16[1,256,640]{2,1,0:T(8,128)(2,1)S(1)}, bf16[1,256,640]{2,1,0:T(8,128)(2,1)S(1)}, u32[]{:S(2)}, u32[]{:S(2)}) collective-permute-start(bf16[1,256,640]{2,1,0:T(8,128)(2,1)S(1)} %fusion.1), channel_id=1, source_target_pairs={{0,4},{1,5},{2,6},{3,7},{4,0},{5,1},{6,2},{7,3},{8,12},{9,13},{10,... | collective-permute-start | bytes 983048 | tf_op jit(solution)/shard_map/ppermute | solution.py:233
  124.8 27.5 %collective-permute-start.23 = (bf16[2,128,896]{2,1,0:T(8,128)(2,1)S(1)}, bf16[2,128,896]{2,1,0:T(8,128)(2,1)S(1)}, u32[]{:S(2)}, u32[]{:S(2)}) collective-permute-start(bf16[2,128,896]{2,1,0:T(8,128)(2,1)S(1)} %bitcast.42), channel_id=1, source_target_pairs={{0,2},{1,3},{2,0},{3,1},{4,6},{5,7},{6,4},{7,5},{8,10},{9,11},{10,... | collective-permute-start | bytes 1376264 | tf_op jit(solution)/shard_map/ppermute | solution.py:233
  150.1 24.3 %collective-permute-start.28 = (bf16[2,384,384]{2,1,0:T(8,128)(2,1)S(1)}, bf16[2,384,384]{2,1,0:T(8,128)(2,1)S(1)}, u32[]{:S(2)}, u32[]{:S(2)}) collective-permute-start(bf16[2,384,384]{2,1,0:T(8,128)(2,1)S(1)} %bitcast.41), channel_id=1, source_target_pairs={{0,2},{1,3},{2,0},{3,1},{4,6},{5,7},{6,4},{7,5},{8,10},{9,11},{10,... | collective-permute-start | bytes 1769480 | tf_op jit(solution)/shard_map/ppermute | solution.py:233
  150.2 33.3 %collective-permute-start.17 = (bf16[4,256,256]{2,1,0:T(8,128)(2,1)S(1)}, bf16[4,256,256]{2,1,0:T(8,128)(2,1)S(1)}, u32[]{:S(2)}, u32[]{:S(2)}) collective-permute-start(bf16[4,256,256]{2,1,0:T(8,128)(2,1)S(1)} %pad_maximum_fusion.1), channel_id=1, source_target_pairs={{0,2},{1,3},{2,0},{3,1},{4,6},{5,7},{6,4},{7,5},{8,10},{9,11},{10,... | collective-permute-start | bytes 1572872 | tf_op jit(solution)/shard_map/ppermute | solution.py:233
  152.3 31.3 %collective-permute-start.24 = (bf16[1,128,896]{2,1,0:T(8,128)(2,1)S(1)}, bf16[1,128,896]{2,1,0:T(8,128)(2,1)S(1)}, u32[]{:S(2)}, u32[]{:S(2)}) collective-permute-start(bf16[1,128,896]{2,1,0:T(8,128)(2,1)S(1)} %fusion.3), channel_id=1, source_target_pairs={{0,4},{1,5},{2,6},{3,7},{4,0},{5,1},{6,2},{7,3},{8,12},{9,13},{10,... | collective-permute-start | bytes 688136 | tf_op jit(solution)/shard_map/ppermute | solution.py:233
  174.5 15.7 %collective-permute-start.29 = (bf16[1,384,384]{2,1,0:T(8,128)(2,1)S(1)}, bf16[1,384,384]{2,1,0:T(8,128)(2,1)S(1)}, u32[]{:S(2)}, u32[]{:S(2)}) collective-permute-start(bf16[1,384,384]{2,1,0:T(8,128)(2,1)S(1)} %fusion.2), channel_id=1, source_target_pairs={{0,4},{1,5},{2,6},{3,7},{4,0},{5,1},{6,2},{7,3},{8,12},{9,13},{10,... | collective-permute-start | bytes 884744 | tf_op jit(solution)/shard_map/ppermute | solution.py:233
  (11 other events, 58.0 us)

commit v6 on v5

--- a/solution.py
+++ b/solution.py
@@ -62,22 +62,10 @@
     sin_ref[...] = jnp.where(front, -sin, sin)
 
 
-def project_kernel(lines, blocks, groups, place_ref, *refs):
-    pieces = refs[: lines * blocks]
-    send_ref, keep_ref, held, weight, sems = refs[-5:]
-    weights = refs[lines * blocks : -5]
+def assemble(lines, blocks, place_ref, pieces, held, sems):
     half = lines // 2
     block_len = pieces[0].shape[0]
-    rows = weights[0].shape[0]
     copies = []
-    start = 0
-    for w, ref in enumerate(weights):
-        member = lax.bitwise_xor(place_ref[1], jnp.int32(w % groups))
-        width = ref.shape[1]
-        there = weight.at[pl.ds(pl.multiple_of(member * rows, rows), rows), pl.ds(start, width)]
-        copies.append(pltpu.make_async_copy(ref, there, sems.at[w]))
-        if w % groups == groups - 1:
-            start += width
     for i in range(lines):
         target = lax.bitwise_xor(jnp.int32(i), place_ref[0])
         slot = jnp.where(target % 2 == 0, half, 0) + target // 2
@@ -85,16 +73,51 @@
             begin = pl.multiple_of((slot * blocks + block) * block_len, block_len)
             n = i * blocks + block
             there = held.at[pl.ds(begin, block_len)]
-            copies.append(pltpu.make_async_copy(pieces[n], there, sems.at[len(weights) + n]))
+            copies.append(pltpu.make_async_copy(pieces[n], there, sems.at[n]))
     for copy in copies:
         copy.start()
-    for copy in copies:
-        copy.wait()
-    middle = held.shape[0] // 2
-    send_ref[...] = jnp.dot(
-        held[:middle], weight[...], preferred_element_type=jnp.float32
-    ).astype(jnp.bfloat16)
-    keep_ref[...] = jnp.dot(held[middle:], weight[...], preferred_element_type=jnp.float32)
+    return copies
+
+
+def project_kernel(lines, groups, chunks, counts, fresh, place_ref, *refs):
+    fresh_count = lines * counts[-1] if fresh else 0
+    whole_count = len(counts) - (1 if fresh else 0)
+    wholes = list(refs[:whole_count])
+    pieces = refs[whole_count : whole_count + fresh_count]
+    refs = refs[whole_count + fresh_count :]
+    weights = refs[: groups * chunks]
+    outs = refs[groups * chunks :]
+    send_ref, keep_ref = outs[:2]
+    if fresh:
+        held, sems = outs[2:]
+        for copy in assemble(lines, counts[-1], place_ref, pieces, held, sems):
+            copy.wait()
+        wholes.append(held)
+    half = lines // 2
+    rows = weights[0].shape[0]
+    length = send_ref.shape[1]
+    begin = 0
+    for held, count in zip(wholes, counts):
+        share = held.shape[0] // lines
+        middle = half * share
+        start = 0
+        for chunk in range(chunks):
+            width = weights[chunk * groups].shape[1]
+            for out_ref, low in ((send_ref, 0), (keep_ref, middle)):
+                total = None
+                for g in range(groups):
+                    member = lax.bitwise_xor(place_ref[1], jnp.int32(g))
+                    lanes = pl.ds(pl.multiple_of(member * rows, rows), rows)
+                    term = jnp.dot(
+                        held[low : low + middle, lanes],
+                        weights[chunk * groups + g][...],
+                        preferred_element_type=jnp.float32,
+                    )
+                    total = term if total is None else total + term
+                total = total.astype(out_ref.dtype).reshape(half, share, width)
+                out_ref[:, begin : begin + share, start : start + width] = total
+            start += width
+        begin += share
 
 
 def kv_kernel(addends, inverse_ref, bias_ref, cos_ref, sin_ref, *refs):
@@ -270,17 +293,20 @@
         for low, high in zip(head_cuts, head_cuts[1:])
     ]
     squares = jnp.sum(jnp.square(raw.astype(f32)), -1).reshape(blocks, block_len)
-    scaled = (raw.astype(f32) * gain_part).astype(bf16)
-    cut = STEMS * block_len
-    sent = [lax.ppermute(piece, axes, first_hop) for piece in (scaled[:cut], scaled[cut:])]
-    squares = tie(squares, sent[0])
     bit = 1
     while bit < lines:
         squares = squares + swap(squares, "fsdp", bit)
         bit *= 2
     inverse = lax.rsqrt(squares / features + 1e-06).reshape(tokens)
     inverse = jnp.broadcast_to(inverse[:, None], (tokens, HD))
-    sent = [piece[i : i + block_len] for piece in sent for i in range(0, len(piece), block_len)]
+    sent = []
+    for block in range(blocks):
+        piece = (hidden[block].astype(f32) * gain_part).astype(bf16)
+        if block == 1:
+            piece = tie(piece, sent[-1], squares)
+        elif block:
+            piece = tie(piece, sent[-1])
+        sent.append(lax.ppermute(piece, axes, first_hop))
 
     head_cuts = [0, (5 * head_count + 7) // 8, head_count]
     w_chunks = [jnp.concatenate([w_key, w_value], 1)] + [
@@ -301,47 +327,67 @@
     )(device_id, parents)
     sent[0] = tie(sent[0], cos, sin, *w_chunks)
     sent[1] = tie(sent[1], w_rows[0][-1])
-    sent[2] = tie(sent[2], squares)
 
     sent = [lax.ppermute(piece, axes, second_hop) for piece in sent]
     held = [{0: piece} for piece in sent]
-    held[-1][0] = tie(held[-1][0], w_rows[1][-1])
     bit = half_lines
-    while bit:
+    while bit > 1:
         for piece in held:
             for j in list(piece):
                 piece[j | bit] = swap(piece[j], "fsdp", bit)
         bit //= 2
-    held = [[piece[j] for j in sorted(piece, key=spread)] for piece in held]
-
-    def project(which, chunks, *after):
-        count = len(which)
-        length = count * block_len
+
+    def last_bit(piece):
+        for j in list(piece):
+            piece[j | 1] = swap(piece[j], "fsdp", 1)
+        return [piece[j] for j in sorted(piece, key=spread)]
+
+    held = [last_bit(piece) for piece in held[:STEMS]] + held[STEMS:]
+
+    assembled = {}
+
+    def project(spans, chunks, *after):
         weights = [w for chunk in chunks for w in w_rows[chunk]]
         width = sum(w_chunks[chunk].shape[1] for chunk in chunks)
-        operands = [held[block][i] for i in range(lines) for block in which]
+        fresh = spans[-1] not in assembled
+        counts = [high - low for low, high in spans]
+        wholes = [assembled[span] for span in spans if span in assembled]
+        pieces = []
+        if fresh:
+            pieces = [held[block][i] for i in range(lines) for block in range(*spans[-1])]
+        operands = wholes + pieces
         operands[0] = tie(operands[0], *after) if after else operands[0]
-        flops = 2 * lines * length * feature_part * width
-        send, keep = pl.pallas_call(
-            functools.partial(project_kernel, lines, count, groups),
-            in_specs=[smem] + [anywhere] * (len(operands) + len(weights)),
-            out_specs=[vmem, vmem],
-            out_shape=[
-                jax.ShapeDtypeStruct((half_lines * length, width), bf16),
-                jax.ShapeDtypeStruct((half_lines * length, width), f32),
-            ],
-            scratch_shapes=[
-                pltpu.VMEM((lines * length, feature_part), bf16),
-                pltpu.VMEM((feature_part, width), bf16),
-                pltpu.SemaphoreType.DMA((len(operands) + len(weights),)),
-            ],
-            compiler_params=pltpu.CompilerParams(vmem_limit_bytes=32 * 2**20),
+        length = sum(counts) * block_len
+        out_specs = [vmem, vmem]
+        out_shape = [
+            jax.ShapeDtypeStruct((half_lines, length, width), bf16),
+            jax.ShapeDtypeStruct((half_lines, length, width), f32),
+        ]
+        scratch = []
+        if fresh:
+            out_specs.append(vmem)
+            out_shape.append(
+                jax.ShapeDtypeStruct((lines * counts[-1] * block_len, feature_part), bf16)
+            )
+            scratch.append(pltpu.SemaphoreType.DMA((len(pieces),)))
+        results = pl.pallas_call(
+            functools.partial(project_kernel, lines, groups, len(chunks), counts, fresh),
+            in_specs=[smem] + [vmem] * len(wholes) + [anywhere] * len(pieces)
+            + [vmem] * len(weights),
+            out_specs=out_specs,
+            out_shape=out_shape,
+            scratch_shapes=scratch,
+            compiler_params=pltpu.CompilerParams(vmem_limit_bytes=24 * 2**20),
             cost_estimate=pl.CostEstimate(
-                flops=flops, bytes_accessed=2 * lines * length * feature_part, transcendentals=0
+                flops=2 * lines * length * feature_part * width,
+                bytes_accessed=2 * lines * length * feature_part,
+                transcendentals=0,
             ),
             name="project",
         )(place, *operands, *weights)
-        return send.reshape(half_lines, length, width), keep.reshape(half_lines, length, width)
+        if fresh:
+            assembled[spans[-1]] = results[2]
+        return results[0], results[1]
 
     class Halving:
         def __init__(self, partial):
@@ -355,15 +401,17 @@
             self.addends.append(self.came)
             self.bit *= 2
 
-        def add(self):
+        def add(self, *after):
+            self.came = tie(self.came, *after) if after else self.came
+            self.addends[-1] = self.came
             total = self.total + self.came.astype(f32)
             self.send = total[1::2].astype(bf16)
             self.total = total[0::2]
 
         def rest(self, *after):
             while self.bit < lines:
-                self.add()
-                self.step(*after)
+                self.add(*after)
+                self.step()
 
     addend_count = 1 + bits_of(lines)
 
@@ -388,36 +436,37 @@
             name="finish_kv",
         )(*operands, *addends)
 
-    early = list(range(STEMS))
-    late = list(range(STEMS, blocks))
-    first = Halving(project(early, [0]))
+    early = (0, STEMS)
+    late = (STEMS, blocks)
+    first = Halving(project([early], [0], w_rows[1][-1]))
     first.step()
-    second = Halving(project(early, [1], first.send))
+    second = Halving(project([early], [1], first.send))
     second.step()
+    for block in range(*late):
+        held[block][0] = tie(held[block][0], second.send)
+        held[block] = last_bit(held[block])
     first.rest(second.send)
-    third = Halving(project(late, [0, 1], second.send, first.send))
+    third = Halving(project([late], [0, 1], first.send))
+    third.step()
+    first.addends[-1] = tie(first.addends[-1], third.send)
     stem_kv = finish_kv(first.addends, 0, STEMS)
 
     tour = [1 << i for i in range(bits_of(groups))]
     tour += [groups << i for i in reversed(range(bits_of(lines)))]
     stems = stem_kv[None]
-
-    def tour_step(stems, bit, *after):
-        came = swap(tie(stems, *after) if after else stems, "branch", bit)
-        return jnp.concatenate([stems, came], 0)
-
-    for bit in tour[: bits_of(groups)]:
-        stems = tour_step(stems, bit)
-    third.step(stem_kv)
-    far_tour = tour[bits_of(groups) :]
-    stems = tour_step(stems, far_tour[0])
-    fourth = Halving(project(early + late, [2], third.send))
-    second.rest(stems if len(far_tour) == 0 else third.send)
-    fourth.step(second.came)
-    third.rest()
-    for bit in far_tour[1:]:
-        stems = tour_step(stems, bit)
-    fourth.rest(third.send)
+    came = swap(stems, "branch", tour[0])
+    second.rest(stem_kv, w_rows[2][-1])
+    last = second
+    for step, bit in enumerate(tour[1:]):
+        stems = jnp.concatenate([stems, tie(came, last.send)], 0)
+        came = swap(stems, "branch", bit)
+        if step == 0:
+            fourth = Halving(project([early, late], [2], stems))
+            fourth.step()
+            third.rest(fourth.send)
+            last = third
+    fourth.rest(stems, second.came)
+    stems = jnp.concatenate([stems, came], 0)
     third.addends[-1] = tie(third.addends[-1], fourth.send)
     late_kv = finish_kv(third.addends, STEMS, blocks - STEMS)
     second_sums, third_sums, fourth_sums = second.addends, third.addends, fourth.addends

time: 196 us -> 168 us (0.86)
  waiting for transfers between devices: 82.6 us -> 63.6 us
  local copies, waits for them, and re-layouts: 6.06 us -> 1.42 us
  Pallas kernels: 33.1 us -> 29.2 us
    ppermute x25, waiting for transfers between devices: 82.6 us -> 63.5 us  [swap(): return lax.ppermute(array, axis, [(i, i ^ bit) for i in range(size)])]
    ppermute x2 -> x3, starting transfers between devices: 14.8 us -> 7.86 us  [shards(): sent.append(lax.ppermute(piece, axes, first_hop))]
    pallas_call x4, Pallas kernels: 21.7 us -> 17.8 us  [project(): pl.pallas_call(functools.partial(project_kernel, lines, groups, len(chunk...]
    ppermute x3, starting transfers between devices: 8.27 us -> 12.1 us  [shards(): sent = [lax.ppermute(piece, axes, second_hop) for piece in sent]]
    slice x3 -> x0, local copies, waits for them, and re-layouts: 3.2 us -> none  [the longest x1 1.3 us: shards(): piece[i:i + block_len]]
    ppermute x25, starting transfers between devices: 46.1 us -> 48.8 us  [swap(): return lax.ppermute(array, axis, [(i, i ^ bit) for i in range(size)])]
  transfers between devices with their start and end apart: 30 -> 31, of which waited for: 12 -> 13; matrix products, arithmetic and copies ran while one was open for 2% -> 1% of each run, Pallas kernels for 15% -> 15%
where the time goes in v6:
time: 168 us; the launch traced here: 167 us
  starting transfers between devices  68.8 us (41%)
  waiting for transfers between devices  63.6 us (38%)
  Pallas kernels  29.2 us (17%)
  other arithmetic  3.77 us (2%)
    ppermute x25, waiting for transfers between devices, swap(): return lax.ppermute(array, axis, [(i, i ^ bit) for i in range(size)])  63.5 us
    ppermute x25, starting transfers between devices, swap(): return lax.ppermute(array, axis, [(i, i ^ bit) for i in range(size)])  48.8 us
    pallas_call x4, Pallas kernels, project(): pl.pallas_call(functools.partial(project_kernel, lines, groups, len(chunk...  17.8 us
    ppermute x3, starting transfers between devices, shards(): sent = [lax.ppermute(piece, axes, second_hop) for piece in sent]  12.1 us
    pallas_call x2, Pallas kernels, attend(): pl.pallas_call(kernel, grid=(1,), in_specs=in_specs, out_specs=anywhere,...  8.95 us
    ppermute x3, starting transfers between devices, shards(): sent.append(lax.ppermute(piece, axes, first_hop))  7.86 us
  transfers between devices with their start and end apart: 31, of which 13 were waited for; matrix products, arithmetic and copies ran while one was open for 1% of the time, Pallas kernels for 15%

profile of v6, /device:TPU:0, one launch (start us, length us, event | category | flops | bytes accessed | tf_op | source)
XLA Modules:
  0.0 167.2 jit_solution(13061367022090062755)
XLA Ops:
  0.7 2.9 %fusion = (bf16[128,2048]{1,0:T(8,128)(2,1)}, bf16[128,2048]{1,0:T(8,128)(2,1)S(1)}, bf16[128,2048]{1,0:T(8,128)(2,1)}) fusion(bf16[3,128,2048]{2,1,0:T(8,128)(2,1)} %param.10, f32[2048]{0:T(1024)S(1)} %dynamic_slice.3), kind=kLoop, calls=%fused_computation.3 | loop fusion | flops 2359296 | bytes 3153920 | tf_op jit(solution)/shard_map/convert_element_type | solution.py:304
  4.6 3.0 %collective-permute-start.4 = (bf16[1024,256]{1,0:T(8,128)(2,1)S(1)}, bf16[1024,256]{1,0:T(8,128)(2,1)S(1)}, u32[]{:S(2)}, u32[]{:S(2)}) collective-permute-start(bf16[1024,256]{1,0:T(8,128)(2,1)S(1)} %constant_dynamic-update-slice_fusion.refs_8_.refs_4_), channel_id=1, source_target_pairs={{0,1},{1,0},{2,3},{3,2},{4,5},{5,4},{6,7},{7,6},{8,9},{9,8},{10,11... | collective-permute-start | bytes 1572872 | tf_op jit(solution)/shard_map/ppermute | solution.py:256
  8.0 2.6 %collective-permute-start = (f32[3,128]{1,0:T(4,128)S(1)}, f32[3,128]{1,0:T(4,128)S(1)}, u32[]{:S(2)}, u32[]{:S(2)}) collective-permute-start(f32[3,128]{1,0:T(4,128)S(1)} %multiply_reduce_fusion), channel_id=1, source_target_pairs={{0,8},{8,0},{16,24},{24,16},{1,9},{9,1},{17,25},{25,17},{2,10},{10... | collective-permute-start | bytes 4616 | tf_op jit(solution)/shard_map/ppermute | solution.py:256
  11.9 3.8 %collective-permute-done.1 = f32[3,128]{1,0:T(4,128)S(1)} collective-permute-done((f32[3,128]{1,0:T(4,128)S(1)}, f32[3,128]{1,0:T(4,128)S(1)}, u32[]{:S(2)}, u32[]{:S(2)}) %collective-permute-start.1) | collective-permute-done | bytes 1568 | tf_op jit(solution)/shard_map/ppermute | solution.py:256
  15.8 5.4 %collective-permute-start.6 = (bf16[128,2048]{1,0:T(8,128)(2,1)}, bf16[128,2048]{1,0:T(8,128)(2,1)}, u32[]{:S(2)}, u32[]{:S(2)}) collective-permute-start(bf16[128,2048]{1,0:T(8,128)(2,1)} %get-tuple-element.41), channel_id=1, source_target_pairs={{0,0},{8,16},{16,8},{24,24},{1,1},{9,17},{17,9},{25,25},{2,26},{10... | collective-permute-start | bytes 1572872 | tf_op jit(solution)/shard_map/ppermute | solution.py:309
  23.0 2.2 %tables.1 = (f32[384,128]{1,0:T(8,128)}, f32[384,128]{1,0:T(8,128)}) custom-call(s32[1]{0:T(128)} %bitcast.device_ref, s32[24]{0:T(128)} %parents_ref.5), custom_call_target="tpu_custom_call" | custom-call | tf_op jit(solution)/shard_map/tables/pallas_call | solution.py:321
  25.2 5.3 %collective-permute-start.3 = (bf16[128,2048]{1,0:T(8,128)(2,1)}, bf16[128,2048]{1,0:T(8,128)(2,1)}, u32[]{:S(2)}, u32[]{:S(2)}) collective-permute-start(bf16[128,2048]{1,0:T(8,128)(2,1)} %copy-done.11), channel_id=1, source_target_pairs={{0,0},{16,18},{8,12},{24,30},{1,1},{17,19},{9,13},{25,31},{26,16},... | collective-permute-start | bytes 1572872 | tf_op jit(solution)/shard_map/ppermute | solution.py:331
  30.5 5.3 %collective-permute-start.7 = (bf16[128,2048]{1,0:T(8,128)(2,1)}, bf16[128,2048]{1,0:T(8,128)(2,1)}, u32[]{:S(2)}, u32[]{:S(2)}) collective-permute-start(bf16[128,2048]{1,0:T(8,128)(2,1)} %collective-permute-done.6), channel_id=1, source_target_pairs={{0,0},{16,18},{8,12},{24,30},{1,1},{17,19},{9,13},{25,31},{26,16},... | collective-permute-start | bytes 1572872 | tf_op jit(solution)/shard_map/ppermute | solution.py:331
  35.9 1.7 %collective-permute-start.16 = (bf16[128,2048]{1,0:T(8,128)(2,1)}, bf16[128,2048]{1,0:T(8,128)(2,1)S(1)}, u32[]{:S(2)}, u32[]{:S(2)}) collective-permute-start(bf16[128,2048]{1,0:T(8,128)(2,1)} %get-tuple-element.49), channel_id=1, source_target_pairs={{0,0},{8,16},{16,8},{24,24},{1,1},{9,17},{17,9},{25,25},{2,26},{10... | collective-permute-start | bytes 1572872 | tf_op jit(solution)/shard_map/ppermute | solution.py:309
  37.6 5.0 %collective-permute-start.8 = (bf16[128,2048]{1,0:T(8,128)(2,1)}, bf16[128,2048]{1,0:T(8,128)(2,1)}, u32[]{:S(2)}, u32[]{:S(2)}) collective-permute-start(bf16[128,2048]{1,0:T(8,128)(2,1)} %collective-permute-done.3.refs_0_), channel_id=1, source_target_pairs={{0,16},{8,24},{16,0},{24,8},{1,17},{9,25},{17,1},{25,9},{2,18},{10... | collective-permute-start | bytes 1572872 | tf_op jit(solution)/shard_map/ppermute | solution.py:256
  42.6 11.2 %collective-permute-start.9 = (bf16[128,2048]{1,0:T(8,128)(2,1)}, bf16[128,2048]{1,0:T(8,128)(2,1)}, u32[]{:S(2)}, u32[]{:S(2)}) collective-permute-start(bf16[128,2048]{1,0:T(8,128)(2,1)} %collective-permute-done.7.refs_1_), channel_id=1, source_target_pairs={{0,16},{8,24},{16,0},{24,8},{1,17},{9,25},{17,1},{25,9},{2,18},{10... | collective-permute-start | bytes 1572872 | tf_op jit(solution)/shard_map/ppermute | solution.py:256
  55.3 2.5 %collective-permute-start.10 = (bf16[128,2048]{1,0:T(8,128)(2,1)}, bf16[128,2048]{1,0:T(8,128)(2,1)}, u32[]{:S(2)}, u32[]{:S(2)}) collective-permute-start(bf16[128,2048]{1,0:T(8,128)(2,1)} %collective-permute-done.3.refs_0_), channel_id=1, source_target_pairs={{0,8},{8,0},{16,24},{24,16},{1,9},{9,1},{17,25},{25,17},{2,10},{10... | collective-permute-start | bytes 1572872 | tf_op jit(solution)/shard_map/ppermute | solution.py:256
  58.3 8.6 %collective-permute-done.9.refs_3_ = bf16[128,2048]{1,0:T(8,128)(2,1)} collective-permute-done((bf16[128,2048]{1,0:T(8,128)(2,1)}, bf16[128,2048]{1,0:T(8,128)(2,1)}, u32[]{:S(2)}, u32[]{:S(2)}) %collective-permute-start.9) | collective-permute-done | bytes 524320 | tf_op jit(solution)/shard_map/ppermute | solution.py:256
  67.8 2.0 %collective-permute-start.18 = (bf16[128,2048]{1,0:T(8,128)(2,1)}, bf16[128,2048]{1,0:T(8,128)(2,1)}, u32[]{:S(2)}, u32[]{:S(2)}) collective-permute-start(bf16[128,2048]{1,0:T(8,128)(2,1)} %collective-permute-done.17.refs_0_), channel_id=1, source_target_pairs={{0,16},{8,24},{16,0},{24,8},{1,17},{9,25},{17,1},{25,9},{2,18},{10... | collective-permute-start | bytes 1572872 | tf_op jit(solution)/shard_map/ppermute | solution.py:256
  70.3 4.0 %project.4 = (bf16[2,256,256]{2,1,0:T(8,128)(2,1)S(1)}, f32[2,256,256]{2,1,0:T(8,128)S(1)}, bf16[1024,2048]{1,0:T(8,128)(2,1)S(1)}) custom-call(s32[2]{0:T(128)S(1)} %pad_add_fusion.place_ref, bf16[128,2048]{1,0:T(8,128)(2,1)} %collective-permute-done.3.refs_0_, bf16[128,2048]{1,0:T(8,128)(2,1)} %collective-permute-done.7.refs_1_, ...), custom_call_target="tpu_custom_call" | custom-call | flops 1073741824 | bytes 4194304 | tf_op jit(solution)/shard_map/project/pallas_call | solution.py:373
  74.4 2.7 %collective-permute-start.14 = (bf16[2,256,256]{2,1,0:T(8,128)(2,1)S(1)}, bf16[2,256,256]{2,1,0:T(8,128)(2,1)S(1)}, u32[]{:S(2)}, u32[]{:S(2)}) collective-permute-start(bf16[2,256,256]{2,1,0:T(8,128)(2,1)S(1)} %get-tuple-element.44), channel_id=1, source_target_pairs={{0,2},{1,3},{2,0},{3,1},{4,6},{5,7},{6,4},{7,5},{8,10},{9,11},{10,... | collective-permute-start | bytes 786440 | tf_op jit(solution)/shard_map/ppermute | solution.py:256
  77.0 4.8 %project.5 = (bf16[2,256,640]{2,1,0:T(8,128)(2,1)S(1)}, f32[2,256,640]{2,1,0:T(8,128)S(1)}) custom-call(s32[2]{0:T(128)S(1)} %pad_add_fusion.place_ref, bf16[1024,2048]{1,0:T(8,128)(2,1)S(1)} %get-tuple-element.59.refs_0_, bf16[1024,640]{1,0:T(8,128)(2,1)S(1)} %slice.73.refs_1_.refs_6_, bf16[1024,640]{1,0:T(8,128)(2,1)} %collective-permute-done.5.refs_2_.refs_7_), custom_call_target="tpu_custom_call" | custom-call | flops 2684354560 | bytes 4194304 | tf_op jit(solution)/shard_map/project/pallas_call | solution.py:373
  83.9 2.1 %collective-permute-start.15 = (bf16[1,256,256]{2,1,0:T(8,128)(2,1)S(1)}, bf16[1,256,256]{2,1,0:T(8,128)(2,1)S(1)}, u32[]{:S(2)}, u32[]{:S(2)}) collective-permute-start(bf16[1,256,256]{2,1,0:T(8,128)(2,1)S(1)} %fusion.6), channel_id=1, source_target_pairs={{0,4},{1,5},{2,6},{3,7},{4,0},{5,1},{6,2},{7,3},{8,12},{9,13},{10,... | collective-permute-start | bytes 393224 | tf_op jit(solution)/shard_map/ppermute | solution.py:256
  86.0 5.0 %project.6 = (bf16[2,128,896]{2,1,0:T(8,128)(2,1)S(1)}, f32[2,128,896]{2,1,0:T(8,128)S(1)}, bf16[512,2048]{1,0:T(8,128)(2,1)S(1)}) custom-call(s32[2]{0:T(128)S(1)} %pad_add_fusion.place_ref, bf16[128,2048]{1,0:T(8,128)(2,1)} %collective-permute-done.17.refs_0_, bf16[128,2048]{1,0:T(8,128)(2,1)} %collective-permute-done.18.refs_1_, ...), custom_call_target="tpu_custom_call" | custom-call | flops 1879048192 | bytes 2097152 | tf_op jit(solution)/shard_map/project/pallas_call | solution.py:373
  91.9 8.0 %collective-permute-done.15.refs_2_ = bf16[1,256,256]{2,1,0:T(8,128)(2,1)S(1)} collective-permute-done((bf16[1,256,256]{2,1,0:T(8,128)(2,1)S(1)}, bf16[1,256,256]{2,1,0:T(8,128)(2,1)S(1)}, u32[]{:S(2)}, u32[]{:S(2)}) %collective-permute-start.15) | collective-permute-done | bytes 131104 | tf_op jit(solution)/shard_map/ppermute | solution.py:256
  102.5 3.2 %collective-permute-done.21 = bf16[1,256,256]{2,1,0:T(8,128)(2,1)S(1)} collective-permute-done((bf16[1,256,256]{2,1,0:T(8,128)(2,1)S(1)}, bf16[1,256,256]{2,1,0:T(8,128)(2,1)S(1)}, u32[]{:S(2)}, u32[]{:S(2)}) %collective-permute-start.21) | collective-permute-done | bytes 131104 | tf_op jit(solution)/shard_map/ppermute | solution.py:256
  105.7 3.4 %collective-permute-start.24 = (bf16[2,256,256]{2,1,0:T(8,128)(2,1)S(1)}, bf16[2,256,256]{2,1,0:T(8,128)(2,1)S(1)}, u32[]{:S(2)}, u32[]{:S(2)}) collective-permute-start(bf16[2,256,256]{2,1,0:T(8,128)(2,1)S(1)} %pad_maximum_fusion.2), channel_id=1, source_target_pairs={{0,4},{1,5},{2,6},{3,7},{4,0},{5,1},{6,2},{7,3},{8,12},{9,13},{10,... | collective-permute-start | bytes 786440 | tf_op jit(solution)/shard_map/ppermute | solution.py:256
  109.3 4.0 %project.7 = (bf16[2,384,384]{2,1,0:T(8,128)(2,1)S(1)}, f32[2,384,384]{2,1,0:T(8,128)S(1)}) custom-call(s32[2]{0:T(128)S(1)} %pad_add_fusion.place_ref, bf16[1024,2048]{1,0:T(8,128)(2,1)S(1)} %get-tuple-element.59.refs_0_, bf16[512,2048]{1,0:T(8,128)(2,1)S(1)} %get-tuple-element.60.refs_1_, bf16[1024,384]{1,0:T(8,128)(2,1)S(1)} %slice.74.refs_2_, ...), custom_call_target="tpu_custom_call" | custom-call | flops 2415919104 | bytes 6291456 | tf_op jit(solution)/shard_map/project/pallas_call | solution.py:373
  113.2 2.8 %collective-permute-start.28 = (bf16[2,384,384]{2,1,0:T(8,128)(2,1)S(1)}, bf16[2,384,384]{2,1,0:T(8,128)(2,1)S(1)}, u32[]{:S(2)}, u32[]{:S(2)}) collective-permute-start(bf16[2,384,384]{2,1,0:T(8,128)(2,1)S(1)} %get-tuple-element.61), channel_id=1, source_target_pairs={{0,2},{1,3},{2,0},{3,1},{4,6},{5,7},{6,4},{7,5},{8,10},{9,11},{10,... | collective-permute-start | bytes 1769480 | tf_op jit(solution)/shard_map/ppermute | solution.py:256
  116.2 13.0 %collective-permute-done.24 = bf16[2,256,256]{2,1,0:T(8,128)(2,1)S(1)} collective-permute-done((bf16[2,256,256]{2,1,0:T(8,128)(2,1)S(1)}, bf16[2,256,256]{2,1,0:T(8,128)(2,1)S(1)}, u32[]{:S(2)}, u32[]{:S(2)}) %collective-permute-start.24) | collective-permute-done | bytes 262176 | tf_op jit(solution)/shard_map/ppermute | solution.py:256
  129.3 2.9 %collective-permute-start.27 = (bf16[1,128,896]{2,1,0:T(8,128)(2,1)S(1)}, bf16[1,128,896]{2,1,0:T(8,128)(2,1)S(1)}, u32[]{:S(2)}, u32[]{:S(2)}) collective-permute-start(bf16[1,128,896]{2,1,0:T(8,128)(2,1)S(1)} %fusion.5), channel_id=1, source_target_pairs={{0,4},{1,5},{2,6},{3,7},{4,0},{5,1},{6,2},{7,3},{8,12},{9,13},{10,... | collective-permute-start | bytes 688136 | tf_op jit(solution)/shard_map/ppermute | solution.py:256
  132.2 4.0 %collective-permute-done.29.refs_4_ = bf16[1,256,640]{2,1,0:T(8,128)(2,1)S(1)} collective-permute-done((bf16[1,256,640]{2,1,0:T(8,128)(2,1)S(1)}, bf16[1,256,640]{2,1,0:T(8,128)(2,1)S(1)}, u32[]{:S(2)}, u32[]{:S(2)}) %collective-permute-start.29) | collective-permute-done | bytes 327712 | tf_op jit(solution)/shard_map/ppermute | solution.py:256
  136.2 8.5 %collective-permute-done.28.refs_3_ = bf16[2,384,384]{2,1,0:T(8,128)(2,1)S(1)} collective-permute-done((bf16[2,384,384]{2,1,0:T(8,128)(2,1)S(1)}, bf16[2,384,384]{2,1,0:T(8,128)(2,1)S(1)}, u32[]{:S(2)}, u32[]{:S(2)}) %collective-permute-start.28) | collective-permute-done | bytes 589856 | tf_op jit(solution)/shard_map/ppermute | solution.py:256
  145.6 6.2 %collective-permute-done.27.refs_2_.refs_7_ = bf16[1,128,896]{2,1,0:T(8,128)(2,1)S(1)} collective-permute-done((bf16[1,128,896]{2,1,0:T(8,128)(2,1)S(1)}, bf16[1,128,896]{2,1,0:T(8,128)(2,1)S(1)}, u32[]{:S(2)}, u32[]{:S(2)}) %collective-permute-start.27) | collective-permute-done | bytes 229408 | tf_op jit(solution)/shard_map/ppermute | solution.py:256
  152.1 5.7 %collective-permute-done.26 = bf16[4,256,256]{2,1,0:T(8,128)(2,1)S(1)} collective-permute-done((bf16[4,256,256]{2,1,0:T(8,128)(2,1)S(1)}, bf16[4,256,256]{2,1,0:T(8,128)(2,1)S(1)}, u32[]{:S(2)}, u32[]{:S(2)}) %collective-permute-start.26) | collective-permute-done | bytes 524320 | tf_op jit(solution)/shard_map/ppermute | solution.py:256
  158.0 5.1 %attend.2.refs_5_ = bf16[384,1024]{1,0:T(8,128)(2,1)} custom-call(s32[1]{0:T(128)} %bitcast.device_ref, s32[24]{0:T(128)S(1)} %copy-done.2, s32[24]{0:T(128)S(1)} %copy-done.3, f32[384,128]{1,0:T(8,128)S(1)} %broadcast_in_dim.31.inverse_ref, f32[1,640]{1,0:T(1,128)S(1)} %broadcast_in_dim.37.bias_ref, f32[384,128]{1,0:T(8,128)S(1)} %copy-done, ...), custom_call_target="tpu_custom_call" | custom-call | flops 1887436800 | bytes 491520 | tf_op jit(solution)/shard_map/attend/pallas_call | solution.py:493
  163.2 3.8 %attend.3 = bf16[384,1024]{1,0:T(8,128)(2,1)} custom-call(s32[1]{0:T(128)} %bitcast.device_ref, s32[24]{0:T(128)S(1)} %copy-done.2, s32[24]{0:T(128)S(1)} %copy-done.3, f32[384,128]{1,0:T(8,128)S(1)} %broadcast_in_dim.31.inverse_ref, f32[1,384]{1,0:T(1,128)S(1)} %broadcast_in_dim.32.bias_ref, ...), custom_call_target="tpu_custom_call", output_to_operand_aliasing={{}: (13, {})} | custom-call | flops 679477248 | bytes 294912 | tf_op jit(solution)/shard_map/attend/pallas_call | solution.py:493
  (94 shorter events, 15.8 us)
Async XLA Ops:
  3.6 17.5 %copy-start.5 = (bf16[1024,1024]{1,0:T(8,128)(2,1)S(1)}, bf16[1024,1024]{1,0:T(8,128)(2,1)}, u32[]{:S(2)}) copy-start(bf16[1024,1024]{1,0:T(8,128)(2,1)} %param.14) | copy-start | bytes 6291460
  3.6 12.2 %collective-permute-start.2 = (bf16[128,2048]{1,0:T(8,128)(2,1)S(1)}, bf16[128,2048]{1,0:T(8,128)(2,1)S(1)}, u32[]{:S(2)}, u32[]{:S(2)}) collective-permute-start(bf16[128,2048]{1,0:T(8,128)(2,1)S(1)} %get-tuple-element.70), channel_id=1, source_target_pairs={{0,0},{8,16},{16,8},{24,24},{1,1},{9,17},{17,9},{25,25},{2,26},{10... | collective-permute-start | bytes 1572872 | tf_op jit(solution)/shard_map/ppermute | solution.py:309
  4.6 16.7 %collective-permute-start.4 = (bf16[1024,256]{1,0:T(8,128)(2,1)S(1)}, bf16[1024,256]{1,0:T(8,128)(2,1)S(1)}, u32[]{:S(2)}, u32[]{:S(2)}) collective-permute-start(bf16[1024,256]{1,0:T(8,128)(2,1)S(1)} %constant_dynamic-update-slice_fusion.refs_8_.refs_4_), channel_id=1, source_target_pairs={{0,1},{1,0},{2,3},{3,2},{4,5},{5,4},{6,7},{7,6},{8,9},{9,8},{10,11... | collective-permute-start | bytes 1572872 | tf_op jit(solution)/shard_map/ppermute | solution.py:256
  8.0 3.4 %collective-permute-start = (f32[3,128]{1,0:T(4,128)S(1)}, f32[3,128]{1,0:T(4,128)S(1)}, u32[]{:S(2)}, u32[]{:S(2)}) collective-permute-start(f32[3,128]{1,0:T(4,128)S(1)} %multiply_reduce_fusion), channel_id=1, source_target_pairs={{0,8},{8,0},{16,24},{24,16},{1,9},{9,1},{17,25},{25,17},{2,10},{10... | collective-permute-start | bytes 4616 | tf_op jit(solution)/shard_map/ppermute | solution.py:256
  11.4 4.4 %collective-permute-start.1 = (f32[3,128]{1,0:T(4,128)S(1)}, f32[3,128]{1,0:T(4,128)S(1)}, u32[]{:S(2)}, u32[]{:S(2)}) collective-permute-start(f32[3,128]{1,0:T(4,128)S(1)} %add.31), channel_id=1, source_target_pairs={{0,16},{8,24},{16,0},{24,8},{1,17},{9,25},{17,1},{25,9},{2,18},{10... | collective-permute-start | bytes 4616 | tf_op jit(solution)/shard_map/ppermute | solution.py:256
  15.8 14.7 %collective-permute-start.6 = (bf16[128,2048]{1,0:T(8,128)(2,1)}, bf16[128,2048]{1,0:T(8,128)(2,1)}, u32[]{:S(2)}, u32[]{:S(2)}) collective-permute-start(bf16[128,2048]{1,0:T(8,128)(2,1)} %get-tuple-element.41), channel_id=1, source_target_pairs={{0,0},{8,16},{16,8},{24,24},{1,1},{9,17},{17,9},{25,25},{2,26},{10... | collective-permute-start | bytes 1572872 | tf_op jit(solution)/shard_map/ppermute | solution.py:309
  21.3 36.6 %collective-permute-start.5 = (bf16[1024,640]{1,0:T(8,128)(2,1)S(1)}, bf16[1024,640]{1,0:T(8,128)(2,1)}, u32[]{:S(2)}, u32[]{:S(2)}) collective-permute-start(bf16[1024,640]{1,0:T(8,128)(2,1)S(1)} %slice.73.refs_1_.refs_6_), channel_id=1, source_target_pairs={{0,1},{1,0},{2,3},{3,2},{4,5},{5,4},{6,7},{7,6},{8,9},{9,8},{10,11... | collective-permute-start | bytes 3932168 | tf_op jit(solution)/shard_map/ppermute | solution.py:256
  25.2 12.4 %collective-permute-start.3 = (bf16[128,2048]{1,0:T(8,128)(2,1)}, bf16[128,2048]{1,0:T(8,128)(2,1)}, u32[]{:S(2)}, u32[]{:S(2)}) collective-permute-start(bf16[128,2048]{1,0:T(8,128)(2,1)} %copy-done.11), channel_id=1, source_target_pairs={{0,0},{16,18},{8,12},{24,30},{1,1},{17,19},{9,13},{25,31},{26,16},... | collective-permute-start | bytes 1572872 | tf_op jit(solution)/shard_map/ppermute | solution.py:331
  30.5 12.1 %collective-permute-start.7 = (bf16[128,2048]{1,0:T(8,128)(2,1)}, bf16[128,2048]{1,0:T(8,128)(2,1)}, u32[]{:S(2)}, u32[]{:S(2)}) collective-permute-start(bf16[128,2048]{1,0:T(8,128)(2,1)} %collective-permute-done.6), channel_id=1, source_target_pairs={{0,0},{16,18},{8,12},{24,30},{1,1},{17,19},{9,13},{25,31},{26,16},... | collective-permute-start | bytes 1572872 | tf_op jit(solution)/shard_map/ppermute | solution.py:331
  35.9 17.9 %collective-permute-start.16 = (bf16[128,2048]{1,0:T(8,128)(2,1)}, bf16[128,2048]{1,0:T(8,128)(2,1)S(1)}, u32[]{:S(2)}, u32[]{:S(2)}) collective-permute-start(bf16[128,2048]{1,0:T(8,128)(2,1)} %get-tuple-element.49), channel_id=1, source_target_pairs={{0,0},{8,16},{16,8},{24,24},{1,1},{9,17},{17,9},{25,25},{2,26},{10... | collective-permute-start | bytes 1572872 | tf_op jit(solution)/shard_map/ppermute | solution.py:309
  37.6 20.2 %collective-permute-start.8 = (bf16[128,2048]{1,0:T(8,128)(2,1)}, bf16[128,2048]{1,0:T(8,128)(2,1)}, u32[]{:S(2)}, u32[]{:S(2)}) collective-permute-start(bf16[128,2048]{1,0:T(8,128)(2,1)} %collective-permute-done.3.refs_0_), channel_id=1, source_target_pairs={{0,16},{8,24},{16,0},{24,8},{1,17},{9,25},{17,1},{25,9},{2,18},{10... | collective-permute-start | bytes 1572872 | tf_op jit(solution)/shard_map/ppermute | solution.py:256
  42.6 24.4 %collective-permute-start.9 = (bf16[128,2048]{1,0:T(8,128)(2,1)}, bf16[128,2048]{1,0:T(8,128)(2,1)}, u32[]{:S(2)}, u32[]{:S(2)}) collective-permute-start(bf16[128,2048]{1,0:T(8,128)(2,1)} %collective-permute-done.7.refs_1_), channel_id=1, source_target_pairs={{0,16},{8,24},{16,0},{24,8},{1,17},{9,25},{17,1},{25,9},{2,18},{10... | collective-permute-start | bytes 1572872 | tf_op jit(solution)/shard_map/ppermute | solution.py:256
  53.8 14.0 %collective-permute-start.17 = (bf16[128,2048]{1,0:T(8,128)(2,1)S(1)}, bf16[128,2048]{1,0:T(8,128)(2,1)}, u32[]{:S(2)}, u32[]{:S(2)}) collective-permute-start(bf16[128,2048]{1,0:T(8,128)(2,1)S(1)} %collective-permute-done.16), channel_id=1, source_target_pairs={{0,0},{16,18},{8,12},{24,30},{1,1},{17,19},{9,13},{25,31},{26,16},... | collective-permute-start | bytes 1572872 | tf_op jit(solution)/shard_map/ppermute | solution.py:331
  55.3 14.6 %collective-permute-start.10 = (bf16[128,2048]{1,0:T(8,128)(2,1)}, bf16[128,2048]{1,0:T(8,128)(2,1)}, u32[]{:S(2)}, u32[]{:S(2)}) collective-permute-start(bf16[128,2048]{1,0:T(8,128)(2,1)} %collective-permute-done.3.refs_0_), channel_id=1, source_target_pairs={{0,8},{8,0},{16,24},{24,16},{1,9},{9,1},{17,25},{25,17},{2,10},{10... | collective-permute-start | bytes 1572872 | tf_op jit(solution)/shard_map/ppermute | solution.py:256
  57.8 12.5 %collective-permute-start.11 = (bf16[128,2048]{1,0:T(8,128)(2,1)}, bf16[128,2048]{1,0:T(8,128)(2,1)}, u32[]{:S(2)}, u32[]{:S(2)}) collective-permute-start(bf16[128,2048]{1,0:T(8,128)(2,1)} %collective-permute-done.7.refs_1_), channel_id=1, source_target_pairs={{0,8},{8,0},{16,24},{24,16},{1,9},{9,1},{17,25},{25,17},{2,10},{10... | collective-permute-start | bytes 1572872 | tf_op jit(solution)/shard_map/ppermute | solution.py:256
  57.9 12.4 %collective-permute-start.12 = (bf16[128,2048]{1,0:T(8,128)(2,1)}, bf16[128,2048]{1,0:T(8,128)(2,1)}, u32[]{:S(2)}, u32[]{:S(2)}) collective-permute-start(bf16[128,2048]{1,0:T(8,128)(2,1)} %collective-permute-done.8.refs_2_), channel_id=1, source_target_pairs={{0,8},{8,0},{16,24},{24,16},{1,9},{9,1},{17,25},{25,17},{2,10},{10... | collective-permute-start | bytes 1572872 | tf_op jit(solution)/shard_map/ppermute | solution.py:256
  67.0 3.4 %collective-permute-start.13 = (bf16[128,2048]{1,0:T(8,128)(2,1)}, bf16[128,2048]{1,0:T(8,128)(2,1)}, u32[]{:S(2)}, u32[]{:S(2)}) collective-permute-start(bf16[128,2048]{1,0:T(8,128)(2,1)} %collective-permute-done.9.refs_3_), channel_id=1, source_target_pairs={{0,8},{8,0},{16,24},{24,16},{1,9},{9,1},{17,25},{25,17},{2,10},{10... | collective-permute-start | bytes 1572872 | tf_op jit(solution)/shard_map/ppermute | solution.py:256
  67.8 14.9 %collective-permute-start.18 = (bf16[128,2048]{1,0:T(8,128)(2,1)}, bf16[128,2048]{1,0:T(8,128)(2,1)}, u32[]{:S(2)}, u32[]{:S(2)}) collective-permute-start(bf16[128,2048]{1,0:T(8,128)(2,1)} %collective-permute-done.17.refs_0_), channel_id=1, source_target_pairs={{0,16},{8,24},{16,0},{24,8},{1,17},{9,25},{17,1},{25,9},{2,18},{10... | collective-permute-start | bytes 1572872 | tf_op jit(solution)/shard_map/ppermute | solution.py:256
  69.8 31.9 %collective-permute-start.23 = (bf16[1024,384]{1,0:T(8,128)(2,1)S(1)}, bf16[1024,384]{1,0:T(8,128)(2,1)S(1)}, u32[]{:S(2)}, u32[]{:S(2)}) collective-permute-start(bf16[1024,384]{1,0:T(8,128)(2,1)S(1)} %slice.74.refs_2_), channel_id=1, source_target_pairs={{0,1},{1,0},{2,3},{3,2},{4,5},{5,4},{6,7},{7,6},{8,9},{9,8},{10,11... | collective-permute-start | bytes 2359304 | tf_op jit(solution)/shard_map/ppermute | solution.py:256
  74.4 9.5 %collective-permute-start.14 = (bf16[2,256,256]{2,1,0:T(8,128)(2,1)S(1)}, bf16[2,256,256]{2,1,0:T(8,128)(2,1)S(1)}, u32[]{:S(2)}, u32[]{:S(2)}) collective-permute-start(bf16[2,256,256]{2,1,0:T(8,128)(2,1)S(1)} %get-tuple-element.44), channel_id=1, source_target_pairs={{0,2},{1,3},{2,0},{3,1},{4,6},{5,7},{6,4},{7,5},{8,10},{9,11},{10,... | collective-permute-start | bytes 786440 | tf_op jit(solution)/shard_map/ppermute | solution.py:256
  81.9 20.5 %collective-permute-start.22 = (bf16[2,256,640]{2,1,0:T(8,128)(2,1)S(1)}, bf16[2,256,640]{2,1,0:T(8,128)(2,1)S(1)}, u32[]{:S(2)}, u32[]{:S(2)}) collective-permute-start(bf16[2,256,640]{2,1,0:T(8,128)(2,1)S(1)} %get-tuple-element.47), channel_id=1, source_target_pairs={{0,2},{1,3},{2,0},{3,1},{4,6},{5,7},{6,4},{7,5},{8,10},{9,11},{10,... | collective-permute-start | bytes 1966088 | tf_op jit(solution)/shard_map/ppermute | solution.py:256
  82.0 4.0 %collective-permute-start.19 = (bf16[128,2048]{1,0:T(8,128)(2,1)}, bf16[128,2048]{1,0:T(8,128)(2,1)S(1)}, u32[]{:S(2)}, u32[]{:S(2)}) collective-permute-start(bf16[128,2048]{1,0:T(8,128)(2,1)} %collective-permute-done.17.refs_0_), channel_id=1, source_target_pairs={{0,8},{8,0},{16,24},{24,16},{1,9},{9,1},{17,25},{25,17},{2,10},{10... | collective-permute-start | bytes 1572872 | tf_op jit(solution)/shard_map/ppermute | solution.py:256
  82.7 3.3 %collective-permute-start.20 = (bf16[128,2048]{1,0:T(8,128)(2,1)}, bf16[128,2048]{1,0:T(8,128)(2,1)S(1)}, u32[]{:S(2)}, u32[]{:S(2)}) collective-permute-start(bf16[128,2048]{1,0:T(8,128)(2,1)} %collective-permute-done.18.refs_1_), channel_id=1, source_target_pairs={{0,8},{8,0},{16,24},{24,16},{1,9},{9,1},{17,25},{25,17},{2,10},{10... | collective-permute-start | bytes 1572872 | tf_op jit(solution)/shard_map/ppermute | solution.py:256
  83.9 16.0 %collective-permute-start.15 = (bf16[1,256,256]{2,1,0:T(8,128)(2,1)S(1)}, bf16[1,256,256]{2,1,0:T(8,128)(2,1)S(1)}, u32[]{:S(2)}, u32[]{:S(2)}) collective-permute-start(bf16[1,256,256]{2,1,0:T(8,128)(2,1)S(1)} %fusion.6), channel_id=1, source_target_pairs={{0,4},{1,5},{2,6},{3,7},{4,0},{5,1},{6,2},{7,3},{8,12},{9,13},{10,... | collective-permute-start | bytes 393224 | tf_op jit(solution)/shard_map/ppermute | solution.py:256
  90.9 25.2 %collective-permute-start.25 = (bf16[2,128,896]{2,1,0:T(8,128)(2,1)S(1)}, bf16[2,128,896]{2,1,0:T(8,128)(2,1)S(1)}, u32[]{:S(2)}, u32[]{:S(2)}) collective-permute-start(bf16[2,128,896]{2,1,0:T(8,128)(2,1)S(1)} %get-tuple-element.52), channel_id=1, source_target_pairs={{0,2},{1,3},{2,0},{3,1},{4,6},{5,7},{6,4},{7,5},{8,10},{9,11},{10,... | collective-permute-start | bytes 1376264 | tf_op jit(solution)/shard_map/ppermute | solution.py:256
  100.2 5.5 %collective-permute-start.21 = (bf16[1,256,256]{2,1,0:T(8,128)(2,1)S(1)}, bf16[1,256,256]{2,1,0:T(8,128)(2,1)S(1)}, u32[]{:S(2)}, u32[]{:S(2)}) collective-permute-start(bf16[1,256,256]{2,1,0:T(8,128)(2,1)S(1)} %bitcast.22), channel_id=1, source_target_pairs={{0,1},{1,0},{2,3},{3,2},{4,5},{5,4},{6,7},{7,6},{8,9},{9,8},{10,11... | collective-permute-start | bytes 393224 | tf_op jit(solution)/shard_map/ppermute | solution.py:256
  105.7 23.4 %collective-permute-start.24 = (bf16[2,256,256]{2,1,0:T(8,128)(2,1)S(1)}, bf16[2,256,256]{2,1,0:T(8,128)(2,1)S(1)}, u32[]{:S(2)}, u32[]{:S(2)}) collective-permute-start(bf16[2,256,256]{2,1,0:T(8,128)(2,1)S(1)} %pad_maximum_fusion.2), channel_id=1, source_target_pairs={{0,4},{1,5},{2,6},{3,7},{4,0},{5,1},{6,2},{7,3},{8,12},{9,13},{10,... | collective-permute-start | bytes 786440 | tf_op jit(solution)/shard_map/ppermute | solution.py:256
  109.2 27.0 %collective-permute-start.29 = (bf16[1,256,640]{2,1,0:T(8,128)(2,1)S(1)}, bf16[1,256,640]{2,1,0:T(8,128)(2,1)S(1)}, u32[]{:S(2)}, u32[]{:S(2)}) collective-permute-start(bf16[1,256,640]{2,1,0:T(8,128)(2,1)S(1)} %fusion.3), channel_id=1, source_target_pairs={{0,4},{1,5},{2,6},{3,7},{4,0},{5,1},{6,2},{7,3},{8,12},{9,13},{10,... | collective-permute-start | bytes 983048 | tf_op jit(solution)/shard_map/ppermute | solution.py:256
  113.2 31.4 %collective-permute-start.28 = (bf16[2,384,384]{2,1,0:T(8,128)(2,1)S(1)}, bf16[2,384,384]{2,1,0:T(8,128)(2,1)S(1)}, u32[]{:S(2)}, u32[]{:S(2)}) collective-permute-start(bf16[2,384,384]{2,1,0:T(8,128)(2,1)S(1)} %get-tuple-element.61), channel_id=1, source_target_pairs={{0,2},{1,3},{2,0},{3,1},{4,6},{5,7},{6,4},{7,5},{8,10},{9,11},{10,... | collective-permute-start | bytes 1769480 | tf_op jit(solution)/shard_map/ppermute | solution.py:256
  129.2 28.6 %collective-permute-start.26 = (bf16[4,256,256]{2,1,0:T(8,128)(2,1)S(1)}, bf16[4,256,256]{2,1,0:T(8,128)(2,1)S(1)}, u32[]{:S(2)}, u32[]{:S(2)}) collective-permute-start(bf16[4,256,256]{2,1,0:T(8,128)(2,1)S(1)} %pad_maximum_fusion.1), channel_id=1, source_target_pairs={{0,2},{1,3},{2,0},{3,1},{4,6},{5,7},{6,4},{7,5},{8,10},{9,11},{10,... | collective-permute-start | bytes 1572872 | tf_op jit(solution)/shard_map/ppermute | solution.py:256
  129.3 22.5 %collective-permute-start.27 = (bf16[1,128,896]{2,1,0:T(8,128)(2,1)S(1)}, bf16[1,128,896]{2,1,0:T(8,128)(2,1)S(1)}, u32[]{:S(2)}, u32[]{:S(2)}) collective-permute-start(bf16[1,128,896]{2,1,0:T(8,128)(2,1)S(1)} %fusion.5), channel_id=1, source_target_pairs={{0,4},{1,5},{2,6},{3,7},{4,0},{5,1},{6,2},{7,3},{8,12},{9,13},{10,... | collective-permute-start | bytes 688136 | tf_op jit(solution)/shard_map/ppermute | solution.py:256
  144.8 18.4 %collective-permute-start.30 = (bf16[1,384,384]{2,1,0:T(8,128)(2,1)S(1)}, bf16[1,384,384]{2,1,0:T(8,128)(2,1)S(1)}, u32[]{:S(2)}, u32[]{:S(2)}) collective-permute-start(bf16[1,384,384]{2,1,0:T(8,128)(2,1)S(1)} %fusion.4), channel_id=1, source_target_pairs={{0,4},{1,5},{2,6},{3,7},{4,0},{5,1},{6,2},{7,3},{8,12},{9,13},{10,... | collective-permute-start | bytes 884744 | tf_op jit(solution)/shard_map/ppermute | solution.py:256
  (11 other events, 61.3 us)

commit v7 on v6

--- a/solution.py
+++ b/solution.py
@@ -77,6 +77,12 @@
     for copy in copies:
         copy.start()
     return copies
+
+
+def assemble_kernel(lines, place_ref, *refs):
+    pieces, (held, sems) = refs[:lines], refs[lines:]
+    for copy in assemble(lines, 1, place_ref, pieces, held, sems):
+        copy.wait()
 
 
 def project_kernel(lines, groups, chunks, counts, fresh, place_ref, *refs):
@@ -292,31 +298,6 @@
         lax.slice_in_dim(w_query, low * HD, high * HD, axis=1)
         for low, high in zip(head_cuts, head_cuts[1:])
     ]
-    squares = jnp.sum(jnp.square(raw.astype(f32)), -1).reshape(blocks, block_len)
-    bit = 1
-    while bit < lines:
-        squares = squares + swap(squares, "fsdp", bit)
-        bit *= 2
-    inverse = lax.rsqrt(squares / features + 1e-06).reshape(tokens)
-    inverse = jnp.broadcast_to(inverse[:, None], (tokens, HD))
-    sent = []
-    for block in range(blocks):
-        piece = (hidden[block].astype(f32) * gain_part).astype(bf16)
-        if block == 1:
-            piece = tie(piece, sent[-1], squares)
-        elif block:
-            piece = tie(piece, sent[-1])
-        sent.append(lax.ppermute(piece, axes, first_hop))
-
-    head_cuts = [0, (5 * head_count + 7) // 8, head_count]
-    w_chunks = [jnp.concatenate([w_key, w_value], 1)] + [
-        lax.slice_in_dim(w_query, low * HD, high * HD, axis=1)
-        for low, high in zip(head_cuts, head_cuts[1:])
-    ]
-    w_rows = []
-    for chunk in w_chunks:
-        outgoing = tie(chunk, w_rows[-1][-1]) if w_rows else chunk
-        w_rows.append([chunk] + [swap(outgoing, "branch", j) for j in range(1, groups)])
 
     cos, sin = pl.pallas_call(
         functools.partial(table_kernel, far_slots, blocks, block_len),
@@ -325,10 +306,31 @@
         out_shape=[jax.ShapeDtypeStruct((tokens, HD), f32)] * 2,
         name="tables",
     )(device_id, parents)
-    sent[0] = tie(sent[0], cos, sin, *w_chunks)
-    sent[1] = tie(sent[1], w_rows[0][-1])
-
+
+    sent = []
+    for block in range(blocks):
+        piece = (hidden[block].astype(f32) * gain_part).astype(bf16)
+        piece = tie(piece, sent[-1], cos, sin, *w_chunks) if block else piece
+        sent.append(lax.ppermute(piece, axes, first_hop))
+
+    w_rows = [None] * len(w_chunks)
+    arrived = None
+    for c in (1, 0, 2):
+        outgoing = w_chunks[c] if arrived is None else tie(w_chunks[c], arrived)
+        w_rows[c] = [w_chunks[c]] + [swap(outgoing, "branch", j) for j in range(1, groups)]
+        arrived = w_rows[c][-1]
+
+    squares = tie(jnp.sum(jnp.square(raw.astype(f32)), -1).reshape(blocks, block_len), sent[1])
+    bit = 1
+    while bit < lines:
+        squares = squares + swap(squares, "fsdp", bit)
+        bit *= 2
+    inverse = lax.rsqrt(squares / features + 1e-06).reshape(tokens)
+    inverse = jnp.broadcast_to(inverse[:, None], (tokens, HD))
+
+    last_sent = sent[-1]
     sent = [lax.ppermute(piece, axes, second_hop) for piece in sent]
+    sent[0] = tie(sent[0], squares, last_sent)
     held = [{0: piece} for piece in sent]
     bit = half_lines
     while bit > 1:
@@ -342,6 +344,8 @@
             piece[j | 1] = swap(piece[j], "fsdp", 1)
         return [piece[j] for j in sorted(piece, key=spread)]
 
+    held[0][half_lines] = tie(held[0][half_lines], w_rows[1][-1])
+    held[1][half_lines] = tie(held[1][half_lines], w_rows[0][-1])
     held = [last_bit(piece) for piece in held[:STEMS]] + held[STEMS:]
 
     assembled = {}
@@ -436,36 +440,46 @@
             name="finish_kv",
         )(*operands, *addends)
 
-    early = (0, STEMS)
-    late = (STEMS, blocks)
-    first = Halving(project([early], [0], w_rows[1][-1]))
+    assembled[(0, 1)] = pl.pallas_call(
+        functools.partial(assemble_kernel, lines),
+        in_specs=[smem] + [anywhere] * lines,
+        out_specs=vmem,
+        out_shape=jax.ShapeDtypeStruct((lines * block_len, feature_part), bf16),
+        scratch_shapes=[pltpu.SemaphoreType.DMA((lines,))],
+        name="assemble",
+    )(place, *held[0])
+
+    early = [(0, 1), (1, STEMS)]
+    late = [(STEMS, blocks)]
+    first = Halving(project(early, [0]))
     first.step()
-    second = Halving(project([early], [1], first.send))
+    second = Halving(project(early, [1], first.send))
     second.step()
-    for block in range(*late):
+    for block in range(STEMS, blocks):
         held[block][0] = tie(held[block][0], second.send)
         held[block] = last_bit(held[block])
     first.rest(second.send)
-    third = Halving(project([late], [0, 1], first.send))
-    third.step()
-    first.addends[-1] = tie(first.addends[-1], third.send)
     stem_kv = finish_kv(first.addends, 0, STEMS)
 
     tour = [1 << i for i in range(bits_of(groups))]
     tour += [groups << i for i in reversed(range(bits_of(lines)))]
     stems = stem_kv[None]
     came = swap(stems, "branch", tour[0])
-    second.rest(stem_kv, w_rows[2][-1])
-    last = second
+    third = Halving(project(late, [0, 1], stem_kv))
+    third.step()
+    second.add(third.send, w_rows[2][-1])
     for step, bit in enumerate(tour[1:]):
-        stems = jnp.concatenate([stems, tie(came, last.send)], 0)
+        stems = jnp.concatenate([stems, tie(came, fourth.send if step else second.send)], 0)
         came = swap(stems, "branch", bit)
         if step == 0:
-            fourth = Halving(project([early, late], [2], stems))
-            fourth.step()
-            third.rest(fourth.send)
-            last = third
-    fourth.rest(stems, second.came)
+            fourth = Halving(project(early + late, [2], stems))
+    second.step(stems)
+    fourth.step(stems)
+    third.add(stems)
+    third.step()
+    second.rest()
+    third.rest()
+    fourth.rest(second.came)
     stems = jnp.concatenate([stems, came], 0)
     third.addends[-1] = tie(third.addends[-1], fourth.send)
     late_kv = finish_kv(third.addends, STEMS, blocks - STEMS)

time: 168 us -> 180 us (1.071)
  waiting for transfers between devices: 63.6 us -> 82 us
  starting transfers between devices: 68.8 us -> 54.3 us
  Pallas kernels: 29.2 us -> 32.7 us
  local copies, waits for them, and re-layouts: 1.42 us -> 3.95 us
  other arithmetic: 3.77 us -> 5.67 us
    ppermute x25, waiting for transfers between devices: 63.5 us -> 82 us  [swap(): return lax.ppermute(array, axis, [(i, i ^ bit) for i in range(size)])]
    ppermute x25, starting transfers between devices: 48.8 us -> 38.2 us  [swap(): return lax.ppermute(array, axis, [(i, i ^ bit) for i in range(size)])]
    ppermute x3, starting transfers between devices: 12.1 us -> 8.28 us  [shards(): sent = [lax.ppermute(piece, axes, second_hop) for piece in sent]]
    pallas_call x0 -> x1, Pallas kernels: none -> 3.57 us  [shards(): pl.pallas_call(functools.partial(assemble_kernel, lines), in_specs=[smem]...]
  transfers between devices with their start and end apart: 31 -> 31, of which waited for: 13 -> 12; matrix products, arithmetic and copies ran while one was open for 1% -> 2% of each run, Pallas kernels for 15% -> 16%
where the time goes in v7:
time: 180 us; the launch traced here: 179 us
  waiting for transfers between devices  82 us (46%)
  starting transfers between devices  54.3 us (30%)
  Pallas kernels  32.7 us (18%)
  other arithmetic  5.67 us (3%)
  local copies, waits for them, and re-layouts  3.95 us (2%)
    ppermute x25, waiting for transfers between devices, swap(): return lax.ppermute(array, axis, [(i, i ^ bit) for i in range(size)])  82 us
    ppermute x25, starting transfers between devices, swap(): return lax.ppermute(array, axis, [(i, i ^ bit) for i in range(size)])  38.2 us
    pallas_call x4, Pallas kernels, project(): pl.pallas_call(functools.partial(project_kernel, lines, groups, len(chunk...  17.9 us
    pallas_call x2, Pallas kernels, attend(): pl.pallas_call(kernel, grid=(1,), in_specs=in_specs, out_specs=anywhere,...  8.82 us
    ppermute x3, starting transfers between devices, shards(): sent = [lax.ppermute(piece, axes, second_hop) for piece in sent]  8.28 us
    ppermute x3, starting transfers between devices, shards(): sent.append(lax.ppermute(piece, axes, first_hop))  7.86 us
  transfers between devices with their start and end apart: 31, of which 12 were waited for; matrix products, arithmetic and copies ran while one was open for 2% of the time, Pallas kernels for 16%

profile of v7, /device:TPU:0, one launch (start us, length us, event | category | flops | bytes accessed | tf_op | source)
XLA Modules:
  0.0 179.3 jit_solution(6846636093834953876)
XLA Ops:
  0.7 2.9 %fusion = (bf16[128,2048]{1,0:T(8,128)(2,1)S(1)}, bf16[128,2048]{1,0:T(8,128)(2,1)}, bf16[128,2048]{1,0:T(8,128)(2,1)}) fusion(bf16[3,128,2048]{2,1,0:T(8,128)(2,1)} %param.10, f32[2048]{0:T(1024)S(1)} %dynamic_slice.3), kind=kLoop, calls=%fused_computation.3 | loop fusion | flops 2359296 | bytes 3153920 | tf_op jit(solution)/shard_map/convert_element_type | solution.py:312
  3.6 5.5 %collective-permute-start = (bf16[128,2048]{1,0:T(8,128)(2,1)}, bf16[128,2048]{1,0:T(8,128)(2,1)}, u32[]{:S(2)}, u32[]{:S(2)}) collective-permute-start(bf16[128,2048]{1,0:T(8,128)(2,1)} %get-tuple-element.75), channel_id=1, source_target_pairs={{0,0},{8,16},{16,8},{24,24},{1,1},{9,17},{17,9},{25,25},{2,26},{10... | collective-permute-start | bytes 1572872 | tf_op jit(solution)/shard_map/ppermute | solution.py:314
  9.2 3.0 %collective-permute-start.7 = (bf16[1024,640]{1,0:T(8,128)(2,1)S(1)}, bf16[1024,640]{1,0:T(8,128)(2,1)}, u32[]{:S(2)}, u32[]{:S(2)}) collective-permute-start(bf16[1024,640]{1,0:T(8,128)(2,1)S(1)} %slice.69.refs_2_.refs_6_), channel_id=1, source_target_pairs={{0,1},{1,0},{2,3},{3,2},{4,5},{5,4},{6,7},{7,6},{8,9},{9,8},{10,11... | collective-permute-start | bytes 3932168 | tf_op jit(solution)/shard_map/ppermute | solution.py:262
  12.3 2.2 %tables.1 = (f32[384,128]{1,0:T(8,128)}, f32[384,128]{1,0:T(8,128)}) custom-call(s32[1]{0:T(128)} %bitcast.device_ref, s32[24]{0:T(128)} %parents_ref.5), custom_call_target="tpu_custom_call" | custom-call | tf_op jit(solution)/shard_map/tables/pallas_call | solution.py:302
  15.6 1.7 collective-permute-start.1
  17.3 5.3 %collective-permute-start.4 = (bf16[128,2048]{1,0:T(8,128)(2,1)}, bf16[128,2048]{1,0:T(8,128)(2,1)}, u32[]{:S(2)}, u32[]{:S(2)}) collective-permute-start(bf16[128,2048]{1,0:T(8,128)(2,1)} %collective-permute-done), channel_id=1, source_target_pairs={{0,0},{16,18},{8,12},{24,30},{1,1},{17,19},{9,13},{25,31},{26,16},... | collective-permute-start | bytes 1572872 | tf_op jit(solution)/shard_map/ppermute | solution.py:332
  24.8 1.8 multiply_reduce_fusion
  26.6 9.6 %collective-permute-start.2 = (f32[3,128]{1,0:T(4,128)S(1)}, f32[3,128]{1,0:T(4,128)S(1)}, u32[]{:S(2)}, u32[]{:S(2)}) collective-permute-start(f32[3,128]{1,0:T(4,128)S(1)} %multiply_reduce_fusion), channel_id=1, source_target_pairs={{0,8},{8,0},{16,24},{24,16},{1,9},{9,1},{17,25},{25,17},{2,10},{10... | collective-permute-start | bytes 4616 | tf_op jit(solution)/shard_map/ppermute | solution.py:262
  38.6 2.0 %collective-permute-done.3 = f32[3,128]{1,0:T(4,128)S(1)} collective-permute-done((f32[3,128]{1,0:T(4,128)S(1)}, f32[3,128]{1,0:T(4,128)S(1)}, u32[]{:S(2)}, u32[]{:S(2)}) %collective-permute-start.3) | collective-permute-done | bytes 1568 | tf_op jit(solution)/shard_map/ppermute | solution.py:262
  40.7 1.6 collective-permute-start.6
  43.8 3.1 %collective-permute-start.11 = (bf16[128,2048]{1,0:T(8,128)(2,1)}, bf16[128,2048]{1,0:T(8,128)(2,1)}, u32[]{:S(2)}, u32[]{:S(2)}) collective-permute-start(bf16[128,2048]{1,0:T(8,128)(2,1)} %collective-permute-done.10.refs_1_), channel_id=1, source_target_pairs={{0,16},{8,24},{16,0},{24,8},{1,17},{9,25},{17,1},{25,9},{2,18},{10... | collective-permute-start | bytes 1572872 | tf_op jit(solution)/shard_map/ppermute | solution.py:262
  48.4 1.6 collective-permute-start.8
  50.0 5.9 %collective-permute-done.6.refs_1_ = bf16[128,2048]{1,0:T(8,128)(2,1)} collective-permute-done((bf16[128,2048]{1,0:T(8,128)(2,1)}, bf16[128,2048]{1,0:T(8,128)(2,1)}, u32[]{:S(2)}, u32[]{:S(2)}) %collective-permute-start.6) | collective-permute-done | bytes 524320 | tf_op jit(solution)/shard_map/ppermute | solution.py:262
  56.4 9.2 %collective-permute-done.11.refs_2_ = bf16[128,2048]{1,0:T(8,128)(2,1)} collective-permute-done((bf16[128,2048]{1,0:T(8,128)(2,1)}, bf16[128,2048]{1,0:T(8,128)(2,1)}, u32[]{:S(2)}, u32[]{:S(2)}) %collective-permute-start.11) | collective-permute-done | bytes 524320 | tf_op jit(solution)/shard_map/ppermute | solution.py:262
  65.6 1.7 collective-permute-start.20
  69.4 3.6 %assemble.1.refs_0_ = bf16[512,2048]{1,0:T(8,128)(2,1)} custom-call(s32[2]{0:T(128)} %pad_add_fusion.place_ref, bf16[128,2048]{1,0:T(8,128)(2,1)} %collective-permute-done.4.refs_0_, bf16[128,2048]{1,0:T(8,128)(2,1)} %collective-permute-done.6.refs_1_, bf16[128,2048]{1,0:T(8,128)(2,1)} %collective-permute-done.8.refs_2_, ...), custom_call_target="tpu_custom_call" | custom-call | tf_op jit(solution)/shard_map/assemble/pallas_call | solution.py:443
  73.0 1.6 copy-done
  74.6 3.4 %project.4 = (bf16[2,256,256]{2,1,0:T(8,128)(2,1)S(1)}, f32[2,256,256]{2,1,0:T(8,128)S(1)}, bf16[512,2048]{1,0:T(8,128)(2,1)S(1)}) custom-call(s32[2]{0:T(128)S(1)} %copy-done.4, bf16[512,2048]{1,0:T(8,128)(2,1)S(1)} %copy-done, bf16[128,2048]{1,0:T(8,128)(2,1)} %collective-permute-done.10.refs_1_, bf16[128,2048]{1,0:T(8,128)(2,1)} %collective-permute-done.11.refs_2_, ...), custom_call_target="tpu_custom_call" | custom-call | flops 1073741824 | bytes 4194304 | tf_op jit(solution)/shard_map/project/pallas_call | solution.py:377
  78.1 4.9 %project.5 = (bf16[2,256,640]{2,1,0:T(8,128)(2,1)S(1)}, f32[2,256,640]{2,1,0:T(8,128)S(1)}) custom-call(s32[2]{0:T(128)S(1)} %copy-done.4, bf16[512,2048]{1,0:T(8,128)(2,1)S(1)} %copy-done, bf16[512,2048]{1,0:T(8,128)(2,1)S(1)} %get-tuple-element.50.refs_1_, bf16[1024,640]{1,0:T(8,128)(2,1)S(1)} %slice.69.refs_2_.refs_6_, ...), custom_call_target="tpu_custom_call" | custom-call | flops 2684354560 | bytes 4194304 | tf_op jit(solution)/shard_map/project/pallas_call | solution.py:377
  83.0 2.0 %collective-permute-start.18 = (bf16[2,256,640]{2,1,0:T(8,128)(2,1)S(1)}, bf16[2,256,640]{2,1,0:T(8,128)(2,1)S(1)}, u32[]{:S(2)}, u32[]{:S(2)}) collective-permute-start(bf16[2,256,640]{2,1,0:T(8,128)(2,1)S(1)} %get-tuple-element.51), channel_id=1, source_target_pairs={{0,2},{1,3},{2,0},{3,1},{4,6},{5,7},{6,4},{7,5},{8,10},{9,11},{10,... | collective-permute-start | bytes 1966088 | tf_op jit(solution)/shard_map/ppermute | solution.py:262
  86.8 14.8 %collective-permute-done.16.refs_2_ = bf16[1,256,256]{2,1,0:T(8,128)(2,1)S(1)} collective-permute-done((bf16[1,256,256]{2,1,0:T(8,128)(2,1)S(1)}, bf16[1,256,256]{2,1,0:T(8,128)(2,1)S(1)}, u32[]{:S(2)}, u32[]{:S(2)}) %collective-permute-start.16) | collective-permute-done | bytes 131104 | tf_op jit(solution)/shard_map/ppermute | solution.py:262
  102.5 5.0 %project.6 = (bf16[2,128,896]{2,1,0:T(8,128)(2,1)S(1)}, f32[2,128,896]{2,1,0:T(8,128)S(1)}, bf16[512,2048]{1,0:T(8,128)(2,1)S(1)}) custom-call(s32[2]{0:T(128)S(1)} %copy-done.4, bf16[128,2048]{1,0:T(8,128)(2,1)} %collective-permute-done.19.refs_0_, bf16[128,2048]{1,0:T(8,128)(2,1)} %collective-permute-done.20.refs_1_, ...), custom_call_target="tpu_custom_call" | custom-call | flops 1879048192 | bytes 2097152 | tf_op jit(solution)/shard_map/project/pallas_call | solution.py:377
  107.7 3.4 %collective-permute-start.24 = (bf16[2,256,256]{2,1,0:T(8,128)(2,1)S(1)}, bf16[2,256,256]{2,1,0:T(8,128)(2,1)S(1)}, u32[]{:S(2)}, u32[]{:S(2)}) collective-permute-start(bf16[2,256,256]{2,1,0:T(8,128)(2,1)S(1)} %pad_maximum_fusion.2), channel_id=1, source_target_pairs={{0,4},{1,5},{2,6},{3,7},{4,0},{5,1},{6,2},{7,3},{8,12},{9,13},{10,... | collective-permute-start | bytes 786440 | tf_op jit(solution)/shard_map/ppermute | solution.py:262
  111.2 4.6 %project.7 = (bf16[2,384,384]{2,1,0:T(8,128)(2,1)S(1)}, f32[2,384,384]{2,1,0:T(8,128)S(1)}) custom-call(s32[2]{0:T(128)S(1)} %copy-done.4, bf16[512,2048]{1,0:T(8,128)(2,1)S(1)} %copy-done.1, bf16[512,2048]{1,0:T(8,128)(2,1)S(1)} %get-tuple-element.50.refs_1_, bf16[512,2048]{1,0:T(8,128)(2,1)S(1)} %get-tuple-element.61.refs_2_, ...), custom_call_target="tpu_custom_call" | custom-call | flops 2415919104 | bytes 6291456 | tf_op jit(solution)/shard_map/project/pallas_call | solution.py:377
  115.9 5.9 %collective-permute-done.24 = bf16[2,256,256]{2,1,0:T(8,128)(2,1)S(1)} collective-permute-done((bf16[2,256,256]{2,1,0:T(8,128)(2,1)S(1)}, bf16[2,256,256]{2,1,0:T(8,128)(2,1)S(1)}, u32[]{:S(2)}, u32[]{:S(2)}) %collective-permute-start.24) | collective-permute-done | bytes 262176 | tf_op jit(solution)/shard_map/ppermute | solution.py:262
  121.9 2.0 %collective-permute-start.25 = (bf16[4,256,256]{2,1,0:T(8,128)(2,1)S(1)}, bf16[4,256,256]{2,1,0:T(8,128)(2,1)S(1)}, u32[]{:S(2)}, u32[]{:S(2)}) collective-permute-start(bf16[4,256,256]{2,1,0:T(8,128)(2,1)S(1)} %pad_maximum_fusion.1), channel_id=1, source_target_pairs={{0,2},{1,3},{2,0},{3,1},{4,6},{5,7},{6,4},{7,5},{8,10},{9,11},{10,... | collective-permute-start | bytes 1572872 | tf_op jit(solution)/shard_map/ppermute | solution.py:262
  124.0 14.7 %collective-permute-done.26.refs_1_.refs_6_ = bf16[2,128,896]{2,1,0:T(8,128)(2,1)S(1)} collective-permute-done((bf16[2,128,896]{2,1,0:T(8,128)(2,1)S(1)}, bf16[2,128,896]{2,1,0:T(8,128)(2,1)S(1)}, u32[]{:S(2)}, u32[]{:S(2)}) %collective-permute-start.26) | collective-permute-done | bytes 458784 | tf_op jit(solution)/shard_map/ppermute | solution.py:262
  138.8 19.9 %collective-permute-done.29.refs_4_ = bf16[1,256,640]{2,1,0:T(8,128)(2,1)S(1)} collective-permute-done((bf16[1,256,640]{2,1,0:T(8,128)(2,1)S(1)}, bf16[1,256,640]{2,1,0:T(8,128)(2,1)S(1)}, u32[]{:S(2)}, u32[]{:S(2)}) %collective-permute-start.29) | collective-permute-done | bytes 327712 | tf_op jit(solution)/shard_map/ppermute | solution.py:262
  158.7 3.5 %collective-permute-start.30 = (bf16[1,384,384]{2,1,0:T(8,128)(2,1)S(1)}, bf16[1,384,384]{2,1,0:T(8,128)(2,1)S(1)}, u32[]{:S(2)}, u32[]{:S(2)}) collective-permute-start(bf16[1,384,384]{2,1,0:T(8,128)(2,1)S(1)} %fusion.4), channel_id=1, source_target_pairs={{0,4},{1,5},{2,6},{3,7},{4,0},{5,1},{6,2},{7,3},{8,12},{9,13},{10,... | collective-permute-start | bytes 884744 | tf_op jit(solution)/shard_map/ppermute | solution.py:262
  163.9 5.0 %attend.2.refs_5_ = bf16[384,1024]{1,0:T(8,128)(2,1)} custom-call(s32[1]{0:T(128)} %bitcast.device_ref, s32[24]{0:T(128)S(1)} %copy-done.5, s32[24]{0:T(128)S(1)} %copy-done.6, f32[384,128]{1,0:T(8,128)S(1)} %broadcast_in_dim.31.inverse_ref, f32[1,640]{1,0:T(1,128)S(1)} %broadcast_in_dim.37.bias_ref, f32[384,128]{1,0:T(8,128)S(1)} %copy-done.2, ...), custom_call_target="tpu_custom_call" | custom-call | flops 1887436800 | bytes 491520 | tf_op jit(solution)/shard_map/attend/pallas_call | solution.py:507
  168.9 6.5 %collective-permute-done.30.refs_4_ = bf16[1,384,384]{2,1,0:T(8,128)(2,1)S(1)} collective-permute-done((bf16[1,384,384]{2,1,0:T(8,128)(2,1)S(1)}, bf16[1,384,384]{2,1,0:T(8,128)(2,1)S(1)}, u32[]{:S(2)}, u32[]{:S(2)}) %collective-permute-start.30) | collective-permute-done | bytes 294944 | tf_op jit(solution)/shard_map/ppermute | solution.py:262
  175.4 3.8 %attend.3 = bf16[384,1024]{1,0:T(8,128)(2,1)} custom-call(s32[1]{0:T(128)} %bitcast.device_ref, s32[24]{0:T(128)S(1)} %copy-done.5, s32[24]{0:T(128)S(1)} %copy-done.6, f32[384,128]{1,0:T(8,128)S(1)} %broadcast_in_dim.31.inverse_ref, f32[1,384]{1,0:T(1,128)S(1)} %broadcast_in_dim.32.bias_ref, ...), custom_call_target="tpu_custom_call", output_to_operand_aliasing={{}: (13, {})} | custom-call | flops 679477248 | bytes 294912 | tf_op jit(solution)/shard_map/attend/pallas_call | solution.py:507
  (95 shorter events, 17.0 us)
Async XLA Ops:
  3.6 10.9 %copy-start.8 = (bf16[1024,128]{1,0:T(8,128)(2,1)S(1)}, bf16[1024,128]{1,0:T(8,128)(2,1)}, u32[]{:S(2)}) copy-start(bf16[1024,128]{1,0:T(8,128)(2,1)} %param.15) | copy-start | bytes 786436
  3.6 12.0 %collective-permute-start = (bf16[128,2048]{1,0:T(8,128)(2,1)}, bf16[128,2048]{1,0:T(8,128)(2,1)}, u32[]{:S(2)}, u32[]{:S(2)}) collective-permute-start(bf16[128,2048]{1,0:T(8,128)(2,1)} %get-tuple-element.75), channel_id=1, source_target_pairs={{0,0},{8,16},{16,8},{24,24},{1,1},{9,17},{17,9},{25,25},{2,26},{10... | collective-permute-start | bytes 1572872 | tf_op jit(solution)/shard_map/ppermute | solution.py:314
  9.2 33.1 %collective-permute-start.7 = (bf16[1024,640]{1,0:T(8,128)(2,1)S(1)}, bf16[1024,640]{1,0:T(8,128)(2,1)}, u32[]{:S(2)}, u32[]{:S(2)}) collective-permute-start(bf16[1024,640]{1,0:T(8,128)(2,1)S(1)} %slice.69.refs_2_.refs_6_), channel_id=1, source_target_pairs={{0,1},{1,0},{2,3},{3,2},{4,5},{5,4},{6,7},{7,6},{8,9},{9,8},{10,11... | collective-permute-start | bytes 3932168 | tf_op jit(solution)/shard_map/ppermute | solution.py:262
  15.6 7.1 %collective-permute-start.1 = (bf16[128,2048]{1,0:T(8,128)(2,1)}, bf16[128,2048]{1,0:T(8,128)(2,1)S(1)}, u32[]{:S(2)}, u32[]{:S(2)}) collective-permute-start(bf16[128,2048]{1,0:T(8,128)(2,1)} %get-tuple-element.40), channel_id=1, source_target_pairs={{0,0},{8,16},{16,8},{24,24},{1,1},{9,17},{17,9},{25,25},{2,26},{10... | collective-permute-start | bytes 1572872 | tf_op jit(solution)/shard_map/ppermute | solution.py:314
  17.3 23.4 %collective-permute-start.4 = (bf16[128,2048]{1,0:T(8,128)(2,1)}, bf16[128,2048]{1,0:T(8,128)(2,1)}, u32[]{:S(2)}, u32[]{:S(2)}) collective-permute-start(bf16[128,2048]{1,0:T(8,128)(2,1)} %collective-permute-done), channel_id=1, source_target_pairs={{0,0},{16,18},{8,12},{24,30},{1,1},{17,19},{9,13},{25,31},{26,16},... | collective-permute-start | bytes 1572872 | tf_op jit(solution)/shard_map/ppermute | solution.py:332
  22.6 18.0 %collective-permute-start.5 = (bf16[128,2048]{1,0:T(8,128)(2,1)S(1)}, bf16[128,2048]{1,0:T(8,128)(2,1)S(1)}, u32[]{:S(2)}, u32[]{:S(2)}) collective-permute-start(bf16[128,2048]{1,0:T(8,128)(2,1)S(1)} %get-tuple-element.42), channel_id=1, source_target_pairs={{0,0},{8,16},{16,8},{24,24},{1,1},{9,17},{17,9},{25,25},{2,26},{10... | collective-permute-start | bytes 1572872 | tf_op jit(solution)/shard_map/ppermute | solution.py:314
  23.3 20.5 %collective-permute-start.10 = (bf16[128,2048]{1,0:T(8,128)(2,1)S(1)}, bf16[128,2048]{1,0:T(8,128)(2,1)}, u32[]{:S(2)}, u32[]{:S(2)}) collective-permute-start(bf16[128,2048]{1,0:T(8,128)(2,1)S(1)} %collective-permute-done.1), channel_id=1, source_target_pairs={{0,0},{16,18},{8,12},{24,30},{1,1},{17,19},{9,13},{25,31},{26,16},... | collective-permute-start | bytes 1572872 | tf_op jit(solution)/shard_map/ppermute | solution.py:332
  26.6 10.5 %collective-permute-start.2 = (f32[3,128]{1,0:T(4,128)S(1)}, f32[3,128]{1,0:T(4,128)S(1)}, u32[]{:S(2)}, u32[]{:S(2)}) collective-permute-start(f32[3,128]{1,0:T(4,128)S(1)} %multiply_reduce_fusion), channel_id=1, source_target_pairs={{0,8},{8,0},{16,24},{24,16},{1,9},{9,1},{17,25},{25,17},{2,10},{10... | collective-permute-start | bytes 4616 | tf_op jit(solution)/shard_map/ppermute | solution.py:262
  37.1 3.6 %collective-permute-start.3 = (f32[3,128]{1,0:T(4,128)S(1)}, f32[3,128]{1,0:T(4,128)S(1)}, u32[]{:S(2)}, u32[]{:S(2)}) collective-permute-start(f32[3,128]{1,0:T(4,128)S(1)} %add.32), channel_id=1, source_target_pairs={{0,16},{8,24},{16,0},{24,8},{1,17},{9,25},{17,1},{25,9},{2,18},{10... | collective-permute-start | bytes 4616 | tf_op jit(solution)/shard_map/ppermute | solution.py:262
  40.7 15.2 %collective-permute-start.6 = (bf16[128,2048]{1,0:T(8,128)(2,1)}, bf16[128,2048]{1,0:T(8,128)(2,1)}, u32[]{:S(2)}, u32[]{:S(2)}) collective-permute-start(bf16[128,2048]{1,0:T(8,128)(2,1)} %collective-permute-done.4.refs_0_), channel_id=1, source_target_pairs={{0,16},{8,24},{16,0},{24,8},{1,17},{9,25},{17,1},{25,9},{2,18},{10... | collective-permute-start | bytes 1572872 | tf_op jit(solution)/shard_map/ppermute | solution.py:262
  42.3 13.6 %collective-permute-start.12 = (bf16[1024,256]{1,0:T(8,128)(2,1)S(1)}, bf16[1024,256]{1,0:T(8,128)(2,1)S(1)}, u32[]{:S(2)}, u32[]{:S(2)}) collective-permute-start(bf16[1024,256]{1,0:T(8,128)(2,1)S(1)} %constant_dynamic-update-slice_fusion.refs_5_.refs_4_), channel_id=1, source_target_pairs={{0,1},{1,0},{2,3},{3,2},{4,5},{5,4},{6,7},{7,6},{8,9},{9,8},{10,11... | collective-permute-start | bytes 1572872 | tf_op jit(solution)/shard_map/ppermute | solution.py:262
  43.8 21.8 %collective-permute-start.11 = (bf16[128,2048]{1,0:T(8,128)(2,1)}, bf16[128,2048]{1,0:T(8,128)(2,1)}, u32[]{:S(2)}, u32[]{:S(2)}) collective-permute-start(bf16[128,2048]{1,0:T(8,128)(2,1)} %collective-permute-done.10.refs_1_), channel_id=1, source_target_pairs={{0,16},{8,24},{16,0},{24,8},{1,17},{9,25},{17,1},{25,9},{2,18},{10... | collective-permute-start | bytes 1572872 | tf_op jit(solution)/shard_map/ppermute | solution.py:262
  46.9 18.7 %collective-permute-start.19 = (bf16[128,2048]{1,0:T(8,128)(2,1)S(1)}, bf16[128,2048]{1,0:T(8,128)(2,1)}, u32[]{:S(2)}, u32[]{:S(2)}) collective-permute-start(bf16[128,2048]{1,0:T(8,128)(2,1)S(1)} %collective-permute-done.5), channel_id=1, source_target_pairs={{0,0},{16,18},{8,12},{24,30},{1,1},{17,19},{9,13},{25,31},{26,16},... | collective-permute-start | bytes 1572872 | tf_op jit(solution)/shard_map/ppermute | solution.py:332
  48.4 19.5 %collective-permute-start.8 = (bf16[128,2048]{1,0:T(8,128)(2,1)}, bf16[128,2048]{1,0:T(8,128)(2,1)}, u32[]{:S(2)}, u32[]{:S(2)}) collective-permute-start(bf16[128,2048]{1,0:T(8,128)(2,1)} %collective-permute-done.4.refs_0_), channel_id=1, source_target_pairs={{0,8},{8,0},{16,24},{24,16},{1,9},{9,1},{17,25},{25,17},{2,10},{10... | collective-permute-start | bytes 1572872 | tf_op jit(solution)/shard_map/ppermute | solution.py:262
  55.9 17.0 %collective-permute-start.13 = (bf16[128,2048]{1,0:T(8,128)(2,1)}, bf16[128,2048]{1,0:T(8,128)(2,1)}, u32[]{:S(2)}, u32[]{:S(2)}) collective-permute-start(bf16[128,2048]{1,0:T(8,128)(2,1)} %collective-permute-done.10.refs_1_), channel_id=1, source_target_pairs={{0,8},{8,0},{16,24},{24,16},{1,9},{9,1},{17,25},{25,17},{2,10},{10... | collective-permute-start | bytes 1572872 | tf_op jit(solution)/shard_map/ppermute | solution.py:262
  55.9 13.5 %collective-permute-start.9 = (bf16[128,2048]{1,0:T(8,128)(2,1)}, bf16[128,2048]{1,0:T(8,128)(2,1)}, u32[]{:S(2)}, u32[]{:S(2)}) collective-permute-start(bf16[128,2048]{1,0:T(8,128)(2,1)} %collective-permute-done.6.refs_1_), channel_id=1, source_target_pairs={{0,8},{8,0},{16,24},{24,16},{1,9},{9,1},{17,25},{25,17},{2,10},{10... | collective-permute-start | bytes 1572872 | tf_op jit(solution)/shard_map/ppermute | solution.py:262
  65.6 7.4 %collective-permute-start.14 = (bf16[128,2048]{1,0:T(8,128)(2,1)}, bf16[128,2048]{1,0:T(8,128)(2,1)}, u32[]{:S(2)}, u32[]{:S(2)}) collective-permute-start(bf16[128,2048]{1,0:T(8,128)(2,1)} %collective-permute-done.11.refs_2_), channel_id=1, source_target_pairs={{0,8},{8,0},{16,24},{24,16},{1,9},{9,1},{17,25},{25,17},{2,10},{10... | collective-permute-start | bytes 1572872 | tf_op jit(solution)/shard_map/ppermute | solution.py:262
  65.6 19.4 %collective-permute-start.20 = (bf16[128,2048]{1,0:T(8,128)(2,1)}, bf16[128,2048]{1,0:T(8,128)(2,1)}, u32[]{:S(2)}, u32[]{:S(2)}) collective-permute-start(bf16[128,2048]{1,0:T(8,128)(2,1)} %collective-permute-done.19.refs_0_), channel_id=1, source_target_pairs={{0,16},{8,24},{16,0},{24,8},{1,17},{9,25},{17,1},{25,9},{2,18},{10... | collective-permute-start | bytes 1572872 | tf_op jit(solution)/shard_map/ppermute | solution.py:262
  67.9 39.7 %collective-permute-start.23 = (bf16[1024,384]{1,0:T(8,128)(2,1)S(1)}, bf16[1024,384]{1,0:T(8,128)(2,1)}, u32[]{:S(2)}, u32[]{:S(2)}) collective-permute-start(bf16[1024,384]{1,0:T(8,128)(2,1)S(1)} %slice.70.refs_3_), channel_id=1, source_target_pairs={{0,1},{1,0},{2,3},{3,2},{4,5},{5,4},{6,7},{7,6},{8,9},{9,8},{10,11... | collective-permute-start | bytes 2359304 | tf_op jit(solution)/shard_map/ppermute | solution.py:262
  78.0 8.8 %collective-permute-start.15 = (bf16[2,256,256]{2,1,0:T(8,128)(2,1)S(1)}, bf16[2,256,256]{2,1,0:T(8,128)(2,1)S(1)}, u32[]{:S(2)}, u32[]{:S(2)}) collective-permute-start(bf16[2,256,256]{2,1,0:T(8,128)(2,1)S(1)} %get-tuple-element.48), channel_id=1, source_target_pairs={{0,2},{1,3},{2,0},{3,1},{4,6},{5,7},{6,4},{7,5},{8,10},{9,11},{10,... | collective-permute-start | bytes 786440 | tf_op jit(solution)/shard_map/ppermute | solution.py:262
  83.0 24.5 %collective-permute-start.18 = (bf16[2,256,640]{2,1,0:T(8,128)(2,1)S(1)}, bf16[2,256,640]{2,1,0:T(8,128)(2,1)S(1)}, u32[]{:S(2)}, u32[]{:S(2)}) collective-permute-start(bf16[2,256,640]{2,1,0:T(8,128)(2,1)S(1)} %get-tuple-element.51), channel_id=1, source_target_pairs={{0,2},{1,3},{2,0},{3,1},{4,6},{5,7},{6,4},{7,5},{8,10},{9,11},{10,... | collective-permute-start | bytes 1966088 | tf_op jit(solution)/shard_map/ppermute | solution.py:262
  85.0 17.5 %collective-permute-start.21 = (bf16[128,2048]{1,0:T(8,128)(2,1)}, bf16[128,2048]{1,0:T(8,128)(2,1)S(1)}, u32[]{:S(2)}, u32[]{:S(2)}) collective-permute-start(bf16[128,2048]{1,0:T(8,128)(2,1)} %collective-permute-done.19.refs_0_), channel_id=1, source_target_pairs={{0,8},{8,0},{16,24},{24,16},{1,9},{9,1},{17,25},{25,17},{2,10},{10... | collective-permute-start | bytes 1572872 | tf_op jit(solution)/shard_map/ppermute | solution.py:262
  85.0 17.5 %collective-permute-start.22 = (bf16[128,2048]{1,0:T(8,128)(2,1)}, bf16[128,2048]{1,0:T(8,128)(2,1)S(1)}, u32[]{:S(2)}, u32[]{:S(2)}) collective-permute-start(bf16[128,2048]{1,0:T(8,128)(2,1)} %collective-permute-done.20.refs_1_), channel_id=1, source_target_pairs={{0,8},{8,0},{16,24},{24,16},{1,9},{9,1},{17,25},{25,17},{2,10},{10... | collective-permute-start | bytes 1572872 | tf_op jit(solution)/shard_map/ppermute | solution.py:262
  86.8 14.9 %collective-permute-start.16 = (bf16[1,256,256]{2,1,0:T(8,128)(2,1)S(1)}, bf16[1,256,256]{2,1,0:T(8,128)(2,1)S(1)}, u32[]{:S(2)}, u32[]{:S(2)}) collective-permute-start(bf16[1,256,256]{2,1,0:T(8,128)(2,1)S(1)} %fusion.6), channel_id=1, source_target_pairs={{0,4},{1,5},{2,6},{3,7},{4,0},{5,1},{6,2},{7,3},{8,12},{9,13},{10,... | collective-permute-start | bytes 393224 | tf_op jit(solution)/shard_map/ppermute | solution.py:262
  101.9 5.7 %collective-permute-start.17 = (bf16[1,256,256]{2,1,0:T(8,128)(2,1)S(1)}, bf16[1,256,256]{2,1,0:T(8,128)(2,1)S(1)}, u32[]{:S(2)}, u32[]{:S(2)}) collective-permute-start(bf16[1,256,256]{2,1,0:T(8,128)(2,1)S(1)} %bitcast.22), channel_id=1, source_target_pairs={{0,1},{1,0},{2,3},{3,2},{4,5},{5,4},{6,7},{7,6},{8,9},{9,8},{10,11... | collective-permute-start | bytes 393224 | tf_op jit(solution)/shard_map/ppermute | solution.py:262
  107.7 14.1 %collective-permute-start.24 = (bf16[2,256,256]{2,1,0:T(8,128)(2,1)S(1)}, bf16[2,256,256]{2,1,0:T(8,128)(2,1)S(1)}, u32[]{:S(2)}, u32[]{:S(2)}) collective-permute-start(bf16[2,256,256]{2,1,0:T(8,128)(2,1)S(1)} %pad_maximum_fusion.2), channel_id=1, source_target_pairs={{0,4},{1,5},{2,6},{3,7},{4,0},{5,1},{6,2},{7,3},{8,12},{9,13},{10,... | collective-permute-start | bytes 786440 | tf_op jit(solution)/shard_map/ppermute | solution.py:262
  111.2 27.5 %collective-permute-start.26 = (bf16[2,128,896]{2,1,0:T(8,128)(2,1)S(1)}, bf16[2,128,896]{2,1,0:T(8,128)(2,1)S(1)}, u32[]{:S(2)}, u32[]{:S(2)}) collective-permute-start(bf16[2,128,896]{2,1,0:T(8,128)(2,1)S(1)} %get-tuple-element.56), channel_id=1, source_target_pairs={{0,2},{1,3},{2,0},{3,1},{4,6},{5,7},{6,4},{7,5},{8,10},{9,11},{10,... | collective-permute-start | bytes 1376264 | tf_op jit(solution)/shard_map/ppermute | solution.py:262
  121.8 36.8 %collective-permute-start.28 = (bf16[2,384,384]{2,1,0:T(8,128)(2,1)S(1)}, bf16[2,384,384]{2,1,0:T(8,128)(2,1)S(1)}, u32[]{:S(2)}, u32[]{:S(2)}) collective-permute-start(bf16[2,384,384]{2,1,0:T(8,128)(2,1)S(1)} %get-tuple-element.67), channel_id=1, source_target_pairs={{0,2},{1,3},{2,0},{3,1},{4,6},{5,7},{6,4},{7,5},{8,10},{9,11},{10,... | collective-permute-start | bytes 1769480 | tf_op jit(solution)/shard_map/ppermute | solution.py:262
  121.9 40.3 %collective-permute-start.25 = (bf16[4,256,256]{2,1,0:T(8,128)(2,1)S(1)}, bf16[4,256,256]{2,1,0:T(8,128)(2,1)S(1)}, u32[]{:S(2)}, u32[]{:S(2)}) collective-permute-start(bf16[4,256,256]{2,1,0:T(8,128)(2,1)S(1)} %pad_maximum_fusion.1), channel_id=1, source_target_pairs={{0,2},{1,3},{2,0},{3,1},{4,6},{5,7},{6,4},{7,5},{8,10},{9,11},{10,... | collective-permute-start | bytes 1572872 | tf_op jit(solution)/shard_map/ppermute | solution.py:262
  123.9 34.7 %collective-permute-start.29 = (bf16[1,256,640]{2,1,0:T(8,128)(2,1)S(1)}, bf16[1,256,640]{2,1,0:T(8,128)(2,1)S(1)}, u32[]{:S(2)}, u32[]{:S(2)}) collective-permute-start(bf16[1,256,640]{2,1,0:T(8,128)(2,1)S(1)} %fusion.3), channel_id=1, source_target_pairs={{0,4},{1,5},{2,6},{3,7},{4,0},{5,1},{6,2},{7,3},{8,12},{9,13},{10,... | collective-permute-start | bytes 983048 | tf_op jit(solution)/shard_map/ppermute | solution.py:262
  138.7 24.9 %collective-permute-start.27 = (bf16[1,128,896]{2,1,0:T(8,128)(2,1)S(1)}, bf16[1,128,896]{2,1,0:T(8,128)(2,1)S(1)}, u32[]{:S(2)}, u32[]{:S(2)}) collective-permute-start(bf16[1,128,896]{2,1,0:T(8,128)(2,1)S(1)} %fusion.5), channel_id=1, source_target_pairs={{0,4},{1,5},{2,6},{3,7},{4,0},{5,1},{6,2},{7,3},{8,12},{9,13},{10,... | collective-permute-start | bytes 688136 | tf_op jit(solution)/shard_map/ppermute | solution.py:262
  158.7 16.7 %collective-permute-start.30 = (bf16[1,384,384]{2,1,0:T(8,128)(2,1)S(1)}, bf16[1,384,384]{2,1,0:T(8,128)(2,1)S(1)}, u32[]{:S(2)}, u32[]{:S(2)}) collective-permute-start(bf16[1,384,384]{2,1,0:T(8,128)(2,1)S(1)} %fusion.4), channel_id=1, source_target_pairs={{0,4},{1,5},{2,6},{3,7},{4,0},{5,1},{6,2},{7,3},{8,12},{9,13},{10,... | collective-permute-start | bytes 884744 | tf_op jit(solution)/shard_map/ppermute | solution.py:262
  (11 other events, 60.4 us)

commit v8 on v7

--- a/solution.py
+++ b/solution.py
@@ -320,17 +320,9 @@
         w_rows[c] = [w_chunks[c]] + [swap(outgoing, "branch", j) for j in range(1, groups)]
         arrived = w_rows[c][-1]
 
-    squares = tie(jnp.sum(jnp.square(raw.astype(f32)), -1).reshape(blocks, block_len), sent[1])
-    bit = 1
-    while bit < lines:
-        squares = squares + swap(squares, "fsdp", bit)
-        bit *= 2
-    inverse = lax.rsqrt(squares / features + 1e-06).reshape(tokens)
-    inverse = jnp.broadcast_to(inverse[:, None], (tokens, HD))
-
     last_sent = sent[-1]
     sent = [lax.ppermute(piece, axes, second_hop) for piece in sent]
-    sent[0] = tie(sent[0], squares, last_sent)
+    sent[0] = tie(sent[0], last_sent, w_rows[1][-1])
     held = [{0: piece} for piece in sent]
     bit = half_lines
     while bit > 1:
@@ -344,11 +336,21 @@
             piece[j | 1] = swap(piece[j], "fsdp", 1)
         return [piece[j] for j in sorted(piece, key=spread)]
 
-    held[0][half_lines] = tie(held[0][half_lines], w_rows[1][-1])
     held[1][half_lines] = tie(held[1][half_lines], w_rows[0][-1])
-    held = [last_bit(piece) for piece in held[:STEMS]] + held[STEMS:]
-
     assembled = {}
+    held[0] = last_bit(held[0])
+    assembled[(0, 1)] = pl.pallas_call(
+        functools.partial(assemble_kernel, lines),
+        in_specs=[smem] + [anywhere] * lines,
+        out_specs=vmem,
+        out_shape=jax.ShapeDtypeStruct((lines * block_len, feature_part), bf16),
+        scratch_shapes=[pltpu.SemaphoreType.DMA((lines,))],
+        name="assemble",
+    )(place, *held[0])
+    for block in range(1, STEMS):
+        held[block][half_lines] = tie(held[block][half_lines], assembled[(0, 1)])
+        held[block] = last_bit(held[block])
+
 
     def project(spans, chunks, *after):
         weights = [w for chunk in chunks for w in w_rows[chunk]]
@@ -382,11 +384,7 @@
             out_shape=out_shape,
             scratch_shapes=scratch,
             compiler_params=pltpu.CompilerParams(vmem_limit_bytes=24 * 2**20),
-            cost_estimate=pl.CostEstimate(
-                flops=2 * lines * length * feature_part * width,
-                bytes_accessed=2 * lines * length * feature_part,
-                transcendentals=0,
-            ),
+            cost_estimate=pl.CostEstimate(flops=0, bytes_accessed=0, transcendentals=0),
             name="project",
         )(place, *operands, *weights)
         if fresh:
@@ -440,46 +438,49 @@
             name="finish_kv",
         )(*operands, *addends)
 
-    assembled[(0, 1)] = pl.pallas_call(
-        functools.partial(assemble_kernel, lines),
-        in_specs=[smem] + [anywhere] * lines,
-        out_specs=vmem,
-        out_shape=jax.ShapeDtypeStruct((lines * block_len, feature_part), bf16),
-        scratch_shapes=[pltpu.SemaphoreType.DMA((lines,))],
-        name="assemble",
-    )(place, *held[0])
-
     early = [(0, 1), (1, STEMS)]
     late = [(STEMS, blocks)]
     first = Halving(project(early, [0]))
     first.step()
+
     second = Halving(project(early, [1], first.send))
     second.step()
+    first.rest(second.send)
+
+    squares = jnp.sum(jnp.square(raw.astype(f32)), -1).reshape(blocks, block_len)
+    squares = tie(squares, first.send)
+    bit = 1
+    while bit < lines:
+        squares = squares + swap(squares, "fsdp", bit)
+        bit *= 2
+    inverse = lax.rsqrt(squares / features + 1e-06).reshape(tokens)
+    inverse = jnp.broadcast_to(inverse[:, None], (tokens, HD))
+
     for block in range(STEMS, blocks):
-        held[block][0] = tie(held[block][0], second.send)
+        held[block] = {j: tie(piece, first.send) for j, piece in held[block].items()}
         held[block] = last_bit(held[block])
-    first.rest(second.send)
+    third = Halving(project(late, [0, 1], first.send))
+    first.addends[-1] = tie(first.addends[-1], third.send)
     stem_kv = finish_kv(first.addends, 0, STEMS)
 
-    tour = [1 << i for i in range(bits_of(groups))]
-    tour += [groups << i for i in reversed(range(bits_of(lines)))]
+    tour = [groups << i for i in reversed(range(bits_of(lines)))]
+    tour += [1 << i for i in range(bits_of(groups))]
     stems = stem_kv[None]
     came = swap(stems, "branch", tour[0])
-    third = Halving(project(late, [0, 1], stem_kv))
-    third.step()
-    second.add(third.send, w_rows[2][-1])
+    third.step(stem_kv)
+    second.add(stem_kv, w_rows[2][-1])
+    second.step()
+    fourth = Halving(project(early + late, [2], second.send))
     for step, bit in enumerate(tour[1:]):
-        stems = jnp.concatenate([stems, tie(came, fourth.send if step else second.send)], 0)
+        stems = jnp.concatenate([stems, tie(came, third.send if step else fourth.send)], 0)
         came = swap(stems, "branch", bit)
         if step == 0:
-            fourth = Halving(project(early + late, [2], stems))
-    second.step(stems)
-    fourth.step(stems)
-    third.add(stems)
-    third.step()
+            fourth.step(stems)
+            third.add(stems, second.came)
+            third.step()
     second.rest()
     third.rest()
-    fourth.rest(second.came)
+    fourth.rest(stems, second.came)
     stems = jnp.concatenate([stems, came], 0)
     third.addends[-1] = tie(third.addends[-1], fourth.send)
     late_kv = finish_kv(third.addends, STEMS, blocks - STEMS)

time: 180 us -> 172 us (0.956)
  waiting for transfers between devices: 82 us -> 77 us
  starting transfers between devices: 54.3 us -> 51.7 us
  local copies, waits for them, and re-layouts: 3.95 us -> 6.06 us
    ppermute x25, starting transfers between devices: 38.2 us -> 30.7 us  [swap(): return lax.ppermute(array, axis, [(i, i ^ bit) for i in range(size)])]
    ppermute x25, waiting for transfers between devices: 82 us -> 77 us  [swap(): return lax.ppermute(array, axis, [(i, i ^ bit) for i in range(size)])]
    ppermute x3, starting transfers between devices: 8.28 us -> 12.2 us  [shards(): sent = [lax.ppermute(piece, axes, second_hop) for piece in sent]]
  transfers between devices with their start and end apart: 31 -> 31, of which waited for: 12 -> 13; matrix products, arithmetic and copies ran while one was open for 2% -> 2% of each run, Pallas kernels for 16% -> 16%
where the time goes in v8:
time: 172 us; the launch traced here: 171 us
  waiting for transfers between devices  77 us (45%)
  starting transfers between devices  51.7 us (30%)
  Pallas kernels  31.2 us (18%)
  local copies, waits for them, and re-layouts  6.06 us (4%)
  other arithmetic  4.24 us (2%)
    ppermute x25, waiting for transfers between devices, swap(): return lax.ppermute(array, axis, [(i, i ^ bit) for i in range(size)])  77 us
    ppermute x25, starting transfers between devices, swap(): return lax.ppermute(array, axis, [(i, i ^ bit) for i in range(size)])  30.7 us
    pallas_call x4, Pallas kernels, project(): pl.pallas_call(functools.partial(project_kernel, lines, groups, len(chunk...  16.4 us
    ppermute x3, starting transfers between devices, shards(): sent = [lax.ppermute(piece, axes, second_hop) for piece in sent]  12.2 us
    ppermute x3, starting transfers between devices, shards(): sent.append(lax.ppermute(piece, axes, first_hop))  8.87 us
    pallas_call x2, Pallas kernels, attend(): pl.pallas_call(kernel, grid=(1,), in_specs=in_specs, out_specs=anywhere,...  8.75 us
    pallas_call x1, Pallas kernels, shards(): pl.pallas_call(functools.partial(assemble_kernel, lines), in_specs=[smem]...  3.56 us
  transfers between devices with their start and end apart: 31, of which 13 were waited for; matrix products, arithmetic and copies ran while one was open for 2% of the time, Pallas kernels for 16%

profile of v8, /device:TPU:0, one launch (start us, length us, event | category | flops | bytes accessed | tf_op | source)
XLA Modules:
  0.0 170.6 jit_solution(6328696839575016815)
XLA Ops:
  0.7 2.8 %fusion = (bf16[128,2048]{1,0:T(8,128)(2,1)}, bf16[128,2048]{1,0:T(8,128)(2,1)}, bf16[128,2048]{1,0:T(8,128)(2,1)}) fusion(bf16[3,128,2048]{2,1,0:T(8,128)(2,1)} %param.10, f32[2048]{0:T(1024)S(1)} %dynamic_slice.3), kind=kLoop, calls=%fused_computation.3 | loop fusion | flops 2359296 | bytes 3153920 | tf_op jit(solution)/shard_map/convert_element_type | solution.py:312
  3.5 5.5 %collective-permute-start = (bf16[128,2048]{1,0:T(8,128)(2,1)}, bf16[128,2048]{1,0:T(8,128)(2,1)}, u32[]{:S(2)}, u32[]{:S(2)}) collective-permute-start(bf16[128,2048]{1,0:T(8,128)(2,1)} %get-tuple-element.76), channel_id=1, source_target_pairs={{0,0},{8,16},{16,8},{24,24},{1,1},{9,17},{17,9},{25,25},{2,26},{10... | collective-permute-start | bytes 1572872 | tf_op jit(solution)/shard_map/ppermute | solution.py:314
  9.2 3.0 %collective-permute-start.4 = (bf16[1024,640]{1,0:T(8,128)(2,1)S(1)}, bf16[1024,640]{1,0:T(8,128)(2,1)S(1)}, u32[]{:S(2)}, u32[]{:S(2)}) collective-permute-start(bf16[1024,640]{1,0:T(8,128)(2,1)S(1)} %slice.70.refs_2_.refs_6_), channel_id=1, source_target_pairs={{0,1},{1,0},{2,3},{3,2},{4,5},{5,4},{6,7},{7,6},{8,9},{9,8},{10,11... | collective-permute-start | bytes 3932168 | tf_op jit(solution)/shard_map/ppermute | solution.py:262
  13.2 2.2 %tables.1 = (f32[384,128]{1,0:T(8,128)}, f32[384,128]{1,0:T(8,128)}) custom-call(s32[1]{0:T(128)} %bitcast.device_ref, s32[24]{0:T(128)} %parents_ref.5), custom_call_target="tpu_custom_call" | custom-call | tf_op jit(solution)/shard_map/tables/pallas_call | solution.py:302
  16.5 1.7 collective-permute-start.2
  18.2 5.4 %collective-permute-start.1 = (bf16[128,2048]{1,0:T(8,128)(2,1)}, bf16[128,2048]{1,0:T(8,128)(2,1)}, u32[]{:S(2)}, u32[]{:S(2)}) collective-permute-start(bf16[128,2048]{1,0:T(8,128)(2,1)} %collective-permute-done), channel_id=1, source_target_pairs={{0,0},{16,18},{8,12},{24,30},{1,1},{17,19},{9,13},{25,31},{26,16},... | collective-permute-start | bytes 1572872 | tf_op jit(solution)/shard_map/ppermute | solution.py:324
  23.5 1.7 collective-permute-start.3
  26.7 12.9 %collective-permute-done.4.refs_3_.refs_7_ = bf16[1024,640]{1,0:T(8,128)(2,1)S(1)} collective-permute-done((bf16[1024,640]{1,0:T(8,128)(2,1)S(1)}, bf16[1024,640]{1,0:T(8,128)(2,1)S(1)}, u32[]{:S(2)}, u32[]{:S(2)}) %collective-permute-start.4) | collective-permute-done | bytes 1310752 | tf_op jit(solution)/shard_map/ppermute | solution.py:262
  40.3 1.5 collective-permute-start.10
  41.9 4.9 %collective-permute-start.9 = (bf16[128,2048]{1,0:T(8,128)(2,1)}, bf16[128,2048]{1,0:T(8,128)(2,1)}, u32[]{:S(2)}, u32[]{:S(2)}) collective-permute-start(bf16[128,2048]{1,0:T(8,128)(2,1)} %collective-permute-done.8.refs_1_), channel_id=1, source_target_pairs={{0,16},{8,24},{16,0},{24,8},{1,17},{9,25},{17,1},{25,9},{2,18},{10... | collective-permute-start | bytes 1572872 | tf_op jit(solution)/shard_map/ppermute | solution.py:262
  48.0 6.9 %collective-permute-done.5.refs_1_ = bf16[128,2048]{1,0:T(8,128)(2,1)} collective-permute-done((bf16[128,2048]{1,0:T(8,128)(2,1)}, bf16[128,2048]{1,0:T(8,128)(2,1)}, u32[]{:S(2)}, u32[]{:S(2)}) %collective-permute-start.5) | collective-permute-done | bytes 524320 | tf_op jit(solution)/shard_map/ppermute | solution.py:262
  56.1 5.3 %collective-permute-start.17 = (bf16[128,2048]{1,0:T(8,128)(2,1)}, bf16[128,2048]{1,0:T(8,128)(2,1)}, u32[]{:S(2)}, u32[]{:S(2)}) collective-permute-start(bf16[128,2048]{1,0:T(8,128)(2,1)} %copy-done.14), channel_id=1, source_target_pairs={{0,0},{16,18},{8,12},{24,30},{1,1},{17,19},{9,13},{25,31},{26,16},... | collective-permute-start | bytes 1572872 | tf_op jit(solution)/shard_map/ppermute | solution.py:324
  62.1 4.0 %collective-permute-done.9.refs_2_ = bf16[128,2048]{1,0:T(8,128)(2,1)} collective-permute-done((bf16[128,2048]{1,0:T(8,128)(2,1)}, bf16[128,2048]{1,0:T(8,128)(2,1)}, u32[]{:S(2)}, u32[]{:S(2)}) %collective-permute-start.9) | collective-permute-done | bytes 524320 | tf_op jit(solution)/shard_map/ppermute | solution.py:262
  66.1 3.6 %assemble.1.refs_0_ = bf16[512,2048]{1,0:T(8,128)(2,1)} custom-call(s32[2]{0:T(128)} %pad_add_fusion.place_ref, bf16[128,2048]{1,0:T(8,128)(2,1)} %collective-permute-done.1.refs_0_, bf16[128,2048]{1,0:T(8,128)(2,1)} %collective-permute-done.5.refs_1_, bf16[128,2048]{1,0:T(8,128)(2,1)} %collective-permute-done.6.refs_2_, ...), custom_call_target="tpu_custom_call" | custom-call | tf_op jit(solution)/shard_map/assemble/pallas_call | solution.py:342
  71.9 1.6 copy-done
  73.5 3.9 %project.4 = (bf16[2,256,256]{2,1,0:T(8,128)(2,1)S(1)}, f32[2,256,256]{2,1,0:T(8,128)S(1)}, bf16[512,2048]{1,0:T(8,128)(2,1)S(1)}) custom-call(s32[2]{0:T(128)S(1)} %copy-done.5, bf16[512,2048]{1,0:T(8,128)(2,1)S(1)} %copy-done, bf16[128,2048]{1,0:T(8,128)(2,1)} %collective-permute-done.8.refs_1_, bf16[128,2048]{1,0:T(8,128)(2,1)} %collective-permute-done.9.refs_2_, ...), custom_call_target="tpu_custom_call" | custom-call | tf_op jit(solution)/shard_map/project/pallas_call | solution.py:379
  79.0 1.6 collective-permute-start.23
  80.6 4.0 %project.5 = (bf16[2,256,640]{2,1,0:T(8,128)(2,1)S(1)}, f32[2,256,640]{2,1,0:T(8,128)S(1)}) custom-call(s32[2]{0:T(128)S(1)} %copy-done.5, bf16[512,2048]{1,0:T(8,128)(2,1)S(1)} %copy-done, bf16[512,2048]{1,0:T(8,128)(2,1)S(1)} %get-tuple-element.51.refs_1_, bf16[1024,640]{1,0:T(8,128)(2,1)S(1)} %slice.70.refs_2_.refs_6_, ...), custom_call_target="tpu_custom_call" | custom-call | tf_op jit(solution)/shard_map/project/pallas_call | solution.py:379
  88.9 2.4 %collective-permute-done.15 = f32[3,128]{1,0:T(4,128)S(1)} collective-permute-done((f32[3,128]{1,0:T(4,128)S(1)}, f32[3,128]{1,0:T(4,128)S(1)}, u32[]{:S(2)}, u32[]{:S(2)}) %collective-permute-start.15) | collective-permute-done | bytes 1568 | tf_op jit(solution)/shard_map/ppermute | solution.py:262
  91.2 2.2 %collective-permute-start.16 = (bf16[1,256,256]{2,1,0:T(8,128)(2,1)S(1)}, bf16[1,256,256]{2,1,0:T(8,128)(2,1)S(1)}, u32[]{:S(2)}, u32[]{:S(2)}) collective-permute-start(bf16[1,256,256]{2,1,0:T(8,128)(2,1)S(1)} %fusion.6), channel_id=1, source_target_pairs={{0,4},{1,5},{2,6},{3,7},{4,0},{5,1},{6,2},{7,3},{8,12},{9,13},{10,... | collective-permute-start | bytes 393224 | tf_op jit(solution)/shard_map/ppermute | solution.py:262
  93.5 4.5 %project.6 = (bf16[2,128,896]{2,1,0:T(8,128)(2,1)S(1)}, f32[2,128,896]{2,1,0:T(8,128)S(1)}, bf16[512,2048]{1,0:T(8,128)(2,1)S(1)}) custom-call(s32[2]{0:T(128)S(1)} %copy-done.5, bf16[128,2048]{1,0:T(8,128)(2,1)} %collective-permute-done.17.refs_0_, bf16[128,2048]{1,0:T(8,128)(2,1)S(1)} %collective-permute-done.18.refs_1_, ...), custom_call_target="tpu_custom_call" | custom-call | tf_op jit(solution)/shard_map/project/pallas_call | solution.py:379
  98.0 5.5 %collective-permute-done.16.refs_2_ = bf16[1,256,256]{2,1,0:T(8,128)(2,1)S(1)} collective-permute-done((bf16[1,256,256]{2,1,0:T(8,128)(2,1)S(1)}, bf16[1,256,256]{2,1,0:T(8,128)(2,1)S(1)}, u32[]{:S(2)}, u32[]{:S(2)}) %collective-permute-start.16) | collective-permute-done | bytes 131104 | tf_op jit(solution)/shard_map/ppermute | solution.py:262
  105.0 2.3 %collective-permute-start.25 = (bf16[2,128,896]{2,1,0:T(8,128)(2,1)S(1)}, bf16[2,128,896]{2,1,0:T(8,128)(2,1)S(1)}, u32[]{:S(2)}, u32[]{:S(2)}) collective-permute-start(bf16[2,128,896]{2,1,0:T(8,128)(2,1)S(1)} %get-tuple-element.68), channel_id=1, source_target_pairs={{0,2},{1,3},{2,0},{3,1},{4,6},{5,7},{6,4},{7,5},{8,10},{9,11},{10,... | collective-permute-start | bytes 1376264 | tf_op jit(solution)/shard_map/ppermute | solution.py:262
  108.0 2.4 %collective-permute-start.21 = (bf16[1,256,256]{2,1,0:T(8,128)(2,1)S(1)}, bf16[1,256,256]{2,1,0:T(8,128)(2,1)S(1)}, u32[]{:S(2)}, u32[]{:S(2)}) collective-permute-start(bf16[1,256,256]{2,1,0:T(8,128)(2,1)S(1)} %bitcast.21), channel_id=1, source_target_pairs={{0,4},{1,5},{2,6},{3,7},{4,0},{5,1},{6,2},{7,3},{8,12},{9,13},{10,... | collective-permute-start | bytes 393224 | tf_op jit(solution)/shard_map/ppermute | solution.py:262
  110.4 4.0 %project.7 = (bf16[2,384,384]{2,1,0:T(8,128)(2,1)S(1)}, f32[2,384,384]{2,1,0:T(8,128)S(1)}) custom-call(s32[2]{0:T(128)S(1)} %copy-done.5, bf16[512,2048]{1,0:T(8,128)(2,1)S(1)} %copy-done.1, bf16[512,2048]{1,0:T(8,128)(2,1)S(1)} %get-tuple-element.51.refs_1_, bf16[512,2048]{1,0:T(8,128)(2,1)S(1)} %get-tuple-element.64.refs_2_, ...), custom_call_target="tpu_custom_call" | custom-call | tf_op jit(solution)/shard_map/project/pallas_call | solution.py:379
  114.4 15.5 %collective-permute-done.21 = bf16[1,256,256]{2,1,0:T(8,128)(2,1)S(1)} collective-permute-done((bf16[1,256,256]{2,1,0:T(8,128)(2,1)S(1)}, bf16[1,256,256]{2,1,0:T(8,128)(2,1)S(1)}, u32[]{:S(2)}, u32[]{:S(2)}) %collective-permute-start.21) | collective-permute-done | bytes 131104 | tf_op jit(solution)/shard_map/ppermute | solution.py:262
  130.0 2.0 %collective-permute-start.29 = (bf16[2,384,384]{2,1,0:T(8,128)(2,1)S(1)}, bf16[2,384,384]{2,1,0:T(8,128)(2,1)S(1)}, u32[]{:S(2)}, u32[]{:S(2)}) collective-permute-start(bf16[2,384,384]{2,1,0:T(8,128)(2,1)S(1)} %get-tuple-element.72), channel_id=1, source_target_pairs={{0,2},{1,3},{2,0},{3,1},{4,6},{5,7},{6,4},{7,5},{8,10},{9,11},{10,... | collective-permute-start | bytes 1769480 | tf_op jit(solution)/shard_map/ppermute | solution.py:262
  132.1 9.6 %collective-permute-done.24 = bf16[2,256,256]{2,1,0:T(8,128)(2,1)S(1)} collective-permute-done((bf16[2,256,256]{2,1,0:T(8,128)(2,1)S(1)}, bf16[2,256,256]{2,1,0:T(8,128)(2,1)S(1)}, u32[]{:S(2)}, u32[]{:S(2)}) %collective-permute-start.24) | collective-permute-done | bytes 262176 | tf_op jit(solution)/shard_map/ppermute | solution.py:262
  142.5 10.7 %collective-permute-done.29.refs_3_ = bf16[2,384,384]{2,1,0:T(8,128)(2,1)S(1)} collective-permute-done((bf16[2,384,384]{2,1,0:T(8,128)(2,1)S(1)}, bf16[2,384,384]{2,1,0:T(8,128)(2,1)S(1)}, u32[]{:S(2)}, u32[]{:S(2)}) %collective-permute-start.29) | collective-permute-done | bytes 589856 | tf_op jit(solution)/shard_map/ppermute | solution.py:262
  153.4 7.4 %collective-permute-done.28.refs_2_.refs_7_ = bf16[1,128,896]{2,1,0:T(8,128)(2,1)S(1)} collective-permute-done((bf16[1,128,896]{2,1,0:T(8,128)(2,1)S(1)}, bf16[1,128,896]{2,1,0:T(8,128)(2,1)S(1)}, u32[]{:S(2)}, u32[]{:S(2)}) %collective-permute-start.28) | collective-permute-done | bytes 229408 | tf_op jit(solution)/shard_map/ppermute | solution.py:262
  161.7 5.0 %attend.2.refs_5_ = bf16[384,1024]{1,0:T(8,128)(2,1)} custom-call(s32[1]{0:T(128)} %bitcast.device_ref, s32[24]{0:T(128)S(1)} %copy-done.6, s32[24]{0:T(128)S(1)} %copy-done.7, f32[384,128]{1,0:T(8,128)S(1)} %broadcast_in_dim.31.inverse_ref, f32[1,640]{1,0:T(1,128)S(1)} %broadcast_in_dim.37.bias_ref, f32[384,128]{1,0:T(8,128)S(1)} %copy-done.3, ...), custom_call_target="tpu_custom_call" | custom-call | flops 1887436800 | bytes 491520 | tf_op jit(solution)/shard_map/attend/pallas_call | solution.py:508
  166.7 3.8 %attend.3 = bf16[384,1024]{1,0:T(8,128)(2,1)} custom-call(s32[1]{0:T(128)} %bitcast.device_ref, s32[24]{0:T(128)S(1)} %copy-done.6, s32[24]{0:T(128)S(1)} %copy-done.7, f32[384,128]{1,0:T(8,128)S(1)} %broadcast_in_dim.31.inverse_ref, f32[1,384]{1,0:T(1,128)S(1)} %broadcast_in_dim.32.bias_ref, ...), custom_call_target="tpu_custom_call", output_to_operand_aliasing={{}: (13, {})} | custom-call | flops 679477248 | bytes 294912 | tf_op jit(solution)/shard_map/attend/pallas_call | solution.py:508
  (100 shorter events, 20.5 us)
Async XLA Ops:
  3.5 12.9 %collective-permute-start = (bf16[128,2048]{1,0:T(8,128)(2,1)}, bf16[128,2048]{1,0:T(8,128)(2,1)}, u32[]{:S(2)}, u32[]{:S(2)}) collective-permute-start(bf16[128,2048]{1,0:T(8,128)(2,1)} %get-tuple-element.76), channel_id=1, source_target_pairs={{0,0},{8,16},{16,8},{24,24},{1,1},{9,17},{17,9},{25,25},{2,26},{10... | collective-permute-start | bytes 1572872 | tf_op jit(solution)/shard_map/ppermute | solution.py:314
  9.2 30.4 %collective-permute-start.4 = (bf16[1024,640]{1,0:T(8,128)(2,1)S(1)}, bf16[1024,640]{1,0:T(8,128)(2,1)S(1)}, u32[]{:S(2)}, u32[]{:S(2)}) collective-permute-start(bf16[1024,640]{1,0:T(8,128)(2,1)S(1)} %slice.70.refs_2_.refs_6_), channel_id=1, source_target_pairs={{0,1},{1,0},{2,3},{3,2},{4,5},{5,4},{6,7},{7,6},{8,9},{9,8},{10,11... | collective-permute-start | bytes 3932168 | tf_op jit(solution)/shard_map/ppermute | solution.py:262
  16.5 7.1 %collective-permute-start.2 = (bf16[128,2048]{1,0:T(8,128)(2,1)}, bf16[128,2048]{1,0:T(8,128)(2,1)S(1)}, u32[]{:S(2)}, u32[]{:S(2)}) collective-permute-start(bf16[128,2048]{1,0:T(8,128)(2,1)} %get-tuple-element.42), channel_id=1, source_target_pairs={{0,0},{8,16},{16,8},{24,24},{1,1},{9,17},{17,9},{25,25},{2,26},{10... | collective-permute-start | bytes 1572872 | tf_op jit(solution)/shard_map/ppermute | solution.py:314
  18.2 8.5 %collective-permute-start.1 = (bf16[128,2048]{1,0:T(8,128)(2,1)}, bf16[128,2048]{1,0:T(8,128)(2,1)}, u32[]{:S(2)}, u32[]{:S(2)}) collective-permute-start(bf16[128,2048]{1,0:T(8,128)(2,1)} %collective-permute-done), channel_id=1, source_target_pairs={{0,0},{16,18},{8,12},{24,30},{1,1},{17,19},{9,13},{25,31},{26,16},... | collective-permute-start | bytes 1572872 | tf_op jit(solution)/shard_map/ppermute | solution.py:324
  23.5 16.0 %collective-permute-start.3 = (bf16[128,2048]{1,0:T(8,128)(2,1)}, bf16[128,2048]{1,0:T(8,128)(2,1)S(1)}, u32[]{:S(2)}, u32[]{:S(2)}) collective-permute-start(bf16[128,2048]{1,0:T(8,128)(2,1)} %get-tuple-element.43), channel_id=1, source_target_pairs={{0,0},{8,16},{16,8},{24,24},{1,1},{9,17},{17,9},{25,25},{2,26},{10... | collective-permute-start | bytes 1572872 | tf_op jit(solution)/shard_map/ppermute | solution.py:314
  25.2 16.7 %collective-permute-start.8 = (bf16[128,2048]{1,0:T(8,128)(2,1)S(1)}, bf16[128,2048]{1,0:T(8,128)(2,1)}, u32[]{:S(2)}, u32[]{:S(2)}) collective-permute-start(bf16[128,2048]{1,0:T(8,128)(2,1)S(1)} %collective-permute-done.2), channel_id=1, source_target_pairs={{0,0},{16,18},{8,12},{24,30},{1,1},{17,19},{9,13},{25,31},{26,16},... | collective-permute-start | bytes 1572872 | tf_op jit(solution)/shard_map/ppermute | solution.py:324
  40.3 14.6 %collective-permute-start.5 = (bf16[128,2048]{1,0:T(8,128)(2,1)}, bf16[128,2048]{1,0:T(8,128)(2,1)}, u32[]{:S(2)}, u32[]{:S(2)}) collective-permute-start(bf16[128,2048]{1,0:T(8,128)(2,1)} %collective-permute-done.1.refs_0_), channel_id=1, source_target_pairs={{0,16},{8,24},{16,0},{24,8},{1,17},{9,25},{17,1},{25,9},{2,18},{10... | collective-permute-start | bytes 1572872 | tf_op jit(solution)/shard_map/ppermute | solution.py:262
  40.3 21.8 %collective-permute-start.10 = (bf16[1024,256]{1,0:T(8,128)(2,1)S(1)}, bf16[1024,256]{1,0:T(8,128)(2,1)}, u32[]{:S(2)}, u32[]{:S(2)}) collective-permute-start(bf16[1024,256]{1,0:T(8,128)(2,1)S(1)} %constant_dynamic-update-slice_fusion.refs_5_.refs_4_), channel_id=1, source_target_pairs={{0,1},{1,0},{2,3},{3,2},{4,5},{5,4},{6,7},{7,6},{8,9},{9,8},{10,11... | collective-permute-start | bytes 1572872 | tf_op jit(solution)/shard_map/ppermute | solution.py:262
  41.9 24.3 %collective-permute-start.9 = (bf16[128,2048]{1,0:T(8,128)(2,1)}, bf16[128,2048]{1,0:T(8,128)(2,1)}, u32[]{:S(2)}, u32[]{:S(2)}) collective-permute-start(bf16[128,2048]{1,0:T(8,128)(2,1)} %collective-permute-done.8.refs_1_), channel_id=1, source_target_pairs={{0,16},{8,24},{16,0},{24,8},{1,17},{9,25},{17,1},{25,9},{2,18},{10... | collective-permute-start | bytes 1572872 | tf_op jit(solution)/shard_map/ppermute | solution.py:262
  46.7 19.4 %collective-permute-start.6 = (bf16[128,2048]{1,0:T(8,128)(2,1)}, bf16[128,2048]{1,0:T(8,128)(2,1)}, u32[]{:S(2)}, u32[]{:S(2)}) collective-permute-start(bf16[128,2048]{1,0:T(8,128)(2,1)} %collective-permute-done.1.refs_0_), channel_id=1, source_target_pairs={{0,8},{8,0},{16,24},{24,16},{1,9},{9,1},{17,25},{25,17},{2,10},{10... | collective-permute-start | bytes 1572872 | tf_op jit(solution)/shard_map/ppermute | solution.py:262
  54.9 11.2 %collective-permute-start.7 = (bf16[128,2048]{1,0:T(8,128)(2,1)}, bf16[128,2048]{1,0:T(8,128)(2,1)}, u32[]{:S(2)}, u32[]{:S(2)}) collective-permute-start(bf16[128,2048]{1,0:T(8,128)(2,1)} %collective-permute-done.5.refs_1_), channel_id=1, source_target_pairs={{0,8},{8,0},{16,24},{24,16},{1,9},{9,1},{17,25},{25,17},{2,10},{10... | collective-permute-start | bytes 1572872 | tf_op jit(solution)/shard_map/ppermute | solution.py:262
  56.1 14.0 %collective-permute-start.17 = (bf16[128,2048]{1,0:T(8,128)(2,1)}, bf16[128,2048]{1,0:T(8,128)(2,1)}, u32[]{:S(2)}, u32[]{:S(2)}) collective-permute-start(bf16[128,2048]{1,0:T(8,128)(2,1)} %copy-done.14), channel_id=1, source_target_pairs={{0,0},{16,18},{8,12},{24,30},{1,1},{17,19},{9,13},{25,31},{26,16},... | collective-permute-start | bytes 1572872 | tf_op jit(solution)/shard_map/ppermute | solution.py:324
  62.1 9.5 %collective-permute-start.11 = (bf16[128,2048]{1,0:T(8,128)(2,1)}, bf16[128,2048]{1,0:T(8,128)(2,1)}, u32[]{:S(2)}, u32[]{:S(2)}) collective-permute-start(bf16[128,2048]{1,0:T(8,128)(2,1)} %collective-permute-done.8.refs_1_), channel_id=1, source_target_pairs={{0,8},{8,0},{16,24},{24,16},{1,9},{9,1},{17,25},{25,17},{2,10},{10... | collective-permute-start | bytes 1572872 | tf_op jit(solution)/shard_map/ppermute | solution.py:262
  69.7 2.2 %collective-permute-start.12 = (bf16[128,2048]{1,0:T(8,128)(2,1)}, bf16[128,2048]{1,0:T(8,128)(2,1)S(1)}, u32[]{:S(2)}, u32[]{:S(2)}) collective-permute-start(bf16[128,2048]{1,0:T(8,128)(2,1)} %collective-permute-done.9.refs_2_), channel_id=1, source_target_pairs={{0,8},{8,0},{16,24},{24,16},{1,9},{9,1},{17,25},{25,17},{2,10},{10... | collective-permute-start | bytes 1572872 | tf_op jit(solution)/shard_map/ppermute | solution.py:262
  70.2 16.7 %collective-permute-start.18 = (bf16[128,2048]{1,0:T(8,128)(2,1)}, bf16[128,2048]{1,0:T(8,128)(2,1)S(1)}, u32[]{:S(2)}, u32[]{:S(2)}) collective-permute-start(bf16[128,2048]{1,0:T(8,128)(2,1)} %collective-permute-done.17.refs_0_), channel_id=1, source_target_pairs={{0,16},{8,24},{16,0},{24,8},{1,17},{9,25},{17,1},{25,9},{2,18},{10... | collective-permute-start | bytes 1572872 | tf_op jit(solution)/shard_map/ppermute | solution.py:262
  77.4 8.5 %collective-permute-start.13 = (bf16[2,256,256]{2,1,0:T(8,128)(2,1)S(1)}, bf16[2,256,256]{2,1,0:T(8,128)(2,1)S(1)}, u32[]{:S(2)}, u32[]{:S(2)}) collective-permute-start(bf16[2,256,256]{2,1,0:T(8,128)(2,1)S(1)} %get-tuple-element.49), channel_id=1, source_target_pairs={{0,2},{1,3},{2,0},{3,1},{4,6},{5,7},{6,4},{7,5},{8,10},{9,11},{10,... | collective-permute-start | bytes 786440 | tf_op jit(solution)/shard_map/ppermute | solution.py:262
  79.0 24.8 %collective-permute-start.23 = (bf16[1024,384]{1,0:T(8,128)(2,1)S(1)}, bf16[1024,384]{1,0:T(8,128)(2,1)S(1)}, u32[]{:S(2)}, u32[]{:S(2)}) collective-permute-start(bf16[1024,384]{1,0:T(8,128)(2,1)S(1)} %copy-done.2), channel_id=1, source_target_pairs={{0,1},{1,0},{2,3},{3,2},{4,5},{5,4},{6,7},{7,6},{8,9},{9,8},{10,11... | collective-permute-start | bytes 2359304 | tf_op jit(solution)/shard_map/ppermute | solution.py:262
  84.6 20.5 %collective-permute-start.22 = (bf16[2,256,640]{2,1,0:T(8,128)(2,1)S(1)}, bf16[2,256,640]{2,1,0:T(8,128)(2,1)S(1)}, u32[]{:S(2)}, u32[]{:S(2)}) collective-permute-start(bf16[2,256,640]{2,1,0:T(8,128)(2,1)S(1)} %get-tuple-element.52), channel_id=1, source_target_pairs={{0,2},{1,3},{2,0},{3,1},{4,6},{5,7},{6,4},{7,5},{8,10},{9,11},{10,... | collective-permute-start | bytes 1966088 | tf_op jit(solution)/shard_map/ppermute | solution.py:262
  85.9 1.7 %collective-permute-start.14 = (f32[3,128]{1,0:T(4,128)S(1)}, f32[3,128]{1,0:T(4,128)S(1)}, u32[]{:S(2)}, u32[]{:S(2)}) collective-permute-start(f32[3,128]{1,0:T(4,128)S(1)} %multiply_reduce_fusion), channel_id=1, source_target_pairs={{0,8},{8,0},{16,24},{24,16},{1,9},{9,1},{17,25},{25,17},{2,10},{10... | collective-permute-start | bytes 4616 | tf_op jit(solution)/shard_map/ppermute | solution.py:262
  86.8 6.6 %collective-permute-start.20 = (bf16[128,2048]{1,0:T(8,128)(2,1)S(1)}, bf16[128,2048]{1,0:T(8,128)(2,1)S(1)}, u32[]{:S(2)}, u32[]{:S(2)}) collective-permute-start(bf16[128,2048]{1,0:T(8,128)(2,1)S(1)} %collective-permute-done.18.refs_1_), channel_id=1, source_target_pairs={{0,8},{8,0},{16,24},{24,16},{1,9},{9,1},{17,25},{25,17},{2,10},{10... | collective-permute-start | bytes 1572872 | tf_op jit(solution)/shard_map/ppermute | solution.py:262
  86.9 6.6 %collective-permute-start.19 = (bf16[128,2048]{1,0:T(8,128)(2,1)}, bf16[128,2048]{1,0:T(8,128)(2,1)S(1)}, u32[]{:S(2)}, u32[]{:S(2)}) collective-permute-start(bf16[128,2048]{1,0:T(8,128)(2,1)} %collective-permute-done.17.refs_0_), channel_id=1, source_target_pairs={{0,8},{8,0},{16,24},{24,16},{1,9},{9,1},{17,25},{25,17},{2,10},{10... | collective-permute-start | bytes 1572872 | tf_op jit(solution)/shard_map/ppermute | solution.py:262
  87.7 3.6 %collective-permute-start.15 = (f32[3,128]{1,0:T(4,128)S(1)}, f32[3,128]{1,0:T(4,128)S(1)}, u32[]{:S(2)}, u32[]{:S(2)}) collective-permute-start(f32[3,128]{1,0:T(4,128)S(1)} %add.34), channel_id=1, source_target_pairs={{0,16},{8,24},{16,0},{24,8},{1,17},{9,25},{17,1},{25,9},{2,18},{10... | collective-permute-start | bytes 4616 | tf_op jit(solution)/shard_map/ppermute | solution.py:262
  91.2 12.3 %collective-permute-start.16 = (bf16[1,256,256]{2,1,0:T(8,128)(2,1)S(1)}, bf16[1,256,256]{2,1,0:T(8,128)(2,1)S(1)}, u32[]{:S(2)}, u32[]{:S(2)}) collective-permute-start(bf16[1,256,256]{2,1,0:T(8,128)(2,1)S(1)} %fusion.6), channel_id=1, source_target_pairs={{0,4},{1,5},{2,6},{3,7},{4,0},{5,1},{6,2},{7,3},{8,12},{9,13},{10,... | collective-permute-start | bytes 393224 | tf_op jit(solution)/shard_map/ppermute | solution.py:262
  105.0 27.0 %collective-permute-start.25 = (bf16[2,128,896]{2,1,0:T(8,128)(2,1)S(1)}, bf16[2,128,896]{2,1,0:T(8,128)(2,1)S(1)}, u32[]{:S(2)}, u32[]{:S(2)}) collective-permute-start(bf16[2,128,896]{2,1,0:T(8,128)(2,1)S(1)} %get-tuple-element.68), channel_id=1, source_target_pairs={{0,2},{1,3},{2,0},{3,1},{4,6},{5,7},{6,4},{7,5},{8,10},{9,11},{10,... | collective-permute-start | bytes 1376264 | tf_op jit(solution)/shard_map/ppermute | solution.py:262
  107.4 24.7 %collective-permute-start.26 = (bf16[1,256,640]{2,1,0:T(8,128)(2,1)S(1)}, bf16[1,256,640]{2,1,0:T(8,128)(2,1)S(1)}, u32[]{:S(2)}, u32[]{:S(2)}) collective-permute-start(bf16[1,256,640]{2,1,0:T(8,128)(2,1)S(1)} %fusion.3), channel_id=1, source_target_pairs={{0,4},{1,5},{2,6},{3,7},{4,0},{5,1},{6,2},{7,3},{8,12},{9,13},{10,... | collective-permute-start | bytes 983048 | tf_op jit(solution)/shard_map/ppermute | solution.py:262
  108.0 21.9 %collective-permute-start.21 = (bf16[1,256,256]{2,1,0:T(8,128)(2,1)S(1)}, bf16[1,256,256]{2,1,0:T(8,128)(2,1)S(1)}, u32[]{:S(2)}, u32[]{:S(2)}) collective-permute-start(bf16[1,256,256]{2,1,0:T(8,128)(2,1)S(1)} %bitcast.21), channel_id=1, source_target_pairs={{0,4},{1,5},{2,6},{3,7},{4,0},{5,1},{6,2},{7,3},{8,12},{9,13},{10,... | collective-permute-start | bytes 393224 | tf_op jit(solution)/shard_map/ppermute | solution.py:262
  114.4 28.0 %copy-start.11 = (f32[1024]{0:T(1024)S(1)}, f32[1024]{0:T(1024)}, u32[]{:S(2)}) copy-start(f32[1024]{0:T(1024)} %param.17) | copy-start | bytes 12292
  129.9 11.8 %collective-permute-start.24 = (bf16[2,256,256]{2,1,0:T(8,128)(2,1)S(1)}, bf16[2,256,256]{2,1,0:T(8,128)(2,1)S(1)}, u32[]{:S(2)}, u32[]{:S(2)}) collective-permute-start(bf16[2,256,256]{2,1,0:T(8,128)(2,1)S(1)} %pad_maximum_fusion.2), channel_id=1, source_target_pairs={{0,2},{1,3},{2,0},{3,1},{4,6},{5,7},{6,4},{7,5},{8,10},{9,11},{10,... | collective-permute-start | bytes 786440 | tf_op jit(solution)/shard_map/ppermute | solution.py:262
  130.0 23.2 %collective-permute-start.29 = (bf16[2,384,384]{2,1,0:T(8,128)(2,1)S(1)}, bf16[2,384,384]{2,1,0:T(8,128)(2,1)S(1)}, u32[]{:S(2)}, u32[]{:S(2)}) collective-permute-start(bf16[2,384,384]{2,1,0:T(8,128)(2,1)S(1)} %get-tuple-element.72), channel_id=1, source_target_pairs={{0,2},{1,3},{2,0},{3,1},{4,6},{5,7},{6,4},{7,5},{8,10},{9,11},{10,... | collective-permute-start | bytes 1769480 | tf_op jit(solution)/shard_map/ppermute | solution.py:262
  141.8 19.3 %collective-permute-start.27 = (bf16[4,256,256]{2,1,0:T(8,128)(2,1)S(1)}, bf16[4,256,256]{2,1,0:T(8,128)(2,1)S(1)}, u32[]{:S(2)}, u32[]{:S(2)}) collective-permute-start(bf16[4,256,256]{2,1,0:T(8,128)(2,1)S(1)} %pad_maximum_fusion.1), channel_id=1, source_target_pairs={{0,1},{1,0},{2,3},{3,2},{4,5},{5,4},{6,7},{7,6},{8,9},{9,8},{10,11... | collective-permute-start | bytes 1572872 | tf_op jit(solution)/shard_map/ppermute | solution.py:262
  142.4 18.4 %collective-permute-start.28 = (bf16[1,128,896]{2,1,0:T(8,128)(2,1)S(1)}, bf16[1,128,896]{2,1,0:T(8,128)(2,1)S(1)}, u32[]{:S(2)}, u32[]{:S(2)}) collective-permute-start(bf16[1,128,896]{2,1,0:T(8,128)(2,1)S(1)} %fusion.5), channel_id=1, source_target_pairs={{0,4},{1,5},{2,6},{3,7},{4,0},{5,1},{6,2},{7,3},{8,12},{9,13},{10,... | collective-permute-start | bytes 688136 | tf_op jit(solution)/shard_map/ppermute | solution.py:262
  153.3 13.4 %collective-permute-start.30 = (bf16[1,384,384]{2,1,0:T(8,128)(2,1)S(1)}, bf16[1,384,384]{2,1,0:T(8,128)(2,1)S(1)}, u32[]{:S(2)}, u32[]{:S(2)}) collective-permute-start(bf16[1,384,384]{2,1,0:T(8,128)(2,1)S(1)} %fusion.4), channel_id=1, source_target_pairs={{0,4},{1,5},{2,6},{3,7},{4,0},{5,1},{6,2},{7,3},{8,12},{9,13},{10,... | collective-permute-start | bytes 884744 | tf_op jit(solution)/shard_map/ppermute | solution.py:262
  (14 other events, 85.7 us)

commit v9 on v8

--- a/solution.py
+++ b/solution.py
@@ -77,12 +77,6 @@
     for copy in copies:
         copy.start()
     return copies
-
-
-def assemble_kernel(lines, place_ref, *refs):
-    pieces, (held, sems) = refs[:lines], refs[lines:]
-    for copy in assemble(lines, 1, place_ref, pieces, held, sems):
-        copy.wait()
 
 
 def project_kernel(lines, groups, chunks, counts, fresh, place_ref, *refs):
@@ -137,8 +131,8 @@
     far_slots, block_len, blocks, heads, first_head, parts, addends, aliased, tour, device_ref,
     parents_ref, lengths_ref, inverse_ref, bias_ref, cos_ref, sin_ref, stems_ref, *refs,
 ):
-    keys = refs[:2]
-    refs = refs[2:]
+    near = refs[:blocks]
+    refs = refs[blocks:]
     sums = [refs[p * addends : (p + 1) * addends] for p in range(len(parts))]
     refs = refs[len(parts) * addends + aliased :]
     out_ref, far_key, far_value, far_mask, held, sems = refs
@@ -165,8 +159,6 @@
     rows = heads * block_len
     column = lax.broadcasted_iota(jnp.int32, (rows, block_len), 1)
     row = lax.broadcasted_iota(jnp.int32, (rows, block_len), 0) % block_len
-    near = [(keys[0], block * block_len) for block in range(STEMS)]
-    near += [(keys[1], (block - STEMS) * block_len) for block in range(STEMS, blocks)]
     copies = []
     for p, (first, count, offset) in enumerate(parts):
         for inside in range(count):
@@ -189,12 +181,8 @@
             )
             scores = [far + far_mask[0:1, :]]
             for other in range(block + 1):
-                ref, begin = near[other]
                 score = lax.dot_general(
-                    query,
-                    ref[begin : begin + block_len, :HD],
-                    contract,
-                    preferred_element_type=jnp.float32,
+                    query, near[other][:, :HD], contract, preferred_element_type=jnp.float32
                 )
                 if other == block or other >= STEMS:
                     seen = column < lengths_ref[first_block + other]
@@ -212,10 +200,9 @@
                 exps[0].astype(jnp.bfloat16), far_value[...], preferred_element_type=jnp.float32
             )
             for other in range(block + 1):
-                ref, begin = near[other]
                 output += jnp.dot(
                     exps[1 + other].astype(jnp.bfloat16),
-                    ref[begin : begin + block_len, HD:],
+                    near[other][:, HD:],
                     preferred_element_type=jnp.float32,
                 )
             output = output / total
@@ -313,16 +300,17 @@
         piece = tie(piece, sent[-1], cos, sin, *w_chunks) if block else piece
         sent.append(lax.ppermute(piece, axes, first_hop))
 
+    last_sent = sent[-1]
+    sent = [lax.ppermute(piece, axes, second_hop) for piece in sent]
     w_rows = [None] * len(w_chunks)
     arrived = None
     for c in (1, 0, 2):
-        outgoing = w_chunks[c] if arrived is None else tie(w_chunks[c], arrived)
+        outgoing = w_chunks[c] if arrived is None else tie(w_chunks[c], arrived, sent[0])
         w_rows[c] = [w_chunks[c]] + [swap(outgoing, "branch", j) for j in range(1, groups)]
         arrived = w_rows[c][-1]
 
+    sent[0] = tie(sent[0], last_sent)
     last_sent = sent[-1]
-    sent = [lax.ppermute(piece, axes, second_hop) for piece in sent]
-    sent[0] = tie(sent[0], last_sent, w_rows[1][-1])
     held = [{0: piece} for piece in sent]
     bit = half_lines
     while bit > 1:
@@ -336,21 +324,9 @@
             piece[j | 1] = swap(piece[j], "fsdp", 1)
         return [piece[j] for j in sorted(piece, key=spread)]
 
-    held[1][half_lines] = tie(held[1][half_lines], w_rows[0][-1])
     assembled = {}
     held[0] = last_bit(held[0])
-    assembled[(0, 1)] = pl.pallas_call(
-        functools.partial(assemble_kernel, lines),
-        in_specs=[smem] + [anywhere] * lines,
-        out_specs=vmem,
-        out_shape=jax.ShapeDtypeStruct((lines * block_len, feature_part), bf16),
-        scratch_shapes=[pltpu.SemaphoreType.DMA((lines,))],
-        name="assemble",
-    )(place, *held[0])
-    for block in range(1, STEMS):
-        held[block][half_lines] = tie(held[block][half_lines], assembled[(0, 1)])
-        held[block] = last_bit(held[block])
-
+    held[1] = last_bit(held[1])
 
     def project(spans, chunks, *after):
         weights = [w for chunk in chunks for w in w_rows[chunk]]
@@ -438,17 +414,20 @@
             name="finish_kv",
         )(*operands, *addends)
 
-    early = [(0, 1), (1, STEMS)]
-    late = [(STEMS, blocks)]
-    first = Halving(project(early, [0]))
-    first.step()
-
-    second = Halving(project(early, [1], first.send))
-    second.step()
-    first.rest(second.send)
+    units = [Halving(project([(0, 1)], [0, 1], last_sent))]
+    units[0].step()
+    for block in range(1, blocks):
+        before = units[-1]
+        if block > 1:
+            held[block] = {j: tie(piece, gate) for j, piece in held[block].items()}
+            held[block] = last_bit(held[block])
+        units.append(Halving(project([(block, block + 1)], [0, 1], before.send)))
+        before.rest(units[-1].send)
+        gate = before.send
+        units[-1].step(gate)
 
     squares = jnp.sum(jnp.square(raw.astype(f32)), -1).reshape(blocks, block_len)
-    squares = tie(squares, first.send)
+    squares = tie(squares, units[STEMS - 1].send)
     bit = 1
     while bit < lines:
         squares = squares + swap(squares, "fsdp", bit)
@@ -456,40 +435,35 @@
     inverse = lax.rsqrt(squares / features + 1e-06).reshape(tokens)
     inverse = jnp.broadcast_to(inverse[:, None], (tokens, HD))
 
-    for block in range(STEMS, blocks):
-        held[block] = {j: tie(piece, first.send) for j, piece in held[block].items()}
-        held[block] = last_bit(held[block])
-    third = Halving(project(late, [0, 1], first.send))
-    first.addends[-1] = tie(first.addends[-1], third.send)
-    stem_kv = finish_kv(first.addends, 0, STEMS)
+    last = Halving(project([(b, b + 1) for b in range(blocks)], [2], units[STEMS - 1].send))
+    stem_kv = []
+    for block in range(STEMS):
+        unit = units[block]
+        unit.addends[-1] = tie(unit.addends[-1], last.send)
+        stem_kv.append(finish_kv(unit.addends, block, 1))
 
     tour = [groups << i for i in reversed(range(bits_of(lines)))]
     tour += [1 << i for i in range(bits_of(groups))]
-    stems = stem_kv[None]
+    stems = jnp.concatenate(stem_kv, 0)[None]
     came = swap(stems, "branch", tour[0])
-    third.step(stem_kv)
-    second.add(stem_kv, w_rows[2][-1])
-    second.step()
-    fourth = Halving(project(early + late, [2], second.send))
+    units[-1].rest(stems)
+    last.step(units[-1].send)
     for step, bit in enumerate(tour[1:]):
-        stems = jnp.concatenate([stems, tie(came, third.send if step else fourth.send)], 0)
+        stems = jnp.concatenate([stems, tie(came, units[-1].send)], 0)
         came = swap(stems, "branch", bit)
-        if step == 0:
-            fourth.step(stems)
-            third.add(stems, second.came)
-            third.step()
-    second.rest()
-    third.rest()
-    fourth.rest(stems, second.came)
+    last.rest(stems)
     stems = jnp.concatenate([stems, came], 0)
-    third.addends[-1] = tie(third.addends[-1], fourth.send)
-    late_kv = finish_kv(third.addends, STEMS, blocks - STEMS)
-    second_sums, third_sums, fourth_sums = second.addends, third.addends, fourth.addends
+    late_kv = []
+    for block in range(STEMS, blocks):
+        unit = units[block]
+        unit.addends[-1] = tie(unit.addends[-1], last.send)
+        late_kv.append(finish_kv(unit.addends, block, 1))
+    keys = stem_kv + late_kv
 
     def attend(heads, first_head, parts, sums, output):
         operands = [
             inverse, query_bias[None, first_head * HD : (first_head + heads) * HD], cos, sin,
-            stems, stem_kv, late_kv,
+            stems, *keys,
         ]
         in_specs = [smem] * 3 + [whole(x) for x in operands]
         for addends in sums:
@@ -504,7 +478,7 @@
             attend_kernel, far_slots, block_len, blocks, heads, first_head, parts, addend_count,
             len(aliases), tour,
         )
-        keys = (far_slots * len(parts) + blocks) * block_len
+        length = (far_slots + blocks) * block_len
         return pl.pallas_call(
             kernel,
             grid=(1,),
@@ -521,19 +495,17 @@
             input_output_aliases=aliases,
             compiler_params=pltpu.CompilerParams(vmem_limit_bytes=40 * 2**20),
             cost_estimate=pl.CostEstimate(
-                flops=4 * tokens * heads * keys * HD,
+                flops=4 * tokens * heads * length * HD,
                 bytes_accessed=2 * tokens * heads * HD,
-                transcendentals=tokens * heads * keys,
+                transcendentals=tokens * heads * length,
             ),
             name="attend",
         )(device_id, parents, lengths, *operands)
 
+    parts = [(block, 1, kv_width) for block in range(blocks)]
+    output = attend(head_cuts[1], 0, parts, [unit.addends for unit in units], None)
     output = attend(
-        head_cuts[1], 0, [(0, STEMS, 0), (STEMS, blocks - STEMS, kv_width)],
-        [second_sums, third_sums], None,
-    )
-    output = attend(
-        head_count - head_cuts[1], head_cuts[1], [(0, blocks, 0)], [fourth_sums], output
+        head_count - head_cuts[1], head_cuts[1], [(0, blocks, 0)], [last.addends], output
     )
     return output.reshape(blocks, block_len, columns)
 

time: 172 us -> 171 us (level)
  starting transfers between devices: 51.7 us -> 62.3 us
  waiting for transfers between devices: 77 us -> 70.8 us
  local copies, waits for them, and re-layouts: 6.06 us -> 2.77 us
    ppermute x25, starting transfers between devices: 30.7 us -> 41.5 us  [swap(): return lax.ppermute(array, axis, [(i, i ^ bit) for i in range(size)])]
    ppermute x25, waiting for transfers between devices: 77 us -> 70.8 us  [swap(): return lax.ppermute(array, axis, [(i, i ^ bit) for i in range(size)])]
    pallas_call x1 -> x0, Pallas kernels: 3.56 us -> none  [shards(): pl.pallas_call(functools.partial(assemble_kernel, lines), in_specs=[smem]...]
    unnamed x31 -> x25, local copies, waits for them, and re-layouts: 2.91 us -> 0.52 us
    pallas_call x4, Pallas kernels: 16.4 us -> 18.4 us  [project(): pl.pallas_call(functools.partial(project_kernel, lines, groups, len(chunk...]
  transfers between devices with their start and end apart: 31 -> 31, of which waited for: 13 -> 12; matrix products, arithmetic and copies ran while one was open for 2% -> 1% of each run, Pallas kernels for 16% -> 15%
where the time goes in v9:
time: 171 us; the launch traced here: 170 us
  waiting for transfers between devices  70.8 us (41%)
  starting transfers between devices  62.3 us (36%)
  Pallas kernels  29.9 us (17%)
  other arithmetic  3.78 us (2%)
  local copies, waits for them, and re-layouts  2.77 us (2%)
    ppermute x25, waiting for transfers between devices, swap(): return lax.ppermute(array, axis, [(i, i ^ bit) for i in range(size)])  70.8 us
    ppermute x25, starting transfers between devices, swap(): return lax.ppermute(array, axis, [(i, i ^ bit) for i in range(size)])  41.5 us
    pallas_call x4, Pallas kernels, project(): pl.pallas_call(functools.partial(project_kernel, lines, groups, len(chunk...  18.4 us
    ppermute x3, starting transfers between devices, shards(): sent = [lax.ppermute(piece, axes, second_hop) for piece in sent]  12.2 us
    pallas_call x2, Pallas kernels, attend(): pl.pallas_call(kernel, grid=(1,), in_specs=in_specs, out_specs=anywhere,...  8.92 us
    ppermute x3, starting transfers between devices, shards(): sent.append(lax.ppermute(piece, axes, first_hop))  8.66 us
  transfers between devices with their start and end apart: 31, of which 12 were waited for; matrix products, arithmetic and copies ran while one was open for 1% of the time, Pallas kernels for 15%

profile of v9, /device:TPU:0, one launch (start us, length us, event | category | flops | bytes accessed | tf_op | source)
XLA Modules:
  0.0 170.1 jit_solution(3638167818906429129)
XLA Ops:
  0.7 2.9 %fusion = (bf16[128,2048]{1,0:T(8,128)(2,1)}, bf16[128,2048]{1,0:T(8,128)(2,1)}, bf16[128,2048]{1,0:T(8,128)(2,1)S(1)}) fusion(bf16[3,128,2048]{2,1,0:T(8,128)(2,1)} %param.10, f32[2048]{0:T(1024)S(1)} %dynamic_slice.3), kind=kLoop, calls=%fused_computation.3 | loop fusion | flops 2359296 | bytes 3153920 | tf_op jit(solution)/shard_map/convert_element_type | solution.py:299
  6.3 2.2 %tables.1 = (f32[384,128]{1,0:T(8,128)}, f32[384,128]{1,0:T(8,128)}) custom-call(s32[1]{0:T(128)} %bitcast.device_ref, s32[24]{0:T(128)} %parents_ref.5), custom_call_target="tpu_custom_call" | custom-call | tf_op jit(solution)/shard_map/tables/pallas_call | solution.py:289
  8.7 1.7 collective-permute-start.1
  10.4 3.0 %collective-permute-start.9 = (bf16[1024,640]{1,0:T(8,128)(2,1)S(1)}, bf16[1024,640]{1,0:T(8,128)(2,1)S(1)}, u32[]{:S(2)}, u32[]{:S(2)}) collective-permute-start(bf16[1024,640]{1,0:T(8,128)(2,1)S(1)} %slice.82.refs_6_), channel_id=1, source_target_pairs={{0,1},{1,0},{2,3},{3,2},{4,5},{5,4},{6,7},{7,6},{8,9},{9,8},{10,11... | collective-permute-start | bytes 3932168 | tf_op jit(solution)/shard_map/ppermute | solution.py:249
  13.3 5.4 %collective-permute-start.3 = (bf16[128,2048]{1,0:T(8,128)(2,1)}, bf16[128,2048]{1,0:T(8,128)(2,1)}, u32[]{:S(2)}, u32[]{:S(2)}) collective-permute-start(bf16[128,2048]{1,0:T(8,128)(2,1)} %collective-permute-done), channel_id=1, source_target_pairs={{0,0},{16,18},{8,12},{24,30},{1,1},{17,19},{9,13},{25,31},{26,16},... | collective-permute-start | bytes 1572872 | tf_op jit(solution)/shard_map/ppermute | solution.py:304
  18.7 5.4 %collective-permute-start.4 = (bf16[128,2048]{1,0:T(8,128)(2,1)}, bf16[128,2048]{1,0:T(8,128)(2,1)}, u32[]{:S(2)}, u32[]{:S(2)}) collective-permute-start(bf16[128,2048]{1,0:T(8,128)(2,1)} %get-tuple-element.45), channel_id=1, source_target_pairs={{0,0},{8,16},{16,8},{24,24},{1,1},{9,17},{17,9},{25,25},{2,26},{10... | collective-permute-start | bytes 1572872 | tf_op jit(solution)/shard_map/ppermute | solution.py:301
  25.5 13.2 %collective-permute-start.6 = (bf16[128,2048]{1,0:T(8,128)(2,1)}, bf16[128,2048]{1,0:T(8,128)(2,1)}, u32[]{:S(2)}, u32[]{:S(2)}) collective-permute-start(bf16[128,2048]{1,0:T(8,128)(2,1)} %collective-permute-done.3.refs_0_), channel_id=1, source_target_pairs={{0,16},{8,24},{16,0},{24,8},{1,17},{9,25},{17,1},{25,9},{2,18},{10... | collective-permute-start | bytes 1572872 | tf_op jit(solution)/shard_map/ppermute | solution.py:249
  38.8 5.4 %collective-permute-start.5 = (bf16[128,2048]{1,0:T(8,128)(2,1)}, bf16[128,2048]{1,0:T(8,128)(2,1)}, u32[]{:S(2)}, u32[]{:S(2)}) collective-permute-start(bf16[128,2048]{1,0:T(8,128)(2,1)} %collective-permute-done.4), channel_id=1, source_target_pairs={{0,0},{16,18},{8,12},{24,30},{1,1},{17,19},{9,13},{25,31},{26,16},... | collective-permute-start | bytes 1572872 | tf_op jit(solution)/shard_map/ppermute | solution.py:304
  44.1 3.7 %collective-permute-start.11 = (bf16[128,2048]{1,0:T(8,128)(2,1)}, bf16[128,2048]{1,0:T(8,128)(2,1)}, u32[]{:S(2)}, u32[]{:S(2)}) collective-permute-start(bf16[128,2048]{1,0:T(8,128)(2,1)} %collective-permute-done.2.refs_0_), channel_id=1, source_target_pairs={{0,16},{8,24},{16,0},{24,8},{1,17},{9,25},{17,1},{25,9},{2,18},{10... | collective-permute-start | bytes 1572872 | tf_op jit(solution)/shard_map/ppermute | solution.py:249
  49.2 2.7 %collective-permute-done.6.refs_1_ = bf16[128,2048]{1,0:T(8,128)(2,1)} collective-permute-done((bf16[128,2048]{1,0:T(8,128)(2,1)}, bf16[128,2048]{1,0:T(8,128)(2,1)}, u32[]{:S(2)}, u32[]{:S(2)}) %collective-permute-start.6) | collective-permute-done | bytes 524320 | tf_op jit(solution)/shard_map/ppermute | solution.py:249
  51.8 5.1 %collective-permute-start.12 = (bf16[128,2048]{1,0:T(8,128)(2,1)}, bf16[128,2048]{1,0:T(8,128)(2,1)S(1)}, u32[]{:S(2)}, u32[]{:S(2)}) collective-permute-start(bf16[128,2048]{1,0:T(8,128)(2,1)} %collective-permute-done.2.refs_0_), channel_id=1, source_target_pairs={{0,8},{8,0},{16,24},{24,16},{1,9},{9,1},{17,25},{25,17},{2,10},{10... | collective-permute-start | bytes 1572872 | tf_op jit(solution)/shard_map/ppermute | solution.py:249
  57.0 6.0 %collective-permute-done.11.refs_1_ = bf16[128,2048]{1,0:T(8,128)(2,1)} collective-permute-done((bf16[128,2048]{1,0:T(8,128)(2,1)}, bf16[128,2048]{1,0:T(8,128)(2,1)}, u32[]{:S(2)}, u32[]{:S(2)}) %collective-permute-start.11) | collective-permute-done | bytes 524320 | tf_op jit(solution)/shard_map/ppermute | solution.py:249
  63.1 5.0 %project.4 = (bf16[2,128,896]{2,1,0:T(8,128)(2,1)S(1)}, f32[2,128,896]{2,1,0:T(8,128)S(1)}, bf16[512,2048]{1,0:T(8,128)(2,1)S(1)}) custom-call(s32[2]{0:T(128)S(1)} %pad_add_fusion.place_ref, bf16[128,2048]{1,0:T(8,128)(2,1)} %collective-permute-done.3.refs_0_, bf16[128,2048]{1,0:T(8,128)(2,1)} %collective-permute-done.6.refs_1_, ...), custom_call_target="tpu_custom_call" | custom-call | tf_op jit(solution)/shard_map/project/pallas_call | solution.py:355
  68.1 1.7 %collective-permute-start.14 = (bf16[2,128,896]{2,1,0:T(8,128)(2,1)S(1)}, bf16[2,128,896]{2,1,0:T(8,128)(2,1)S(1)}, u32[]{:S(2)}, u32[]{:S(2)}) collective-permute-start(bf16[2,128,896]{2,1,0:T(8,128)(2,1)S(1)} %get-tuple-element.49), channel_id=1, source_target_pairs={{0,2},{1,3},{2,0},{3,1},{4,6},{5,7},{6,4},{7,5},{8,10},{9,11},{10,... | collective-permute-start | bytes 1376264 | tf_op jit(solution)/shard_map/ppermute | solution.py:249
  69.9 1.7 %collective-permute-start.16 = (bf16[128,2048]{1,0:T(8,128)(2,1)}, bf16[128,2048]{1,0:T(8,128)(2,1)S(1)}, u32[]{:S(2)}, u32[]{:S(2)}) collective-permute-start(bf16[128,2048]{1,0:T(8,128)(2,1)} %collective-permute-done.5.refs_0_), channel_id=1, source_target_pairs={{0,16},{8,24},{16,0},{24,8},{1,17},{9,25},{17,1},{25,9},{2,18},{10... | collective-permute-start | bytes 1572872 | tf_op jit(solution)/shard_map/ppermute | solution.py:249
  71.6 4.8 %project.5 = (bf16[2,128,896]{2,1,0:T(8,128)(2,1)S(1)}, f32[2,128,896]{2,1,0:T(8,128)S(1)}, bf16[512,2048]{1,0:T(8,128)(2,1)S(1)}) custom-call(s32[2]{0:T(128)S(1)} %pad_add_fusion.place_ref, bf16[128,2048]{1,0:T(8,128)(2,1)} %collective-permute-done.2.refs_0_, bf16[128,2048]{1,0:T(8,128)(2,1)} %collective-permute-done.11.refs_1_, ...), custom_call_target="tpu_custom_call" | custom-call | tf_op jit(solution)/shard_map/project/pallas_call | solution.py:355
  76.4 4.7 %collective-permute-done.14.refs_1_.refs_4_ = bf16[2,128,896]{2,1,0:T(8,128)(2,1)S(1)} collective-permute-done((bf16[2,128,896]{2,1,0:T(8,128)(2,1)S(1)}, bf16[2,128,896]{2,1,0:T(8,128)(2,1)S(1)}, u32[]{:S(2)}, u32[]{:S(2)}) %collective-permute-start.14) | collective-permute-done | bytes 458784 | tf_op jit(solution)/shard_map/ppermute | solution.py:249
  81.2 3.0 %collective-permute-done.16.refs_1_ = bf16[128,2048]{1,0:T(8,128)(2,1)S(1)} collective-permute-done((bf16[128,2048]{1,0:T(8,128)(2,1)}, bf16[128,2048]{1,0:T(8,128)(2,1)S(1)}, u32[]{:S(2)}, u32[]{:S(2)}) %collective-permute-start.16) | collective-permute-done | bytes 524320 | tf_op jit(solution)/shard_map/ppermute | solution.py:249
  86.9 2.6 %collective-permute-start.21 = (bf16[1,128,896]{2,1,0:T(8,128)(2,1)S(1)}, bf16[1,128,896]{2,1,0:T(8,128)(2,1)S(1)}, u32[]{:S(2)}, u32[]{:S(2)}) collective-permute-start(bf16[1,128,896]{2,1,0:T(8,128)(2,1)S(1)} %fusion.6), channel_id=1, source_target_pairs={{0,4},{1,5},{2,6},{3,7},{4,0},{5,1},{6,2},{7,3},{8,12},{9,13},{10,... | collective-permute-start | bytes 688136 | tf_op jit(solution)/shard_map/ppermute | solution.py:249
  89.6 4.6 %project.6 = (bf16[2,128,896]{2,1,0:T(8,128)(2,1)S(1)}, f32[2,128,896]{2,1,0:T(8,128)S(1)}, bf16[512,2048]{1,0:T(8,128)(2,1)S(1)}) custom-call(s32[2]{0:T(128)S(1)} %pad_add_fusion.place_ref, bf16[128,2048]{1,0:T(8,128)(2,1)} %collective-permute-done.5.refs_0_, bf16[128,2048]{1,0:T(8,128)(2,1)S(1)} %collective-permute-done.16.refs_1_, ...), custom_call_target="tpu_custom_call" | custom-call | tf_op jit(solution)/shard_map/project/pallas_call | solution.py:355
  94.1 7.8 %collective-permute-done.15.refs_1_.refs_7_ = bf16[2,128,896]{2,1,0:T(8,128)(2,1)S(1)} collective-permute-done((bf16[2,128,896]{2,1,0:T(8,128)(2,1)S(1)}, bf16[2,128,896]{2,1,0:T(8,128)(2,1)S(1)}, u32[]{:S(2)}, u32[]{:S(2)}) %collective-permute-start.15) | collective-permute-done | bytes 458784 | tf_op jit(solution)/shard_map/ppermute | solution.py:249
  103.3 1.7 %collective-permute-start.20 = (f32[3,128]{1,0:T(4,128)S(1)}, f32[3,128]{1,0:T(4,128)S(1)}, u32[]{:S(2)}, u32[]{:S(2)}) collective-permute-start(f32[3,128]{1,0:T(4,128)S(1)} %add.35), channel_id=1, source_target_pairs={{0,16},{8,24},{16,0},{24,8},{1,17},{9,25},{17,1},{25,9},{2,18},{10... | collective-permute-start | bytes 4616 | tf_op jit(solution)/shard_map/ppermute | solution.py:249
  106.6 4.0 %project.7 = (bf16[2,384,384]{2,1,0:T(8,128)(2,1)S(1)}, f32[2,384,384]{2,1,0:T(8,128)S(1)}) custom-call(s32[2]{0:T(128)S(1)} %pad_add_fusion.place_ref, bf16[512,2048]{1,0:T(8,128)(2,1)S(1)} %get-tuple-element.63.refs_0_, bf16[512,2048]{1,0:T(8,128)(2,1)S(1)} %get-tuple-element.64.refs_1_, bf16[512,2048]{1,0:T(8,128)(2,1)S(1)} %get-tuple-element.65.refs_2_, ...), custom_call_target="tpu_custom_call" | custom-call | tf_op jit(solution)/shard_map/project/pallas_call | solution.py:355
  110.8 6.6 %collective-permute-done.23.refs_2_.refs_8_ = bf16[1,128,896]{2,1,0:T(8,128)(2,1)S(1)} collective-permute-done((bf16[1,128,896]{2,1,0:T(8,128)(2,1)S(1)}, bf16[1,128,896]{2,1,0:T(8,128)(2,1)S(1)}, u32[]{:S(2)}, u32[]{:S(2)}) %collective-permute-start.23) | collective-permute-done | bytes 229408 | tf_op jit(solution)/shard_map/ppermute | solution.py:249
  117.7 5.9 %collective-permute-done.25.refs_1_.refs_10_ = bf16[2,128,896]{2,1,0:T(8,128)(2,1)S(1)} collective-permute-done((bf16[2,128,896]{2,1,0:T(8,128)(2,1)S(1)}, bf16[2,128,896]{2,1,0:T(8,128)(2,1)S(1)}, u32[]{:S(2)}, u32[]{:S(2)}) %collective-permute-start.25) | collective-permute-done | bytes 458784 | tf_op jit(solution)/shard_map/ppermute | solution.py:249
  123.7 3.1 %collective-permute-done.24 = bf16[1,256,256]{2,1,0:T(8,128)(2,1)S(1)} collective-permute-done((bf16[1,256,256]{2,1,0:T(8,128)(2,1)S(1)}, bf16[1,256,256]{2,1,0:T(8,128)(2,1)S(1)}, u32[]{:S(2)}, u32[]{:S(2)}) %collective-permute-start.24) | collective-permute-done | bytes 131104 | tf_op jit(solution)/shard_map/ppermute | solution.py:249
  126.8 2.0 %collective-permute-start.29 = (bf16[2,384,384]{2,1,0:T(8,128)(2,1)S(1)}, bf16[2,384,384]{2,1,0:T(8,128)(2,1)S(1)}, u32[]{:S(2)}, u32[]{:S(2)}) collective-permute-start(bf16[2,384,384]{2,1,0:T(8,128)(2,1)S(1)} %get-tuple-element.76), channel_id=1, source_target_pairs={{0,2},{1,3},{2,0},{3,1},{4,6},{5,7},{6,4},{7,5},{8,10},{9,11},{10,... | collective-permute-start | bytes 1769480 | tf_op jit(solution)/shard_map/ppermute | solution.py:249
  128.9 7.2 %collective-permute-done.26 = bf16[2,256,256]{2,1,0:T(8,128)(2,1)S(1)} collective-permute-done((bf16[2,256,256]{2,1,0:T(8,128)(2,1)S(1)}, bf16[2,256,256]{2,1,0:T(8,128)(2,1)S(1)}, u32[]{:S(2)}, u32[]{:S(2)}) %collective-permute-start.26) | collective-permute-done | bytes 262176 | tf_op jit(solution)/shard_map/ppermute | solution.py:249
  137.2 15.0 %collective-permute-done.29.refs_4_ = bf16[2,384,384]{2,1,0:T(8,128)(2,1)S(1)} collective-permute-done((bf16[2,384,384]{2,1,0:T(8,128)(2,1)S(1)}, bf16[2,384,384]{2,1,0:T(8,128)(2,1)S(1)}, u32[]{:S(2)}, u32[]{:S(2)}) %collective-permute-start.29) | collective-permute-done | bytes 589856 | tf_op jit(solution)/shard_map/ppermute | solution.py:249
  153.3 5.1 %attend.2.refs_6_ = bf16[384,1024]{1,0:T(8,128)(2,1)} custom-call(s32[1]{0:T(128)} %bitcast.device_ref, s32[24]{0:T(128)S(1)} %copy-done.3, s32[24]{0:T(128)S(1)} %copy-done.4, f32[384,128]{1,0:T(8,128)S(1)} %broadcast_in_dim.33.inverse_ref, f32[1,640]{1,0:T(1,128)S(1)} %broadcast_in_dim.40.bias_ref, f32[384,128]{1,0:T(8,128)S(1)} %copy-done.1, ...), custom_call_target="tpu_custom_call" | custom-call | flops 1132462080 | bytes 491520 | tf_op jit(solution)/shard_map/attend/pallas_call | solution.py:482
  158.4 7.8 %collective-permute-done.30.refs_5_ = bf16[1,384,384]{2,1,0:T(8,128)(2,1)S(1)} collective-permute-done((bf16[1,384,384]{2,1,0:T(8,128)(2,1)S(1)}, bf16[1,384,384]{2,1,0:T(8,128)(2,1)S(1)}, u32[]{:S(2)}, u32[]{:S(2)}) %collective-permute-start.30) | collective-permute-done | bytes 294944 | tf_op jit(solution)/shard_map/ppermute | solution.py:249
  166.1 3.8 %attend.3 = bf16[384,1024]{1,0:T(8,128)(2,1)} custom-call(s32[1]{0:T(128)} %bitcast.device_ref, s32[24]{0:T(128)S(1)} %copy-done.3, s32[24]{0:T(128)S(1)} %copy-done.4, f32[384,128]{1,0:T(8,128)S(1)} %broadcast_in_dim.33.inverse_ref, f32[1,384]{1,0:T(1,128)S(1)} %broadcast_in_dim.34.bias_ref, ...), custom_call_target="tpu_custom_call", output_to_operand_aliasing={{}: (14, {})} | custom-call | flops 679477248 | bytes 294912 | tf_op jit(solution)/shard_map/attend/pallas_call | solution.py:482
  (92 shorter events, 14.9 us)
Async XLA Ops:
  3.6 5.1 %collective-permute-start = (bf16[128,2048]{1,0:T(8,128)(2,1)S(1)}, bf16[128,2048]{1,0:T(8,128)(2,1)}, u32[]{:S(2)}, u32[]{:S(2)}) collective-permute-start(bf16[128,2048]{1,0:T(8,128)(2,1)S(1)} %get-tuple-element.81), channel_id=1, source_target_pairs={{0,0},{8,16},{16,8},{24,24},{1,1},{9,17},{17,9},{25,25},{2,26},{10... | collective-permute-start | bytes 1572872 | tf_op jit(solution)/shard_map/ppermute | solution.py:301
  8.7 10.0 %collective-permute-start.1 = (bf16[128,2048]{1,0:T(8,128)(2,1)}, bf16[128,2048]{1,0:T(8,128)(2,1)S(1)}, u32[]{:S(2)}, u32[]{:S(2)}) collective-permute-start(bf16[128,2048]{1,0:T(8,128)(2,1)} %get-tuple-element.44), channel_id=1, source_target_pairs={{0,0},{8,16},{16,8},{24,24},{1,1},{9,17},{17,9},{25,25},{2,26},{10... | collective-permute-start | bytes 1572872 | tf_op jit(solution)/shard_map/ppermute | solution.py:301
  10.4 37.4 %collective-permute-start.9 = (bf16[1024,640]{1,0:T(8,128)(2,1)S(1)}, bf16[1024,640]{1,0:T(8,128)(2,1)S(1)}, u32[]{:S(2)}, u32[]{:S(2)}) collective-permute-start(bf16[1024,640]{1,0:T(8,128)(2,1)S(1)} %slice.82.refs_6_), channel_id=1, source_target_pairs={{0,1},{1,0},{2,3},{3,2},{4,5},{5,4},{6,7},{7,6},{8,9},{9,8},{10,11... | collective-permute-start | bytes 3932168 | tf_op jit(solution)/shard_map/ppermute | solution.py:249
  13.3 12.2 %collective-permute-start.3 = (bf16[128,2048]{1,0:T(8,128)(2,1)}, bf16[128,2048]{1,0:T(8,128)(2,1)}, u32[]{:S(2)}, u32[]{:S(2)}) collective-permute-start(bf16[128,2048]{1,0:T(8,128)(2,1)} %collective-permute-done), channel_id=1, source_target_pairs={{0,0},{16,18},{8,12},{24,30},{1,1},{17,19},{9,13},{25,31},{26,16},... | collective-permute-start | bytes 1572872 | tf_op jit(solution)/shard_map/ppermute | solution.py:304
  18.7 6.8 %collective-permute-start.4 = (bf16[128,2048]{1,0:T(8,128)(2,1)}, bf16[128,2048]{1,0:T(8,128)(2,1)}, u32[]{:S(2)}, u32[]{:S(2)}) collective-permute-start(bf16[128,2048]{1,0:T(8,128)(2,1)} %get-tuple-element.45), channel_id=1, source_target_pairs={{0,0},{8,16},{16,8},{24,24},{1,1},{9,17},{17,9},{25,25},{2,26},{10... | collective-permute-start | bytes 1572872 | tf_op jit(solution)/shard_map/ppermute | solution.py:301
  24.1 20.1 %collective-permute-start.2 = (bf16[128,2048]{1,0:T(8,128)(2,1)S(1)}, bf16[128,2048]{1,0:T(8,128)(2,1)}, u32[]{:S(2)}, u32[]{:S(2)}) collective-permute-start(bf16[128,2048]{1,0:T(8,128)(2,1)S(1)} %collective-permute-done.1), channel_id=1, source_target_pairs={{0,0},{16,18},{8,12},{24,30},{1,1},{17,19},{9,13},{25,31},{26,16},... | collective-permute-start | bytes 1572872 | tf_op jit(solution)/shard_map/ppermute | solution.py:304
  25.5 26.3 %collective-permute-start.6 = (bf16[128,2048]{1,0:T(8,128)(2,1)}, bf16[128,2048]{1,0:T(8,128)(2,1)}, u32[]{:S(2)}, u32[]{:S(2)}) collective-permute-start(bf16[128,2048]{1,0:T(8,128)(2,1)} %collective-permute-done.3.refs_0_), channel_id=1, source_target_pairs={{0,16},{8,24},{16,0},{24,8},{1,17},{9,25},{17,1},{25,9},{2,18},{10... | collective-permute-start | bytes 1572872 | tf_op jit(solution)/shard_map/ppermute | solution.py:249
  38.8 13.1 %collective-permute-start.5 = (bf16[128,2048]{1,0:T(8,128)(2,1)}, bf16[128,2048]{1,0:T(8,128)(2,1)}, u32[]{:S(2)}, u32[]{:S(2)}) collective-permute-start(bf16[128,2048]{1,0:T(8,128)(2,1)} %collective-permute-done.4), channel_id=1, source_target_pairs={{0,0},{16,18},{8,12},{24,30},{1,1},{17,19},{9,13},{25,31},{26,16},... | collective-permute-start | bytes 1572872 | tf_op jit(solution)/shard_map/ppermute | solution.py:304
  44.1 18.9 %collective-permute-start.11 = (bf16[128,2048]{1,0:T(8,128)(2,1)}, bf16[128,2048]{1,0:T(8,128)(2,1)}, u32[]{:S(2)}, u32[]{:S(2)}) collective-permute-start(bf16[128,2048]{1,0:T(8,128)(2,1)} %collective-permute-done.2.refs_0_), channel_id=1, source_target_pairs={{0,16},{8,24},{16,0},{24,8},{1,17},{9,25},{17,1},{25,9},{2,18},{10... | collective-permute-start | bytes 1572872 | tf_op jit(solution)/shard_map/ppermute | solution.py:249
  47.8 15.3 %collective-permute-start.10 = (bf16[1024,256]{1,0:T(8,128)(2,1)S(1)}, bf16[1024,256]{1,0:T(8,128)(2,1)}, u32[]{:S(2)}, u32[]{:S(2)}) collective-permute-start(bf16[1024,256]{1,0:T(8,128)(2,1)S(1)} %constant_dynamic-update-slice_fusion.refs_4_), channel_id=1, source_target_pairs={{0,1},{1,0},{2,3},{3,2},{4,5},{5,4},{6,7},{7,6},{8,9},{9,8},{10,11... | collective-permute-start | bytes 1572872 | tf_op jit(solution)/shard_map/ppermute | solution.py:249
  48.3 14.8 %collective-permute-start.7 = (bf16[128,2048]{1,0:T(8,128)(2,1)}, bf16[128,2048]{1,0:T(8,128)(2,1)}, u32[]{:S(2)}, u32[]{:S(2)}) collective-permute-start(bf16[128,2048]{1,0:T(8,128)(2,1)} %collective-permute-done.3.refs_0_), channel_id=1, source_target_pairs={{0,8},{8,0},{16,24},{24,16},{1,9},{9,1},{17,25},{25,17},{2,10},{10... | collective-permute-start | bytes 1572872 | tf_op jit(solution)/shard_map/ppermute | solution.py:249
  51.8 11.3 %collective-permute-start.8 = (bf16[128,2048]{1,0:T(8,128)(2,1)}, bf16[128,2048]{1,0:T(8,128)(2,1)}, u32[]{:S(2)}, u32[]{:S(2)}) collective-permute-start(bf16[128,2048]{1,0:T(8,128)(2,1)} %collective-permute-done.6.refs_1_), channel_id=1, source_target_pairs={{0,8},{8,0},{16,24},{24,16},{1,9},{9,1},{17,25},{25,17},{2,10},{10... | collective-permute-start | bytes 1572872 | tf_op jit(solution)/shard_map/ppermute | solution.py:249
  51.8 19.8 %collective-permute-start.12 = (bf16[128,2048]{1,0:T(8,128)(2,1)}, bf16[128,2048]{1,0:T(8,128)(2,1)S(1)}, u32[]{:S(2)}, u32[]{:S(2)}) collective-permute-start(bf16[128,2048]{1,0:T(8,128)(2,1)} %collective-permute-done.2.refs_0_), channel_id=1, source_target_pairs={{0,8},{8,0},{16,24},{24,16},{1,9},{9,1},{17,25},{25,17},{2,10},{10... | collective-permute-start | bytes 1572872 | tf_op jit(solution)/shard_map/ppermute | solution.py:249
  63.0 8.6 %collective-permute-start.13 = (bf16[128,2048]{1,0:T(8,128)(2,1)}, bf16[128,2048]{1,0:T(8,128)(2,1)S(1)}, u32[]{:S(2)}, u32[]{:S(2)}) collective-permute-start(bf16[128,2048]{1,0:T(8,128)(2,1)} %collective-permute-done.11.refs_1_), channel_id=1, source_target_pairs={{0,8},{8,0},{16,24},{24,16},{1,9},{9,1},{17,25},{25,17},{2,10},{10... | collective-permute-start | bytes 1572872 | tf_op jit(solution)/shard_map/ppermute | solution.py:249
  68.1 13.0 %collective-permute-start.14 = (bf16[2,128,896]{2,1,0:T(8,128)(2,1)S(1)}, bf16[2,128,896]{2,1,0:T(8,128)(2,1)S(1)}, u32[]{:S(2)}, u32[]{:S(2)}) collective-permute-start(bf16[2,128,896]{2,1,0:T(8,128)(2,1)S(1)} %get-tuple-element.49), channel_id=1, source_target_pairs={{0,2},{1,3},{2,0},{3,1},{4,6},{5,7},{6,4},{7,5},{8,10},{9,11},{10,... | collective-permute-start | bytes 1376264 | tf_op jit(solution)/shard_map/ppermute | solution.py:249
  69.9 14.3 %collective-permute-start.16 = (bf16[128,2048]{1,0:T(8,128)(2,1)}, bf16[128,2048]{1,0:T(8,128)(2,1)S(1)}, u32[]{:S(2)}, u32[]{:S(2)}) collective-permute-start(bf16[128,2048]{1,0:T(8,128)(2,1)} %collective-permute-done.5.refs_0_), channel_id=1, source_target_pairs={{0,16},{8,24},{16,0},{24,8},{1,17},{9,25},{17,1},{25,9},{2,18},{10... | collective-permute-start | bytes 1572872 | tf_op jit(solution)/shard_map/ppermute | solution.py:249
  84.1 5.4 %collective-permute-start.18 = (bf16[128,2048]{1,0:T(8,128)(2,1)S(1)}, bf16[128,2048]{1,0:T(8,128)(2,1)S(1)}, u32[]{:S(2)}, u32[]{:S(2)}) collective-permute-start(bf16[128,2048]{1,0:T(8,128)(2,1)S(1)} %collective-permute-done.16.refs_1_), channel_id=1, source_target_pairs={{0,8},{8,0},{16,24},{24,16},{1,9},{9,1},{17,25},{25,17},{2,10},{10... | collective-permute-start | bytes 1572872 | tf_op jit(solution)/shard_map/ppermute | solution.py:249
  84.1 5.4 %collective-permute-start.17 = (bf16[128,2048]{1,0:T(8,128)(2,1)}, bf16[128,2048]{1,0:T(8,128)(2,1)S(1)}, u32[]{:S(2)}, u32[]{:S(2)}) collective-permute-start(bf16[128,2048]{1,0:T(8,128)(2,1)} %collective-permute-done.5.refs_0_), channel_id=1, source_target_pairs={{0,8},{8,0},{16,24},{24,16},{1,9},{9,1},{17,25},{25,17},{2,10},{10... | collective-permute-start | bytes 1572872 | tf_op jit(solution)/shard_map/ppermute | solution.py:249
  84.6 17.3 %collective-permute-start.15 = (bf16[2,128,896]{2,1,0:T(8,128)(2,1)S(1)}, bf16[2,128,896]{2,1,0:T(8,128)(2,1)S(1)}, u32[]{:S(2)}, u32[]{:S(2)}) collective-permute-start(bf16[2,128,896]{2,1,0:T(8,128)(2,1)S(1)} %get-tuple-element.55), channel_id=1, source_target_pairs={{0,2},{1,3},{2,0},{3,1},{4,6},{5,7},{6,4},{7,5},{8,10},{9,11},{10,... | collective-permute-start | bytes 1376264 | tf_op jit(solution)/shard_map/ppermute | solution.py:249
  85.0 21.6 %collective-permute-start.22 = (bf16[1024,384]{1,0:T(8,128)(2,1)S(1)}, bf16[1024,384]{1,0:T(8,128)(2,1)S(1)}, u32[]{:S(2)}, u32[]{:S(2)}) collective-permute-start(bf16[1024,384]{1,0:T(8,128)(2,1)S(1)} %copy-done), channel_id=1, source_target_pairs={{0,1},{1,0},{2,3},{3,2},{4,5},{5,4},{6,7},{7,6},{8,9},{9,8},{10,11... | collective-permute-start | bytes 2359304 | tf_op jit(solution)/shard_map/ppermute | solution.py:249
  86.9 23.6 %collective-permute-start.21 = (bf16[1,128,896]{2,1,0:T(8,128)(2,1)S(1)}, bf16[1,128,896]{2,1,0:T(8,128)(2,1)S(1)}, u32[]{:S(2)}, u32[]{:S(2)}) collective-permute-start(bf16[1,128,896]{2,1,0:T(8,128)(2,1)S(1)} %fusion.6), channel_id=1, source_target_pairs={{0,4},{1,5},{2,6},{3,7},{4,0},{5,1},{6,2},{7,3},{8,12},{9,13},{10,... | collective-permute-start | bytes 688136 | tf_op jit(solution)/shard_map/ppermute | solution.py:249
  102.0 1.2 collective-permute-start.19
  103.3 7.3 %collective-permute-start.20 = (f32[3,128]{1,0:T(4,128)S(1)}, f32[3,128]{1,0:T(4,128)S(1)}, u32[]{:S(2)}, u32[]{:S(2)}) collective-permute-start(f32[3,128]{1,0:T(4,128)S(1)} %add.35), channel_id=1, source_target_pairs={{0,16},{8,24},{16,0},{24,8},{1,17},{9,25},{17,1},{25,9},{2,18},{10... | collective-permute-start | bytes 4616 | tf_op jit(solution)/shard_map/ppermute | solution.py:249
  105.0 12.4 %collective-permute-start.23 = (bf16[1,128,896]{2,1,0:T(8,128)(2,1)S(1)}, bf16[1,128,896]{2,1,0:T(8,128)(2,1)S(1)}, u32[]{:S(2)}, u32[]{:S(2)}) collective-permute-start(bf16[1,128,896]{2,1,0:T(8,128)(2,1)S(1)} %fusion.5), channel_id=1, source_target_pairs={{0,4},{1,5},{2,6},{3,7},{4,0},{5,1},{6,2},{7,3},{8,12},{9,13},{10,... | collective-permute-start | bytes 688136 | tf_op jit(solution)/shard_map/ppermute | solution.py:249
  105.1 18.5 %collective-permute-start.25 = (bf16[2,128,896]{2,1,0:T(8,128)(2,1)S(1)}, bf16[2,128,896]{2,1,0:T(8,128)(2,1)S(1)}, u32[]{:S(2)}, u32[]{:S(2)}) collective-permute-start(bf16[2,128,896]{2,1,0:T(8,128)(2,1)S(1)} %get-tuple-element.71), channel_id=1, source_target_pairs={{0,2},{1,3},{2,0},{3,1},{4,6},{5,7},{6,4},{7,5},{8,10},{9,11},{10,... | collective-permute-start | bytes 1376264 | tf_op jit(solution)/shard_map/ppermute | solution.py:249
  117.6 9.1 %collective-permute-start.24 = (bf16[1,256,256]{2,1,0:T(8,128)(2,1)S(1)}, bf16[1,256,256]{2,1,0:T(8,128)(2,1)S(1)}, u32[]{:S(2)}, u32[]{:S(2)}) collective-permute-start(bf16[1,256,256]{2,1,0:T(8,128)(2,1)S(1)} %maximum_bitcast_fusion), channel_id=1, source_target_pairs={{0,4},{1,5},{2,6},{3,7},{4,0},{5,1},{6,2},{7,3},{8,12},{9,13},{10,... | collective-permute-start | bytes 393224 | tf_op jit(solution)/shard_map/ppermute | solution.py:249
  123.7 28.7 %copy-start.9 = (f32[1024]{0:T(1024)S(1)}, f32[1024]{0:T(1024)}, u32[]{:S(2)}) copy-start(f32[1024]{0:T(1024)} %param.17) | copy-start | bytes 12292
  126.8 9.3 %collective-permute-start.26 = (bf16[2,256,256]{2,1,0:T(8,128)(2,1)S(1)}, bf16[2,256,256]{2,1,0:T(8,128)(2,1)S(1)}, u32[]{:S(2)}, u32[]{:S(2)}) collective-permute-start(bf16[2,256,256]{2,1,0:T(8,128)(2,1)S(1)} %pad_maximum_fusion.2), channel_id=1, source_target_pairs={{0,2},{1,3},{2,0},{3,1},{4,6},{5,7},{6,4},{7,5},{8,10},{9,11},{10,... | collective-permute-start | bytes 786440 | tf_op jit(solution)/shard_map/ppermute | solution.py:249
  126.8 25.3 %collective-permute-start.29 = (bf16[2,384,384]{2,1,0:T(8,128)(2,1)S(1)}, bf16[2,384,384]{2,1,0:T(8,128)(2,1)S(1)}, u32[]{:S(2)}, u32[]{:S(2)}) collective-permute-start(bf16[2,384,384]{2,1,0:T(8,128)(2,1)S(1)} %get-tuple-element.76), channel_id=1, source_target_pairs={{0,2},{1,3},{2,0},{3,1},{4,6},{5,7},{6,4},{7,5},{8,10},{9,11},{10,... | collective-permute-start | bytes 1769480 | tf_op jit(solution)/shard_map/ppermute | solution.py:249
  136.1 16.5 %collective-permute-start.27 = (bf16[4,256,256]{2,1,0:T(8,128)(2,1)S(1)}, bf16[4,256,256]{2,1,0:T(8,128)(2,1)S(1)}, u32[]{:S(2)}, u32[]{:S(2)}) collective-permute-start(bf16[4,256,256]{2,1,0:T(8,128)(2,1)S(1)} %pad_maximum_fusion.1), channel_id=1, source_target_pairs={{0,1},{1,0},{2,3},{3,2},{4,5},{5,4},{6,7},{7,6},{8,9},{9,8},{10,11... | collective-permute-start | bytes 1572872 | tf_op jit(solution)/shard_map/ppermute | solution.py:249
  137.0 15.4 %collective-permute-start.28 = (bf16[1,128,896]{2,1,0:T(8,128)(2,1)S(1)}, bf16[1,128,896]{2,1,0:T(8,128)(2,1)S(1)}, u32[]{:S(2)}, u32[]{:S(2)}) collective-permute-start(bf16[1,128,896]{2,1,0:T(8,128)(2,1)S(1)} %fusion.4), channel_id=1, source_target_pairs={{0,4},{1,5},{2,6},{3,7},{4,0},{5,1},{6,2},{7,3},{8,12},{9,13},{10,... | collective-permute-start | bytes 688136 | tf_op jit(solution)/shard_map/ppermute | solution.py:249
  152.3 13.9 %collective-permute-start.30 = (bf16[1,384,384]{2,1,0:T(8,128)(2,1)S(1)}, bf16[1,384,384]{2,1,0:T(8,128)(2,1)S(1)}, u32[]{:S(2)}, u32[]{:S(2)}) collective-permute-start(bf16[1,384,384]{2,1,0:T(8,128)(2,1)S(1)} %fusion.3), channel_id=1, source_target_pairs={{0,4},{1,5},{2,6},{3,7},{4,0},{5,1},{6,2},{7,3},{8,12},{9,13},{10,... | collective-permute-start | bytes 884744 | tf_op jit(solution)/shard_map/ppermute | solution.py:249
  (11 other events, 98.0 us)

commit v10 on v9

--- a/solution.py
+++ b/solution.py
@@ -271,6 +271,7 @@
 
     first_hop = []
     second_hop = []
+    both_hops = []
     for z in range(lines):
         for g in range(groups):
             for feature in range(lines):
@@ -278,7 +279,9 @@
                 there = feature * groups + g
                 stop = middle(z, feature) * branches + here
                 first_hop.append((feature * branches + here, stop))
-                second_hop.append((stop, landing(z, feature) * branches + there))
+                end = landing(z, feature) * branches + there
+                second_hop.append((stop, end))
+                both_hops.append((feature * branches + here, end))
     axes = ("fsdp", "branch")
     head_cuts = [0, (5 * head_count + 7) // 8, head_count]
     w_chunks = [jnp.concatenate([w_key, w_value], 1)] + [
@@ -294,14 +297,13 @@
         name="tables",
     )(device_id, parents)
 
-    sent = []
-    for block in range(blocks):
-        piece = (hidden[block].astype(f32) * gain_part).astype(bf16)
-        piece = tie(piece, sent[-1], cos, sin, *w_chunks) if block else piece
+    scaled = [(hidden[block].astype(f32) * gain_part).astype(bf16) for block in range(blocks)]
+    sent = [lax.ppermute(scaled[0], axes, both_hops)]
+    for block in range(1, blocks):
+        piece = tie(scaled[block], sent[-1], cos, sin, *w_chunks) if block > 1 else scaled[block]
         sent.append(lax.ppermute(piece, axes, first_hop))
-
     last_sent = sent[-1]
-    sent = [lax.ppermute(piece, axes, second_hop) for piece in sent]
+    sent = sent[:1] + [lax.ppermute(piece, axes, second_hop) for piece in sent[1:]]
     w_rows = [None] * len(w_chunks)
     arrived = None
     for c in (1, 0, 2):
@@ -310,6 +312,7 @@
         arrived = w_rows[c][-1]
 
     sent[0] = tie(sent[0], last_sent)
+    sent[1] = tie(sent[1], w_rows[1][-1])
     last_sent = sent[-1]
     held = [{0: piece} for piece in sent]
     bit = half_lines
@@ -418,13 +421,13 @@
     units[0].step()
     for block in range(1, blocks):
         before = units[-1]
+        gate = before.came
+        before.rest()
         if block > 1:
             held[block] = {j: tie(piece, gate) for j, piece in held[block].items()}
             held[block] = last_bit(held[block])
         units.append(Halving(project([(block, block + 1)], [0, 1], before.send)))
-        before.rest(units[-1].send)
-        gate = before.send
-        units[-1].step(gate)
+        units[-1].step()
 
     squares = jnp.sum(jnp.square(raw.astype(f32)), -1).reshape(blocks, block_len)
     squares = tie(squares, units[STEMS - 1].send)
@@ -435,19 +438,19 @@
     inverse = lax.rsqrt(squares / features + 1e-06).reshape(tokens)
     inverse = jnp.broadcast_to(inverse[:, None], (tokens, HD))
 
-    last = Halving(project([(b, b + 1) for b in range(blocks)], [2], units[STEMS - 1].send))
     stem_kv = []
     for block in range(STEMS):
         unit = units[block]
-        unit.addends[-1] = tie(unit.addends[-1], last.send)
+        unit.addends[-1] = tie(unit.addends[-1], units[-1].send)
         stem_kv.append(finish_kv(unit.addends, block, 1))
 
     tour = [groups << i for i in reversed(range(bits_of(lines)))]
     tour += [1 << i for i in range(bits_of(groups))]
     stems = jnp.concatenate(stem_kv, 0)[None]
     came = swap(stems, "branch", tour[0])
-    units[-1].rest(stems)
-    last.step(units[-1].send)
+    last = Halving(project([(b, b + 1) for b in range(blocks)], [2], stems))
+    last.step()
+    units[-1].rest(last.send)
     for step, bit in enumerate(tour[1:]):
         stems = jnp.concatenate([stems, tie(came, units[-1].send)], 0)
         came = swap(stems, "branch", bit)

time: 171 us -> 180 us (1.053)
  waiting for transfers between devices: 70.8 us -> 76.6 us
    ppermute x25, waiting for transfers between devices: 70.8 us -> 76.6 us  [swap(): return lax.ppermute(array, axis, [(i, i ^ bit) for i in range(size)])]
    ppermute x25, starting transfers between devices: 41.5 us -> 36 us  [swap(): return lax.ppermute(array, axis, [(i, i ^ bit) for i in range(size)])]
    ppermute x3, starting transfers between devices: 12.2 us -> 16.1 us  [the longest x2 10.7 us: shards(): lax.ppermute(piece, axes, second_hop)]
    ppermute x3 -> x2, starting transfers between devices: 8.66 us -> 10.9 us  [shards(): sent.append(lax.ppermute(piece, axes, first_hop))]
  transfers between devices with their start and end apart: 31 -> 30, of which waited for: 12 -> 10; matrix products, arithmetic and copies ran while one was open for 1% -> 2% of each run, Pallas kernels for 15% -> 15%
where the time goes in v10:
time: 180 us; the launch traced here: 178 us
  waiting for transfers between devices  76.6 us (43%)
  starting transfers between devices  63 us (35%)
  Pallas kernels  29.8 us (17%)
  local copies, waits for them, and re-layouts  4.05 us (2%)
  other arithmetic  3.73 us (2%)
    ppermute x25, waiting for transfers between devices, swap(): return lax.ppermute(array, axis, [(i, i ^ bit) for i in range(size)])  76.6 us
    ppermute x25, starting transfers between devices, swap(): return lax.ppermute(array, axis, [(i, i ^ bit) for i in range(size)])  36 us
    pallas_call x4, Pallas kernels, project(): pl.pallas_call(functools.partial(project_kernel, lines, groups, len(chunk...  18.4 us
    ppermute x2, starting transfers between devices, shards(): sent.append(lax.ppermute(piece, axes, first_hop))  10.9 us
    ppermute x2, starting transfers between devices, shards(): lax.ppermute(piece, axes, second_hop)  10.7 us
    pallas_call x2, Pallas kernels, attend(): pl.pallas_call(kernel, grid=(1,), in_specs=in_specs, out_specs=anywhere,...  8.92 us
    ppermute x1, starting transfers between devices, shards(): sent = [lax.ppermute(scaled[0], axes, both_hops)]  5.37 us
  transfers between devices with their start and end apart: 30, of which 10 were waited for; matrix products, arithmetic and copies ran while one was open for 2% of the time, Pallas kernels for 15%

profile of v10, /device:TPU:0, one launch (start us, length us, event | category | flops | bytes accessed | tf_op | source)
XLA Modules:
  0.0 177.7 jit_solution(16369741350856317553)
XLA Ops:
  0.7 2.8 %fusion = (bf16[128,2048]{1,0:T(8,128)(2,1)}, bf16[128,2048]{1,0:T(8,128)(2,1)}, bf16[128,2048]{1,0:T(8,128)(2,1)}) fusion(bf16[3,128,2048]{2,1,0:T(8,128)(2,1)} %param.10, f32[2048]{0:T(1024)S(1)} %dynamic_slice.3), kind=kLoop, calls=%fused_computation.3 | loop fusion | flops 2359296 | bytes 3153920 | tf_op jit(solution)/shard_map/convert_element_type | solution.py:300
  3.5 5.5 %collective-permute-start = (bf16[128,2048]{1,0:T(8,128)(2,1)}, bf16[128,2048]{1,0:T(8,128)(2,1)}, u32[]{:S(2)}, u32[]{:S(2)}) collective-permute-start(bf16[128,2048]{1,0:T(8,128)(2,1)} %get-tuple-element.70), channel_id=1, source_target_pairs={{0,0},{8,16},{16,8},{24,24},{1,1},{9,17},{17,9},{25,25},{2,26},{10... | collective-permute-start | bytes 1572872 | tf_op jit(solution)/shard_map/ppermute | solution.py:304
  9.2 3.0 %collective-permute-start.2 = (bf16[1024,640]{1,0:T(8,128)(2,1)S(1)}, bf16[1024,640]{1,0:T(8,128)(2,1)S(1)}, u32[]{:S(2)}, u32[]{:S(2)}) collective-permute-start(bf16[1024,640]{1,0:T(8,128)(2,1)S(1)} %slice.81.refs_6_), channel_id=1, source_target_pairs={{0,1},{1,0},{2,3},{3,2},{4,5},{5,4},{6,7},{7,6},{8,9},{9,8},{10,11... | collective-permute-start | bytes 3932168 | tf_op jit(solution)/shard_map/ppermute | solution.py:249
  12.2 5.4 %collective-permute-start.3 = (bf16[128,2048]{1,0:T(8,128)(2,1)}, bf16[128,2048]{1,0:T(8,128)(2,1)}, u32[]{:S(2)}, u32[]{:S(2)}) collective-permute-start(bf16[128,2048]{1,0:T(8,128)(2,1)} %get-tuple-element.71), channel_id=1, source_target_pairs={{0,0},{8,18},{16,12},{24,30},{1,1},{9,19},{17,13},{25,31},{2,16},{... | collective-permute-start | bytes 1572872 | tf_op jit(solution)/shard_map/ppermute | solution.py:301
  18.5 2.2 %tables.1 = (f32[384,128]{1,0:T(8,128)}, f32[384,128]{1,0:T(8,128)}) custom-call(s32[1]{0:T(128)} %bitcast.device_ref, s32[24]{0:T(128)} %parents_ref.5), custom_call_target="tpu_custom_call" | custom-call | tf_op jit(solution)/shard_map/tables/pallas_call | solution.py:292
  20.8 1.0 constant_dynamic-update-slice_fusion.refs_4_
  21.8 5.4 %collective-permute-start.4 = (bf16[128,2048]{1,0:T(8,128)(2,1)}, bf16[128,2048]{1,0:T(8,128)(2,1)}, u32[]{:S(2)}, u32[]{:S(2)}) collective-permute-start(bf16[128,2048]{1,0:T(8,128)(2,1)} %get-tuple-element.40), channel_id=1, source_target_pairs={{0,0},{8,16},{16,8},{24,24},{1,1},{9,17},{17,9},{25,25},{2,26},{10... | collective-permute-start | bytes 1572872 | tf_op jit(solution)/shard_map/ppermute | solution.py:304
  27.2 9.7 %collective-permute-start.6 = (bf16[128,2048]{1,0:T(8,128)(2,1)}, bf16[128,2048]{1,0:T(8,128)(2,1)}, u32[]{:S(2)}, u32[]{:S(2)}) collective-permute-start(bf16[128,2048]{1,0:T(8,128)(2,1)} %collective-permute-done.3.refs_0_), channel_id=1, source_target_pairs={{0,16},{8,24},{16,0},{24,8},{1,17},{9,25},{17,1},{25,9},{2,18},{10... | collective-permute-start | bytes 1572872 | tf_op jit(solution)/shard_map/ppermute | solution.py:249
  36.8 5.4 %collective-permute-start.1 = (bf16[128,2048]{1,0:T(8,128)(2,1)}, bf16[128,2048]{1,0:T(8,128)(2,1)}, u32[]{:S(2)}, u32[]{:S(2)}) collective-permute-start(bf16[128,2048]{1,0:T(8,128)(2,1)} %collective-permute-done), channel_id=1, source_target_pairs={{0,0},{16,18},{8,12},{24,30},{1,1},{17,19},{9,13},{25,31},{26,16},... | collective-permute-start | bytes 1572872 | tf_op jit(solution)/shard_map/ppermute | solution.py:306
  42.2 1.7 collective-permute-start.7
  43.9 5.4 %collective-permute-start.5 = (bf16[128,2048]{1,0:T(8,128)(2,1)}, bf16[128,2048]{1,0:T(8,128)(2,1)}, u32[]{:S(2)}, u32[]{:S(2)}) collective-permute-start(bf16[128,2048]{1,0:T(8,128)(2,1)} %collective-permute-done.4), channel_id=1, source_target_pairs={{0,0},{16,18},{8,12},{24,30},{1,1},{17,19},{9,13},{25,31},{26,16},... | collective-permute-start | bytes 1572872 | tf_op jit(solution)/shard_map/ppermute | solution.py:306
  49.8 2.3 %collective-permute-start.11 = (bf16[128,2048]{1,0:T(8,128)(2,1)}, bf16[128,2048]{1,0:T(8,128)(2,1)}, u32[]{:S(2)}, u32[]{:S(2)}) collective-permute-start(bf16[128,2048]{1,0:T(8,128)(2,1)} %collective-permute-done.1.refs_0_), channel_id=1, source_target_pairs={{0,16},{8,24},{16,0},{24,8},{1,17},{9,25},{17,1},{25,9},{2,18},{10... | collective-permute-start | bytes 1572872 | tf_op jit(solution)/shard_map/ppermute | solution.py:249
  52.2 7.7 %collective-permute-done.9.refs_5_ = bf16[1024,256]{1,0:T(8,128)(2,1)} collective-permute-done((bf16[1024,256]{1,0:T(8,128)(2,1)S(1)}, bf16[1024,256]{1,0:T(8,128)(2,1)}, u32[]{:S(2)}, u32[]{:S(2)}) %collective-permute-start.9) | collective-permute-done | bytes 524320 | tf_op jit(solution)/shard_map/ppermute | solution.py:249
  59.8 5.0 %project.4 = (bf16[2,128,896]{2,1,0:T(8,128)(2,1)S(1)}, f32[2,128,896]{2,1,0:T(8,128)S(1)}, bf16[512,2048]{1,0:T(8,128)(2,1)S(1)}) custom-call(s32[2]{0:T(128)S(1)} %pad_add_fusion.place_ref, bf16[128,2048]{1,0:T(8,128)(2,1)} %collective-permute-done.3.refs_0_, bf16[128,2048]{1,0:T(8,128)(2,1)} %collective-permute-done.6.refs_1_, ...), custom_call_target="tpu_custom_call" | custom-call | tf_op jit(solution)/shard_map/project/pallas_call | solution.py:358
  64.8 8.7 %collective-permute-start.10 = (bf16[2,128,896]{2,1,0:T(8,128)(2,1)S(1)}, bf16[2,128,896]{2,1,0:T(8,128)(2,1)S(1)}, u32[]{:S(2)}, u32[]{:S(2)}) collective-permute-start(bf16[2,128,896]{2,1,0:T(8,128)(2,1)S(1)} %get-tuple-element.45), channel_id=1, source_target_pairs={{0,2},{1,3},{2,0},{3,1},{4,6},{5,7},{6,4},{7,5},{8,10},{9,11},{10,... | collective-permute-start | bytes 1376264 | tf_op jit(solution)/shard_map/ppermute | solution.py:249
  74.0 10.2 %collective-permute-done.10.refs_1_.refs_4_ = bf16[2,128,896]{2,1,0:T(8,128)(2,1)S(1)} collective-permute-done((bf16[2,128,896]{2,1,0:T(8,128)(2,1)S(1)}, bf16[2,128,896]{2,1,0:T(8,128)(2,1)S(1)}, u32[]{:S(2)}, u32[]{:S(2)}) %collective-permute-start.10) | collective-permute-done | bytes 458784 | tf_op jit(solution)/shard_map/ppermute | solution.py:249
  84.4 4.8 %project.5 = (bf16[2,128,896]{2,1,0:T(8,128)(2,1)S(1)}, f32[2,128,896]{2,1,0:T(8,128)S(1)}, bf16[512,2048]{1,0:T(8,128)(2,1)S(1)}) custom-call(s32[2]{0:T(128)S(1)} %pad_add_fusion.place_ref, bf16[128,2048]{1,0:T(8,128)(2,1)} %collective-permute-done.1.refs_0_, bf16[128,2048]{1,0:T(8,128)(2,1)} %collective-permute-done.11.refs_1_, ...), custom_call_target="tpu_custom_call" | custom-call | tf_op jit(solution)/shard_map/project/pallas_call | solution.py:358
  90.8 10.5 %collective-permute-done.14.refs_1_.refs_7_ = bf16[2,128,896]{2,1,0:T(8,128)(2,1)S(1)} collective-permute-done((bf16[2,128,896]{2,1,0:T(8,128)(2,1)S(1)}, bf16[2,128,896]{2,1,0:T(8,128)(2,1)S(1)}, u32[]{:S(2)}, u32[]{:S(2)}) %collective-permute-start.14) | collective-permute-done | bytes 458784 | tf_op jit(solution)/shard_map/ppermute | solution.py:249
  102.0 1.9 %collective-permute-done.15 = f32[3,128]{1,0:T(4,128)S(1)} collective-permute-done((f32[3,128]{1,0:T(4,128)S(1)}, f32[3,128]{1,0:T(4,128)S(1)}, u32[]{:S(2)}, u32[]{:S(2)}) %collective-permute-start.15) | collective-permute-done | bytes 1568 | tf_op jit(solution)/shard_map/ppermute | solution.py:249
  103.9 1.1 collective-permute-start.16
  105.2 2.9 %collective-permute-start.21 = (bf16[1,128,896]{2,1,0:T(8,128)(2,1)S(1)}, bf16[1,128,896]{2,1,0:T(8,128)(2,1)S(1)}, u32[]{:S(2)}, u32[]{:S(2)}) collective-permute-start(bf16[1,128,896]{2,1,0:T(8,128)(2,1)S(1)} %fusion.5), channel_id=1, source_target_pairs={{0,4},{1,5},{2,6},{3,7},{4,0},{5,1},{6,2},{7,3},{8,12},{9,13},{10,... | collective-permute-start | bytes 688136 | tf_op jit(solution)/shard_map/ppermute | solution.py:249
  108.1 4.6 %project.6 = (bf16[2,128,896]{2,1,0:T(8,128)(2,1)S(1)}, f32[2,128,896]{2,1,0:T(8,128)S(1)}, bf16[512,2048]{1,0:T(8,128)(2,1)S(1)}) custom-call(s32[2]{0:T(128)S(1)} %pad_add_fusion.place_ref, bf16[128,2048]{1,0:T(8,128)(2,1)} %collective-permute-done.5.refs_0_, bf16[128,2048]{1,0:T(8,128)(2,1)S(1)} %collective-permute-done.18.refs_1_, ...), custom_call_target="tpu_custom_call" | custom-call | tf_op jit(solution)/shard_map/project/pallas_call | solution.py:358
  113.6 10.2 %collective-permute-done.17.refs_2_.refs_5_ = bf16[1,128,896]{2,1,0:T(8,128)(2,1)S(1)} collective-permute-done((bf16[1,128,896]{2,1,0:T(8,128)(2,1)S(1)}, bf16[1,128,896]{2,1,0:T(8,128)(2,1)S(1)}, u32[]{:S(2)}, u32[]{:S(2)}) %collective-permute-start.17) | collective-permute-done | bytes 229408 | tf_op jit(solution)/shard_map/ppermute | solution.py:249
  123.8 4.5 %collective-permute-done.21.refs_2_.refs_8_ = bf16[1,128,896]{2,1,0:T(8,128)(2,1)S(1)} collective-permute-done((bf16[1,128,896]{2,1,0:T(8,128)(2,1)S(1)}, bf16[1,128,896]{2,1,0:T(8,128)(2,1)S(1)}, u32[]{:S(2)}, u32[]{:S(2)}) %collective-permute-start.21) | collective-permute-done | bytes 229408 | tf_op jit(solution)/shard_map/ppermute | solution.py:249
  128.8 4.0 %project.7 = (bf16[2,384,384]{2,1,0:T(8,128)(2,1)S(1)}, f32[2,384,384]{2,1,0:T(8,128)S(1)}) custom-call(s32[2]{0:T(128)S(1)} %pad_add_fusion.place_ref, bf16[512,2048]{1,0:T(8,128)(2,1)S(1)} %get-tuple-element.58.refs_0_, bf16[512,2048]{1,0:T(8,128)(2,1)S(1)} %get-tuple-element.59.refs_1_, bf16[512,2048]{1,0:T(8,128)(2,1)S(1)} %get-tuple-element.60.refs_2_, ...), custom_call_target="tpu_custom_call" | custom-call | tf_op jit(solution)/shard_map/project/pallas_call | solution.py:358
  132.8 3.9 %collective-permute-done.23.refs_1_.refs_10_ = bf16[2,128,896]{2,1,0:T(8,128)(2,1)S(1)} collective-permute-done((bf16[2,128,896]{2,1,0:T(8,128)(2,1)S(1)}, bf16[2,128,896]{2,1,0:T(8,128)(2,1)S(1)}, u32[]{:S(2)}, u32[]{:S(2)}) %collective-permute-start.23) | collective-permute-done | bytes 458784 | tf_op jit(solution)/shard_map/ppermute | solution.py:249
  136.8 2.0 %collective-permute-start.28 = (bf16[2,384,384]{2,1,0:T(8,128)(2,1)S(1)}, bf16[2,384,384]{2,1,0:T(8,128)(2,1)S(1)}, u32[]{:S(2)}, u32[]{:S(2)}) collective-permute-start(bf16[2,384,384]{2,1,0:T(8,128)(2,1)S(1)} %get-tuple-element.62), channel_id=1, source_target_pairs={{0,2},{1,3},{2,0},{3,1},{4,6},{5,7},{6,4},{7,5},{8,10},{9,11},{10,... | collective-permute-start | bytes 1769480 | tf_op jit(solution)/shard_map/ppermute | solution.py:249
  138.8 7.2 %collective-permute-done.25 = bf16[2,256,256]{2,1,0:T(8,128)(2,1)S(1)} collective-permute-done((bf16[2,256,256]{2,1,0:T(8,128)(2,1)S(1)}, bf16[2,256,256]{2,1,0:T(8,128)(2,1)S(1)}, u32[]{:S(2)}, u32[]{:S(2)}) %collective-permute-start.25) | collective-permute-done | bytes 262176 | tf_op jit(solution)/shard_map/ppermute | solution.py:249
  146.5 13.9 %collective-permute-done.28.refs_4_ = bf16[2,384,384]{2,1,0:T(8,128)(2,1)S(1)} collective-permute-done((bf16[2,384,384]{2,1,0:T(8,128)(2,1)S(1)}, bf16[2,384,384]{2,1,0:T(8,128)(2,1)S(1)}, u32[]{:S(2)}, u32[]{:S(2)}) %collective-permute-start.28) | collective-permute-done | bytes 589856 | tf_op jit(solution)/shard_map/ppermute | solution.py:249
  162.0 5.1 %attend.2.refs_6_ = bf16[384,1024]{1,0:T(8,128)(2,1)} custom-call(s32[1]{0:T(128)} %bitcast.device_ref, s32[24]{0:T(128)S(1)} %copy-done.3, s32[24]{0:T(128)S(1)} %copy-done.4, f32[384,128]{1,0:T(8,128)S(1)} %broadcast_in_dim.33.inverse_ref, f32[1,640]{1,0:T(1,128)S(1)} %broadcast_in_dim.40.bias_ref, f32[384,128]{1,0:T(8,128)S(1)} %copy-done.1, ...), custom_call_target="tpu_custom_call" | custom-call | flops 1132462080 | bytes 491520 | tf_op jit(solution)/shard_map/attend/pallas_call | solution.py:485
  167.1 6.7 %collective-permute-done.29.refs_5_ = bf16[1,384,384]{2,1,0:T(8,128)(2,1)S(1)} collective-permute-done((bf16[1,384,384]{2,1,0:T(8,128)(2,1)S(1)}, bf16[1,384,384]{2,1,0:T(8,128)(2,1)S(1)}, u32[]{:S(2)}, u32[]{:S(2)}) %collective-permute-start.29) | collective-permute-done | bytes 294944 | tf_op jit(solution)/shard_map/ppermute | solution.py:249
  173.7 3.8 %attend.3 = bf16[384,1024]{1,0:T(8,128)(2,1)} custom-call(s32[1]{0:T(128)} %bitcast.device_ref, s32[24]{0:T(128)S(1)} %copy-done.3, s32[24]{0:T(128)S(1)} %copy-done.4, f32[384,128]{1,0:T(8,128)S(1)} %broadcast_in_dim.33.inverse_ref, f32[1,384]{1,0:T(1,128)S(1)} %broadcast_in_dim.34.bias_ref, ...), custom_call_target="tpu_custom_call", output_to_operand_aliasing={{}: (14, {})} | custom-call | flops 679477248 | bytes 294912 | tf_op jit(solution)/shard_map/attend/pallas_call | solution.py:485
  (88 shorter events, 9.0 us)
Async XLA Ops:
  3.5 17.2 %copy-start.7 = (bf16[1024,128]{1,0:T(8,128)(2,1)S(1)}, bf16[1024,128]{1,0:T(8,128)(2,1)}, u32[]{:S(2)}) copy-start(bf16[1024,128]{1,0:T(8,128)(2,1)} %param.15) | copy-start | bytes 786436
  3.5 18.3 %collective-permute-start = (bf16[128,2048]{1,0:T(8,128)(2,1)}, bf16[128,2048]{1,0:T(8,128)(2,1)}, u32[]{:S(2)}, u32[]{:S(2)}) collective-permute-start(bf16[128,2048]{1,0:T(8,128)(2,1)} %get-tuple-element.70), channel_id=1, source_target_pairs={{0,0},{8,16},{16,8},{24,24},{1,1},{9,17},{17,9},{25,25},{2,26},{10... | collective-permute-start | bytes 1572872 | tf_op jit(solution)/shard_map/ppermute | solution.py:304
  9.2 40.1 %collective-permute-start.2 = (bf16[1024,640]{1,0:T(8,128)(2,1)S(1)}, bf16[1024,640]{1,0:T(8,128)(2,1)S(1)}, u32[]{:S(2)}, u32[]{:S(2)}) collective-permute-start(bf16[1024,640]{1,0:T(8,128)(2,1)S(1)} %slice.81.refs_6_), channel_id=1, source_target_pairs={{0,1},{1,0},{2,3},{3,2},{4,5},{5,4},{6,7},{7,6},{8,9},{9,8},{10,11... | collective-permute-start | bytes 3932168 | tf_op jit(solution)/shard_map/ppermute | solution.py:249
  12.2 15.0 %collective-permute-start.3 = (bf16[128,2048]{1,0:T(8,128)(2,1)}, bf16[128,2048]{1,0:T(8,128)(2,1)}, u32[]{:S(2)}, u32[]{:S(2)}) collective-permute-start(bf16[128,2048]{1,0:T(8,128)(2,1)} %get-tuple-element.71), channel_id=1, source_target_pairs={{0,0},{8,18},{16,12},{24,30},{1,1},{9,19},{17,13},{25,31},{2,16},{... | collective-permute-start | bytes 1572872 | tf_op jit(solution)/shard_map/ppermute | solution.py:301
  21.8 5.4 %collective-permute-start.4 = (bf16[128,2048]{1,0:T(8,128)(2,1)}, bf16[128,2048]{1,0:T(8,128)(2,1)}, u32[]{:S(2)}, u32[]{:S(2)}) collective-permute-start(bf16[128,2048]{1,0:T(8,128)(2,1)} %get-tuple-element.40), channel_id=1, source_target_pairs={{0,0},{8,16},{16,8},{24,24},{1,1},{9,17},{17,9},{25,25},{2,26},{10... | collective-permute-start | bytes 1572872 | tf_op jit(solution)/shard_map/ppermute | solution.py:304
  27.2 22.6 %collective-permute-start.6 = (bf16[128,2048]{1,0:T(8,128)(2,1)}, bf16[128,2048]{1,0:T(8,128)(2,1)}, u32[]{:S(2)}, u32[]{:S(2)}) collective-permute-start(bf16[128,2048]{1,0:T(8,128)(2,1)} %collective-permute-done.3.refs_0_), channel_id=1, source_target_pairs={{0,16},{8,24},{16,0},{24,8},{1,17},{9,25},{17,1},{25,9},{2,18},{10... | collective-permute-start | bytes 1572872 | tf_op jit(solution)/shard_map/ppermute | solution.py:249
  36.8 12.9 %collective-permute-start.1 = (bf16[128,2048]{1,0:T(8,128)(2,1)}, bf16[128,2048]{1,0:T(8,128)(2,1)}, u32[]{:S(2)}, u32[]{:S(2)}) collective-permute-start(bf16[128,2048]{1,0:T(8,128)(2,1)} %collective-permute-done), channel_id=1, source_target_pairs={{0,0},{16,18},{8,12},{24,30},{1,1},{17,19},{9,13},{25,31},{26,16},... | collective-permute-start | bytes 1572872 | tf_op jit(solution)/shard_map/ppermute | solution.py:306
  42.2 9.9 %collective-permute-start.7 = (bf16[128,2048]{1,0:T(8,128)(2,1)}, bf16[128,2048]{1,0:T(8,128)(2,1)}, u32[]{:S(2)}, u32[]{:S(2)}) collective-permute-start(bf16[128,2048]{1,0:T(8,128)(2,1)} %collective-permute-done.3.refs_0_), channel_id=1, source_target_pairs={{0,8},{8,0},{16,24},{24,16},{1,9},{9,1},{17,25},{25,17},{2,10},{10... | collective-permute-start | bytes 1572872 | tf_op jit(solution)/shard_map/ppermute | solution.py:249
  43.9 8.3 %collective-permute-start.5 = (bf16[128,2048]{1,0:T(8,128)(2,1)}, bf16[128,2048]{1,0:T(8,128)(2,1)}, u32[]{:S(2)}, u32[]{:S(2)}) collective-permute-start(bf16[128,2048]{1,0:T(8,128)(2,1)} %collective-permute-done.4), channel_id=1, source_target_pairs={{0,0},{16,18},{8,12},{24,30},{1,1},{17,19},{9,13},{25,31},{26,16},... | collective-permute-start | bytes 1572872 | tf_op jit(solution)/shard_map/ppermute | solution.py:306
  49.2 10.6 %collective-permute-start.9 = (bf16[1024,256]{1,0:T(8,128)(2,1)S(1)}, bf16[1024,256]{1,0:T(8,128)(2,1)}, u32[]{:S(2)}, u32[]{:S(2)}) collective-permute-start(bf16[1024,256]{1,0:T(8,128)(2,1)S(1)} %constant_dynamic-update-slice_fusion.refs_4_), channel_id=1, source_target_pairs={{0,1},{1,0},{2,3},{3,2},{4,5},{5,4},{6,7},{7,6},{8,9},{9,8},{10,11... | collective-permute-start | bytes 1572872 | tf_op jit(solution)/shard_map/ppermute | solution.py:249
  49.8 10.1 %collective-permute-start.8 = (bf16[128,2048]{1,0:T(8,128)(2,1)}, bf16[128,2048]{1,0:T(8,128)(2,1)}, u32[]{:S(2)}, u32[]{:S(2)}) collective-permute-start(bf16[128,2048]{1,0:T(8,128)(2,1)} %collective-permute-done.6.refs_1_), channel_id=1, source_target_pairs={{0,8},{8,0},{16,24},{24,16},{1,9},{9,1},{17,25},{25,17},{2,10},{10... | collective-permute-start | bytes 1572872 | tf_op jit(solution)/shard_map/ppermute | solution.py:249
  49.8 23.7 %collective-permute-start.11 = (bf16[128,2048]{1,0:T(8,128)(2,1)}, bf16[128,2048]{1,0:T(8,128)(2,1)}, u32[]{:S(2)}, u32[]{:S(2)}) collective-permute-start(bf16[128,2048]{1,0:T(8,128)(2,1)} %collective-permute-done.1.refs_0_), channel_id=1, source_target_pairs={{0,16},{8,24},{16,0},{24,8},{1,17},{9,25},{17,1},{25,9},{2,18},{10... | collective-permute-start | bytes 1572872 | tf_op jit(solution)/shard_map/ppermute | solution.py:249
  64.8 19.4 %collective-permute-start.10 = (bf16[2,128,896]{2,1,0:T(8,128)(2,1)S(1)}, bf16[2,128,896]{2,1,0:T(8,128)(2,1)S(1)}, u32[]{:S(2)}, u32[]{:S(2)}) collective-permute-start(bf16[2,128,896]{2,1,0:T(8,128)(2,1)S(1)} %get-tuple-element.45), channel_id=1, source_target_pairs={{0,2},{1,3},{2,0},{3,1},{4,6},{5,7},{6,4},{7,5},{8,10},{9,11},{10,... | collective-permute-start | bytes 1376264 | tf_op jit(solution)/shard_map/ppermute | solution.py:249
  73.5 10.8 %collective-permute-start.12 = (bf16[128,2048]{1,0:T(8,128)(2,1)}, bf16[128,2048]{1,0:T(8,128)(2,1)S(1)}, u32[]{:S(2)}, u32[]{:S(2)}) collective-permute-start(bf16[128,2048]{1,0:T(8,128)(2,1)} %collective-permute-done.1.refs_0_), channel_id=1, source_target_pairs={{0,8},{8,0},{16,24},{24,16},{1,9},{9,1},{17,25},{25,17},{2,10},{10... | collective-permute-start | bytes 1572872 | tf_op jit(solution)/shard_map/ppermute | solution.py:249
  73.5 10.8 %collective-permute-start.13 = (bf16[128,2048]{1,0:T(8,128)(2,1)}, bf16[128,2048]{1,0:T(8,128)(2,1)S(1)}, u32[]{:S(2)}, u32[]{:S(2)}) collective-permute-start(bf16[128,2048]{1,0:T(8,128)(2,1)} %collective-permute-done.11.refs_1_), channel_id=1, source_target_pairs={{0,8},{8,0},{16,24},{24,16},{1,9},{9,1},{17,25},{25,17},{2,10},{10... | collective-permute-start | bytes 1572872 | tf_op jit(solution)/shard_map/ppermute | solution.py:249
  74.0 16.8 %collective-permute-start.18 = (bf16[128,2048]{1,0:T(8,128)(2,1)}, bf16[128,2048]{1,0:T(8,128)(2,1)S(1)}, u32[]{:S(2)}, u32[]{:S(2)}) collective-permute-start(bf16[128,2048]{1,0:T(8,128)(2,1)} %collective-permute-done.5.refs_0_), channel_id=1, source_target_pairs={{0,16},{8,24},{16,0},{24,8},{1,17},{9,25},{17,1},{25,9},{2,18},{10... | collective-permute-start | bytes 1572872 | tf_op jit(solution)/shard_map/ppermute | solution.py:249
  89.2 12.0 %collective-permute-start.14 = (bf16[2,128,896]{2,1,0:T(8,128)(2,1)S(1)}, bf16[2,128,896]{2,1,0:T(8,128)(2,1)S(1)}, u32[]{:S(2)}, u32[]{:S(2)}) collective-permute-start(bf16[2,128,896]{2,1,0:T(8,128)(2,1)S(1)} %get-tuple-element.48), channel_id=1, source_target_pairs={{0,2},{1,3},{2,0},{3,1},{4,6},{5,7},{6,4},{7,5},{8,10},{9,11},{10,... | collective-permute-start | bytes 1376264 | tf_op jit(solution)/shard_map/ppermute | solution.py:249
  90.3 38.4 %collective-permute-start.24 = (bf16[1024,384]{1,0:T(8,128)(2,1)S(1)}, bf16[1024,384]{1,0:T(8,128)(2,1)S(1)}, u32[]{:S(2)}, u32[]{:S(2)}) collective-permute-start(bf16[1024,384]{1,0:T(8,128)(2,1)S(1)} %copy-done), channel_id=1, source_target_pairs={{0,1},{1,0},{2,3},{3,2},{4,5},{5,4},{6,7},{7,6},{8,9},{9,8},{10,11... | collective-permute-start | bytes 2359304 | tf_op jit(solution)/shard_map/ppermute | solution.py:249
  101.3 3.9 %collective-permute-start.20 = (bf16[128,2048]{1,0:T(8,128)(2,1)S(1)}, bf16[128,2048]{1,0:T(8,128)(2,1)S(1)}, u32[]{:S(2)}, u32[]{:S(2)}) collective-permute-start(bf16[128,2048]{1,0:T(8,128)(2,1)S(1)} %collective-permute-done.18.refs_1_), channel_id=1, source_target_pairs={{0,8},{8,0},{16,24},{24,16},{1,9},{9,1},{17,25},{25,17},{2,10},{10... | collective-permute-start | bytes 1572872 | tf_op jit(solution)/shard_map/ppermute | solution.py:249
  101.3 6.8 %collective-permute-start.19 = (bf16[128,2048]{1,0:T(8,128)(2,1)}, bf16[128,2048]{1,0:T(8,128)(2,1)S(1)}, u32[]{:S(2)}, u32[]{:S(2)}) collective-permute-start(bf16[128,2048]{1,0:T(8,128)(2,1)} %collective-permute-done.5.refs_0_), channel_id=1, source_target_pairs={{0,8},{8,0},{16,24},{24,16},{1,9},{9,1},{17,25},{25,17},{2,10},{10... | collective-permute-start | bytes 1572872 | tf_op jit(solution)/shard_map/ppermute | solution.py:249
  101.9 2.1 %collective-permute-start.15 = (f32[3,128]{1,0:T(4,128)S(1)}, f32[3,128]{1,0:T(4,128)S(1)}, u32[]{:S(2)}, u32[]{:S(2)}) collective-permute-start(f32[3,128]{1,0:T(4,128)S(1)} %multiply_reduce_fusion), channel_id=1, source_target_pairs={{0,8},{8,0},{16,24},{24,16},{1,9},{9,1},{17,25},{25,17},{2,10},{10... | collective-permute-start | bytes 4616 | tf_op jit(solution)/shard_map/ppermute | solution.py:249
  103.9 9.7 %collective-permute-start.16 = (f32[3,128]{1,0:T(4,128)S(1)}, f32[3,128]{1,0:T(4,128)S(1)}, u32[]{:S(2)}, u32[]{:S(2)}) collective-permute-start(f32[3,128]{1,0:T(4,128)S(1)} %add.35), channel_id=1, source_target_pairs={{0,16},{8,24},{16,0},{24,8},{1,17},{9,25},{17,1},{25,9},{2,18},{10... | collective-permute-start | bytes 4616 | tf_op jit(solution)/shard_map/ppermute | solution.py:249
  105.1 18.7 %collective-permute-start.17 = (bf16[1,128,896]{2,1,0:T(8,128)(2,1)S(1)}, bf16[1,128,896]{2,1,0:T(8,128)(2,1)S(1)}, u32[]{:S(2)}, u32[]{:S(2)}) collective-permute-start(bf16[1,128,896]{2,1,0:T(8,128)(2,1)S(1)} %fusion.6), channel_id=1, source_target_pairs={{0,4},{1,5},{2,6},{3,7},{4,0},{5,1},{6,2},{7,3},{8,12},{9,13},{10,... | collective-permute-start | bytes 688136 | tf_op jit(solution)/shard_map/ppermute | solution.py:249
  105.2 23.1 %collective-permute-start.21 = (bf16[1,128,896]{2,1,0:T(8,128)(2,1)S(1)}, bf16[1,128,896]{2,1,0:T(8,128)(2,1)S(1)}, u32[]{:S(2)}, u32[]{:S(2)}) collective-permute-start(bf16[1,128,896]{2,1,0:T(8,128)(2,1)S(1)} %fusion.5), channel_id=1, source_target_pairs={{0,4},{1,5},{2,6},{3,7},{4,0},{5,1},{6,2},{7,3},{8,12},{9,13},{10,... | collective-permute-start | bytes 688136 | tf_op jit(solution)/shard_map/ppermute | solution.py:249
  112.6 24.0 %collective-permute-start.23 = (bf16[2,128,896]{2,1,0:T(8,128)(2,1)S(1)}, bf16[2,128,896]{2,1,0:T(8,128)(2,1)S(1)}, u32[]{:S(2)}, u32[]{:S(2)}) collective-permute-start(bf16[2,128,896]{2,1,0:T(8,128)(2,1)S(1)} %get-tuple-element.53), channel_id=1, source_target_pairs={{0,2},{1,3},{2,0},{3,1},{4,6},{5,7},{6,4},{7,5},{8,10},{9,11},{10,... | collective-permute-start | bytes 1376264 | tf_op jit(solution)/shard_map/ppermute | solution.py:249
  128.7 8.0 %collective-permute-start.22 = (bf16[1,256,256]{2,1,0:T(8,128)(2,1)S(1)}, bf16[1,256,256]{2,1,0:T(8,128)(2,1)S(1)}, u32[]{:S(2)}, u32[]{:S(2)}) collective-permute-start(bf16[1,256,256]{2,1,0:T(8,128)(2,1)S(1)} %maximum_bitcast_fusion), channel_id=1, source_target_pairs={{0,4},{1,5},{2,6},{3,7},{4,0},{5,1},{6,2},{7,3},{8,12},{9,13},{10,... | collective-permute-start | bytes 393224 | tf_op jit(solution)/shard_map/ppermute | solution.py:249
  136.7 24.4 %copy-start.8 = (f32[1024]{0:T(1024)S(1)}, f32[1024]{0:T(1024)}, u32[]{:S(2)}) copy-start(f32[1024]{0:T(1024)} %param.17) | copy-start | bytes 12292
  136.7 9.3 %collective-permute-start.25 = (bf16[2,256,256]{2,1,0:T(8,128)(2,1)S(1)}, bf16[2,256,256]{2,1,0:T(8,128)(2,1)S(1)}, u32[]{:S(2)}, u32[]{:S(2)}) collective-permute-start(bf16[2,256,256]{2,1,0:T(8,128)(2,1)S(1)} %pad_maximum_fusion.2), channel_id=1, source_target_pairs={{0,2},{1,3},{2,0},{3,1},{4,6},{5,7},{6,4},{7,5},{8,10},{9,11},{10,... | collective-permute-start | bytes 786440 | tf_op jit(solution)/shard_map/ppermute | solution.py:249
  136.8 23.5 %collective-permute-start.28 = (bf16[2,384,384]{2,1,0:T(8,128)(2,1)S(1)}, bf16[2,384,384]{2,1,0:T(8,128)(2,1)S(1)}, u32[]{:S(2)}, u32[]{:S(2)}) collective-permute-start(bf16[2,384,384]{2,1,0:T(8,128)(2,1)S(1)} %get-tuple-element.62), channel_id=1, source_target_pairs={{0,2},{1,3},{2,0},{3,1},{4,6},{5,7},{6,4},{7,5},{8,10},{9,11},{10,... | collective-permute-start | bytes 1769480 | tf_op jit(solution)/shard_map/ppermute | solution.py:249
  146.1 15.2 %collective-permute-start.26 = (bf16[4,256,256]{2,1,0:T(8,128)(2,1)S(1)}, bf16[4,256,256]{2,1,0:T(8,128)(2,1)S(1)}, u32[]{:S(2)}, u32[]{:S(2)}) collective-permute-start(bf16[4,256,256]{2,1,0:T(8,128)(2,1)S(1)} %pad_maximum_fusion.1), channel_id=1, source_target_pairs={{0,1},{1,0},{2,3},{3,2},{4,5},{5,4},{6,7},{7,6},{8,9},{9,8},{10,11... | collective-permute-start | bytes 1572872 | tf_op jit(solution)/shard_map/ppermute | solution.py:249
  146.2 14.9 %collective-permute-start.27 = (bf16[1,128,896]{2,1,0:T(8,128)(2,1)S(1)}, bf16[1,128,896]{2,1,0:T(8,128)(2,1)S(1)}, u32[]{:S(2)}, u32[]{:S(2)}) collective-permute-start(bf16[1,128,896]{2,1,0:T(8,128)(2,1)S(1)} %fusion.4), channel_id=1, source_target_pairs={{0,4},{1,5},{2,6},{3,7},{4,0},{5,1},{6,2},{7,3},{8,12},{9,13},{10,... | collective-permute-start | bytes 688136 | tf_op jit(solution)/shard_map/ppermute | solution.py:249
  160.4 13.3 %collective-permute-start.29 = (bf16[1,384,384]{2,1,0:T(8,128)(2,1)S(1)}, bf16[1,384,384]{2,1,0:T(8,128)(2,1)S(1)}, u32[]{:S(2)}, u32[]{:S(2)}) collective-permute-start(bf16[1,384,384]{2,1,0:T(8,128)(2,1)S(1)} %fusion.3), channel_id=1, source_target_pairs={{0,4},{1,5},{2,6},{3,7},{4,0},{5,1},{6,2},{7,3},{8,12},{9,13},{10,... | collective-permute-start | bytes 884744 | tf_op jit(solution)/shard_map/ppermute | solution.py:249
  (9 other events, 73.2 us)

commit v11 on v8

--- a/solution.py
+++ b/solution.py
@@ -77,12 +77,6 @@
     for copy in copies:
         copy.start()
     return copies
-
-
-def assemble_kernel(lines, place_ref, *refs):
-    pieces, (held, sems) = refs[:lines], refs[lines:]
-    for copy in assemble(lines, 1, place_ref, pieces, held, sems):
-        copy.wait()
 
 
 def project_kernel(lines, groups, chunks, counts, fresh, place_ref, *refs):
@@ -313,16 +307,18 @@
         piece = tie(piece, sent[-1], cos, sin, *w_chunks) if block else piece
         sent.append(lax.ppermute(piece, axes, first_hop))
 
+    last_sent = sent[-1]
+    sent = [lax.ppermute(piece, axes, second_hop) for piece in sent]
     w_rows = [None] * len(w_chunks)
     arrived = None
     for c in (1, 0, 2):
-        outgoing = w_chunks[c] if arrived is None else tie(w_chunks[c], arrived)
+        outgoing = w_chunks[c] if arrived is None else tie(w_chunks[c], arrived, sent[1])
         w_rows[c] = [w_chunks[c]] + [swap(outgoing, "branch", j) for j in range(1, groups)]
         arrived = w_rows[c][-1]
 
+    sent[0] = tie(sent[0], last_sent)
+    sent[1] = tie(sent[1], w_rows[1][-1])
     last_sent = sent[-1]
-    sent = [lax.ppermute(piece, axes, second_hop) for piece in sent]
-    sent[0] = tie(sent[0], last_sent, w_rows[1][-1])
     held = [{0: piece} for piece in sent]
     bit = half_lines
     while bit > 1:
@@ -336,21 +332,9 @@
             piece[j | 1] = swap(piece[j], "fsdp", 1)
         return [piece[j] for j in sorted(piece, key=spread)]
 
-    held[1][half_lines] = tie(held[1][half_lines], w_rows[0][-1])
     assembled = {}
     held[0] = last_bit(held[0])
-    assembled[(0, 1)] = pl.pallas_call(
-        functools.partial(assemble_kernel, lines),
-        in_specs=[smem] + [anywhere] * lines,
-        out_specs=vmem,
-        out_shape=jax.ShapeDtypeStruct((lines * block_len, feature_part), bf16),
-        scratch_shapes=[pltpu.SemaphoreType.DMA((lines,))],
-        name="assemble",
-    )(place, *held[0])
-    for block in range(1, STEMS):
-        held[block][half_lines] = tie(held[block][half_lines], assembled[(0, 1)])
-        held[block] = last_bit(held[block])
-
+    held[1] = last_bit(held[1])
 
     def project(spans, chunks, *after):
         weights = [w for chunk in chunks for w in w_rows[chunk]]
@@ -438,11 +422,10 @@
             name="finish_kv",
         )(*operands, *addends)
 
-    early = [(0, 1), (1, STEMS)]
+    early = [(0, STEMS)]
     late = [(STEMS, blocks)]
     first = Halving(project(early, [0]))
     first.step()
-
     second = Halving(project(early, [1], first.send))
     second.step()
     first.rest(second.send)
@@ -457,9 +440,10 @@
     inverse = jnp.broadcast_to(inverse[:, None], (tokens, HD))
 
     for block in range(STEMS, blocks):
-        held[block] = {j: tie(piece, first.send) for j, piece in held[block].items()}
+        held[block] = {j: tie(piece, second.send) for j, piece in held[block].items()}
         held[block] = last_bit(held[block])
     third = Halving(project(late, [0, 1], first.send))
+    third.step()
     first.addends[-1] = tie(first.addends[-1], third.send)
     stem_kv = finish_kv(first.addends, 0, STEMS)
 
@@ -467,16 +451,15 @@
     tour += [1 << i for i in range(bits_of(groups))]
     stems = stem_kv[None]
     came = swap(stems, "branch", tour[0])
-    third.step(stem_kv)
     second.add(stem_kv, w_rows[2][-1])
-    second.step()
     fourth = Halving(project(early + late, [2], second.send))
     for step, bit in enumerate(tour[1:]):
         stems = jnp.concatenate([stems, tie(came, third.send if step else fourth.send)], 0)
         came = swap(stems, "branch", bit)
         if step == 0:
+            second.step(stems)
             fourth.step(stems)
-            third.add(stems, second.came)
+            third.add(stems)
             third.step()
     second.rest()
     third.rest()

time: 172 us -> 161 us (0.936)
  waiting for transfers between devices: 77 us -> 49.1 us
  starting transfers between devices: 51.7 us -> 71.8 us
  Pallas kernels: 31.2 us -> 28.2 us
    ppermute x25, waiting for transfers between devices: 77 us -> 49.1 us  [swap(): return lax.ppermute(array, axis, [(i, i ^ bit) for i in range(size)])]
    ppermute x25, starting transfers between devices: 30.7 us -> 58.3 us  [swap(): return lax.ppermute(array, axis, [(i, i ^ bit) for i in range(size)])]
    ppermute x3, starting transfers between devices: 12.2 us -> 4.6 us  [shards(): sent = [lax.ppermute(piece, axes, second_hop) for piece in sent]]
    pallas_call x1 -> x0, Pallas kernels: 3.56 us -> none  [shards(): pl.pallas_call(functools.partial(assemble_kernel, lines), in_specs=[smem]...]
  transfers between devices with their start and end apart: 31 -> 31, of which waited for: 13 -> 10; matrix products, arithmetic and copies ran while one was open for 2% -> 2% of each run, Pallas kernels for 16% -> 15%
where the time goes in v11:
time: 161 us
  starting transfers between devices  71.8 us (45%)
  waiting for transfers between devices  49.1 us (30%)
  Pallas kernels  28.2 us (18%)
  local copies, waits for them, and re-layouts  7.33 us (5%)
  other arithmetic  3.66 us (2%)
    ppermute x25, starting transfers between devices, swap(): return lax.ppermute(array, axis, [(i, i ^ bit) for i in range(size)])  58.3 us
    ppermute x25, waiting for transfers between devices, swap(): return lax.ppermute(array, axis, [(i, i ^ bit) for i in range(size)])  49.1 us
    pallas_call x4, Pallas kernels, project(): pl.pallas_call(functools.partial(project_kernel, lines, groups, len(chunk...  17 us
    ppermute x3, starting transfers between devices, shards(): sent.append(lax.ppermute(piece, axes, first_hop))  8.87 us
    pallas_call x2, Pallas kernels, attend(): pl.pallas_call(kernel, grid=(1,), in_specs=in_specs, out_specs=anywhere,...  8.74 us
    ppermute x3, starting transfers between devices, shards(): sent = [lax.ppermute(piece, axes, second_hop) for piece in sent]  4.6 us
    unnamed x31, local copies, waits for them, and re-layouts  4.19 us
  transfers between devices with their start and end apart: 31, of which 10 were waited for; matrix products, arithmetic and copies ran while one was open for 2% of the time, Pallas kernels for 15%

profile of v11, /device:TPU:0, one launch (start us, length us, event | category | flops | bytes accessed | tf_op | source)
XLA Modules:
  0.0 160.5 jit_solution(124303402413295312)
XLA Ops:
  0.7 2.8 %fusion = (bf16[128,2048]{1,0:T(8,128)(2,1)}, bf16[128,2048]{1,0:T(8,128)(2,1)}, bf16[128,2048]{1,0:T(8,128)(2,1)}) fusion(bf16[3,128,2048]{2,1,0:T(8,128)(2,1)} %param.10, f32[2048]{0:T(1024)S(1)} %dynamic_slice.3), kind=kLoop, calls=%fused_computation.3 | loop fusion | flops 2359296 | bytes 3153920 | tf_op jit(solution)/shard_map/convert_element_type | solution.py:306
  3.5 5.5 %collective-permute-start = (bf16[128,2048]{1,0:T(8,128)(2,1)}, bf16[128,2048]{1,0:T(8,128)(2,1)}, u32[]{:S(2)}, u32[]{:S(2)}) collective-permute-start(bf16[128,2048]{1,0:T(8,128)(2,1)} %get-tuple-element.74), channel_id=1, source_target_pairs={{0,0},{8,16},{16,8},{24,24},{1,1},{9,17},{17,9},{25,25},{2,26},{10... | collective-permute-start | bytes 1572872 | tf_op jit(solution)/shard_map/ppermute | solution.py:308
  9.1 3.0 %collective-permute-start.5 = (bf16[1024,640]{1,0:T(8,128)(2,1)S(1)}, bf16[1024,640]{1,0:T(8,128)(2,1)S(1)}, u32[]{:S(2)}, u32[]{:S(2)}) collective-permute-start(bf16[1024,640]{1,0:T(8,128)(2,1)S(1)} %slice.70.refs_1_.refs_6_), channel_id=1, source_target_pairs={{0,1},{1,0},{2,3},{3,2},{4,5},{5,4},{6,7},{7,6},{8,9},{9,8},{10,11... | collective-permute-start | bytes 3932168 | tf_op jit(solution)/shard_map/ppermute | solution.py:256
  13.2 2.2 %tables.1 = (f32[384,128]{1,0:T(8,128)}, f32[384,128]{1,0:T(8,128)}) custom-call(s32[1]{0:T(128)} %bitcast.device_ref, s32[24]{0:T(128)} %parents_ref.5), custom_call_target="tpu_custom_call" | custom-call | tf_op jit(solution)/shard_map/tables/pallas_call | solution.py:296
  16.4 1.7 %collective-permute-start.2 = (bf16[128,2048]{1,0:T(8,128)(2,1)}, bf16[128,2048]{1,0:T(8,128)(2,1)S(1)}, u32[]{:S(2)}, u32[]{:S(2)}) collective-permute-start(bf16[128,2048]{1,0:T(8,128)(2,1)} %get-tuple-element.41), channel_id=1, source_target_pairs={{0,0},{8,16},{16,8},{24,24},{1,1},{9,17},{17,9},{25,25},{2,26},{10... | collective-permute-start | bytes 1572872 | tf_op jit(solution)/shard_map/ppermute | solution.py:308
  19.8 1.7 %collective-permute-start.3 = (bf16[128,2048]{1,0:T(8,128)(2,1)}, bf16[128,2048]{1,0:T(8,128)(2,1)S(1)}, u32[]{:S(2)}, u32[]{:S(2)}) collective-permute-start(bf16[128,2048]{1,0:T(8,128)(2,1)} %get-tuple-element.42), channel_id=1, source_target_pairs={{0,0},{8,16},{16,8},{24,24},{1,1},{9,17},{17,9},{25,25},{2,26},{10... | collective-permute-start | bytes 1572872 | tf_op jit(solution)/shard_map/ppermute | solution.py:308
  23.0 15.8 %collective-permute-start.6 = (bf16[128,2048]{1,0:T(8,128)(2,1)S(1)}, bf16[128,2048]{1,0:T(8,128)(2,1)}, u32[]{:S(2)}, u32[]{:S(2)}) collective-permute-start(bf16[128,2048]{1,0:T(8,128)(2,1)S(1)} %collective-permute-done.1.refs_0_), channel_id=1, source_target_pairs={{0,16},{8,24},{16,0},{24,8},{1,17},{9,25},{17,1},{25,9},{2,18},{10... | collective-permute-start | bytes 1572872 | tf_op jit(solution)/shard_map/ppermute | solution.py:256
  38.8 2.2 %collective-permute-start.8 = (bf16[128,2048]{1,0:T(8,128)(2,1)S(1)}, bf16[128,2048]{1,0:T(8,128)(2,1)S(1)}, u32[]{:S(2)}, u32[]{:S(2)}) collective-permute-start(bf16[128,2048]{1,0:T(8,128)(2,1)S(1)} %collective-permute-done.1.refs_0_), channel_id=1, source_target_pairs={{0,8},{8,0},{16,24},{24,16},{1,9},{9,1},{17,25},{25,17},{2,10},{10... | collective-permute-start | bytes 1572872 | tf_op jit(solution)/shard_map/ppermute | solution.py:256
  41.8 4.9 %collective-permute-start.7 = (bf16[128,2048]{1,0:T(8,128)(2,1)}, bf16[128,2048]{1,0:T(8,128)(2,1)}, u32[]{:S(2)}, u32[]{:S(2)}) collective-permute-start(bf16[128,2048]{1,0:T(8,128)(2,1)} %collective-permute-done.4.refs_1_), channel_id=1, source_target_pairs={{0,16},{8,24},{16,0},{24,8},{1,17},{9,25},{17,1},{25,9},{2,18},{10... | collective-permute-start | bytes 1572872 | tf_op jit(solution)/shard_map/ppermute | solution.py:256
  48.2 1.8 %collective-permute-start.9 = (bf16[128,2048]{1,0:T(8,128)(2,1)}, bf16[128,2048]{1,0:T(8,128)(2,1)}, u32[]{:S(2)}, u32[]{:S(2)}) collective-permute-start(bf16[128,2048]{1,0:T(8,128)(2,1)} %collective-permute-done.4.refs_1_), channel_id=1, source_target_pairs={{0,8},{8,0},{16,24},{24,16},{1,9},{9,1},{17,25},{25,17},{2,10},{10... | collective-permute-start | bytes 1572872 | tf_op jit(solution)/shard_map/ppermute | solution.py:256
  50.0 2.2 %collective-permute-start.12 = (bf16[1024,256]{1,0:T(8,128)(2,1)S(1)}, bf16[1024,256]{1,0:T(8,128)(2,1)}, u32[]{:S(2)}, u32[]{:S(2)}) collective-permute-start(bf16[1024,256]{1,0:T(8,128)(2,1)S(1)} %constant_dynamic-update-slice_fusion.refs_8_.refs_4_), channel_id=1, source_target_pairs={{0,1},{1,0},{2,3},{3,2},{4,5},{5,4},{6,7},{7,6},{8,9},{9,8},{10,11... | collective-permute-start | bytes 1572872 | tf_op jit(solution)/shard_map/ppermute | solution.py:256
  53.0 3.1 %collective-permute-start.10 = (bf16[128,2048]{1,0:T(8,128)(2,1)}, bf16[128,2048]{1,0:T(8,128)(2,1)}, u32[]{:S(2)}, u32[]{:S(2)}) collective-permute-start(bf16[128,2048]{1,0:T(8,128)(2,1)} %collective-permute-done.6.refs_2_), channel_id=1, source_target_pairs={{0,8},{8,0},{16,24},{24,16},{1,9},{9,1},{17,25},{25,17},{2,10},{10... | collective-permute-start | bytes 1572872 | tf_op jit(solution)/shard_map/ppermute | solution.py:256
  56.1 4.8 %collective-permute-done.7.refs_3_ = bf16[128,2048]{1,0:T(8,128)(2,1)} collective-permute-done((bf16[128,2048]{1,0:T(8,128)(2,1)}, bf16[128,2048]{1,0:T(8,128)(2,1)}, u32[]{:S(2)}, u32[]{:S(2)}) %collective-permute-start.7) | collective-permute-done | bytes 524320 | tf_op jit(solution)/shard_map/ppermute | solution.py:256
  60.9 1.8 %collective-permute-start.11 = (bf16[128,2048]{1,0:T(8,128)(2,1)}, bf16[128,2048]{1,0:T(8,128)(2,1)}, u32[]{:S(2)}, u32[]{:S(2)}) collective-permute-start(bf16[128,2048]{1,0:T(8,128)(2,1)} %collective-permute-done.7.refs_3_), channel_id=1, source_target_pairs={{0,8},{8,0},{16,24},{24,16},{1,9},{9,1},{17,25},{25,17},{2,10},{10... | collective-permute-start | bytes 1572872 | tf_op jit(solution)/shard_map/ppermute | solution.py:256
  62.7 2.3 %collective-permute-start.18 = (bf16[128,2048]{1,0:T(8,128)(2,1)}, bf16[128,2048]{1,0:T(8,128)(2,1)}, u32[]{:S(2)}, u32[]{:S(2)}) collective-permute-start(bf16[128,2048]{1,0:T(8,128)(2,1)} %collective-permute-done.17.refs_0_), channel_id=1, source_target_pairs={{0,16},{8,24},{16,0},{24,8},{1,17},{9,25},{17,1},{25,9},{2,18},{10... | collective-permute-start | bytes 1572872 | tf_op jit(solution)/shard_map/ppermute | solution.py:256
  67.2 4.4 %project.4 = (bf16[2,256,256]{2,1,0:T(8,128)(2,1)S(1)}, f32[2,256,256]{2,1,0:T(8,128)S(1)}, bf16[1024,2048]{1,0:T(8,128)(2,1)S(1)}) custom-call(s32[2]{0:T(128)S(1)} %pad_add_fusion.place_ref, bf16[128,2048]{1,0:T(8,128)(2,1)S(1)} %copy-done.4, bf16[128,2048]{1,0:T(8,128)(2,1)} %collective-permute-done.4.refs_1_, ...), custom_call_target="tpu_custom_call" | custom-call | tf_op jit(solution)/shard_map/project/pallas_call | solution.py:363
  71.6 2.3 %collective-permute-start.13 = (bf16[2,256,256]{2,1,0:T(8,128)(2,1)S(1)}, bf16[2,256,256]{2,1,0:T(8,128)(2,1)S(1)}, u32[]{:S(2)}, u32[]{:S(2)}) collective-permute-start(bf16[2,256,256]{2,1,0:T(8,128)(2,1)S(1)} %get-tuple-element.47), channel_id=1, source_target_pairs={{0,2},{1,3},{2,0},{3,1},{4,6},{5,7},{6,4},{7,5},{8,10},{9,11},{10,... | collective-permute-start | bytes 786440 | tf_op jit(solution)/shard_map/ppermute | solution.py:256
  75.5 4.0 %project.5 = (bf16[2,256,640]{2,1,0:T(8,128)(2,1)S(1)}, f32[2,256,640]{2,1,0:T(8,128)S(1)}) custom-call(s32[2]{0:T(128)S(1)} %pad_add_fusion.place_ref, bf16[1024,2048]{1,0:T(8,128)(2,1)S(1)} %get-tuple-element.61.refs_0_, bf16[1024,640]{1,0:T(8,128)(2,1)S(1)} %slice.70.refs_1_.refs_6_, bf16[1024,640]{1,0:T(8,128)(2,1)S(1)} %collective-permute-done.5.refs_2_.refs_7_), custom_call_target="tpu_custom_call" | custom-call | tf_op jit(solution)/shard_map/project/pallas_call | solution.py:363
  82.0 2.7 %collective-permute-start.15 = (f32[3,128]{1,0:T(4,128)S(1)}, f32[3,128]{1,0:T(4,128)S(1)}, u32[]{:S(2)}, u32[]{:S(2)}) collective-permute-start(f32[3,128]{1,0:T(4,128)S(1)} %add.34), channel_id=1, source_target_pairs={{0,16},{8,24},{16,0},{24,8},{1,17},{9,25},{17,1},{25,9},{2,18},{10... | collective-permute-start | bytes 4616 | tf_op jit(solution)/shard_map/ppermute | solution.py:256
  86.3 2.2 %collective-permute-start.16 = (bf16[1,256,256]{2,1,0:T(8,128)(2,1)S(1)}, bf16[1,256,256]{2,1,0:T(8,128)(2,1)S(1)}, u32[]{:S(2)}, u32[]{:S(2)}) collective-permute-start(bf16[1,256,256]{2,1,0:T(8,128)(2,1)S(1)} %fusion.6), channel_id=1, source_target_pairs={{0,4},{1,5},{2,6},{3,7},{4,0},{5,1},{6,2},{7,3},{8,12},{9,13},{10,... | collective-permute-start | bytes 393224 | tf_op jit(solution)/shard_map/ppermute | solution.py:256
  88.4 4.7 %project.6 = (bf16[2,128,896]{2,1,0:T(8,128)(2,1)S(1)}, f32[2,128,896]{2,1,0:T(8,128)S(1)}, bf16[512,2048]{1,0:T(8,128)(2,1)S(1)}) custom-call(s32[2]{0:T(128)S(1)} %pad_add_fusion.place_ref, bf16[128,2048]{1,0:T(8,128)(2,1)} %collective-permute-done.17.refs_0_, bf16[128,2048]{1,0:T(8,128)(2,1)} %collective-permute-done.18.refs_1_, ...), custom_call_target="tpu_custom_call" | custom-call | tf_op jit(solution)/shard_map/project/pallas_call | solution.py:363
  94.4 3.7 %collective-permute-done.16.refs_2_ = bf16[1,256,256]{2,1,0:T(8,128)(2,1)S(1)} collective-permute-done((bf16[1,256,256]{2,1,0:T(8,128)(2,1)S(1)}, bf16[1,256,256]{2,1,0:T(8,128)(2,1)S(1)}, u32[]{:S(2)}, u32[]{:S(2)}) %collective-permute-start.16) | collective-permute-done | bytes 131104 | tf_op jit(solution)/shard_map/ppermute | solution.py:256
  98.3 3.4 %collective-permute-start.21 = (bf16[1,256,256]{2,1,0:T(8,128)(2,1)S(1)}, bf16[1,256,256]{2,1,0:T(8,128)(2,1)S(1)}, u32[]{:S(2)}, u32[]{:S(2)}) collective-permute-start(bf16[1,256,256]{2,1,0:T(8,128)(2,1)S(1)} %bitcast.21), channel_id=1, source_target_pairs={{0,4},{1,5},{2,6},{3,7},{4,0},{5,1},{6,2},{7,3},{8,12},{9,13},{10,... | collective-permute-start | bytes 393224 | tf_op jit(solution)/shard_map/ppermute | solution.py:256
  101.8 4.0 %project.7 = (bf16[2,384,384]{2,1,0:T(8,128)(2,1)S(1)}, f32[2,384,384]{2,1,0:T(8,128)S(1)}) custom-call(s32[2]{0:T(128)S(1)} %pad_add_fusion.place_ref, bf16[1024,2048]{1,0:T(8,128)(2,1)S(1)} %get-tuple-element.61.refs_0_, bf16[512,2048]{1,0:T(8,128)(2,1)S(1)} %get-tuple-element.62.refs_1_, bf16[1024,384]{1,0:T(8,128)(2,1)S(1)} %copy-done, ...), custom_call_target="tpu_custom_call" | custom-call | tf_op jit(solution)/shard_map/project/pallas_call | solution.py:363
  105.8 3.6 %collective-permute-done.21 = bf16[1,256,256]{2,1,0:T(8,128)(2,1)S(1)} collective-permute-done((bf16[1,256,256]{2,1,0:T(8,128)(2,1)S(1)}, bf16[1,256,256]{2,1,0:T(8,128)(2,1)S(1)}, u32[]{:S(2)}, u32[]{:S(2)}) %collective-permute-start.21) | collective-permute-done | bytes 131104 | tf_op jit(solution)/shard_map/ppermute | solution.py:256
  109.4 4.3 %collective-permute-start.24 = (bf16[2,256,256]{2,1,0:T(8,128)(2,1)S(1)}, bf16[2,256,256]{2,1,0:T(8,128)(2,1)S(1)}, u32[]{:S(2)}, u32[]{:S(2)}) collective-permute-start(bf16[2,256,256]{2,1,0:T(8,128)(2,1)S(1)} %pad_maximum_fusion.2), channel_id=1, source_target_pairs={{0,2},{1,3},{2,0},{3,1},{4,6},{5,7},{6,4},{7,5},{8,10},{9,11},{10,... | collective-permute-start | bytes 786440 | tf_op jit(solution)/shard_map/ppermute | solution.py:256
  115.0 11.1 %collective-permute-done.24 = bf16[2,256,256]{2,1,0:T(8,128)(2,1)S(1)} collective-permute-done((bf16[2,256,256]{2,1,0:T(8,128)(2,1)S(1)}, bf16[2,256,256]{2,1,0:T(8,128)(2,1)S(1)}, u32[]{:S(2)}, u32[]{:S(2)}) %collective-permute-start.24) | collective-permute-done | bytes 262176 | tf_op jit(solution)/shard_map/ppermute | solution.py:256
  127.5 4.3 %collective-permute-done.29.refs_4_ = bf16[1,256,640]{2,1,0:T(8,128)(2,1)S(1)} collective-permute-done((bf16[1,256,640]{2,1,0:T(8,128)(2,1)S(1)}, bf16[1,256,640]{2,1,0:T(8,128)(2,1)S(1)}, u32[]{:S(2)}, u32[]{:S(2)}) %collective-permute-start.29) | collective-permute-done | bytes 327712 | tf_op jit(solution)/shard_map/ppermute | solution.py:256
  131.8 11.2 %collective-permute-done.28.refs_3_ = bf16[2,384,384]{2,1,0:T(8,128)(2,1)S(1)} collective-permute-done((bf16[2,384,384]{2,1,0:T(8,128)(2,1)S(1)}, bf16[2,384,384]{2,1,0:T(8,128)(2,1)S(1)}, u32[]{:S(2)}, u32[]{:S(2)}) %collective-permute-start.28) | collective-permute-done | bytes 589856 | tf_op jit(solution)/shard_map/ppermute | solution.py:256
  144.2 5.0 %attend.2.refs_5_ = bf16[384,1024]{1,0:T(8,128)(2,1)} custom-call(s32[1]{0:T(128)} %bitcast.device_ref, s32[24]{0:T(128)S(1)} %copy-done.7, s32[24]{0:T(128)S(1)} %copy-done.8, f32[384,128]{1,0:T(8,128)S(1)} %broadcast_in_dim.31.inverse_ref, f32[1,640]{1,0:T(1,128)S(1)} %broadcast_in_dim.37.bias_ref, f32[384,128]{1,0:T(8,128)S(1)} %copy-done.1, ...), custom_call_target="tpu_custom_call" | custom-call | flops 1887436800 | bytes 491520 | tf_op jit(solution)/shard_map/attend/pallas_call | solution.py:491
  149.2 7.4 %collective-permute-done.30.refs_4_ = bf16[1,384,384]{2,1,0:T(8,128)(2,1)S(1)} collective-permute-done((bf16[1,384,384]{2,1,0:T(8,128)(2,1)S(1)}, bf16[1,384,384]{2,1,0:T(8,128)(2,1)S(1)}, u32[]{:S(2)}, u32[]{:S(2)}) %collective-permute-start.30) | collective-permute-done | bytes 294944 | tf_op jit(solution)/shard_map/ppermute | solution.py:256
  156.6 3.7 %attend.3 = bf16[384,1024]{1,0:T(8,128)(2,1)} custom-call(s32[1]{0:T(128)} %bitcast.device_ref, s32[24]{0:T(128)S(1)} %copy-done.7, s32[24]{0:T(128)S(1)} %copy-done.8, f32[384,128]{1,0:T(8,128)S(1)} %broadcast_in_dim.31.inverse_ref, f32[1,384]{1,0:T(1,128)S(1)} %broadcast_in_dim.32.bias_ref, ...), custom_call_target="tpu_custom_call", output_to_operand_aliasing={{}: (13, {})} | custom-call | flops 679477248 | bytes 294912 | tf_op jit(solution)/shard_map/attend/pallas_call | solution.py:491
  (99 shorter events, 22.3 us)
Async XLA Ops:
  3.5 12.9 %collective-permute-start = (bf16[128,2048]{1,0:T(8,128)(2,1)}, bf16[128,2048]{1,0:T(8,128)(2,1)}, u32[]{:S(2)}, u32[]{:S(2)}) collective-permute-start(bf16[128,2048]{1,0:T(8,128)(2,1)} %get-tuple-element.74), channel_id=1, source_target_pairs={{0,0},{8,16},{16,8},{24,24},{1,1},{9,17},{17,9},{25,25},{2,26},{10... | collective-permute-start | bytes 1572872 | tf_op jit(solution)/shard_map/ppermute | solution.py:308
  9.1 32.6 %collective-permute-start.5 = (bf16[1024,640]{1,0:T(8,128)(2,1)S(1)}, bf16[1024,640]{1,0:T(8,128)(2,1)S(1)}, u32[]{:S(2)}, u32[]{:S(2)}) collective-permute-start(bf16[1024,640]{1,0:T(8,128)(2,1)S(1)} %slice.70.refs_1_.refs_6_), channel_id=1, source_target_pairs={{0,1},{1,0},{2,3},{3,2},{4,5},{5,4},{6,7},{7,6},{8,9},{9,8},{10,11... | collective-permute-start | bytes 3932168 | tf_op jit(solution)/shard_map/ppermute | solution.py:256
  16.4 3.4 %collective-permute-start.2 = (bf16[128,2048]{1,0:T(8,128)(2,1)}, bf16[128,2048]{1,0:T(8,128)(2,1)S(1)}, u32[]{:S(2)}, u32[]{:S(2)}) collective-permute-start(bf16[128,2048]{1,0:T(8,128)(2,1)} %get-tuple-element.41), channel_id=1, source_target_pairs={{0,0},{8,16},{16,8},{24,24},{1,1},{9,17},{17,9},{25,25},{2,26},{10... | collective-permute-start | bytes 1572872 | tf_op jit(solution)/shard_map/ppermute | solution.py:308
  18.1 4.8 %collective-permute-start.1 = (bf16[128,2048]{1,0:T(8,128)(2,1)}, bf16[128,2048]{1,0:T(8,128)(2,1)S(1)}, u32[]{:S(2)}, u32[]{:S(2)}) collective-permute-start(bf16[128,2048]{1,0:T(8,128)(2,1)} %collective-permute-done), channel_id=1, source_target_pairs={{0,0},{16,18},{8,12},{24,30},{1,1},{17,19},{9,13},{25,31},{26,16},... | collective-permute-start | bytes 1572872 | tf_op jit(solution)/shard_map/ppermute | solution.py:311
  19.8 3.2 %collective-permute-start.3 = (bf16[128,2048]{1,0:T(8,128)(2,1)}, bf16[128,2048]{1,0:T(8,128)(2,1)S(1)}, u32[]{:S(2)}, u32[]{:S(2)}) collective-permute-start(bf16[128,2048]{1,0:T(8,128)(2,1)} %get-tuple-element.42), channel_id=1, source_target_pairs={{0,0},{8,16},{16,8},{24,24},{1,1},{9,17},{17,9},{25,25},{2,26},{10... | collective-permute-start | bytes 1572872 | tf_op jit(solution)/shard_map/ppermute | solution.py:308
  21.5 20.3 %collective-permute-start.4 = (bf16[128,2048]{1,0:T(8,128)(2,1)S(1)}, bf16[128,2048]{1,0:T(8,128)(2,1)}, u32[]{:S(2)}, u32[]{:S(2)}) collective-permute-start(bf16[128,2048]{1,0:T(8,128)(2,1)S(1)} %collective-permute-done.2), channel_id=1, source_target_pairs={{0,0},{16,18},{8,12},{24,30},{1,1},{17,19},{9,13},{25,31},{26,16},... | collective-permute-start | bytes 1572872 | tf_op jit(solution)/shard_map/ppermute | solution.py:311
  23.0 27.0 %collective-permute-start.6 = (bf16[128,2048]{1,0:T(8,128)(2,1)S(1)}, bf16[128,2048]{1,0:T(8,128)(2,1)}, u32[]{:S(2)}, u32[]{:S(2)}) collective-permute-start(bf16[128,2048]{1,0:T(8,128)(2,1)S(1)} %collective-permute-done.1.refs_0_), channel_id=1, source_target_pairs={{0,16},{8,24},{16,0},{24,8},{1,17},{9,25},{17,1},{25,9},{2,18},{10... | collective-permute-start | bytes 1572872 | tf_op jit(solution)/shard_map/ppermute | solution.py:256
  38.8 13.4 %collective-permute-start.8 = (bf16[128,2048]{1,0:T(8,128)(2,1)S(1)}, bf16[128,2048]{1,0:T(8,128)(2,1)S(1)}, u32[]{:S(2)}, u32[]{:S(2)}) collective-permute-start(bf16[128,2048]{1,0:T(8,128)(2,1)S(1)} %collective-permute-done.1.refs_0_), channel_id=1, source_target_pairs={{0,8},{8,0},{16,24},{24,16},{1,9},{9,1},{17,25},{25,17},{2,10},{10... | collective-permute-start | bytes 1572872 | tf_op jit(solution)/shard_map/ppermute | solution.py:256
  41.8 19.1 %collective-permute-start.7 = (bf16[128,2048]{1,0:T(8,128)(2,1)}, bf16[128,2048]{1,0:T(8,128)(2,1)}, u32[]{:S(2)}, u32[]{:S(2)}) collective-permute-start(bf16[128,2048]{1,0:T(8,128)(2,1)} %collective-permute-done.4.refs_1_), channel_id=1, source_target_pairs={{0,16},{8,24},{16,0},{24,8},{1,17},{9,25},{17,1},{25,9},{2,18},{10... | collective-permute-start | bytes 1572872 | tf_op jit(solution)/shard_map/ppermute | solution.py:256
  46.7 16.0 %collective-permute-start.17 = (bf16[128,2048]{1,0:T(8,128)(2,1)S(1)}, bf16[128,2048]{1,0:T(8,128)(2,1)}, u32[]{:S(2)}, u32[]{:S(2)}) collective-permute-start(bf16[128,2048]{1,0:T(8,128)(2,1)S(1)} %collective-permute-done.3), channel_id=1, source_target_pairs={{0,0},{16,18},{8,12},{24,30},{1,1},{17,19},{9,13},{25,31},{26,16},... | collective-permute-start | bytes 1572872 | tf_op jit(solution)/shard_map/ppermute | solution.py:311
  48.2 17.0 %collective-permute-start.9 = (bf16[128,2048]{1,0:T(8,128)(2,1)}, bf16[128,2048]{1,0:T(8,128)(2,1)}, u32[]{:S(2)}, u32[]{:S(2)}) collective-permute-start(bf16[128,2048]{1,0:T(8,128)(2,1)} %collective-permute-done.4.refs_1_), channel_id=1, source_target_pairs={{0,8},{8,0},{16,24},{24,16},{1,9},{9,1},{17,25},{25,17},{2,10},{10... | collective-permute-start | bytes 1572872 | tf_op jit(solution)/shard_map/ppermute | solution.py:256
  50.0 15.1 %collective-permute-start.12 = (bf16[1024,256]{1,0:T(8,128)(2,1)S(1)}, bf16[1024,256]{1,0:T(8,128)(2,1)}, u32[]{:S(2)}, u32[]{:S(2)}) collective-permute-start(bf16[1024,256]{1,0:T(8,128)(2,1)S(1)} %constant_dynamic-update-slice_fusion.refs_8_.refs_4_), channel_id=1, source_target_pairs={{0,1},{1,0},{2,3},{3,2},{4,5},{5,4},{6,7},{7,6},{8,9},{9,8},{10,11... | collective-permute-start | bytes 1572872 | tf_op jit(solution)/shard_map/ppermute | solution.py:256
  53.0 12.1 %collective-permute-start.10 = (bf16[128,2048]{1,0:T(8,128)(2,1)}, bf16[128,2048]{1,0:T(8,128)(2,1)}, u32[]{:S(2)}, u32[]{:S(2)}) collective-permute-start(bf16[128,2048]{1,0:T(8,128)(2,1)} %collective-permute-done.6.refs_2_), channel_id=1, source_target_pairs={{0,8},{8,0},{16,24},{24,16},{1,9},{9,1},{17,25},{25,17},{2,10},{10... | collective-permute-start | bytes 1572872 | tf_op jit(solution)/shard_map/ppermute | solution.py:256
  60.9 4.3 %collective-permute-start.11 = (bf16[128,2048]{1,0:T(8,128)(2,1)}, bf16[128,2048]{1,0:T(8,128)(2,1)}, u32[]{:S(2)}, u32[]{:S(2)}) collective-permute-start(bf16[128,2048]{1,0:T(8,128)(2,1)} %collective-permute-done.7.refs_3_), channel_id=1, source_target_pairs={{0,8},{8,0},{16,24},{24,16},{1,9},{9,1},{17,25},{25,17},{2,10},{10... | collective-permute-start | bytes 1572872 | tf_op jit(solution)/shard_map/ppermute | solution.py:256
  62.7 17.4 %collective-permute-start.18 = (bf16[128,2048]{1,0:T(8,128)(2,1)}, bf16[128,2048]{1,0:T(8,128)(2,1)}, u32[]{:S(2)}, u32[]{:S(2)}) collective-permute-start(bf16[128,2048]{1,0:T(8,128)(2,1)} %collective-permute-done.17.refs_0_), channel_id=1, source_target_pairs={{0,16},{8,24},{16,0},{24,8},{1,17},{9,25},{17,1},{25,9},{2,18},{10... | collective-permute-start | bytes 1572872 | tf_op jit(solution)/shard_map/ppermute | solution.py:256
  71.6 9.0 %collective-permute-start.13 = (bf16[2,256,256]{2,1,0:T(8,128)(2,1)S(1)}, bf16[2,256,256]{2,1,0:T(8,128)(2,1)S(1)}, u32[]{:S(2)}, u32[]{:S(2)}) collective-permute-start(bf16[2,256,256]{2,1,0:T(8,128)(2,1)S(1)} %get-tuple-element.47), channel_id=1, source_target_pairs={{0,2},{1,3},{2,0},{3,1},{4,6},{5,7},{6,4},{7,5},{8,10},{9,11},{10,... | collective-permute-start | bytes 786440 | tf_op jit(solution)/shard_map/ppermute | solution.py:256
  74.3 27.4 %collective-permute-start.23 = (bf16[1024,384]{1,0:T(8,128)(2,1)S(1)}, bf16[1024,384]{1,0:T(8,128)(2,1)S(1)}, u32[]{:S(2)}, u32[]{:S(2)}) collective-permute-start(bf16[1024,384]{1,0:T(8,128)(2,1)S(1)} %copy-done), channel_id=1, source_target_pairs={{0,1},{1,0},{2,3},{3,2},{4,5},{5,4},{6,7},{7,6},{8,9},{9,8},{10,11... | collective-permute-start | bytes 2359304 | tf_op jit(solution)/shard_map/ppermute | solution.py:256
  79.4 22.3 %collective-permute-start.22 = (bf16[2,256,640]{2,1,0:T(8,128)(2,1)S(1)}, bf16[2,256,640]{2,1,0:T(8,128)(2,1)S(1)}, u32[]{:S(2)}, u32[]{:S(2)}) collective-permute-start(bf16[2,256,640]{2,1,0:T(8,128)(2,1)S(1)} %get-tuple-element.50), channel_id=1, source_target_pairs={{0,2},{1,3},{2,0},{3,1},{4,6},{5,7},{6,4},{7,5},{8,10},{9,11},{10,... | collective-permute-start | bytes 1966088 | tf_op jit(solution)/shard_map/ppermute | solution.py:256
  80.1 8.3 %collective-permute-start.20 = (bf16[128,2048]{1,0:T(8,128)(2,1)}, bf16[128,2048]{1,0:T(8,128)(2,1)S(1)}, u32[]{:S(2)}, u32[]{:S(2)}) collective-permute-start(bf16[128,2048]{1,0:T(8,128)(2,1)} %collective-permute-done.18.refs_1_), channel_id=1, source_target_pairs={{0,8},{8,0},{16,24},{24,16},{1,9},{9,1},{17,25},{25,17},{2,10},{10... | collective-permute-start | bytes 1572872 | tf_op jit(solution)/shard_map/ppermute | solution.py:256
  80.1 8.3 %collective-permute-start.19 = (bf16[128,2048]{1,0:T(8,128)(2,1)}, bf16[128,2048]{1,0:T(8,128)(2,1)S(1)}, u32[]{:S(2)}, u32[]{:S(2)}) collective-permute-start(bf16[128,2048]{1,0:T(8,128)(2,1)} %collective-permute-done.17.refs_0_), channel_id=1, source_target_pairs={{0,8},{8,0},{16,24},{24,16},{1,9},{9,1},{17,25},{25,17},{2,10},{10... | collective-permute-start | bytes 1572872 | tf_op jit(solution)/shard_map/ppermute | solution.py:256
  80.6 1.4 collective-permute-start.14
  82.0 4.2 %collective-permute-start.15 = (f32[3,128]{1,0:T(4,128)S(1)}, f32[3,128]{1,0:T(4,128)S(1)}, u32[]{:S(2)}, u32[]{:S(2)}) collective-permute-start(f32[3,128]{1,0:T(4,128)S(1)} %add.34), channel_id=1, source_target_pairs={{0,16},{8,24},{16,0},{24,8},{1,17},{9,25},{17,1},{25,9},{2,18},{10... | collective-permute-start | bytes 4616 | tf_op jit(solution)/shard_map/ppermute | solution.py:256
  86.3 11.8 %collective-permute-start.16 = (bf16[1,256,256]{2,1,0:T(8,128)(2,1)S(1)}, bf16[1,256,256]{2,1,0:T(8,128)(2,1)S(1)}, u32[]{:S(2)}, u32[]{:S(2)}) collective-permute-start(bf16[1,256,256]{2,1,0:T(8,128)(2,1)S(1)} %fusion.6), channel_id=1, source_target_pairs={{0,4},{1,5},{2,6},{3,7},{4,0},{5,1},{6,2},{7,3},{8,12},{9,13},{10,... | collective-permute-start | bytes 393224 | tf_op jit(solution)/shard_map/ppermute | solution.py:256
  93.1 21.8 %collective-permute-start.25 = (bf16[2,128,896]{2,1,0:T(8,128)(2,1)S(1)}, bf16[2,128,896]{2,1,0:T(8,128)(2,1)S(1)}, u32[]{:S(2)}, u32[]{:S(2)}) collective-permute-start(bf16[2,128,896]{2,1,0:T(8,128)(2,1)S(1)} %get-tuple-element.56), channel_id=1, source_target_pairs={{0,2},{1,3},{2,0},{3,1},{4,6},{5,7},{6,4},{7,5},{8,10},{9,11},{10,... | collective-permute-start | bytes 1376264 | tf_op jit(solution)/shard_map/ppermute | solution.py:256
  98.3 11.1 %collective-permute-start.21 = (bf16[1,256,256]{2,1,0:T(8,128)(2,1)S(1)}, bf16[1,256,256]{2,1,0:T(8,128)(2,1)S(1)}, u32[]{:S(2)}, u32[]{:S(2)}) collective-permute-start(bf16[1,256,256]{2,1,0:T(8,128)(2,1)S(1)} %bitcast.21), channel_id=1, source_target_pairs={{0,4},{1,5},{2,6},{3,7},{4,0},{5,1},{6,2},{7,3},{8,12},{9,13},{10,... | collective-permute-start | bytes 393224 | tf_op jit(solution)/shard_map/ppermute | solution.py:256
  105.8 21.2 %copy-start.12 = (f32[1024]{0:T(1024)S(1)}, f32[1024]{0:T(1024)}, u32[]{:S(2)}) copy-start(f32[1024]{0:T(1024)} %param.17) | copy-start | bytes 12292
  109.4 16.6 %collective-permute-start.24 = (bf16[2,256,256]{2,1,0:T(8,128)(2,1)S(1)}, bf16[2,256,256]{2,1,0:T(8,128)(2,1)S(1)}, u32[]{:S(2)}, u32[]{:S(2)}) collective-permute-start(bf16[2,256,256]{2,1,0:T(8,128)(2,1)S(1)} %pad_maximum_fusion.2), channel_id=1, source_target_pairs={{0,2},{1,3},{2,0},{3,1},{4,6},{5,7},{6,4},{7,5},{8,10},{9,11},{10,... | collective-permute-start | bytes 786440 | tf_op jit(solution)/shard_map/ppermute | solution.py:256
  113.7 18.1 %collective-permute-start.29 = (bf16[1,256,640]{2,1,0:T(8,128)(2,1)S(1)}, bf16[1,256,640]{2,1,0:T(8,128)(2,1)S(1)}, u32[]{:S(2)}, u32[]{:S(2)}) collective-permute-start(bf16[1,256,640]{2,1,0:T(8,128)(2,1)S(1)} %fusion.3), channel_id=1, source_target_pairs={{0,4},{1,5},{2,6},{3,7},{4,0},{5,1},{6,2},{7,3},{8,12},{9,13},{10,... | collective-permute-start | bytes 983048 | tf_op jit(solution)/shard_map/ppermute | solution.py:256
  113.7 29.3 %collective-permute-start.28 = (bf16[2,384,384]{2,1,0:T(8,128)(2,1)S(1)}, bf16[2,384,384]{2,1,0:T(8,128)(2,1)S(1)}, u32[]{:S(2)}, u32[]{:S(2)}) collective-permute-start(bf16[2,384,384]{2,1,0:T(8,128)(2,1)S(1)} %get-tuple-element.69), channel_id=1, source_target_pairs={{0,2},{1,3},{2,0},{3,1},{4,6},{5,7},{6,4},{7,5},{8,10},{9,11},{10,... | collective-permute-start | bytes 1769480 | tf_op jit(solution)/shard_map/ppermute | solution.py:256
  126.1 17.5 %collective-permute-start.26 = (bf16[4,256,256]{2,1,0:T(8,128)(2,1)S(1)}, bf16[4,256,256]{2,1,0:T(8,128)(2,1)S(1)}, u32[]{:S(2)}, u32[]{:S(2)}) collective-permute-start(bf16[4,256,256]{2,1,0:T(8,128)(2,1)S(1)} %pad_maximum_fusion.1), channel_id=1, source_target_pairs={{0,1},{1,0},{2,3},{3,2},{4,5},{5,4},{6,7},{7,6},{8,9},{9,8},{10,11... | collective-permute-start | bytes 1572872 | tf_op jit(solution)/shard_map/ppermute | solution.py:256
  127.0 16.3 %collective-permute-start.27 = (bf16[1,128,896]{2,1,0:T(8,128)(2,1)S(1)}, bf16[1,128,896]{2,1,0:T(8,128)(2,1)S(1)}, u32[]{:S(2)}, u32[]{:S(2)}) collective-permute-start(bf16[1,128,896]{2,1,0:T(8,128)(2,1)S(1)} %fusion.5), channel_id=1, source_target_pairs={{0,4},{1,5},{2,6},{3,7},{4,0},{5,1},{6,2},{7,3},{8,12},{9,13},{10,... | collective-permute-start | bytes 688136 | tf_op jit(solution)/shard_map/ppermute | solution.py:256
  143.0 13.6 %collective-permute-start.30 = (bf16[1,384,384]{2,1,0:T(8,128)(2,1)S(1)}, bf16[1,384,384]{2,1,0:T(8,128)(2,1)S(1)}, u32[]{:S(2)}, u32[]{:S(2)}) collective-permute-start(bf16[1,384,384]{2,1,0:T(8,128)(2,1)S(1)} %fusion.4), channel_id=1, source_target_pairs={{0,4},{1,5},{2,6},{3,7},{4,0},{5,1},{6,2},{7,3},{8,12},{9,13},{10,... | collective-permute-start | bytes 884744 | tf_op jit(solution)/shard_map/ppermute | solution.py:256
  (14 other events, 71.6 us)

commit v12 on v11

--- a/solution.py
+++ b/solution.py
@@ -287,7 +287,7 @@
                 first_hop.append((feature * branches + here, stop))
                 second_hop.append((stop, landing(z, feature) * branches + there))
     axes = ("fsdp", "branch")
-    head_cuts = [0, (5 * head_count + 7) // 8, head_count]
+    head_cuts = [0, (3 * head_count + 3) // 4, head_count]
     w_chunks = [jnp.concatenate([w_key, w_value], 1)] + [
         lax.slice_in_dim(w_query, low * HD, high * HD, axis=1)
         for low, high in zip(head_cuts, head_cuts[1:])
@@ -327,6 +327,15 @@
                 piece[j | bit] = swap(piece[j], "fsdp", bit)
         bit //= 2
 
+    squares = jnp.sum(jnp.square(raw.astype(f32)), -1).reshape(blocks, block_len)
+    squares = tie(squares, held[0][half_lines])
+    bit = 1
+    while bit < lines:
+        squares = squares + swap(squares, "fsdp", bit)
+        bit *= 2
+    inverse = lax.rsqrt(squares / features + 1e-06).reshape(tokens)
+    inverse = jnp.broadcast_to(inverse[:, None], (tokens, HD))
+
     def last_bit(piece):
         for j in list(piece):
             piece[j | 1] = swap(piece[j], "fsdp", 1)
@@ -334,6 +343,7 @@
 
     assembled = {}
     held[0] = last_bit(held[0])
+    held[1][half_lines] = tie(held[1][half_lines], w_rows[0][-1])
     held[1] = last_bit(held[1])
 
     def project(spans, chunks, *after):
@@ -424,20 +434,11 @@
 
     early = [(0, STEMS)]
     late = [(STEMS, blocks)]
-    first = Halving(project(early, [0]))
+    first = Halving(project(early, [0], squares, last_sent))
     first.step()
     second = Halving(project(early, [1], first.send))
-    second.step()
     first.rest(second.send)
-
-    squares = jnp.sum(jnp.square(raw.astype(f32)), -1).reshape(blocks, block_len)
-    squares = tie(squares, first.send)
-    bit = 1
-    while bit < lines:
-        squares = squares + swap(squares, "fsdp", bit)
-        bit *= 2
-    inverse = lax.rsqrt(squares / features + 1e-06).reshape(tokens)
-    inverse = jnp.broadcast_to(inverse[:, None], (tokens, HD))
+    second.step(first.send)
 
     for block in range(STEMS, blocks):
         held[block] = {j: tie(piece, second.send) for j, piece in held[block].items()}
@@ -453,11 +454,11 @@
     came = swap(stems, "branch", tour[0])
     second.add(stem_kv, w_rows[2][-1])
     fourth = Halving(project(early + late, [2], second.send))
+    second.step(fourth.send)
     for step, bit in enumerate(tour[1:]):
         stems = jnp.concatenate([stems, tie(came, third.send if step else fourth.send)], 0)
         came = swap(stems, "branch", bit)
         if step == 0:
-            second.step(stems)
             fourth.step(stems)
             third.add(stems)
             third.step()

time: 161 us -> 171 us (1.062)
  waiting for transfers between devices: 49.1 us -> 55.7 us
  starting transfers between devices: 71.8 us -> 75.7 us
  Pallas kernels: 28.2 us -> 25.6 us
    ppermute x3, starting transfers between devices: 4.6 us -> 12.2 us  [shards(): sent = [lax.ppermute(piece, axes, second_hop) for piece in sent]]
    ppermute x25, starting transfers between devices: 58.3 us -> 51 us  [swap(): return lax.ppermute(array, axis, [(i, i ^ bit) for i in range(size)])]
    ppermute x25, waiting for transfers between devices: 49.1 us -> 55.6 us  [swap(): return lax.ppermute(array, axis, [(i, i ^ bit) for i in range(size)])]
    ppermute x3, starting transfers between devices: 8.87 us -> 12.5 us  [shards(): sent.append(lax.ppermute(piece, axes, first_hop))]
    pallas_call x4, Pallas kernels: 17 us -> 14.4 us  [project(): pl.pallas_call(functools.partial(project_kernel, lines, groups, len(chunk...]
    unnamed x31 -> x29, local copies, waits for them, and re-layouts: 4.19 us -> 4.18 us
  transfers between devices with their start and end apart: 31 -> 31, of which waited for: 10 -> 14; matrix products, arithmetic and copies ran while one was open for 2% -> 3% of each run, Pallas kernels for 15% -> 11%
where the time goes in v12:
time: 171 us; the launch traced here: 170 us
  starting transfers between devices  75.7 us (44%)
  waiting for transfers between devices  55.7 us (33%)
  Pallas kernels  25.6 us (15%)
  local copies, waits for them, and re-layouts  7.21 us (4%)
  other arithmetic  5.1 us (3%)
    ppermute x25, waiting for transfers between devices, swap(): return lax.ppermute(array, axis, [(i, i ^ bit) for i in range(size)])  55.6 us
    ppermute x25, starting transfers between devices, swap(): return lax.ppermute(array, axis, [(i, i ^ bit) for i in range(size)])  51 us
    pallas_call x4, Pallas kernels, project(): pl.pallas_call(functools.partial(project_kernel, lines, groups, len(chunk...  14.4 us
    ppermute x3, starting transfers between devices, shards(): sent.append(lax.ppermute(piece, axes, first_hop))  12.5 us
    ppermute x3, starting transfers between devices, shards(): sent = [lax.ppermute(piece, axes, second_hop) for piece in sent]  12.2 us
    pallas_call x2, Pallas kernels, attend(): pl.pallas_call(kernel, grid=(1,), in_specs=in_specs, out_specs=anywhere,...  8.75 us
    unnamed x29, local copies, waits for them, and re-layouts  4.18 us
  transfers between devices with their start and end apart: 31, of which 14 were waited for; matrix products, arithmetic and copies ran while one was open for 3% of the time, Pallas kernels for 11%

profile of v12, /device:TPU:0, one launch (start us, length us, event | category | flops | bytes accessed | tf_op | source)
XLA Modules:
  0.0 169.7 jit_solution(12001900965603101953)
XLA Ops:
  0.7 2.8 %fusion = (bf16[128,2048]{1,0:T(8,128)(2,1)}, bf16[128,2048]{1,0:T(8,128)(2,1)}, bf16[128,2048]{1,0:T(8,128)(2,1)}) fusion(bf16[3,128,2048]{2,1,0:T(8,128)(2,1)} %param.10, f32[2048]{0:T(1024)S(1)} %dynamic_slice.3), kind=kLoop, calls=%fused_computation.3 | loop fusion | flops 2359296 | bytes 3153920 | tf_op jit(solution)/shard_map/convert_element_type | solution.py:306
  3.5 5.5 %collective-permute-start = (bf16[128,2048]{1,0:T(8,128)(2,1)}, bf16[128,2048]{1,0:T(8,128)(2,1)}, u32[]{:S(2)}, u32[]{:S(2)}) collective-permute-start(bf16[128,2048]{1,0:T(8,128)(2,1)} %get-tuple-element.82), channel_id=1, source_target_pairs={{0,0},{8,16},{16,8},{24,24},{1,1},{9,17},{17,9},{25,25},{2,26},{10... | collective-permute-start | bytes 1572872 | tf_op jit(solution)/shard_map/ppermute | solution.py:308
  9.2 3.0 %collective-permute-start.9 = (bf16[1024,768]{1,0:T(8,128)(2,1)S(1)}, bf16[1024,768]{1,0:T(8,128)(2,1)S(1)}, u32[]{:S(2)}, u32[]{:S(2)}) collective-permute-start(bf16[1024,768]{1,0:T(8,128)(2,1)S(1)} %slice.70.refs_1_.refs_6_), channel_id=1, source_target_pairs={{0,1},{1,0},{2,3},{3,2},{4,5},{5,4},{6,7},{7,6},{8,9},{9,8},{10,11... | collective-permute-start | bytes 4718600 | tf_op jit(solution)/shard_map/ppermute | solution.py:256
  13.1 2.2 %tables.1 = (f32[384,128]{1,0:T(8,128)}, f32[384,128]{1,0:T(8,128)}) custom-call(s32[1]{0:T(128)} %bitcast.device_ref, s32[24]{0:T(128)} %parents_ref.5), custom_call_target="tpu_custom_call" | custom-call | tf_op jit(solution)/shard_map/tables/pallas_call | solution.py:296
  18.0 5.4 %collective-permute-start.1 = (bf16[128,2048]{1,0:T(8,128)(2,1)}, bf16[128,2048]{1,0:T(8,128)(2,1)}, u32[]{:S(2)}, u32[]{:S(2)}) collective-permute-start(bf16[128,2048]{1,0:T(8,128)(2,1)} %collective-permute-done), channel_id=1, source_target_pairs={{0,0},{16,18},{8,12},{24,30},{1,1},{17,19},{9,13},{25,31},{26,16},... | collective-permute-start | bytes 1572872 | tf_op jit(solution)/shard_map/ppermute | solution.py:311
  23.4 5.4 %collective-permute-start.3 = (bf16[128,2048]{1,0:T(8,128)(2,1)}, bf16[128,2048]{1,0:T(8,128)(2,1)}, u32[]{:S(2)}, u32[]{:S(2)}) collective-permute-start(bf16[128,2048]{1,0:T(8,128)(2,1)} %get-tuple-element.45), channel_id=1, source_target_pairs={{0,0},{8,16},{16,8},{24,24},{1,1},{9,17},{17,9},{25,25},{2,26},{10... | collective-permute-start | bytes 1572872 | tf_op jit(solution)/shard_map/ppermute | solution.py:308
  30.2 8.7 %collective-permute-start.4 = (bf16[128,2048]{1,0:T(8,128)(2,1)}, bf16[128,2048]{1,0:T(8,128)(2,1)}, u32[]{:S(2)}, u32[]{:S(2)}) collective-permute-start(bf16[128,2048]{1,0:T(8,128)(2,1)} %collective-permute-done.1.refs_0_), channel_id=1, source_target_pairs={{0,16},{8,24},{16,0},{24,8},{1,17},{9,25},{17,1},{25,9},{2,18},{10... | collective-permute-start | bytes 1572872 | tf_op jit(solution)/shard_map/ppermute | solution.py:256
  38.9 6.2 %collective-permute-done.9.refs_2_.refs_7_ = bf16[1024,768]{1,0:T(8,128)(2,1)S(1)} collective-permute-done((bf16[1024,768]{1,0:T(8,128)(2,1)S(1)}, bf16[1024,768]{1,0:T(8,128)(2,1)S(1)}, u32[]{:S(2)}, u32[]{:S(2)}) %collective-permute-start.9) | collective-permute-done | bytes 1572896 | tf_op jit(solution)/shard_map/ppermute | solution.py:256
  50.8 1.9 %collective-permute-start.5 = (f32[3,128]{1,0:T(4,128)S(1)}, f32[3,128]{1,0:T(4,128)S(1)}, u32[]{:S(2)}, u32[]{:S(2)}) collective-permute-start(f32[3,128]{1,0:T(4,128)S(1)} %multiply_reduce_fusion), channel_id=1, source_target_pairs={{0,8},{8,0},{16,24},{24,16},{1,9},{9,1},{17,25},{25,17},{2,10},{10... | collective-permute-start | bytes 4616 | tf_op jit(solution)/shard_map/ppermute | solution.py:256
  53.5 2.5 %collective-permute-start.6 = (f32[3,128]{1,0:T(4,128)S(1)}, f32[3,128]{1,0:T(4,128)S(1)}, u32[]{:S(2)}, u32[]{:S(2)}) collective-permute-start(f32[3,128]{1,0:T(4,128)S(1)} %add.32), channel_id=1, source_target_pairs={{0,16},{8,24},{16,0},{24,8},{1,17},{9,25},{17,1},{25,9},{2,18},{10... | collective-permute-start | bytes 4616 | tf_op jit(solution)/shard_map/ppermute | solution.py:256
  56.0 5.3 %collective-permute-start.7 = (bf16[128,2048]{1,0:T(8,128)(2,1)}, bf16[128,2048]{1,0:T(8,128)(2,1)}, u32[]{:S(2)}, u32[]{:S(2)}) collective-permute-start(bf16[128,2048]{1,0:T(8,128)(2,1)} %collective-permute-done.3), channel_id=1, source_target_pairs={{0,0},{16,18},{8,12},{24,30},{1,1},{17,19},{9,13},{25,31},{26,16},... | collective-permute-start | bytes 1572872 | tf_op jit(solution)/shard_map/ppermute | solution.py:311
  68.0 4.0 %project.4 = (bf16[2,256,256]{2,1,0:T(8,128)(2,1)S(1)}, f32[2,256,256]{2,1,0:T(8,128)S(1)}, bf16[1024,2048]{1,0:T(8,128)(2,1)S(1)}) custom-call(s32[2]{0:T(128)S(1)} %pad_add_fusion.place_ref, bf16[128,2048]{1,0:T(8,128)(2,1)} %collective-permute-done.1.refs_0_, bf16[128,2048]{1,0:T(8,128)(2,1)} %collective-permute-done.8.refs_1_, ...), custom_call_target="tpu_custom_call" | custom-call | tf_op jit(solution)/shard_map/project/pallas_call | solution.py:373
  72.1 6.9 %collective-permute-start.16 = (bf16[2,256,256]{2,1,0:T(8,128)(2,1)S(1)}, bf16[2,256,256]{2,1,0:T(8,128)(2,1)S(1)}, u32[]{:S(2)}, u32[]{:S(2)}) collective-permute-start(bf16[2,256,256]{2,1,0:T(8,128)(2,1)S(1)} %get-tuple-element.53), channel_id=1, source_target_pairs={{0,2},{1,3},{2,0},{3,1},{4,6},{5,7},{6,4},{7,5},{8,10},{9,11},{10,... | collective-permute-start | bytes 786440 | tf_op jit(solution)/shard_map/ppermute | solution.py:256
  80.4 4.0 %project.5 = (bf16[2,256,768]{2,1,0:T(8,128)(2,1)S(1)}, f32[2,256,768]{2,1,0:T(8,128)S(1)}) custom-call(s32[2]{0:T(128)S(1)} %pad_add_fusion.place_ref, bf16[1024,2048]{1,0:T(8,128)(2,1)S(1)} %get-tuple-element.67.refs_0_, bf16[1024,768]{1,0:T(8,128)(2,1)S(1)} %slice.70.refs_1_.refs_6_, bf16[1024,768]{1,0:T(8,128)(2,1)S(1)} %collective-permute-done.9.refs_2_.refs_7_), custom_call_target="tpu_custom_call" | custom-call | tf_op jit(solution)/shard_map/project/pallas_call | solution.py:373
  87.1 5.5 %collective-permute-done.18.refs_1_ = bf16[128,2048]{1,0:T(8,128)(2,1)S(1)} collective-permute-done((bf16[128,2048]{1,0:T(8,128)(2,1)}, bf16[128,2048]{1,0:T(8,128)(2,1)S(1)}, u32[]{:S(2)}, u32[]{:S(2)}) %collective-permute-start.18) | collective-permute-done | bytes 524320 | tf_op jit(solution)/shard_map/ppermute | solution.py:256
  93.2 2.1 %collective-permute-start.23 = (bf16[1024,256]{1,0:T(8,128)(2,1)S(1)}, bf16[1024,256]{1,0:T(8,128)(2,1)S(1)}, u32[]{:S(2)}, u32[]{:S(2)}) collective-permute-start(bf16[1024,256]{1,0:T(8,128)(2,1)S(1)} %copy-done.4), channel_id=1, source_target_pairs={{0,1},{1,0},{2,3},{3,2},{4,5},{5,4},{6,7},{7,6},{8,9},{9,8},{10,11... | collective-permute-start | bytes 1572872 | tf_op jit(solution)/shard_map/ppermute | solution.py:256
  95.8 4.0 %project.6 = (bf16[2,128,1024]{2,1,0:T(8,128)(2,1)S(1)}, f32[2,128,1024]{2,1,0:T(8,128)S(1)}, bf16[512,2048]{1,0:T(8,128)(2,1)S(1)}) custom-call(s32[2]{0:T(128)S(1)} %pad_add_fusion.place_ref, bf16[128,2048]{1,0:T(8,128)(2,1)} %collective-permute-done.7.refs_0_, bf16[128,2048]{1,0:T(8,128)(2,1)S(1)} %collective-permute-done.18.refs_1_, ...), custom_call_target="tpu_custom_call" | custom-call | tf_op jit(solution)/shard_map/project/pallas_call | solution.py:373
  99.8 2.0 %collective-permute-start.25 = (bf16[2,128,1024]{2,1,0:T(8,128)(2,1)S(1)}, bf16[2,128,1024]{2,1,0:T(8,128)(2,1)S(1)}, u32[]{:S(2)}, u32[]{:S(2)}) collective-permute-start(bf16[2,128,1024]{2,1,0:T(8,128)(2,1)S(1)} %get-tuple-element.61), channel_id=1, source_target_pairs={{0,2},{1,3},{2,0},{3,1},{4,6},{5,7},{6,4},{7,5},{8,10},{9,11},{10,... | collective-permute-start | bytes 1572872 | tf_op jit(solution)/shard_map/ppermute | solution.py:256
  101.8 6.1 %collective-permute-done.17.refs_2_ = bf16[1,256,256]{2,1,0:T(8,128)(2,1)S(1)} collective-permute-done((bf16[1,256,256]{2,1,0:T(8,128)(2,1)S(1)}, bf16[1,256,256]{2,1,0:T(8,128)(2,1)S(1)}, u32[]{:S(2)}, u32[]{:S(2)}) %collective-permute-start.17) | collective-permute-done | bytes 131104 | tf_op jit(solution)/shard_map/ppermute | solution.py:256
  108.2 3.4 %collective-permute-start.21 = (bf16[1,256,256]{2,1,0:T(8,128)(2,1)S(1)}, bf16[1,256,256]{2,1,0:T(8,128)(2,1)S(1)}, u32[]{:S(2)}, u32[]{:S(2)}) collective-permute-start(bf16[1,256,256]{2,1,0:T(8,128)(2,1)S(1)} %bitcast.23), channel_id=1, source_target_pairs={{0,4},{1,5},{2,6},{3,7},{4,0},{5,1},{6,2},{7,3},{8,12},{9,13},{10,... | collective-permute-start | bytes 393224 | tf_op jit(solution)/shard_map/ppermute | solution.py:256
  111.7 2.3 %project.7 = (bf16[2,384,256]{2,1,0:T(8,128)(2,1)S(1)}, f32[2,384,256]{2,1,0:T(8,128)S(1)}) custom-call(s32[2]{0:T(128)S(1)} %pad_add_fusion.place_ref, bf16[1024,2048]{1,0:T(8,128)(2,1)S(1)} %get-tuple-element.67.refs_0_, bf16[512,2048]{1,0:T(8,128)(2,1)S(1)} %get-tuple-element.68.refs_1_, bf16[1024,256]{1,0:T(8,128)(2,1)S(1)} %copy-done.4, ...), custom_call_target="tpu_custom_call" | custom-call | tf_op jit(solution)/shard_map/project/pallas_call | solution.py:373
  114.1 6.4 %collective-permute-done.21 = bf16[1,256,256]{2,1,0:T(8,128)(2,1)S(1)} collective-permute-done((bf16[1,256,256]{2,1,0:T(8,128)(2,1)S(1)}, bf16[1,256,256]{2,1,0:T(8,128)(2,1)S(1)}, u32[]{:S(2)}, u32[]{:S(2)}) %collective-permute-start.21) | collective-permute-done | bytes 131104 | tf_op jit(solution)/shard_map/ppermute | solution.py:256
  120.5 2.8 %collective-permute-start.24 = (bf16[2,256,256]{2,1,0:T(8,128)(2,1)S(1)}, bf16[2,256,256]{2,1,0:T(8,128)(2,1)S(1)}, u32[]{:S(2)}, u32[]{:S(2)}) collective-permute-start(bf16[2,256,256]{2,1,0:T(8,128)(2,1)S(1)} %pad_maximum_fusion.2), channel_id=1, source_target_pairs={{0,2},{1,3},{2,0},{3,1},{4,6},{5,7},{6,4},{7,5},{8,10},{9,11},{10,... | collective-permute-start | bytes 786440 | tf_op jit(solution)/shard_map/ppermute | solution.py:256
  124.1 2.0 %collective-permute-start.28 = (bf16[2,384,256]{2,1,0:T(8,128)(2,1)S(1)}, bf16[2,384,256]{2,1,0:T(8,128)(2,1)S(1)}, u32[]{:S(2)}, u32[]{:S(2)}) collective-permute-start(bf16[2,384,256]{2,1,0:T(8,128)(2,1)S(1)} %get-tuple-element.75), channel_id=1, source_target_pairs={{0,2},{1,3},{2,0},{3,1},{4,6},{5,7},{6,4},{7,5},{8,10},{9,11},{10,... | collective-permute-start | bytes 1179656 | tf_op jit(solution)/shard_map/ppermute | solution.py:256
  126.2 7.5 %collective-permute-done.24 = bf16[2,256,256]{2,1,0:T(8,128)(2,1)S(1)} collective-permute-done((bf16[2,256,256]{2,1,0:T(8,128)(2,1)S(1)}, bf16[2,256,256]{2,1,0:T(8,128)(2,1)S(1)}, u32[]{:S(2)}, u32[]{:S(2)}) %collective-permute-start.24) | collective-permute-done | bytes 262176 | tf_op jit(solution)/shard_map/ppermute | solution.py:256
  133.7 2.1 %collective-permute-start.26 = (bf16[4,256,256]{2,1,0:T(8,128)(2,1)S(1)}, bf16[4,256,256]{2,1,0:T(8,128)(2,1)S(1)}, u32[]{:S(2)}, u32[]{:S(2)}) collective-permute-start(bf16[4,256,256]{2,1,0:T(8,128)(2,1)S(1)} %pad_maximum_fusion.1), channel_id=1, source_target_pairs={{0,1},{1,0},{2,3},{3,2},{4,5},{5,4},{6,7},{7,6},{8,9},{9,8},{10,11... | collective-permute-start | bytes 1572872 | tf_op jit(solution)/shard_map/ppermute | solution.py:256
  135.8 3.9 %collective-permute-start.27 = (bf16[1,128,1024]{2,1,0:T(8,128)(2,1)S(1)}, bf16[1,128,1024]{2,1,0:T(8,128)(2,1)S(1)}, u32[]{:S(2)}, u32[]{:S(2)}) collective-permute-start(bf16[1,128,1024]{2,1,0:T(8,128)(2,1)S(1)} %fusion.4), channel_id=1, source_target_pairs={{0,4},{1,5},{2,6},{3,7},{4,0},{5,1},{6,2},{7,3},{8,12},{9,13},{10,... | collective-permute-start | bytes 786440 | tf_op jit(solution)/shard_map/ppermute | solution.py:256
  139.6 5.1 %collective-permute-done.29.refs_4_ = bf16[1,256,768]{2,1,0:T(8,128)(2,1)S(1)} collective-permute-done((bf16[1,256,768]{2,1,0:T(8,128)(2,1)S(1)}, bf16[1,256,768]{2,1,0:T(8,128)(2,1)S(1)}, u32[]{:S(2)}, u32[]{:S(2)}) %collective-permute-start.29) | collective-permute-done | bytes 393248 | tf_op jit(solution)/shard_map/ppermute | solution.py:256
  144.8 5.2 %collective-permute-done.28.refs_3_ = bf16[2,384,256]{2,1,0:T(8,128)(2,1)S(1)} collective-permute-done((bf16[2,384,256]{2,1,0:T(8,128)(2,1)S(1)}, bf16[2,384,256]{2,1,0:T(8,128)(2,1)S(1)}, u32[]{:S(2)}, u32[]{:S(2)}) %collective-permute-start.28) | collective-permute-done | bytes 393248 | tf_op jit(solution)/shard_map/ppermute | solution.py:256
  151.6 8.3 %collective-permute-done.27.refs_2_.refs_7_ = bf16[1,128,1024]{2,1,0:T(8,128)(2,1)S(1)} collective-permute-done((bf16[1,128,1024]{2,1,0:T(8,128)(2,1)S(1)}, bf16[1,128,1024]{2,1,0:T(8,128)(2,1)S(1)}, u32[]{:S(2)}, u32[]{:S(2)}) %collective-permute-start.27) | collective-permute-done | bytes 262176 | tf_op jit(solution)/shard_map/ppermute | solution.py:256
  160.8 5.6 %attend.2.refs_5_ = bf16[384,1024]{1,0:T(8,128)(2,1)} custom-call(s32[1]{0:T(128)} %bitcast.device_ref, s32[24]{0:T(128)S(1)} %copy-done.7, s32[24]{0:T(128)S(1)} %copy-done.8, f32[384,128]{1,0:T(8,128)S(1)} %broadcast_in_dim.31.inverse_ref, f32[1,768]{1,0:T(1,128)S(1)} %broadcast_in_dim.37.bias_ref, f32[384,128]{1,0:T(8,128)S(1)} %copy-done.5, ...), custom_call_target="tpu_custom_call" | custom-call | flops 2264924160 | bytes 589824 | tf_op jit(solution)/shard_map/attend/pallas_call | solution.py:492
  166.4 3.1 %attend.3 = bf16[384,1024]{1,0:T(8,128)(2,1)} custom-call(s32[1]{0:T(128)} %bitcast.device_ref, s32[24]{0:T(128)S(1)} %copy-done.7, s32[24]{0:T(128)S(1)} %copy-done.8, f32[384,128]{1,0:T(8,128)S(1)} %broadcast_in_dim.31.inverse_ref, f32[1,256]{1,0:T(1,128)S(1)} %bitcast.29, f32[384,128]{1,0:T(8,128)S(1)} %copy-done.5, ...), custom_call_target="tpu_custom_call", output_to_operand_aliasing={{}: (13, {})} | custom-call | flops 452984832 | bytes 196608 | tf_op jit(solution)/shard_map/attend/pallas_call | solution.py:492
  (97 shorter events, 27.8 us)
Async XLA Ops:
  3.5 12.8 %collective-permute-start = (bf16[128,2048]{1,0:T(8,128)(2,1)}, bf16[128,2048]{1,0:T(8,128)(2,1)}, u32[]{:S(2)}, u32[]{:S(2)}) collective-permute-start(bf16[128,2048]{1,0:T(8,128)(2,1)} %get-tuple-element.82), channel_id=1, source_target_pairs={{0,0},{8,16},{16,8},{24,24},{1,1},{9,17},{17,9},{25,25},{2,26},{10... | collective-permute-start | bytes 1572872 | tf_op jit(solution)/shard_map/ppermute | solution.py:308
  9.2 36.0 %collective-permute-start.9 = (bf16[1024,768]{1,0:T(8,128)(2,1)S(1)}, bf16[1024,768]{1,0:T(8,128)(2,1)S(1)}, u32[]{:S(2)}, u32[]{:S(2)}) collective-permute-start(bf16[1024,768]{1,0:T(8,128)(2,1)S(1)} %slice.70.refs_1_.refs_6_), channel_id=1, source_target_pairs={{0,1},{1,0},{2,3},{3,2},{4,5},{5,4},{6,7},{7,6},{8,9},{9,8},{10,11... | collective-permute-start | bytes 4718600 | tf_op jit(solution)/shard_map/ppermute | solution.py:256
  16.3 7.1 %collective-permute-start.2 = (bf16[128,2048]{1,0:T(8,128)(2,1)}, bf16[128,2048]{1,0:T(8,128)(2,1)S(1)}, u32[]{:S(2)}, u32[]{:S(2)}) collective-permute-start(bf16[128,2048]{1,0:T(8,128)(2,1)} %get-tuple-element.44), channel_id=1, source_target_pairs={{0,0},{8,16},{16,8},{24,24},{1,1},{9,17},{17,9},{25,25},{2,26},{10... | collective-permute-start | bytes 1572872 | tf_op jit(solution)/shard_map/ppermute | solution.py:308
  18.0 12.2 %collective-permute-start.1 = (bf16[128,2048]{1,0:T(8,128)(2,1)}, bf16[128,2048]{1,0:T(8,128)(2,1)}, u32[]{:S(2)}, u32[]{:S(2)}) collective-permute-start(bf16[128,2048]{1,0:T(8,128)(2,1)} %collective-permute-done), channel_id=1, source_target_pairs={{0,0},{16,18},{8,12},{24,30},{1,1},{17,19},{9,13},{25,31},{26,16},... | collective-permute-start | bytes 1572872 | tf_op jit(solution)/shard_map/ppermute | solution.py:311
  23.4 6.8 %collective-permute-start.3 = (bf16[128,2048]{1,0:T(8,128)(2,1)}, bf16[128,2048]{1,0:T(8,128)(2,1)}, u32[]{:S(2)}, u32[]{:S(2)}) collective-permute-start(bf16[128,2048]{1,0:T(8,128)(2,1)} %get-tuple-element.45), channel_id=1, source_target_pairs={{0,0},{8,16},{16,8},{24,24},{1,1},{9,17},{17,9},{25,25},{2,26},{10... | collective-permute-start | bytes 1572872 | tf_op jit(solution)/shard_map/ppermute | solution.py:308
  28.8 10.2 %collective-permute-start.8 = (bf16[128,2048]{1,0:T(8,128)(2,1)S(1)}, bf16[128,2048]{1,0:T(8,128)(2,1)}, u32[]{:S(2)}, u32[]{:S(2)}) collective-permute-start(bf16[128,2048]{1,0:T(8,128)(2,1)S(1)} %collective-permute-done.2), channel_id=1, source_target_pairs={{0,0},{16,18},{8,12},{24,30},{1,1},{17,19},{9,13},{25,31},{26,16},... | collective-permute-start | bytes 1572872 | tf_op jit(solution)/shard_map/ppermute | solution.py:311
  30.2 20.6 %collective-permute-start.4 = (bf16[128,2048]{1,0:T(8,128)(2,1)}, bf16[128,2048]{1,0:T(8,128)(2,1)}, u32[]{:S(2)}, u32[]{:S(2)}) collective-permute-start(bf16[128,2048]{1,0:T(8,128)(2,1)} %collective-permute-done.1.refs_0_), channel_id=1, source_target_pairs={{0,16},{8,24},{16,0},{24,8},{1,17},{9,25},{17,1},{25,9},{2,18},{10... | collective-permute-start | bytes 1572872 | tf_op jit(solution)/shard_map/ppermute | solution.py:256
  45.1 16.3 %collective-permute-start.11 = (bf16[1024,256]{1,0:T(8,128)(2,1)S(1)}, bf16[1024,256]{1,0:T(8,128)(2,1)S(1)}, u32[]{:S(2)}, u32[]{:S(2)}) collective-permute-start(bf16[1024,256]{1,0:T(8,128)(2,1)S(1)} %constant_dynamic-update-slice_fusion.refs_8_.refs_4_), channel_id=1, source_target_pairs={{0,1},{1,0},{2,3},{3,2},{4,5},{5,4},{6,7},{7,6},{8,9},{9,8},{10,11... | collective-permute-start | bytes 1572872 | tf_op jit(solution)/shard_map/ppermute | solution.py:256
  47.4 15.2 %collective-permute-start.10 = (bf16[128,2048]{1,0:T(8,128)(2,1)}, bf16[128,2048]{1,0:T(8,128)(2,1)}, u32[]{:S(2)}, u32[]{:S(2)}) collective-permute-start(bf16[128,2048]{1,0:T(8,128)(2,1)} %collective-permute-done.8.refs_1_), channel_id=1, source_target_pairs={{0,16},{8,24},{16,0},{24,8},{1,17},{9,25},{17,1},{25,9},{2,18},{10... | collective-permute-start | bytes 1572872 | tf_op jit(solution)/shard_map/ppermute | solution.py:256
  50.8 2.7 %collective-permute-start.5 = (f32[3,128]{1,0:T(4,128)S(1)}, f32[3,128]{1,0:T(4,128)S(1)}, u32[]{:S(2)}, u32[]{:S(2)}) collective-permute-start(f32[3,128]{1,0:T(4,128)S(1)} %multiply_reduce_fusion), channel_id=1, source_target_pairs={{0,8},{8,0},{16,24},{24,16},{1,9},{9,1},{17,25},{25,17},{2,10},{10... | collective-permute-start | bytes 4616 | tf_op jit(solution)/shard_map/ppermute | solution.py:256
  53.5 9.5 %collective-permute-start.6 = (f32[3,128]{1,0:T(4,128)S(1)}, f32[3,128]{1,0:T(4,128)S(1)}, u32[]{:S(2)}, u32[]{:S(2)}) collective-permute-start(f32[3,128]{1,0:T(4,128)S(1)} %add.32), channel_id=1, source_target_pairs={{0,16},{8,24},{16,0},{24,8},{1,17},{9,25},{17,1},{25,9},{2,18},{10... | collective-permute-start | bytes 4616 | tf_op jit(solution)/shard_map/ppermute | solution.py:256
  56.0 7.2 %collective-permute-start.12 = (bf16[128,2048]{1,0:T(8,128)(2,1)}, bf16[128,2048]{1,0:T(8,128)(2,1)}, u32[]{:S(2)}, u32[]{:S(2)}) collective-permute-start(bf16[128,2048]{1,0:T(8,128)(2,1)} %collective-permute-done.1.refs_0_), channel_id=1, source_target_pairs={{0,8},{8,0},{16,24},{24,16},{1,9},{9,1},{17,25},{25,17},{2,10},{10... | collective-permute-start | bytes 1572872 | tf_op jit(solution)/shard_map/ppermute | solution.py:256
  56.0 7.2 %collective-permute-start.7 = (bf16[128,2048]{1,0:T(8,128)(2,1)}, bf16[128,2048]{1,0:T(8,128)(2,1)}, u32[]{:S(2)}, u32[]{:S(2)}) collective-permute-start(bf16[128,2048]{1,0:T(8,128)(2,1)} %collective-permute-done.3), channel_id=1, source_target_pairs={{0,0},{16,18},{8,12},{24,30},{1,1},{17,19},{9,13},{25,31},{26,16},... | collective-permute-start | bytes 1572872 | tf_op jit(solution)/shard_map/ppermute | solution.py:311
  62.2 2.3 %collective-permute-start.13 = (bf16[128,2048]{1,0:T(8,128)(2,1)}, bf16[128,2048]{1,0:T(8,128)(2,1)}, u32[]{:S(2)}, u32[]{:S(2)}) collective-permute-start(bf16[128,2048]{1,0:T(8,128)(2,1)} %collective-permute-done.8.refs_1_), channel_id=1, source_target_pairs={{0,8},{8,0},{16,24},{24,16},{1,9},{9,1},{17,25},{25,17},{2,10},{10... | collective-permute-start | bytes 1572872 | tf_op jit(solution)/shard_map/ppermute | solution.py:256
  62.6 2.6 %collective-permute-start.15 = (bf16[128,2048]{1,0:T(8,128)(2,1)}, bf16[128,2048]{1,0:T(8,128)(2,1)}, u32[]{:S(2)}, u32[]{:S(2)}) collective-permute-start(bf16[128,2048]{1,0:T(8,128)(2,1)} %collective-permute-done.10.refs_3_), channel_id=1, source_target_pairs={{0,8},{8,0},{16,24},{24,16},{1,9},{9,1},{17,25},{25,17},{2,10},{10... | collective-permute-start | bytes 1572872 | tf_op jit(solution)/shard_map/ppermute | solution.py:256
  63.1 2.9 %collective-permute-start.14 = (bf16[128,2048]{1,0:T(8,128)(2,1)}, bf16[128,2048]{1,0:T(8,128)(2,1)}, u32[]{:S(2)}, u32[]{:S(2)}) collective-permute-start(bf16[128,2048]{1,0:T(8,128)(2,1)} %collective-permute-done.4.refs_2_), channel_id=1, source_target_pairs={{0,8},{8,0},{16,24},{24,16},{1,9},{9,1},{17,25},{25,17},{2,10},{10... | collective-permute-start | bytes 1572872 | tf_op jit(solution)/shard_map/ppermute | solution.py:256
  72.1 13.6 %collective-permute-start.16 = (bf16[2,256,256]{2,1,0:T(8,128)(2,1)S(1)}, bf16[2,256,256]{2,1,0:T(8,128)(2,1)S(1)}, u32[]{:S(2)}, u32[]{:S(2)}) collective-permute-start(bf16[2,256,256]{2,1,0:T(8,128)(2,1)S(1)} %get-tuple-element.53), channel_id=1, source_target_pairs={{0,2},{1,3},{2,0},{3,1},{4,6},{5,7},{6,4},{7,5},{8,10},{9,11},{10,... | collective-permute-start | bytes 786440 | tf_op jit(solution)/shard_map/ppermute | solution.py:256
  79.0 13.6 %collective-permute-start.18 = (bf16[128,2048]{1,0:T(8,128)(2,1)}, bf16[128,2048]{1,0:T(8,128)(2,1)S(1)}, u32[]{:S(2)}, u32[]{:S(2)}) collective-permute-start(bf16[128,2048]{1,0:T(8,128)(2,1)} %collective-permute-done.7.refs_0_), channel_id=1, source_target_pairs={{0,16},{8,24},{16,0},{24,8},{1,17},{9,25},{17,1},{25,9},{2,18},{10... | collective-permute-start | bytes 1572872 | tf_op jit(solution)/shard_map/ppermute | solution.py:256
  80.4 15.0 %copy-start.13 = (f32[128]{0:T(128)S(1)}, f32[128]{0:T(128)}, u32[]{:S(2)}) copy-start(f32[128]{0:T(128)} %param.18) | copy-start | bytes 1540
  85.7 26.0 %collective-permute-start.22 = (bf16[2,256,768]{2,1,0:T(8,128)(2,1)S(1)}, bf16[2,256,768]{2,1,0:T(8,128)(2,1)S(1)}, u32[]{:S(2)}, u32[]{:S(2)}) collective-permute-start(bf16[2,256,768]{2,1,0:T(8,128)(2,1)S(1)} %get-tuple-element.64), channel_id=1, source_target_pairs={{0,2},{1,3},{2,0},{3,1},{4,6},{5,7},{6,4},{7,5},{8,10},{9,11},{10,... | collective-permute-start | bytes 2359304 | tf_op jit(solution)/shard_map/ppermute | solution.py:256
  92.7 3.1 %collective-permute-start.20 = (bf16[128,2048]{1,0:T(8,128)(2,1)S(1)}, bf16[128,2048]{1,0:T(8,128)(2,1)S(1)}, u32[]{:S(2)}, u32[]{:S(2)}) collective-permute-start(bf16[128,2048]{1,0:T(8,128)(2,1)S(1)} %collective-permute-done.18.refs_1_), channel_id=1, source_target_pairs={{0,8},{8,0},{16,24},{24,16},{1,9},{9,1},{17,25},{25,17},{2,10},{10... | collective-permute-start | bytes 1572872 | tf_op jit(solution)/shard_map/ppermute | solution.py:256
  92.7 3.1 %collective-permute-start.19 = (bf16[128,2048]{1,0:T(8,128)(2,1)}, bf16[128,2048]{1,0:T(8,128)(2,1)S(1)}, u32[]{:S(2)}, u32[]{:S(2)}) collective-permute-start(bf16[128,2048]{1,0:T(8,128)(2,1)} %collective-permute-done.7.refs_0_), channel_id=1, source_target_pairs={{0,8},{8,0},{16,24},{24,16},{1,9},{9,1},{17,25},{25,17},{2,10},{10... | collective-permute-start | bytes 1572872 | tf_op jit(solution)/shard_map/ppermute | solution.py:256
  93.2 18.5 %collective-permute-start.23 = (bf16[1024,256]{1,0:T(8,128)(2,1)S(1)}, bf16[1024,256]{1,0:T(8,128)(2,1)S(1)}, u32[]{:S(2)}, u32[]{:S(2)}) collective-permute-start(bf16[1024,256]{1,0:T(8,128)(2,1)S(1)} %copy-done.4), channel_id=1, source_target_pairs={{0,1},{1,0},{2,3},{3,2},{4,5},{5,4},{6,7},{7,6},{8,9},{9,8},{10,11... | collective-permute-start | bytes 1572872 | tf_op jit(solution)/shard_map/ppermute | solution.py:256
  95.4 12.5 %collective-permute-start.17 = (bf16[1,256,256]{2,1,0:T(8,128)(2,1)S(1)}, bf16[1,256,256]{2,1,0:T(8,128)(2,1)S(1)}, u32[]{:S(2)}, u32[]{:S(2)}) collective-permute-start(bf16[1,256,256]{2,1,0:T(8,128)(2,1)S(1)} %fusion.6), channel_id=1, source_target_pairs={{0,4},{1,5},{2,6},{3,7},{4,0},{5,1},{6,2},{7,3},{8,12},{9,13},{10,... | collective-permute-start | bytes 393224 | tf_op jit(solution)/shard_map/ppermute | solution.py:256
  99.8 26.3 %collective-permute-start.25 = (bf16[2,128,1024]{2,1,0:T(8,128)(2,1)S(1)}, bf16[2,128,1024]{2,1,0:T(8,128)(2,1)S(1)}, u32[]{:S(2)}, u32[]{:S(2)}) collective-permute-start(bf16[2,128,1024]{2,1,0:T(8,128)(2,1)S(1)} %get-tuple-element.61), channel_id=1, source_target_pairs={{0,2},{1,3},{2,0},{3,1},{4,6},{5,7},{6,4},{7,5},{8,10},{9,11},{10,... | collective-permute-start | bytes 1572872 | tf_op jit(solution)/shard_map/ppermute | solution.py:256
  108.2 12.3 %collective-permute-start.21 = (bf16[1,256,256]{2,1,0:T(8,128)(2,1)S(1)}, bf16[1,256,256]{2,1,0:T(8,128)(2,1)S(1)}, u32[]{:S(2)}, u32[]{:S(2)}) collective-permute-start(bf16[1,256,256]{2,1,0:T(8,128)(2,1)S(1)} %bitcast.23), channel_id=1, source_target_pairs={{0,4},{1,5},{2,6},{3,7},{4,0},{5,1},{6,2},{7,3},{8,12},{9,13},{10,... | collective-permute-start | bytes 393224 | tf_op jit(solution)/shard_map/ppermute | solution.py:256
  120.5 13.1 %collective-permute-start.24 = (bf16[2,256,256]{2,1,0:T(8,128)(2,1)S(1)}, bf16[2,256,256]{2,1,0:T(8,128)(2,1)S(1)}, u32[]{:S(2)}, u32[]{:S(2)}) collective-permute-start(bf16[2,256,256]{2,1,0:T(8,128)(2,1)S(1)} %pad_maximum_fusion.2), channel_id=1, source_target_pairs={{0,2},{1,3},{2,0},{3,1},{4,6},{5,7},{6,4},{7,5},{8,10},{9,11},{10,... | collective-permute-start | bytes 786440 | tf_op jit(solution)/shard_map/ppermute | solution.py:256
  123.3 21.4 %collective-permute-start.29 = (bf16[1,256,768]{2,1,0:T(8,128)(2,1)S(1)}, bf16[1,256,768]{2,1,0:T(8,128)(2,1)S(1)}, u32[]{:S(2)}, u32[]{:S(2)}) collective-permute-start(bf16[1,256,768]{2,1,0:T(8,128)(2,1)S(1)} %fusion.3), channel_id=1, source_target_pairs={{0,4},{1,5},{2,6},{3,7},{4,0},{5,1},{6,2},{7,3},{8,12},{9,13},{10,... | collective-permute-start | bytes 1179656 | tf_op jit(solution)/shard_map/ppermute | solution.py:256
  124.1 25.9 %collective-permute-start.28 = (bf16[2,384,256]{2,1,0:T(8,128)(2,1)S(1)}, bf16[2,384,256]{2,1,0:T(8,128)(2,1)S(1)}, u32[]{:S(2)}, u32[]{:S(2)}) collective-permute-start(bf16[2,384,256]{2,1,0:T(8,128)(2,1)S(1)} %get-tuple-element.75), channel_id=1, source_target_pairs={{0,2},{1,3},{2,0},{3,1},{4,6},{5,7},{6,4},{7,5},{8,10},{9,11},{10,... | collective-permute-start | bytes 1179656 | tf_op jit(solution)/shard_map/ppermute | solution.py:256
  133.7 26.4 %collective-permute-start.26 = (bf16[4,256,256]{2,1,0:T(8,128)(2,1)S(1)}, bf16[4,256,256]{2,1,0:T(8,128)(2,1)S(1)}, u32[]{:S(2)}, u32[]{:S(2)}) collective-permute-start(bf16[4,256,256]{2,1,0:T(8,128)(2,1)S(1)} %pad_maximum_fusion.1), channel_id=1, source_target_pairs={{0,1},{1,0},{2,3},{3,2},{4,5},{5,4},{6,7},{7,6},{8,9},{9,8},{10,11... | collective-permute-start | bytes 1572872 | tf_op jit(solution)/shard_map/ppermute | solution.py:256
  135.8 24.1 %collective-permute-start.27 = (bf16[1,128,1024]{2,1,0:T(8,128)(2,1)S(1)}, bf16[1,128,1024]{2,1,0:T(8,128)(2,1)S(1)}, u32[]{:S(2)}, u32[]{:S(2)}) collective-permute-start(bf16[1,128,1024]{2,1,0:T(8,128)(2,1)S(1)} %fusion.4), channel_id=1, source_target_pairs={{0,4},{1,5},{2,6},{3,7},{4,0},{5,1},{6,2},{7,3},{8,12},{9,13},{10,... | collective-permute-start | bytes 786440 | tf_op jit(solution)/shard_map/ppermute | solution.py:256
  150.1 16.3 %collective-permute-start.30 = (bf16[1,384,256]{2,1,0:T(8,128)(2,1)S(1)}, bf16[1,384,256]{2,1,0:T(8,128)(2,1)S(1)}, u32[]{:S(2)}, u32[]{:S(2)}) collective-permute-start(bf16[1,384,256]{2,1,0:T(8,128)(2,1)S(1)} %fusion.5), channel_id=1, source_target_pairs={{0,4},{1,5},{2,6},{3,7},{4,0},{5,1},{6,2},{7,3},{8,12},{9,13},{10,... | collective-permute-start | bytes 589832 | tf_op jit(solution)/shard_map/ppermute | solution.py:256
  (13 other events, 94.2 us)

commit v13 on v11

--- a/solution.py
+++ b/solution.py
@@ -368,7 +368,11 @@
             out_shape=out_shape,
             scratch_shapes=scratch,
             compiler_params=pltpu.CompilerParams(vmem_limit_bytes=24 * 2**20),
-            cost_estimate=pl.CostEstimate(flops=0, bytes_accessed=0, transcendentals=0),
+            cost_estimate=pl.CostEstimate(
+                flops=0,
+                bytes_accessed=0,
+                transcendentals=0,
+            ),
             name="project",
         )(place, *operands, *weights)
         if fresh:
@@ -452,14 +456,14 @@
     stems = stem_kv[None]
     came = swap(stems, "branch", tour[0])
     second.add(stem_kv, w_rows[2][-1])
-    fourth = Halving(project(early + late, [2], second.send))
+    fourth = Halving(project(early + late, [2], second.send, came))
+    second.step(came)
     for step, bit in enumerate(tour[1:]):
-        stems = jnp.concatenate([stems, tie(came, third.send if step else fourth.send)], 0)
+        stems = jnp.concatenate([stems, tie(came, third.send if step else second.send)], 0)
         came = swap(stems, "branch", bit)
         if step == 0:
-            second.step(stems)
             fourth.step(stems)
-            third.add(stems)
+            third.add(stems, second.came)
             third.step()
     second.rest()
     third.rest()

time: 161 us -> 165 us (1.025)
  waiting for transfers between devices: 49.1 us -> 51.7 us
    ppermute x25, starting transfers between devices: 58.3 us -> 51 us  [swap(): return lax.ppermute(array, axis, [(i, i ^ bit) for i in range(size)])]
    ppermute x3, starting transfers between devices: 4.6 us -> 8.52 us  [shards(): sent = [lax.ppermute(piece, axes, second_hop) for piece in sent]]
    ppermute x3, starting transfers between devices: 8.87 us -> 12.5 us  [shards(): sent.append(lax.ppermute(piece, axes, first_hop))]
    ppermute x25, waiting for transfers between devices: 49.1 us -> 51.7 us  [swap(): return lax.ppermute(array, axis, [(i, i ^ bit) for i in range(size)])]
  transfers between devices with their start and end apart: 31 -> 31, of which waited for: 10 -> 9; matrix products, arithmetic and copies ran while one was open for 2% -> 2% of each run, Pallas kernels for 15% -> 15%
where the time goes in v13:
time: 165 us; the launch traced here: 163 us
  starting transfers between devices  72.1 us (44%)
  waiting for transfers between devices  51.7 us (31%)
  Pallas kernels  28.1 us (17%)
  local copies, waits for them, and re-layouts  7.33 us (4%)
  other arithmetic  3.66 us (2%)
    ppermute x25, waiting for transfers between devices, swap(): return lax.ppermute(array, axis, [(i, i ^ bit) for i in range(size)])  51.7 us
    ppermute x25, starting transfers between devices, swap(): return lax.ppermute(array, axis, [(i, i ^ bit) for i in range(size)])  51 us
    pallas_call x4, Pallas kernels, project(): pl.pallas_call(functools.partial(project_kernel, lines, groups, len(chunk...  16.9 us
    ppermute x3, starting transfers between devices, shards(): sent.append(lax.ppermute(piece, axes, first_hop))  12.5 us
    pallas_call x2, Pallas kernels, attend(): pl.pallas_call(kernel, grid=(1,), in_specs=in_specs, out_specs=anywhere,...  8.73 us
    ppermute x3, starting transfers between devices, shards(): sent = [lax.ppermute(piece, axes, second_hop) for piece in sent]  8.52 us
    unnamed x31, local copies, waits for them, and re-layouts  4.19 us
  transfers between devices with their start and end apart: 31, of which 9 were waited for; matrix products, arithmetic and copies ran while one was open for 2% of the time, Pallas kernels for 15%

profile of v13, /device:TPU:0, one launch (start us, length us, event | category | flops | bytes accessed | tf_op | source)
XLA Modules:
  0.0 163.3 jit_solution(5938451733880116014)
XLA Ops:
  0.7 2.8 %fusion = (bf16[128,2048]{1,0:T(8,128)(2,1)}, bf16[128,2048]{1,0:T(8,128)(2,1)}, bf16[128,2048]{1,0:T(8,128)(2,1)}) fusion(bf16[3,128,2048]{2,1,0:T(8,128)(2,1)} %param.10, f32[2048]{0:T(1024)S(1)} %dynamic_slice.3), kind=kLoop, calls=%fused_computation.3 | loop fusion | flops 2359296 | bytes 3153920 | tf_op jit(solution)/shard_map/convert_element_type | solution.py:306
  3.5 5.5 %collective-permute-start = (bf16[128,2048]{1,0:T(8,128)(2,1)}, bf16[128,2048]{1,0:T(8,128)(2,1)}, u32[]{:S(2)}, u32[]{:S(2)}) collective-permute-start(bf16[128,2048]{1,0:T(8,128)(2,1)} %get-tuple-element.74), channel_id=1, source_target_pairs={{0,0},{8,16},{16,8},{24,24},{1,1},{9,17},{17,9},{25,25},{2,26},{10... | collective-permute-start | bytes 1572872 | tf_op jit(solution)/shard_map/ppermute | solution.py:308
  9.1 3.0 %collective-permute-start.5 = (bf16[1024,640]{1,0:T(8,128)(2,1)S(1)}, bf16[1024,640]{1,0:T(8,128)(2,1)S(1)}, u32[]{:S(2)}, u32[]{:S(2)}) collective-permute-start(bf16[1024,640]{1,0:T(8,128)(2,1)S(1)} %slice.70.refs_1_.refs_6_), channel_id=1, source_target_pairs={{0,1},{1,0},{2,3},{3,2},{4,5},{5,4},{6,7},{7,6},{8,9},{9,8},{10,11... | collective-permute-start | bytes 3932168 | tf_op jit(solution)/shard_map/ppermute | solution.py:256
  13.2 2.2 %tables.1 = (f32[384,128]{1,0:T(8,128)}, f32[384,128]{1,0:T(8,128)}) custom-call(s32[1]{0:T(128)} %bitcast.device_ref, s32[24]{0:T(128)} %parents_ref.5), custom_call_target="tpu_custom_call" | custom-call | tf_op jit(solution)/shard_map/tables/pallas_call | solution.py:296
  16.4 1.7 %collective-permute-start.2 = (bf16[128,2048]{1,0:T(8,128)(2,1)}, bf16[128,2048]{1,0:T(8,128)(2,1)S(1)}, u32[]{:S(2)}, u32[]{:S(2)}) collective-permute-start(bf16[128,2048]{1,0:T(8,128)(2,1)} %get-tuple-element.41), channel_id=1, source_target_pairs={{0,0},{8,16},{16,8},{24,24},{1,1},{9,17},{17,9},{25,25},{2,26},{10... | collective-permute-start | bytes 1572872 | tf_op jit(solution)/shard_map/ppermute | solution.py:308
  18.1 1.7 %collective-permute-start.1 = (bf16[128,2048]{1,0:T(8,128)(2,1)}, bf16[128,2048]{1,0:T(8,128)(2,1)S(1)}, u32[]{:S(2)}, u32[]{:S(2)}) collective-permute-start(bf16[128,2048]{1,0:T(8,128)(2,1)} %collective-permute-done), channel_id=1, source_target_pairs={{0,0},{16,18},{8,12},{24,30},{1,1},{17,19},{9,13},{25,31},{26,16},... | collective-permute-start | bytes 1572872 | tf_op jit(solution)/shard_map/ppermute | solution.py:311
  19.8 5.4 %collective-permute-start.3 = (bf16[128,2048]{1,0:T(8,128)(2,1)}, bf16[128,2048]{1,0:T(8,128)(2,1)}, u32[]{:S(2)}, u32[]{:S(2)}) collective-permute-start(bf16[128,2048]{1,0:T(8,128)(2,1)} %get-tuple-element.42), channel_id=1, source_target_pairs={{0,0},{8,16},{16,8},{24,24},{1,1},{9,17},{17,9},{25,25},{2,26},{10... | collective-permute-start | bytes 1572872 | tf_op jit(solution)/shard_map/ppermute | solution.py:308
  26.7 12.2 %collective-permute-start.6 = (bf16[128,2048]{1,0:T(8,128)(2,1)S(1)}, bf16[128,2048]{1,0:T(8,128)(2,1)}, u32[]{:S(2)}, u32[]{:S(2)}) collective-permute-start(bf16[128,2048]{1,0:T(8,128)(2,1)S(1)} %collective-permute-done.1.refs_0_), channel_id=1, source_target_pairs={{0,16},{8,24},{16,0},{24,8},{1,17},{9,25},{17,1},{25,9},{2,18},{10... | collective-permute-start | bytes 1572872 | tf_op jit(solution)/shard_map/ppermute | solution.py:256
  38.9 2.1 %collective-permute-start.8 = (bf16[128,2048]{1,0:T(8,128)(2,1)S(1)}, bf16[128,2048]{1,0:T(8,128)(2,1)S(1)}, u32[]{:S(2)}, u32[]{:S(2)}) collective-permute-start(bf16[128,2048]{1,0:T(8,128)(2,1)S(1)} %collective-permute-done.1.refs_0_), channel_id=1, source_target_pairs={{0,8},{8,0},{16,24},{24,16},{1,9},{9,1},{17,25},{25,17},{2,10},{10... | collective-permute-start | bytes 1572872 | tf_op jit(solution)/shard_map/ppermute | solution.py:256
  41.8 4.9 %collective-permute-start.7 = (bf16[128,2048]{1,0:T(8,128)(2,1)}, bf16[128,2048]{1,0:T(8,128)(2,1)}, u32[]{:S(2)}, u32[]{:S(2)}) collective-permute-start(bf16[128,2048]{1,0:T(8,128)(2,1)} %collective-permute-done.4.refs_1_), channel_id=1, source_target_pairs={{0,16},{8,24},{16,0},{24,8},{1,17},{9,25},{17,1},{25,9},{2,18},{10... | collective-permute-start | bytes 1572872 | tf_op jit(solution)/shard_map/ppermute | solution.py:256
  46.7 5.4 %collective-permute-start.17 = (bf16[128,2048]{1,0:T(8,128)(2,1)}, bf16[128,2048]{1,0:T(8,128)(2,1)}, u32[]{:S(2)}, u32[]{:S(2)}) collective-permute-start(bf16[128,2048]{1,0:T(8,128)(2,1)} %collective-permute-done.3), channel_id=1, source_target_pairs={{0,0},{16,18},{8,12},{24,30},{1,1},{17,19},{9,13},{25,31},{26,16},... | collective-permute-start | bytes 1572872 | tf_op jit(solution)/shard_map/ppermute | solution.py:311
  54.5 1.6 %collective-permute-start.10 = (bf16[128,2048]{1,0:T(8,128)(2,1)}, bf16[128,2048]{1,0:T(8,128)(2,1)}, u32[]{:S(2)}, u32[]{:S(2)}) collective-permute-start(bf16[128,2048]{1,0:T(8,128)(2,1)} %collective-permute-done.6.refs_2_), channel_id=1, source_target_pairs={{0,8},{8,0},{16,24},{24,16},{1,9},{9,1},{17,25},{25,17},{2,10},{10... | collective-permute-start | bytes 1572872 | tf_op jit(solution)/shard_map/ppermute | solution.py:256
  56.1 5.0 %collective-permute-done.7.refs_3_ = bf16[128,2048]{1,0:T(8,128)(2,1)} collective-permute-done((bf16[128,2048]{1,0:T(8,128)(2,1)}, bf16[128,2048]{1,0:T(8,128)(2,1)}, u32[]{:S(2)}, u32[]{:S(2)}) %collective-permute-start.7) | collective-permute-done | bytes 524320 | tf_op jit(solution)/shard_map/ppermute | solution.py:256
  61.1 2.0 %collective-permute-start.11 = (bf16[128,2048]{1,0:T(8,128)(2,1)}, bf16[128,2048]{1,0:T(8,128)(2,1)}, u32[]{:S(2)}, u32[]{:S(2)}) collective-permute-start(bf16[128,2048]{1,0:T(8,128)(2,1)} %collective-permute-done.7.refs_3_), channel_id=1, source_target_pairs={{0,8},{8,0},{16,24},{24,16},{1,9},{9,1},{17,25},{25,17},{2,10},{10... | collective-permute-start | bytes 1572872 | tf_op jit(solution)/shard_map/ppermute | solution.py:256
  63.1 2.0 %collective-permute-start.18 = (bf16[128,2048]{1,0:T(8,128)(2,1)}, bf16[128,2048]{1,0:T(8,128)(2,1)S(1)}, u32[]{:S(2)}, u32[]{:S(2)}) collective-permute-start(bf16[128,2048]{1,0:T(8,128)(2,1)} %collective-permute-done.17.refs_0_), channel_id=1, source_target_pairs={{0,16},{8,24},{16,0},{24,8},{1,17},{9,25},{17,1},{25,9},{2,18},{10... | collective-permute-start | bytes 1572872 | tf_op jit(solution)/shard_map/ppermute | solution.py:256
  67.3 4.4 %project.4 = (bf16[2,256,256]{2,1,0:T(8,128)(2,1)S(1)}, f32[2,256,256]{2,1,0:T(8,128)S(1)}, bf16[1024,2048]{1,0:T(8,128)(2,1)S(1)}) custom-call(s32[2]{0:T(128)S(1)} %pad_add_fusion.place_ref, bf16[128,2048]{1,0:T(8,128)(2,1)S(1)} %copy-done.4, bf16[128,2048]{1,0:T(8,128)(2,1)} %collective-permute-done.4.refs_1_, ...), custom_call_target="tpu_custom_call" | custom-call | tf_op jit(solution)/shard_map/project/pallas_call | solution.py:363
  71.8 2.2 %collective-permute-start.13 = (bf16[2,256,256]{2,1,0:T(8,128)(2,1)S(1)}, bf16[2,256,256]{2,1,0:T(8,128)(2,1)S(1)}, u32[]{:S(2)}, u32[]{:S(2)}) collective-permute-start(bf16[2,256,256]{2,1,0:T(8,128)(2,1)S(1)} %get-tuple-element.47), channel_id=1, source_target_pairs={{0,2},{1,3},{2,0},{3,1},{4,6},{5,7},{6,4},{7,5},{8,10},{9,11},{10,... | collective-permute-start | bytes 786440 | tf_op jit(solution)/shard_map/ppermute | solution.py:256
  75.3 4.0 %project.5 = (bf16[2,256,640]{2,1,0:T(8,128)(2,1)S(1)}, f32[2,256,640]{2,1,0:T(8,128)S(1)}) custom-call(s32[2]{0:T(128)S(1)} %pad_add_fusion.place_ref, bf16[1024,2048]{1,0:T(8,128)(2,1)S(1)} %get-tuple-element.66.refs_0_, bf16[1024,640]{1,0:T(8,128)(2,1)S(1)} %slice.70.refs_1_.refs_6_, bf16[1024,640]{1,0:T(8,128)(2,1)S(1)} %collective-permute-done.5.refs_2_.refs_7_), custom_call_target="tpu_custom_call" | custom-call | tf_op jit(solution)/shard_map/project/pallas_call | solution.py:363
  82.1 1.9 %collective-permute-start.15 = (f32[3,128]{1,0:T(4,128)S(1)}, f32[3,128]{1,0:T(4,128)S(1)}, u32[]{:S(2)}, u32[]{:S(2)}) collective-permute-start(f32[3,128]{1,0:T(4,128)S(1)} %add.34), channel_id=1, source_target_pairs={{0,16},{8,24},{16,0},{24,8},{1,17},{9,25},{17,1},{25,9},{2,18},{10... | collective-permute-start | bytes 4616 | tf_op jit(solution)/shard_map/ppermute | solution.py:256
  85.7 2.1 %collective-permute-start.16 = (bf16[1,256,256]{2,1,0:T(8,128)(2,1)S(1)}, bf16[1,256,256]{2,1,0:T(8,128)(2,1)S(1)}, u32[]{:S(2)}, u32[]{:S(2)}) collective-permute-start(bf16[1,256,256]{2,1,0:T(8,128)(2,1)S(1)} %fusion.6), channel_id=1, source_target_pairs={{0,4},{1,5},{2,6},{3,7},{4,0},{5,1},{6,2},{7,3},{8,12},{9,13},{10,... | collective-permute-start | bytes 393224 | tf_op jit(solution)/shard_map/ppermute | solution.py:256
  87.8 4.5 %project.6 = (bf16[2,128,896]{2,1,0:T(8,128)(2,1)S(1)}, f32[2,128,896]{2,1,0:T(8,128)S(1)}, bf16[512,2048]{1,0:T(8,128)(2,1)S(1)}) custom-call(s32[2]{0:T(128)S(1)} %pad_add_fusion.place_ref, bf16[128,2048]{1,0:T(8,128)(2,1)} %collective-permute-done.17.refs_0_, bf16[128,2048]{1,0:T(8,128)(2,1)S(1)} %collective-permute-done.18.refs_1_, ...), custom_call_target="tpu_custom_call" | custom-call | tf_op jit(solution)/shard_map/project/pallas_call | solution.py:363
  93.8 4.9 %collective-permute-done.16.refs_2_ = bf16[1,256,256]{2,1,0:T(8,128)(2,1)S(1)} collective-permute-done((bf16[1,256,256]{2,1,0:T(8,128)(2,1)S(1)}, bf16[1,256,256]{2,1,0:T(8,128)(2,1)S(1)}, u32[]{:S(2)}, u32[]{:S(2)}) %collective-permute-start.16) | collective-permute-done | bytes 131104 | tf_op jit(solution)/shard_map/ppermute | solution.py:256
  98.9 3.4 %collective-permute-start.21 = (bf16[1,256,256]{2,1,0:T(8,128)(2,1)S(1)}, bf16[1,256,256]{2,1,0:T(8,128)(2,1)S(1)}, u32[]{:S(2)}, u32[]{:S(2)}) collective-permute-start(bf16[1,256,256]{2,1,0:T(8,128)(2,1)S(1)} %bitcast.21), channel_id=1, source_target_pairs={{0,4},{1,5},{2,6},{3,7},{4,0},{5,1},{6,2},{7,3},{8,12},{9,13},{10,... | collective-permute-start | bytes 393224 | tf_op jit(solution)/shard_map/ppermute | solution.py:256
  102.4 8.3 %collective-permute-done.21 = bf16[1,256,256]{2,1,0:T(8,128)(2,1)S(1)} collective-permute-done((bf16[1,256,256]{2,1,0:T(8,128)(2,1)S(1)}, bf16[1,256,256]{2,1,0:T(8,128)(2,1)S(1)}, u32[]{:S(2)}, u32[]{:S(2)}) %collective-permute-start.21) | collective-permute-done | bytes 131104 | tf_op jit(solution)/shard_map/ppermute | solution.py:256
  110.7 3.4 %collective-permute-start.26 = (bf16[1,256,640]{2,1,0:T(8,128)(2,1)S(1)}, bf16[1,256,640]{2,1,0:T(8,128)(2,1)S(1)}, u32[]{:S(2)}, u32[]{:S(2)}) collective-permute-start(bf16[1,256,640]{2,1,0:T(8,128)(2,1)S(1)} %fusion.3), channel_id=1, source_target_pairs={{0,4},{1,5},{2,6},{3,7},{4,0},{5,1},{6,2},{7,3},{8,12},{9,13},{10,... | collective-permute-start | bytes 983048 | tf_op jit(solution)/shard_map/ppermute | solution.py:256
  114.2 4.0 %project.7 = (bf16[2,384,384]{2,1,0:T(8,128)(2,1)S(1)}, f32[2,384,384]{2,1,0:T(8,128)S(1)}) custom-call(s32[2]{0:T(128)S(1)} %pad_add_fusion.place_ref, bf16[1024,2048]{1,0:T(8,128)(2,1)S(1)} %get-tuple-element.66.refs_0_, bf16[512,2048]{1,0:T(8,128)(2,1)S(1)} %get-tuple-element.67.refs_1_, bf16[1024,384]{1,0:T(8,128)(2,1)S(1)} %copy-done, ...), custom_call_target="tpu_custom_call" | custom-call | tf_op jit(solution)/shard_map/project/pallas_call | solution.py:363
  118.2 2.1 %collective-permute-start.29 = (bf16[2,384,384]{2,1,0:T(8,128)(2,1)S(1)}, bf16[2,384,384]{2,1,0:T(8,128)(2,1)S(1)}, u32[]{:S(2)}, u32[]{:S(2)}) collective-permute-start(bf16[2,384,384]{2,1,0:T(8,128)(2,1)S(1)} %get-tuple-element.70), channel_id=1, source_target_pairs={{0,2},{1,3},{2,0},{3,1},{4,6},{5,7},{6,4},{7,5},{8,10},{9,11},{10,... | collective-permute-start | bytes 1769480 | tf_op jit(solution)/shard_map/ppermute | solution.py:256
  120.3 8.4 %collective-permute-done.26.refs_4_ = bf16[1,256,640]{2,1,0:T(8,128)(2,1)S(1)} collective-permute-done((bf16[1,256,640]{2,1,0:T(8,128)(2,1)S(1)}, bf16[1,256,640]{2,1,0:T(8,128)(2,1)S(1)}, u32[]{:S(2)}, u32[]{:S(2)}) %collective-permute-start.26) | collective-permute-done | bytes 327712 | tf_op jit(solution)/shard_map/ppermute | solution.py:256
  131.5 14.3 %collective-permute-done.29.refs_3_ = bf16[2,384,384]{2,1,0:T(8,128)(2,1)S(1)} collective-permute-done((bf16[2,384,384]{2,1,0:T(8,128)(2,1)S(1)}, bf16[2,384,384]{2,1,0:T(8,128)(2,1)S(1)}, u32[]{:S(2)}, u32[]{:S(2)}) %collective-permute-start.29) | collective-permute-done | bytes 589856 | tf_op jit(solution)/shard_map/ppermute | solution.py:256
  146.8 5.0 %attend.2.refs_5_ = bf16[384,1024]{1,0:T(8,128)(2,1)} custom-call(s32[1]{0:T(128)} %bitcast.device_ref, s32[24]{0:T(128)S(1)} %copy-done.7, s32[24]{0:T(128)S(1)} %copy-done.8, f32[384,128]{1,0:T(8,128)S(1)} %broadcast_in_dim.31.inverse_ref, f32[1,640]{1,0:T(1,128)S(1)} %broadcast_in_dim.37.bias_ref, f32[384,128]{1,0:T(8,128)S(1)} %copy-done.1, ...), custom_call_target="tpu_custom_call" | custom-call | flops 1887436800 | bytes 491520 | tf_op jit(solution)/shard_map/attend/pallas_call | solution.py:495
  151.8 7.6 %collective-permute-done.30.refs_4_ = bf16[1,384,384]{2,1,0:T(8,128)(2,1)S(1)} collective-permute-done((bf16[1,384,384]{2,1,0:T(8,128)(2,1)S(1)}, bf16[1,384,384]{2,1,0:T(8,128)(2,1)S(1)}, u32[]{:S(2)}, u32[]{:S(2)}) %collective-permute-start.30) | collective-permute-done | bytes 294944 | tf_op jit(solution)/shard_map/ppermute | solution.py:256
  159.4 3.7 %attend.3 = bf16[384,1024]{1,0:T(8,128)(2,1)} custom-call(s32[1]{0:T(128)} %bitcast.device_ref, s32[24]{0:T(128)S(1)} %copy-done.7, s32[24]{0:T(128)S(1)} %copy-done.8, f32[384,128]{1,0:T(8,128)S(1)} %broadcast_in_dim.31.inverse_ref, f32[1,384]{1,0:T(1,128)S(1)} %broadcast_in_dim.32.bias_ref, ...), custom_call_target="tpu_custom_call", output_to_operand_aliasing={{}: (13, {})} | custom-call | flops 679477248 | bytes 294912 | tf_op jit(solution)/shard_map/attend/pallas_call | solution.py:495
  (99 shorter events, 21.2 us)
Async XLA Ops:
  3.5 12.9 %collective-permute-start = (bf16[128,2048]{1,0:T(8,128)(2,1)}, bf16[128,2048]{1,0:T(8,128)(2,1)}, u32[]{:S(2)}, u32[]{:S(2)}) collective-permute-start(bf16[128,2048]{1,0:T(8,128)(2,1)} %get-tuple-element.74), channel_id=1, source_target_pairs={{0,0},{8,16},{16,8},{24,24},{1,1},{9,17},{17,9},{25,25},{2,26},{10... | collective-permute-start | bytes 1572872 | tf_op jit(solution)/shard_map/ppermute | solution.py:308
  9.1 32.6 %collective-permute-start.5 = (bf16[1024,640]{1,0:T(8,128)(2,1)S(1)}, bf16[1024,640]{1,0:T(8,128)(2,1)S(1)}, u32[]{:S(2)}, u32[]{:S(2)}) collective-permute-start(bf16[1024,640]{1,0:T(8,128)(2,1)S(1)} %slice.70.refs_1_.refs_6_), channel_id=1, source_target_pairs={{0,1},{1,0},{2,3},{3,2},{4,5},{5,4},{6,7},{7,6},{8,9},{9,8},{10,11... | collective-permute-start | bytes 3932168 | tf_op jit(solution)/shard_map/ppermute | solution.py:256
  16.4 3.4 %collective-permute-start.2 = (bf16[128,2048]{1,0:T(8,128)(2,1)}, bf16[128,2048]{1,0:T(8,128)(2,1)S(1)}, u32[]{:S(2)}, u32[]{:S(2)}) collective-permute-start(bf16[128,2048]{1,0:T(8,128)(2,1)} %get-tuple-element.41), channel_id=1, source_target_pairs={{0,0},{8,16},{16,8},{24,24},{1,1},{9,17},{17,9},{25,25},{2,26},{10... | collective-permute-start | bytes 1572872 | tf_op jit(solution)/shard_map/ppermute | solution.py:308
  18.1 8.5 %collective-permute-start.1 = (bf16[128,2048]{1,0:T(8,128)(2,1)}, bf16[128,2048]{1,0:T(8,128)(2,1)S(1)}, u32[]{:S(2)}, u32[]{:S(2)}) collective-permute-start(bf16[128,2048]{1,0:T(8,128)(2,1)} %collective-permute-done), channel_id=1, source_target_pairs={{0,0},{16,18},{8,12},{24,30},{1,1},{17,19},{9,13},{25,31},{26,16},... | collective-permute-start | bytes 1572872 | tf_op jit(solution)/shard_map/ppermute | solution.py:311
  19.8 6.8 %collective-permute-start.3 = (bf16[128,2048]{1,0:T(8,128)(2,1)}, bf16[128,2048]{1,0:T(8,128)(2,1)}, u32[]{:S(2)}, u32[]{:S(2)}) collective-permute-start(bf16[128,2048]{1,0:T(8,128)(2,1)} %get-tuple-element.42), channel_id=1, source_target_pairs={{0,0},{8,16},{16,8},{24,24},{1,1},{9,17},{17,9},{25,25},{2,26},{10... | collective-permute-start | bytes 1572872 | tf_op jit(solution)/shard_map/ppermute | solution.py:308
  25.2 16.6 %collective-permute-start.4 = (bf16[128,2048]{1,0:T(8,128)(2,1)S(1)}, bf16[128,2048]{1,0:T(8,128)(2,1)}, u32[]{:S(2)}, u32[]{:S(2)}) collective-permute-start(bf16[128,2048]{1,0:T(8,128)(2,1)S(1)} %collective-permute-done.2), channel_id=1, source_target_pairs={{0,0},{16,18},{8,12},{24,30},{1,1},{17,19},{9,13},{25,31},{26,16},... | collective-permute-start | bytes 1572872 | tf_op jit(solution)/shard_map/ppermute | solution.py:311
  26.7 25.4 %collective-permute-start.6 = (bf16[128,2048]{1,0:T(8,128)(2,1)S(1)}, bf16[128,2048]{1,0:T(8,128)(2,1)}, u32[]{:S(2)}, u32[]{:S(2)}) collective-permute-start(bf16[128,2048]{1,0:T(8,128)(2,1)S(1)} %collective-permute-done.1.refs_0_), channel_id=1, source_target_pairs={{0,16},{8,24},{16,0},{24,8},{1,17},{9,25},{17,1},{25,9},{2,18},{10... | collective-permute-start | bytes 1572872 | tf_op jit(solution)/shard_map/ppermute | solution.py:256
  38.9 14.8 %collective-permute-start.8 = (bf16[128,2048]{1,0:T(8,128)(2,1)S(1)}, bf16[128,2048]{1,0:T(8,128)(2,1)S(1)}, u32[]{:S(2)}, u32[]{:S(2)}) collective-permute-start(bf16[128,2048]{1,0:T(8,128)(2,1)S(1)} %collective-permute-done.1.refs_0_), channel_id=1, source_target_pairs={{0,8},{8,0},{16,24},{24,16},{1,9},{9,1},{17,25},{25,17},{2,10},{10... | collective-permute-start | bytes 1572872 | tf_op jit(solution)/shard_map/ppermute | solution.py:256
  41.8 19.3 %collective-permute-start.7 = (bf16[128,2048]{1,0:T(8,128)(2,1)}, bf16[128,2048]{1,0:T(8,128)(2,1)}, u32[]{:S(2)}, u32[]{:S(2)}) collective-permute-start(bf16[128,2048]{1,0:T(8,128)(2,1)} %collective-permute-done.4.refs_1_), channel_id=1, source_target_pairs={{0,16},{8,24},{16,0},{24,8},{1,17},{9,25},{17,1},{25,9},{2,18},{10... | collective-permute-start | bytes 1572872 | tf_op jit(solution)/shard_map/ppermute | solution.py:256
  46.7 16.4 %collective-permute-start.17 = (bf16[128,2048]{1,0:T(8,128)(2,1)}, bf16[128,2048]{1,0:T(8,128)(2,1)}, u32[]{:S(2)}, u32[]{:S(2)}) collective-permute-start(bf16[128,2048]{1,0:T(8,128)(2,1)} %collective-permute-done.3), channel_id=1, source_target_pairs={{0,0},{16,18},{8,12},{24,30},{1,1},{17,19},{9,13},{25,31},{26,16},... | collective-permute-start | bytes 1572872 | tf_op jit(solution)/shard_map/ppermute | solution.py:311
  52.1 13.2 %collective-permute-start.9 = (bf16[128,2048]{1,0:T(8,128)(2,1)}, bf16[128,2048]{1,0:T(8,128)(2,1)}, u32[]{:S(2)}, u32[]{:S(2)}) collective-permute-start(bf16[128,2048]{1,0:T(8,128)(2,1)} %collective-permute-done.4.refs_1_), channel_id=1, source_target_pairs={{0,8},{8,0},{16,24},{24,16},{1,9},{9,1},{17,25},{25,17},{2,10},{10... | collective-permute-start | bytes 1572872 | tf_op jit(solution)/shard_map/ppermute | solution.py:256
  52.1 13.1 %collective-permute-start.12 = (bf16[1024,256]{1,0:T(8,128)(2,1)S(1)}, bf16[1024,256]{1,0:T(8,128)(2,1)}, u32[]{:S(2)}, u32[]{:S(2)}) collective-permute-start(bf16[1024,256]{1,0:T(8,128)(2,1)S(1)} %constant_dynamic-update-slice_fusion.refs_8_.refs_4_), channel_id=1, source_target_pairs={{0,1},{1,0},{2,3},{3,2},{4,5},{5,4},{6,7},{7,6},{8,9},{9,8},{10,11... | collective-permute-start | bytes 1572872 | tf_op jit(solution)/shard_map/ppermute | solution.py:256
  54.5 10.8 %collective-permute-start.10 = (bf16[128,2048]{1,0:T(8,128)(2,1)}, bf16[128,2048]{1,0:T(8,128)(2,1)}, u32[]{:S(2)}, u32[]{:S(2)}) collective-permute-start(bf16[128,2048]{1,0:T(8,128)(2,1)} %collective-permute-done.6.refs_2_), channel_id=1, source_target_pairs={{0,8},{8,0},{16,24},{24,16},{1,9},{9,1},{17,25},{25,17},{2,10},{10... | collective-permute-start | bytes 1572872 | tf_op jit(solution)/shard_map/ppermute | solution.py:256
  61.1 4.1 %collective-permute-start.11 = (bf16[128,2048]{1,0:T(8,128)(2,1)}, bf16[128,2048]{1,0:T(8,128)(2,1)}, u32[]{:S(2)}, u32[]{:S(2)}) collective-permute-start(bf16[128,2048]{1,0:T(8,128)(2,1)} %collective-permute-done.7.refs_3_), channel_id=1, source_target_pairs={{0,8},{8,0},{16,24},{24,16},{1,9},{9,1},{17,25},{25,17},{2,10},{10... | collective-permute-start | bytes 1572872 | tf_op jit(solution)/shard_map/ppermute | solution.py:256
  63.1 18.2 %collective-permute-start.18 = (bf16[128,2048]{1,0:T(8,128)(2,1)}, bf16[128,2048]{1,0:T(8,128)(2,1)S(1)}, u32[]{:S(2)}, u32[]{:S(2)}) collective-permute-start(bf16[128,2048]{1,0:T(8,128)(2,1)} %collective-permute-done.17.refs_0_), channel_id=1, source_target_pairs={{0,16},{8,24},{16,0},{24,8},{1,17},{9,25},{17,1},{25,9},{2,18},{10... | collective-permute-start | bytes 1572872 | tf_op jit(solution)/shard_map/ppermute | solution.py:256
  71.8 9.0 %collective-permute-start.13 = (bf16[2,256,256]{2,1,0:T(8,128)(2,1)S(1)}, bf16[2,256,256]{2,1,0:T(8,128)(2,1)S(1)}, u32[]{:S(2)}, u32[]{:S(2)}) collective-permute-start(bf16[2,256,256]{2,1,0:T(8,128)(2,1)S(1)} %get-tuple-element.47), channel_id=1, source_target_pairs={{0,2},{1,3},{2,0},{3,1},{4,6},{5,7},{6,4},{7,5},{8,10},{9,11},{10,... | collective-permute-start | bytes 786440 | tf_op jit(solution)/shard_map/ppermute | solution.py:256
  74.3 28.0 %collective-permute-start.23 = (bf16[1024,384]{1,0:T(8,128)(2,1)S(1)}, bf16[1024,384]{1,0:T(8,128)(2,1)S(1)}, u32[]{:S(2)}, u32[]{:S(2)}) collective-permute-start(bf16[1024,384]{1,0:T(8,128)(2,1)S(1)} %copy-done), channel_id=1, source_target_pairs={{0,1},{1,0},{2,3},{3,2},{4,5},{5,4},{6,7},{7,6},{8,9},{9,8},{10,11... | collective-permute-start | bytes 2359304 | tf_op jit(solution)/shard_map/ppermute | solution.py:256
  79.3 23.0 %collective-permute-start.22 = (bf16[2,256,640]{2,1,0:T(8,128)(2,1)S(1)}, bf16[2,256,640]{2,1,0:T(8,128)(2,1)S(1)}, u32[]{:S(2)}, u32[]{:S(2)}) collective-permute-start(bf16[2,256,640]{2,1,0:T(8,128)(2,1)S(1)} %get-tuple-element.50), channel_id=1, source_target_pairs={{0,2},{1,3},{2,0},{3,1},{4,6},{5,7},{6,4},{7,5},{8,10},{9,11},{10,... | collective-permute-start | bytes 1966088 | tf_op jit(solution)/shard_map/ppermute | solution.py:256
  80.8 1.3 collective-permute-start.14
  81.3 6.5 %collective-permute-start.20 = (bf16[128,2048]{1,0:T(8,128)(2,1)S(1)}, bf16[128,2048]{1,0:T(8,128)(2,1)S(1)}, u32[]{:S(2)}, u32[]{:S(2)}) collective-permute-start(bf16[128,2048]{1,0:T(8,128)(2,1)S(1)} %collective-permute-done.18.refs_1_), channel_id=1, source_target_pairs={{0,8},{8,0},{16,24},{24,16},{1,9},{9,1},{17,25},{25,17},{2,10},{10... | collective-permute-start | bytes 1572872 | tf_op jit(solution)/shard_map/ppermute | solution.py:256
  81.4 6.4 %collective-permute-start.19 = (bf16[128,2048]{1,0:T(8,128)(2,1)}, bf16[128,2048]{1,0:T(8,128)(2,1)S(1)}, u32[]{:S(2)}, u32[]{:S(2)}) collective-permute-start(bf16[128,2048]{1,0:T(8,128)(2,1)} %collective-permute-done.17.refs_0_), channel_id=1, source_target_pairs={{0,8},{8,0},{16,24},{24,16},{1,9},{9,1},{17,25},{25,17},{2,10},{10... | collective-permute-start | bytes 1572872 | tf_op jit(solution)/shard_map/ppermute | solution.py:256
  82.1 3.6 %collective-permute-start.15 = (f32[3,128]{1,0:T(4,128)S(1)}, f32[3,128]{1,0:T(4,128)S(1)}, u32[]{:S(2)}, u32[]{:S(2)}) collective-permute-start(f32[3,128]{1,0:T(4,128)S(1)} %add.34), channel_id=1, source_target_pairs={{0,16},{8,24},{16,0},{24,8},{1,17},{9,25},{17,1},{25,9},{2,18},{10... | collective-permute-start | bytes 4616 | tf_op jit(solution)/shard_map/ppermute | solution.py:256
  85.7 12.9 %collective-permute-start.16 = (bf16[1,256,256]{2,1,0:T(8,128)(2,1)S(1)}, bf16[1,256,256]{2,1,0:T(8,128)(2,1)S(1)}, u32[]{:S(2)}, u32[]{:S(2)}) collective-permute-start(bf16[1,256,256]{2,1,0:T(8,128)(2,1)S(1)} %fusion.6), channel_id=1, source_target_pairs={{0,4},{1,5},{2,6},{3,7},{4,0},{5,1},{6,2},{7,3},{8,12},{9,13},{10,... | collective-permute-start | bytes 393224 | tf_op jit(solution)/shard_map/ppermute | solution.py:256
  92.3 36.3 %collective-permute-start.25 = (bf16[2,128,896]{2,1,0:T(8,128)(2,1)S(1)}, bf16[2,128,896]{2,1,0:T(8,128)(2,1)S(1)}, u32[]{:S(2)}, u32[]{:S(2)}) collective-permute-start(bf16[2,128,896]{2,1,0:T(8,128)(2,1)S(1)} %get-tuple-element.56), channel_id=1, source_target_pairs={{0,2},{1,3},{2,0},{3,1},{4,6},{5,7},{6,4},{7,5},{8,10},{9,11},{10,... | collective-permute-start | bytes 1376264 | tf_op jit(solution)/shard_map/ppermute | solution.py:256
  98.9 11.8 %collective-permute-start.21 = (bf16[1,256,256]{2,1,0:T(8,128)(2,1)S(1)}, bf16[1,256,256]{2,1,0:T(8,128)(2,1)S(1)}, u32[]{:S(2)}, u32[]{:S(2)}) collective-permute-start(bf16[1,256,256]{2,1,0:T(8,128)(2,1)S(1)} %bitcast.21), channel_id=1, source_target_pairs={{0,4},{1,5},{2,6},{3,7},{4,0},{5,1},{6,2},{7,3},{8,12},{9,13},{10,... | collective-permute-start | bytes 393224 | tf_op jit(solution)/shard_map/ppermute | solution.py:256
  110.7 17.9 %collective-permute-start.26 = (bf16[1,256,640]{2,1,0:T(8,128)(2,1)S(1)}, bf16[1,256,640]{2,1,0:T(8,128)(2,1)S(1)}, u32[]{:S(2)}, u32[]{:S(2)}) collective-permute-start(bf16[1,256,640]{2,1,0:T(8,128)(2,1)S(1)} %fusion.3), channel_id=1, source_target_pairs={{0,4},{1,5},{2,6},{3,7},{4,0},{5,1},{6,2},{7,3},{8,12},{9,13},{10,... | collective-permute-start | bytes 983048 | tf_op jit(solution)/shard_map/ppermute | solution.py:256
  114.1 15.9 %collective-permute-start.24 = (bf16[2,256,256]{2,1,0:T(8,128)(2,1)S(1)}, bf16[2,256,256]{2,1,0:T(8,128)(2,1)S(1)}, u32[]{:S(2)}, u32[]{:S(2)}) collective-permute-start(bf16[2,256,256]{2,1,0:T(8,128)(2,1)S(1)} %pad_maximum_fusion.2), channel_id=1, source_target_pairs={{0,2},{1,3},{2,0},{3,1},{4,6},{5,7},{6,4},{7,5},{8,10},{9,11},{10,... | collective-permute-start | bytes 786440 | tf_op jit(solution)/shard_map/ppermute | solution.py:256
  118.2 12.8 %copy-start.12 = (f32[1024]{0:T(1024)S(1)}, f32[1024]{0:T(1024)}, u32[]{:S(2)}) copy-start(f32[1024]{0:T(1024)} %param.17) | copy-start | bytes 12292
  118.2 27.6 %collective-permute-start.29 = (bf16[2,384,384]{2,1,0:T(8,128)(2,1)S(1)}, bf16[2,384,384]{2,1,0:T(8,128)(2,1)S(1)}, u32[]{:S(2)}, u32[]{:S(2)}) collective-permute-start(bf16[2,384,384]{2,1,0:T(8,128)(2,1)S(1)} %get-tuple-element.70), channel_id=1, source_target_pairs={{0,2},{1,3},{2,0},{3,1},{4,6},{5,7},{6,4},{7,5},{8,10},{9,11},{10,... | collective-permute-start | bytes 1769480 | tf_op jit(solution)/shard_map/ppermute | solution.py:256
  130.1 16.1 %collective-permute-start.27 = (bf16[4,256,256]{2,1,0:T(8,128)(2,1)S(1)}, bf16[4,256,256]{2,1,0:T(8,128)(2,1)S(1)}, u32[]{:S(2)}, u32[]{:S(2)}) collective-permute-start(bf16[4,256,256]{2,1,0:T(8,128)(2,1)S(1)} %pad_maximum_fusion.1), channel_id=1, source_target_pairs={{0,1},{1,0},{2,3},{3,2},{4,5},{5,4},{6,7},{7,6},{8,9},{9,8},{10,11... | collective-permute-start | bytes 1572872 | tf_op jit(solution)/shard_map/ppermute | solution.py:256
  131.1 14.9 %collective-permute-start.28 = (bf16[1,128,896]{2,1,0:T(8,128)(2,1)S(1)}, bf16[1,128,896]{2,1,0:T(8,128)(2,1)S(1)}, u32[]{:S(2)}, u32[]{:S(2)}) collective-permute-start(bf16[1,128,896]{2,1,0:T(8,128)(2,1)S(1)} %fusion.5), channel_id=1, source_target_pairs={{0,4},{1,5},{2,6},{3,7},{4,0},{5,1},{6,2},{7,3},{8,12},{9,13},{10,... | collective-permute-start | bytes 688136 | tf_op jit(solution)/shard_map/ppermute | solution.py:256
  145.9 13.5 %collective-permute-start.30 = (bf16[1,384,384]{2,1,0:T(8,128)(2,1)S(1)}, bf16[1,384,384]{2,1,0:T(8,128)(2,1)S(1)}, u32[]{:S(2)}, u32[]{:S(2)}) collective-permute-start(bf16[1,384,384]{2,1,0:T(8,128)(2,1)S(1)} %fusion.4), channel_id=1, source_target_pairs={{0,4},{1,5},{2,6},{3,7},{4,0},{5,1},{6,2},{7,3},{8,12},{9,13},{10,... | collective-permute-start | bytes 884744 | tf_op jit(solution)/shard_map/ppermute | solution.py:256
  (14 other events, 69.4 us)
